TPU v7x, 32 devices: a whole 2x2x4 slice. The times are simulated.
32 devices in a mesh: dp: 4 (over y, core), ctx: 2 (over x), expert: 4 (over z).
Axes of the slice: x: 2, y: 2, z: 4, core: 2. Of those that a mesh axis runs over, the one named last changes fastest.
Arguments:
- tokens: bfloat16 [16, 1024, 512], P(('dp', 'expert'), 'ctx'), may hold values from -6 to 6
- cotangent: bfloat16 [16, 1024, 512], P(('dp', 'expert'), 'ctx'), may hold values from -6 to 6
- pad_mask: int32 [16, 1024], P(('dp', 'expert'), 'ctx'), may hold values from 0 to 1, as said below
- expert_ids: int32 [16, 1024, 2], P(('dp', 'expert'), 'ctx'), may hold values from 0 to 15, all different within a row
- slot_priority: int32 [16, 1024], P(('dp', 'expert'), 'ctx'), may hold values from 0 to 65535
- shared_slots: bfloat16 [4160, 512], P(('dp', 'ctx', 'expert')), may hold values from -1.5 to 1.5
- shared_first: float32 [4160, 512], P(('dp', 'ctx', 'expert')), may hold values from -1000 to 1000
- shared_second: float32 [4160, 512], P(('dp', 'ctx', 'expert')), may hold values from 0.1 to 200000
- shared_owner: int32 [2066], replicated, may hold values from 0 to 4159, as said below
- expert_slots: bfloat16 [4, 16384, 512], P('expert', ('dp', 'ctx')), may hold values from -5 to 5
- expert_first: float32 [4, 16384, 512], P('expert', ('dp', 'ctx')), may hold values from -1000 to 1000
- expert_second: float32 [4, 16384, 512], P('expert', ('dp', 'ctx')), may hold values from 0.01 to 200000
- expert_owner: int32 [4, 16384], P('expert'), may hold values from 0 to 16383, as said below
Outputs:
- block_out: bfloat16 [16, 1024, 512], P(('dp', 'expert'), 'ctx')
- tokens_grad: float32 [16, 1024, 512], P(('dp', 'expert'), 'ctx')
- shared_grad: float32 [4160, 512], P(('dp', 'ctx', 'expert'))
- shared_first_new: float32 [4160, 512], P(('dp', 'ctx', 'expert'))
- shared_second_new: float32 [4160, 512], P(('dp', 'ctx', 'expert'))
- shared_weight_new: float32 [4160, 512], P(('dp', 'ctx', 'expert'))
- expert_grad: float32 [4, 16384, 512], P('expert', ('dp', 'ctx'))
- expert_first_new: float32 [4, 16384, 512], P('expert', ('dp', 'ctx'))
- expert_second_new: float32 [4, 16384, 512], P('expert', ('dp', 'ctx'))
- expert_weight_new: float32 [4, 16384, 512], P('expert', ('dp', 'ctx'))
Inputs may be any that keep to these rules, and one draw needn't show every extreme that they name: `pad_mask`: in each image the zeros are its last positions, 1 to 64 of them; some image has exactly 64 and some exactly one. `shared_owner`: distinct slots; the rows owned by a device lie in its own 130 slots, and some device has all 130 of them filled. Unnamed slots are not read. `expert_owner`: each row is a permutation of the 16384 slots: every device of an expert index owns exactly 2048 of its rows, in any order.
All inputs are finite; a program needn't handle non-finite values.
Results may differ from a plain program's by a relative error of at most 0.014.
Values may be sent and summed in bfloat16 or wider, within the bound.
No kernel may reach another device: no remote copies, remote signals or barrier semaphores. Data moves between devices by JAX's collectives and lax.ppermute only.
A program may use at most 192 MiB of HBM per device.

v0:
```python
import math

import jax
import jax.numpy as jnp
from jax import lax
from jax.sharding import PartitionSpec as P

HEADS = 8
HEAD_DIM = 64
FF = 2048
EXP_DEV = 4


MASKED_SCORE = -1e30
MOMENT_DECAY = 0.5
LEARN_RATE = 0.05
WEIGHT_DECAY = 0.1
EPSILON = 1e-08
NORM_EPSILON = 1e-06


def layer_norm(values, gain_rows):
    center = values - jnp.mean(values, axis=-1, keepdims=True)
    spread = jnp.mean(center * center, axis=-1, keepdims=True)
    return center * lax.rsqrt(spread + NORM_EPSILON) * gain_rows


def routing(chosen, priority, live_rows, expert_count, capacity):
    tok_count = chosen.shape[0]
    token_ids = jnp.arange(tok_count, dtype=jnp.int32)
    ranking = jnp.argsort(priority * tok_count + token_ids)
    labels = jnp.arange(expert_count, dtype=jnp.int32)
    wanted = jnp.any(chosen[:, :, None] == labels[None, None, :], axis=1) & (
        live_rows[:, None] == 1
    )
    wanted = wanted.astype(jnp.int32)
    ranked = wanted[ranking]
    before = jnp.cumsum(ranked, axis=0) - ranked
    position = jnp.zeros_like(before).at[ranking].set(before)
    slot_taken = jnp.take_along_axis(position, chosen, axis=1)
    kept_pair = (slot_taken < capacity) & (live_rows[:, None] == 1)
    target = jnp.where(kept_pair, chosen * capacity + slot_taken, expert_count * capacity)
    owners = jnp.broadcast_to(token_ids[:, None], chosen.shape)
    source = (
        jnp.zeros((expert_count * capacity,), jnp.int32)
        .at[target.reshape(-1)]
        .set(owners.reshape(-1), mode="drop")
    )
    filled = (
        jnp.zeros((expert_count * capacity,), jnp.int32).at[target.reshape(-1)].set(1, mode="drop")
    )
    slot_index = jnp.where(kept_pair, chosen * capacity + slot_taken, 0)
    return (slot_index, kept_pair.astype(jnp.int32), source, filled)


def head_view(values):
    return values.reshape(values.shape[0], values.shape[1], HEADS, HEAD_DIM)


def score_block(queries, key_rows, keep_mask):
    score = jnp.einsum(
        "iqhe,ikhe->ihqk", queries, head_view(key_rows), preferred_element_type=jnp.float32
    ) * HEAD_DIM ** (-0.5)
    return jnp.where(keep_mask[:, None, None, :] > 0, score, MASKED_SCORE)


def stats_step(running, portion, queries):
    row_max, row_sum = running
    key_rows, keep_mask = portion
    score = score_block(queries, key_rows, keep_mask)
    keep_wide = keep_mask.astype(jnp.float32)[:, None, None, :]
    new_max = jnp.maximum(row_max, jnp.max(score, axis=-1))
    row_sum = row_sum * jnp.exp(row_max - new_max) + jnp.sum(
        jnp.exp(score - new_max[..., None]) * keep_wide, axis=-1
    )
    return (new_max, row_sum)


def value_step(running, portion, queries, log_sum):
    key_rows, value_rows, keep_mask = portion
    score = score_block(queries, key_rows, keep_mask)
    keep_wide = keep_mask.astype(jnp.float32)[:, None, None, :]
    attn_prob = (jnp.exp(score - log_sum[..., None]) * keep_wide).astype(jnp.bfloat16)
    return running + jnp.einsum(
        "ihqk,ikhe->iqhe", attn_prob, head_view(value_rows), preferred_element_type=jnp.float32
    )


def grad_step(grad_query, portion, queries, log_sum, grad_out, row_delta):
    key_rows, value_rows, keep_mask = portion
    score = score_block(queries, key_rows, keep_mask)
    keep_wide = keep_mask.astype(jnp.float32)[:, None, None, :]
    attn_prob = jnp.exp(score - log_sum[..., None]) * keep_wide
    prob_low = attn_prob.astype(jnp.bfloat16)
    grad_value = jnp.einsum(
        "ihqk,iqhe->ikhe", prob_low, grad_out, preferred_element_type=jnp.float32
    )
    grad_prob = jnp.einsum(
        "iqhe,ikhe->ihqk", grad_out, head_view(value_rows), preferred_element_type=jnp.float32
    )
    grad_score = (attn_prob * (grad_prob - row_delta[..., None])).astype(jnp.bfloat16)
    score_scale = HEAD_DIM ** (-0.5)
    grad_query = (
        grad_query
        + jnp.einsum(
            "ihqk,ikhe->iqhe", grad_score, head_view(key_rows), preferred_element_type=jnp.float32
        )
        * score_scale
    )
    grad_key = (
        jnp.einsum("ihqk,iqhe->ikhe", grad_score, queries, preferred_element_type=jnp.float32)
        * score_scale
    )
    return (grad_query, jnp.stack([grad_key, grad_value]))


def each_block(step_fn, running, arrays, block_len):
    total_len = arrays[0].shape[1]
    size_rows = math.gcd(total_len, block_len)

    def one_turn(number, current):
        offset = number * size_rows
        portion = tuple(
            (lax.dynamic_slice_in_dim(member, offset, size_rows, 1) for member in arrays)
        )
        return step_fn(current, portion)

    return lax.fori_loop(0, total_len // size_rows, one_turn, running)


def adam_update(gradient, first_old, second_old, weight):
    first_new = MOMENT_DECAY * first_old + (1.0 - MOMENT_DECAY) * gradient
    second_new = MOMENT_DECAY * second_old + (1.0 - MOMENT_DECAY) * gradient * gradient
    weight_new = weight - LEARN_RATE * (
        first_new / (jnp.sqrt(second_new) + EPSILON) + WEIGHT_DECAY * weight
    )
    return (first_new, second_new, weight_new)


def on_device(
    tokens,
    cotangent,
    pad_mask,
    expert_ids,
    slot_priority,
    shared_slots,
    shared_first,
    shared_second,
    shared_owner,
    expert_slots,
    expert_first,
    expert_second,
    expert_owner,
):
    img_count, part_len, features = tokens.shape
    tok_count = img_count * part_len
    expert_count = EXP_DEV * lax.axis_size("expert")
    capacity = (10 * tok_count + 4 * expert_count - 1) // (4 * expert_count)
    all_shared = lax.all_gather(shared_slots, ("dp", "ctx", "expert"), axis=0, tiled=True)
    all_expert = lax.all_gather(expert_slots, ("dp", "ctx"), axis=1, tiled=True)
    pieces = all_shared[shared_owner]
    w_qkv = pieces[: 3 * features]
    w_attn_out = pieces[3 * features : 4 * features]
    w_router = pieces[4 * features : 4 * features + expert_count]
    gain_one = pieces[4 * features + expert_count].astype(jnp.float32)
    gain_two = pieces[4 * features + expert_count + 1].astype(jnp.float32)
    expert_rows = all_expert[0][expert_owner[0]].reshape(EXP_DEV, 2, FF, features)
    w_in = expert_rows[:, 0]
    w_out = expert_rows[:, 1]
    inputs = tokens.reshape(tok_count, features).astype(jnp.float32)
    keep_mask = pad_mask.astype(jnp.bfloat16)
    keep_rows = pad_mask.reshape(tok_count).astype(jnp.float32)
    normed_one, norm_one_back = jax.vjp(layer_norm, inputs, gain_one)
    normed_low = normed_one.astype(jnp.bfloat16)
    qkv_rows = lax.dot_general(
        normed_low, w_qkv, (((1,), (1,)), ((), ())), preferred_element_type=jnp.float32
    ).astype(jnp.bfloat16)
    query_rows = qkv_rows[:, :features].reshape(img_count, part_len, features)
    key_rows = qkv_rows[:, features : 2 * features].reshape(img_count, part_len, features)
    value_rows = qkv_rows[:, 2 * features :].reshape(img_count, part_len, features)
    queries = head_view(query_rows)
    start_max = jnp.full((img_count, HEADS, part_len), MASKED_SCORE, jnp.float32)
    start_sum = jnp.zeros((img_count, HEADS, part_len), jnp.float32)
    start_out = jnp.zeros((img_count, part_len, HEADS, HEAD_DIM), jnp.float32)
    whole_keys, whole_values, whole_keep = (
        lax.all_gather(key_rows, "ctx", axis=1, tiled=True),
        lax.all_gather(value_rows, "ctx", axis=1, tiled=True),
        lax.all_gather(keep_mask, "ctx", axis=1, tiled=True),
    )
    row_max, row_sum = each_block(
        lambda running, portion: stats_step(running, portion, queries),
        (start_max, start_sum),
        (whole_keys, whole_keep),
        part_len,
    )
    log_sum = row_max + jnp.log(row_sum)
    attended = each_block(
        lambda running, portion: value_step(running, portion, queries, log_sum),
        start_out,
        (whole_keys, whole_values, whole_keep),
        part_len,
    )
    attended_low = attended.reshape(tok_count, features).astype(jnp.bfloat16)
    branch = jnp.dot(attended_low, w_attn_out, preferred_element_type=jnp.float32)
    residual = inputs + branch
    normed_two, norm_two_back = jax.vjp(layer_norm, residual, gain_two)
    mixed_low = normed_two.astype(jnp.bfloat16)
    logits = lax.dot_general(
        mixed_low, w_router, (((1,), (1,)), ((), ())), preferred_element_type=jnp.float32
    )
    router_prob = jax.nn.softmax(logits, axis=-1)
    chosen = expert_ids.reshape(tok_count, 2)
    slot_index, kept_pair, source, filled = routing(
        chosen,
        slot_priority.reshape(tok_count),
        pad_mask.reshape(tok_count),
        expert_count,
        capacity,
    )
    filled_low = filled.astype(jnp.bfloat16)
    dispatched = (mixed_low[source] * filled_low[:, None]).reshape(expert_count, capacity, features)
    received = lax.all_to_all(dispatched, "expert", split_axis=0, concat_axis=1, tiled=True)
    hidden = jnp.einsum("ecd,efd->ecf", received, w_in, preferred_element_type=jnp.float32)
    active, gelu_back = jax.vjp(lambda pre_act: jax.nn.gelu(pre_act, approximate=False), hidden)
    active_low = active.astype(jnp.bfloat16)
    result = jnp.einsum(
        "ecf,efd->ecd", active_low, w_out, preferred_element_type=jnp.float32
    ).astype(jnp.bfloat16)
    returned = lax.all_to_all(result, "expert", split_axis=1, concat_axis=0, tiled=True).reshape(
        expert_count * capacity, features
    )
    kept_float = kept_pair.astype(jnp.float32)
    gate_value = jnp.take_along_axis(router_prob, chosen, axis=1) * kept_float
    picked = returned[slot_index].astype(jnp.float32)
    mixture = jnp.sum(gate_value[:, :, None] * picked, axis=1)
    output = (residual + mixture).astype(jnp.bfloat16).reshape(tokens.shape)
    grad_rows = cotangent.reshape(tok_count, features).astype(jnp.float32) * keep_rows[:, None]
    grad_gate = jnp.sum(grad_rows[:, None, :] * picked, axis=-1) * kept_float
    labels = jnp.arange(expert_count, dtype=jnp.int32)
    grad_prob = jnp.sum(
        (chosen[:, :, None] == labels[None, None, :]).astype(jnp.float32) * grad_gate[:, :, None],
        axis=1,
    )
    grad_logits = router_prob * (
        grad_prob - jnp.sum(grad_prob * router_prob, axis=-1, keepdims=True)
    )
    grad_logits_low = grad_logits.astype(jnp.bfloat16)
    slot_expert = jnp.arange(expert_count * capacity, dtype=jnp.int32) // capacity
    slot_gate = jnp.take_along_axis(router_prob[source], slot_expert[:, None], axis=1)[
        :, 0
    ] * filled.astype(jnp.float32)
    grad_result = (
        (grad_rows[source] * slot_gate[:, None])
        .astype(jnp.bfloat16)
        .reshape(expert_count, capacity, features)
    )
    grad_received = lax.all_to_all(grad_result, "expert", split_axis=0, concat_axis=1, tiled=True)
    grad_active = jnp.einsum(
        "ecd,efd->ecf", grad_received, w_out, preferred_element_type=jnp.float32
    )
    grad_hidden = gelu_back(grad_active)[0].astype(jnp.bfloat16)
    grad_w_out = jnp.einsum(
        "ecf,ecd->efd", active_low, grad_received, preferred_element_type=jnp.float32
    )
    grad_w_in = jnp.einsum(
        "ecf,ecd->efd", grad_hidden, received, preferred_element_type=jnp.float32
    )
    grad_sent = jnp.einsum(
        "ecf,efd->ecd", grad_hidden, w_in, preferred_element_type=jnp.float32
    ).astype(jnp.bfloat16)
    grad_back = lax.all_to_all(
        grad_sent, "expert", split_axis=1, concat_axis=0, tiled=True
    ).reshape(expert_count * capacity, features)
    grad_mixed = jnp.sum(grad_back[slot_index].astype(jnp.float32) * kept_float[:, :, None], axis=1)
    grad_mixed = grad_mixed + jnp.dot(grad_logits_low, w_router, preferred_element_type=jnp.float32)
    grad_router = lax.dot_general(
        grad_logits_low, mixed_low, (((0,), (0,)), ((), ())), preferred_element_type=jnp.float32
    )
    grad_residual_part, grad_gain_two = norm_two_back(grad_mixed)
    grad_residual = grad_rows + grad_residual_part
    grad_branch = grad_residual.astype(jnp.bfloat16)
    grad_w_attn_out = lax.dot_general(
        attended_low, grad_branch, (((0,), (0,)), ((), ())), preferred_element_type=jnp.float32
    )
    grad_attended = lax.dot_general(
        grad_branch, w_attn_out, (((1,), (1,)), ((), ())), preferred_element_type=jnp.float32
    ).astype(jnp.bfloat16)
    grad_out = head_view(grad_attended.reshape(img_count, part_len, features))
    row_delta = jnp.transpose(jnp.sum(grad_out.astype(jnp.float32) * attended, axis=-1), (0, 2, 1))
    start_grad = jnp.zeros((img_count, part_len, HEADS, HEAD_DIM), jnp.float32)
    whole_grads = jnp.zeros((2, img_count, whole_keys.shape[1], HEADS, HEAD_DIM), jnp.float32)

    def grad_turn(number, current):
        grad_query, grads_all = current
        offset = number * part_len
        portion = tuple(
            (
                lax.dynamic_slice_in_dim(member, offset, part_len, 1)
                for member in (whole_keys, whole_values, whole_keep)
            )
        )
        grad_query, grad_block = grad_step(
            grad_query, portion, queries, log_sum, grad_out, row_delta
        )
        grads_all = lax.dynamic_update_slice_in_dim(grads_all, grad_block, offset, 2)
        return (grad_query, grads_all)

    grad_query, whole_grads = lax.fori_loop(
        0, whole_keys.shape[1] // part_len, grad_turn, (start_grad, whole_grads)
    )
    grad_pair = lax.psum_scatter(whole_grads, "ctx", scatter_dimension=2, tiled=True)
    grad_qkv = jnp.concatenate(
        [
            grad_query.reshape(tok_count, features),
            grad_pair[0].reshape(tok_count, features),
            grad_pair[1].reshape(tok_count, features),
        ],
        axis=1,
    ).astype(jnp.bfloat16)
    grad_w_qkv = lax.dot_general(
        grad_qkv, normed_low, (((0,), (0,)), ((), ())), preferred_element_type=jnp.float32
    )
    grad_normed = jnp.dot(grad_qkv, w_qkv, preferred_element_type=jnp.float32)
    grad_input_part, grad_gain_one = norm_one_back(grad_normed)
    grad_tokens = (grad_residual + grad_input_part).reshape(tokens.shape)
    shared_pieces = jnp.concatenate(
        [grad_w_qkv, grad_w_attn_out, grad_router, grad_gain_one[None, :], grad_gain_two[None, :]],
        axis=0,
    )
    shared_layout = jnp.zeros(all_shared.shape, jnp.float32).at[shared_owner].set(shared_pieces)
    shared_grad = lax.psum_scatter(
        shared_layout, ("dp", "ctx", "expert"), scatter_dimension=0, tiled=True
    )
    expert_pieces = jnp.stack([grad_w_in, grad_w_out], axis=1).reshape(EXP_DEV * 2 * FF, features)
    expert_layout = (
        jnp.zeros(all_expert.shape, jnp.float32).at[0, expert_owner[0]].set(expert_pieces)
    )
    expert_grad = lax.psum_scatter(expert_layout, ("dp", "ctx"), scatter_dimension=1, tiled=True)
    shared_first_new, shared_second_new, shared_weight_new = adam_update(
        shared_grad, shared_first, shared_second, shared_slots.astype(jnp.float32)
    )
    expert_first_new, expert_second_new, expert_weight_new = adam_update(
        expert_grad, expert_first, expert_second, expert_slots.astype(jnp.float32)
    )
    return (
        output,
        grad_tokens,
        shared_grad,
        shared_first_new,
        shared_second_new,
        shared_weight_new,
        expert_grad,
        expert_first_new,
        expert_second_new,
        expert_weight_new,
    )


def solution(mesh):
    return jax.shard_map(
        on_device,
        mesh=mesh,
        in_specs=(
            P(("dp", "expert"), "ctx", None),
            P(("dp", "expert"), "ctx", None),
            P(("dp", "expert"), "ctx"),
            P(("dp", "expert"), "ctx", None),
            P(("dp", "expert"), "ctx"),
            P(("dp", "ctx", "expert"), None),
            P(("dp", "ctx", "expert"), None),
            P(("dp", "ctx", "expert"), None),
            P(),
            P("expert", ("dp", "ctx"), None),
            P("expert", ("dp", "ctx"), None),
            P("expert", ("dp", "ctx"), None),
            P("expert", None),
        ),
        out_specs=(
            P(("dp", "expert"), "ctx", None),
            P(("dp", "expert"), "ctx", None),
            P(("dp", "ctx", "expert"), None),
            P(("dp", "ctx", "expert"), None),
            P(("dp", "ctx", "expert"), None),
            P(("dp", "ctx", "expert"), None),
            P("expert", ("dp", "ctx"), None),
            P("expert", ("dp", "ctx"), None),
            P("expert", ("dp", "ctx"), None),
            P("expert", ("dp", "ctx"), None),
        ),
        check_vma=False,
    )
```

profile of v0, /device:TPU:0, one launch (start us, length us, event | category | flops | bytes accessed | tf_op | source)
XLA Modules:
  0.0 968.8 jit_solution(7651686530202669124)
XLA Ops:
  10.9 65.7 %all-gather.14.cloned.1.call-done = bf16[32,130,512]{2,1,0:T(8,128)(2,1)} async-done(((bf16[1,130,512]{2,1,0:T(8,128)(2,1)}), bf16[32,130,512]{2,1,0:T(8,128)(2,1)}) %all-gather.14.cloned.1.call-update) | async-done | bytes 4259856 | tf_op jit(solution)/shard_map/all_gather | solution.py:159
  76.6 7.1 reshape.957
  83.7 9.9 %gather_fusion = bf16[2066,512]{1,0:T(8,128)(2,1)S(1)} fusion(bf16[4160,512]{1,0:T(8,128)(2,1)} %reshape.957, s32[3072]{0:T(1024)S(1)} %pad_clamp_fusion), kind=kCustom, calls=%fused_computation | custom fusion | bytes 4239432 | tf_op jit(solution)/shard_map/gather | solution.py:161
  107.0 7.1 gather_fusion.9
  129.7 10.6 %all-gather.10.cloned.1.call-done = bf16[1024,512]{1,0:T(8,128)(2,1)} async-done(((bf16[512,512]{1,0:T(8,128)(2,1)}), bf16[1024,512]{1,0:T(8,128)(2,1)}) %all-gather.10.cloned.1.call-update) | async-done | bytes 1048592 | tf_op jit(solution)/shard_map/all_gather | solution.py:187
  141.8 9.3 while.46
  151.1 13.6 %while.47 = (s32[]{:T(128)}, f32[1,512,8,64]{1,3,2,0:T(8,128)}, bf16[1,1024,512]{1,2,0:T(8,128)(2,1)S(1)}, bf16[1,1024]{1,0:T(2,128)(2,1)S(1)}, bf16[1,1024,512]...) while((s32[]{:T(128)}, f32[1,512,8,64]{1,3,2,0:T(8,128)}, ...), condition=%wide.region_7.8_spmd.clone, body=%wide.region_6.7_spmd.clone.sunk | while | flops 547883008 | bytes 5790905 | solution.py:128
  152.2 5.6 fusion.167
  159.0 5.7 fusion.167
  195.1 8.2 gather_fusion.10
  206.5 6.7 all-to-all-done
  219.8 28.8 %all-to-all-done.2 = bf16[16,80,512]{2,1,0:T(8,128)(2,1)} async-done(((bf16[16,80,512]{2,1,0:T(8,128)(2,1)}), bf16[16,80,512]{2,1,0:T(8,128)(2,1)}, u32[]{:S(2)}, u32[]{:S(2)}) %all-to-all-start.2) | async-done | bytes 1310752 | tf_op jit(solution)/shard_map/all_to_all | solution.py:257
  250.0 75.0 %gather_fusion.3 = bf16[16384,512]{1,0:T(8,128)(2,1)} fusion(bf16[16384,512]{1,0:T(8,128)(2,1)} %bitcast.316, s32[16384]{0:T(1024)S(1)} %broadcast_clamp_fusion), kind=kCustom, calls=%fused_computation.3 | custom fusion | bytes 33619968 | tf_op jit(solution)/shard_map/gather | solution.py:167
  325.0 8.6 fusion.50
  333.6 24.8 %multiply_convert_fusion.7 = (bf16[4,320,2048]{2,1,0:T(8,128)(2,1)}, f32[4,320,2048]{2,1,0:T(8,128)}) fusion(f32[4,320,2048]{2,1,0:T(8,128)S(1)} %get-tuple-element.782, u8[320,2048]{1,0:T(8,128)(4,1)S(1)} %get-tuple-element.698, u8[320,2048]{1,0:T(8,128)(4,1)S(1)} %get-tuple-element.697), kind=kLoop, calls=%fused_computation.76 | loop fusion | flops 183500800 | bytes 27525120 | tf_op jit(solution)/shard_map/convert_element_type | solution.py:225
  358.5 14.8 %add_convert_fusion = bf16[4,320,2048]{2,1,0:T(8,128)(2,1)} fusion(f32[4,320,2048]{2,1,0:T(8,128)} %get-tuple-element.763, f32[4,320,2048]{2,1,0:T(8,128)} %copy-done.20, bf16[4,320,512]{2,1,0:T(8,128)(2,1)S(1)} %bitcast.338, bf16[4,2,2048,512]{3,2,1,0:T(8,128)(2,1)} %bitcast.327), kind=kOutput, calls=%fused_computation.75 | convolution fusion | flops 2721054720 | bytes 35913728 | tf_op jit(solution)/shard_map/ecd,efd->ecf/dot_general | solution.py:258
  373.3 7.8 fusion.52
  386.7 7.8 fusion.51
  396.7 20.8 %all-to-all-done.3 = bf16[4,320,512]{2,0,1:T(4,128)(2,1)S(1)} async-done(((bf16[4,320,512]{2,0,1:T(4,128)(2,1)}), bf16[4,320,512]{2,0,1:T(4,128)(2,1)S(1)}, u32[]{:S(2)}, u32[]{:S(2)}) %all-to-all-start.3) | async-done | bytes 1310752 | tf_op jit(solution)/shard_map/all_to_all | solution.py:271
  422.8 9.1 gather_fusion.8
  433.5 19.2 %all-to-all-done.1 = bf16[4,320,512]{2,0,1:T(4,128)(2,1)} async-done(((bf16[4,320,512]{2,0,1:T(4,128)(2,1)}), bf16[4,320,512]{2,0,1:T(4,128)(2,1)}, u32[]{:S(2)}, u32[]{:S(2)}) %all-to-all-start.1) | async-done | bytes 1310752 | tf_op jit(solution)/shard_map/all_to_all | solution.py:229
  497.5 25.2 %while.48 = (s32[]{:T(128)}, f32[1,512,8,64]{1,3,2,0:T(8,128)}, f32[2,1,1024,8,64]{2,4,3,1,0:T(8,128)}, bf16[1,1024,512]{1,2,0:T(8,128)(2,1)S(1)}, bf16[1,1024]{...) while((s32[]{:T(128)}, f32[1,512,8,64]{1,3,2,0:T(8,128)}, ...), condition=%wide.region_28.29_spmd.clone, body=%wide.region_27.28_spmd.clone.sunk | while | flops 1368918016 | bytes 96003936 | solution.py:308
  523.4 13.4 %convolution_bitcast_fusion = f32[4,1,2048,512]{3,2,0,1:T(8,128)} fusion(bf16[4,320,2048]{2,1,0:T(8,128)(2,1)} %get-tuple-element.762, bf16[4,320,512]{2,1,0:T(8,128)(2,1)} %bitcast.339), kind=kOutput, calls=%fused_computation.95 | convolution fusion | flops 2684354560 | bytes 23330816 | tf_op jit(solution)/shard_map/ecf,ecd->efd/dot_general | solution.py:262
  536.8 8.4 convolution_bitcast_fusion.1
  545.2 13.1 %pad_maximum_fusion = f32[4,2,2048,512]{3,2,0,1:T(8,128)S(1)} fusion(f32[4,1,2048,512]{3,2,0,1:T(8,128)} %convolution_bitcast_fusion, f32[4,1,2048,512]{3,2,0,1:T(8,128)} %convolution_bitcast_fusion.1), kind=kLoop, calls=%fused_computation.65 | loop fusion | flops 8388608 | bytes 67108864 | tf_op jit(solution)/shard_map/stack | solution.py:334
  558.3 11.3 %copy.207 = f32[4,2,2048,512]{3,2,1,0:T(8,128)} copy(f32[4,2,2048,512]{3,2,0,1:T(8,128)S(1)} %pad_maximum_fusion) | data formatting | bytes 67108864 | tf_op jit(solution)/shard_map/stack | solution.py:334
  569.6 81.7 %scatter_custom_fusion.4 = f32[16384,512]{1,0:T(8,128)} fusion(s32[16384]{0:T(1024)S(1)} %broadcast_select_fusion, f32[16384,512]{1,0:T(8,128)} %bitcast.324, f32[]{:T(128)} %constant.278.clone.1), kind=kCustom, calls=%fused_computation.66 | custom fusion | bytes 33554944
  665.5 11.0 %concatenate.11 = f32[2066,512]{1,0:T(8,128)} concatenate(f32[1536,512]{1,0:T(8,128)} %fusion.67, f32[512,512]{1,0:T(8,128)S(1)} %fusion.115, f32[16,512]{1,0:T(8,128)S(1)} %fusion.116, f32[1,512]{1,0:T(1,128)S(1)} %bitcast.382, f32[1,512]{1,0:T(1,128)S(1)} %bitcast.383), dimensions={0} | concatenate | bytes 8462336 | tf_op jit(solution)/shard_map/concatenate | solution.py:326
  676.5 19.0 %scatter_custom_fusion.3 = f32[4160,512]{1,0:T(8,128)} fusion(s32[2066]{0:T(1024)} %copy-done.59, f32[2066,512]{1,0:T(8,128)} %concatenate.11, f32[]{:T(128)} %constant.278.clone.1), kind=kCustom, calls=%fused_computation.101 | custom fusion | bytes 8520192 | tf_op jit(solution)/shard_map/scatter | solution.py:330
  695.5 195.9 %fusion = f32[136,512]{1,0:T(8,128)S(1)} fusion(f32[4160,512]{1,0:T(8,128)} %scatter_custom_fusion.3), kind=kCustom, calls=%all-reduce-scatter | all-reduce-scatter fusion | flops 2228225 | bytes 8798208
  905.1 46.6 %reduce-scatter.7.cloned.1.call-done = f32[1,2048,512]{2,1,0:T(8,128)} async-done(((f32[1,16384,512]{2,1,0:T(8,128)}), f32[1,2048,512]{2,1,0:T(8,128)}) %reduce-scatter.7.cloned.1.call-update) | async-done | bytes 4194320 | tf_op jit(solution)/shard_map/reduce_scatter | solution.py:338
  951.7 9.8 %convert_subtract_fusion = (f32[1,2048,512]{2,1,0:T(8,128)}, f32[1,2048,512]{2,1,0:T(8,128)}, f32[1,2048,512]{2,1,0:T(8,128)}) fusion(bf16[1,2048,512]{2,1,0:T(8,128)(2,1)} %param.28, f32[1,2048,512]{2,1,0:T(8,128)} %reduce-scatter.7.cloned.1.call-done, f32[1,2048,512]{2,1,0:T(8,128)} %param.30, f32[1,2048,512]{2,1,0:T(8,128)} %param.29), kind=kLoop, calls=%fused_computation.99 | loop fusion | flops 13631488 | bytes 27262976 | tf_op jit(solution)/shard_map/sub | solution.py:134
  (396 shorter events, 198.6 us)
Async XLA Ops:
  7.2 69.4 %all-gather.14.cloned.1.call-start = ((), (), s32[]{:S(2)}) async-start(), calls=%async_computation.11 | async-start | bytes 4595712 | tf_op jit(solution)/shard_map/all_gather | solution.py:159
  7.9 120.3 %all-gather.12.cloned.1.call-start = ((), (), s32[]{:S(2)}) async-start(), calls=%async_computation.10 | async-start | bytes 1572864 | tf_op jit(solution)/shard_map/all_gather | solution.py:186
  9.2 157.6 %copy-start.14 = (bf16[1,512,512]{1,2,0:T(8,128)(2,1)}, bf16[1,512,512]{1,2,0:T(8,128)(2,1)S(1)}, u32[]{:S(2)}) copy-start(bf16[1,512,512]{1,2,0:T(8,128)(2,1)S(1)} %copy.173) | copy-start | bytes 1572868
  10.7 83.0 %copy-start.60 = (f32[512]{0:T(512)}, f32[512]{0:T(512)S(1)}, u32[]{:S(2)}) copy-start(f32[512]{0:T(512)S(1)} %broadcast_multiply_fusion.3) | copy-start | bytes 6148
  10.9 82.7 %copy-start.75 = (f32[512]{0:T(512)}, f32[512]{0:T(512)S(1)}, u32[]{:S(2)}) copy-start(f32[512]{0:T(512)S(1)} %fusion.65) | copy-start | bytes 6148
  10.9 82.8 %copy-start.71 = (f32[512]{0:T(512)}, f32[512]{0:T(512)S(1)}, u32[]{:S(2)}) copy-start(f32[512]{0:T(512)S(1)} %fusion.101) | copy-start | bytes 6148
  93.7 75.1 %copy-start.67 = (f32[1,512]{1,0:T(1,128)}, f32[1,512]{1,0:T(1,128)S(1)}, u32[]{:S(2)}) copy-start(f32[1,512]{1,0:T(1,128)S(1)} %get-tuple-element.770) | copy-start | bytes 6148
  96.1 44.2 %all-gather.10.cloned.1.call-start = ((), (), s32[]{:S(2)}) async-start(), calls=%async_computation.9 | async-start | bytes 1572864 | tf_op jit(solution)/shard_map/all_gather | solution.py:187
  96.8 153.1 %all-gather.8.cloned.1.call-start = ((), (), s32[]{:S(2)}) async-start(), calls=%async_computation.6 | async-start | bytes 18874368 | tf_op jit(solution)/shard_map/all_gather | solution.py:160
  123.2 60.1 %copy-start.64 = (f32[1,512]{1,0:T(1,128)}, f32[1,512]{1,0:T(1,128)S(1)}, u32[]{:S(2)}) copy-start(f32[1,512]{1,0:T(1,128)S(1)} %get-tuple-element.778) | copy-start | bytes 6148
  177.4 35.8 %all-to-all-start = ((bf16[16,80,512]{2,1,0:T(8,128)(2,1)}), bf16[16,80,512]{2,1,0:T(8,128)(2,1)S(1)}, u32[]{:S(2)}, u32[]{:S(2)}) async-start(bf16[16,80,512]{2,1,0:T(8,128)(2,1)} %broadcast_multiply_fusion), calls=%async_computation | async-start | bytes 2621440 | tf_op jit(solution)/shard_map/all_to_all | solution.py:222
  195.1 22.5 %copy-start.54 = (s32[1,16384]{1,0:T(1,128)S(1)}, s32[1,16384]{1,0:T(1,128)}, u32[]{:S(2)}) copy-start(s32[1,16384]{1,0:T(1,128)} %param.31) | copy-start | bytes 196612
  213.1 35.4 %all-to-all-start.2 = ((bf16[16,80,512]{2,1,0:T(8,128)(2,1)}), bf16[16,80,512]{2,1,0:T(8,128)(2,1)}, u32[]{:S(2)}, u32[]{:S(2)}) async-start(bf16[16,80,512]{2,1,0:T(8,128)(2,1)} %multiply_convert_fusion.8), calls=%async_computation.2 | async-start | bytes 2621440 | tf_op jit(solution)/shard_map/all_to_all | solution.py:257
  219.8 105.2 %copy-start.28 = (bf16[4,4,80,512]{3,2,1,0:T(8,128)(2,1)}, bf16[4,4,80,512]{3,2,1,0:T(8,128)(2,1)S(1)}, u32[]{:S(2)}) copy-start(bf16[4,4,80,512]{3,2,1,0:T(8,128)(2,1)S(1)} %copy.189) | copy-start | bytes 3932164
  249.9 108.5 %copy-start.30 = (bf16[4,4,80,512]{3,2,1,0:T(8,128)(2,1)}, bf16[4,4,80,512]{3,2,1,0:T(8,128)(2,1)S(1)}, u32[]{:S(2)}) copy-start(bf16[4,4,80,512]{3,2,1,0:T(8,128)(2,1)S(1)} %copy.198) | copy-start | bytes 3932164
  333.6 24.8 %copy-start.20 = (f32[4,320,2048]{2,1,0:T(8,128)}, f32[4,320,2048]{2,1,0:T(8,128)S(1)}, u32[]{:S(2)}) copy-start(f32[4,320,2048]{2,1,0:T(8,128)S(1)} %get-tuple-element.782) | copy-start | bytes 31457284
  383.2 34.3 %all-to-all-start.3 = ((bf16[4,320,512]{2,0,1:T(4,128)(2,1)}), bf16[4,320,512]{2,0,1:T(4,128)(2,1)S(1)}, u32[]{:S(2)}, u32[]{:S(2)}) async-start(bf16[4,320,512]{2,0,1:T(4,128)(2,1)} %copy.199), calls=%async_computation.3 | async-start | bytes 2621440 | tf_op jit(solution)/shard_map/all_to_all | solution.py:271
  386.7 35.1 %copy-start.17 = (s32[1024]{0:T(1024)S(1)}, s32[1024]{0:T(1024)}, u32[]{:S(2)}) copy-start(s32[1024]{0:T(1024)} %copy-done.16) | copy-start | bytes 12292
  386.7 35.6 %copy-start.36 = (s32[1,512,2]{2,1,0:T(8,128)S(1)}, s32[1,512,2]{2,1,0:T(8,128)}, u32[]{:S(2)}) copy-start(s32[1,512,2]{2,1,0:T(8,128)} %copy-done.35) | copy-start | bytes 12292
  386.7 35.6 %copy-start.83 = (pred[512]{0:T(512)(128)(4,1)S(1)}, pred[512]{0:T(512)(128)(4,1)}, u32[]{:S(2)}) copy-start(pred[512]{0:T(512)(128)(4,1)} %copy-done.82) | copy-start | bytes 1540
  386.7 36.0 %copy-start.3 = (s32[1024]{0:T(1024)S(1)}, s32[1024]{0:T(1024)}, u32[]{:S(2)}) copy-start(s32[1024]{0:T(1024)} %copy-done.2) | copy-start | bytes 12292
  417.5 35.2 %all-to-all-start.1 = ((bf16[4,320,512]{2,0,1:T(4,128)(2,1)}), bf16[4,320,512]{2,0,1:T(4,128)(2,1)}, u32[]{:S(2)}, u32[]{:S(2)}) async-start(bf16[4,320,512]{2,0,1:T(4,128)(2,1)} %copy.192), calls=%async_computation.1 | async-start | bytes 2621440 | tf_op jit(solution)/shard_map/all_to_all | solution.py:229
  421.8 234.5 %reduce-scatter.5.cloned.1.call-start = ((), (), s32[]{:S(2)}) async-start(), calls=%async_computation.7 | async-start | bytes 6291456 | tf_op jit(solution)/shard_map/reduce_scatter | solution.py:311
  497.4 25.3 %copy-start.44 = (s32[16384,1]{0,1:T(1,128)S(1)}, s32[16384,1]{0,1:T(1,128)}, u32[]{:S(2)}) copy-start(s32[16384,1]{0,1:T(1,128)} %copy-done.43) | copy-start | bytes 196612
  497.4 25.3 %copy-start.88 = (s32[2]{0:T(128)S(1)}, s32[2]{0:T(128)}, u32[]{:S(2)}) copy-start(s32[2]{0:T(128)} %constant.343) | copy-start | bytes 28
  497.5 25.6 %copy-start.87 = (s32[2]{0:T(128)S(1)}, s32[2]{0:T(128)}, u32[]{:S(2)}) copy-start(s32[2]{0:T(128)} %constant.346) | copy-start | bytes 28
  522.7 429.0 %reduce-scatter.7.cloned.1.call-start = ((), (), s32[]{:S(2)}) async-start(), calls=%async_computation.8 | async-start | bytes 37748736 | tf_op jit(solution)/shard_map/reduce_scatter | solution.py:338
  676.5 219.6 %copy-start.22 = (f32[512,512]{0,1:T(8,128)S(1)}, f32[512,512]{0,1:T(8,128)}, u32[]{:S(2)}) copy-start(f32[512,512]{0,1:T(8,128)} %copy-done.21) | copy-start | bytes 3145732
  676.5 219.6 %copy-start.25 = (bf16[1,512,512]{1,2,0:T(8,128)(2,1)S(1)}, bf16[1,512,512]{1,2,0:T(8,128)(2,1)}, u32[]{:S(2)}) copy-start(bf16[1,512,512]{1,2,0:T(8,128)(2,1)} %copy-done.23) | copy-start | bytes 1572868
  676.5 219.6 %copy-start.66 = (f32[1,512]{1,0:T(1,128)S(1)}, f32[1,512]{1,0:T(1,128)}, u32[]{:S(2)}) copy-start(f32[1,512]{1,0:T(1,128)} %copy-done.64) | copy-start | bytes 6148
  891.4 9.3 collective-permute-start
  893.4 7.3 collective-permute-start.1
  (76 other events, 610.1 us)
Sparse Core Ops, SparseCore 0:
  10.8 65.6 all-gather.13
  96.2 20.6 all-gather.11
  119.1 21.2 all-gather.9
  142.1 89.8 all-gather.7
  522.8 52.4 reduce-scatter.4
  651.5 300.1 reduce-scatter.6
where the time goes:
time: 978 us; the launch traced here: 969 us
  local copies, waits for them, and re-layouts  326 us (33%)
  blocking collectives  201 us (21%)
  waiting for transfers between devices  200 us (20%)
  matrix products  112 us (11%)
  other arithmetic  92.4 us (9%)
  starting transfers between devices  20.9 us (2%)
  between operations  16.2 us (2%)
    unnamed x1, blocking collectives  196 us
    unnamed x184, local copies, waits for them, and re-layouts  106 us
    gather x1, local copies, waits for them, and re-layouts, on_device(): all_expert[0][expert_owner[0]].reshape(EXP_DEV, 2, FF, features)  75 us
    all_gather x1, waiting for transfers between devices, on_device(): lax.all_gather(shared_slots, ('dp', 'ctx', 'expert'), axis=0, tiled=True)  65.7 us
    reduce_scatter x1, waiting for transfers between devices, on_device(): lax.psum_scatter(expert_layout, ('dp', 'ctx'), scatter_dimension=1, tiled...  46.6 us
    all_to_all x1, waiting for transfers between devices, on_device(): lax.all_to_all(grad_result, 'expert', split_axis=0, concat_axis=1, tiled=...  28.8 us
    convert_element_type x1, other arithmetic, on_device(): active_low = active.astype(jnp.bfloat16)  24.8 us
    all_to_all x1, waiting for transfers between devices, on_device(): lax.all_to_all(grad_sent, 'expert', split_axis=1, concat_axis=0, tiled=True)  20.8 us
  transfers between devices with their start and end apart: 12, of which 7 were waited for; matrix products, arithmetic and copies ran while one was open for 51% of the time, Pallas kernels for 0%

commit v1 on v0

--- a/solution.py
+++ b/solution.py
@@ -1,8 +1,11 @@
+import functools
 import math
 
 import jax
 import jax.numpy as jnp
 from jax import lax
+from jax.experimental import pallas as pl
+from jax.experimental.pallas import tpu as pltpu
 from jax.sharding import PartitionSpec as P
 
 HEADS = 8
@@ -356,9 +359,681 @@
     )
 
 
+F32 = jnp.float32
+BF16 = jnp.bfloat16
+I32 = jnp.int32
+LANES = 128
+MASKED = -1e30
+VMEM_LIMIT = 56 * 1024 * 1024
+
+
+def dot_nn(left, right):
+    return lax.dot_general(left, right, (((1,), (0,)), ((), ())), preferred_element_type=F32)
+
+
+def dot_nt(left, right):
+    return lax.dot_general(left, right, (((1,), (1,)), ((), ())), preferred_element_type=F32)
+
+
+def dot_tn(left, right):
+    return lax.dot_general(left, right, (((0,), (0,)), ((), ())), preferred_element_type=F32)
+
+
+def iota(shape, dim):
+    return lax.broadcasted_iota(I32, shape, dim)
+
+
+def as_bf16(mask):
+    return jnp.where(mask, 1.0, 0.0).astype(BF16)
+
+
+def kernel_call(body, out_shape, scratch=(), grid=None, in_specs=None, out_specs=None, cost=None):
+    extra = {}
+    if grid is not None:
+        extra = dict(grid=grid, in_specs=in_specs, out_specs=out_specs)
+    flops, moved = cost if cost else (1e8, 1e6)
+    return pl.pallas_call(
+        body,
+        out_shape=out_shape,
+        scratch_shapes=list(scratch),
+        compiler_params=pltpu.CompilerParams(vmem_limit_bytes=VMEM_LIMIT),
+        cost_estimate=pl.CostEstimate(flops=int(flops), bytes_accessed=int(moved), transcendentals=0),
+        **extra,
+    )
+
+
+def sds(shape, dtype):
+    return jax.ShapeDtypeStruct(shape, dtype)
+
+
+def route_body(n_exp, capacity, ids_ref, prio_ref, live_ref, cot_ref, row_ref, col_ref, sent_ref):
+    toks = ids_ref.shape[1]
+    half = capacity // 2
+    prio_row = prio_ref[...]
+    prio_col = jnp.transpose(jnp.broadcast_to(prio_row, (8, toks)))[:, :1]
+    earlier = (prio_col < prio_row) | (
+        (prio_col == prio_row) & (iota((toks, toks), 0) < iota((toks, toks), 1))
+    )
+    live = live_ref[...] > 0.0
+    labels = iota((n_exp, toks), 0)
+    first, second = ids_ref[0:1, :], ids_ref[1:2, :]
+    wanted = ((labels == first) | (labels == second)) & live
+    taken = dot_nn(as_bf16(wanted), as_bf16(earlier))
+    places = []
+    for chosen in (first, second):
+        slot = jnp.sum(jnp.where(labels == chosen, taken, 0.0), axis=0, keepdims=True).astype(I32)
+        kept = live & (slot < capacity)
+        shard = chosen >> 2
+        local = chosen & 3
+        core = (slot >= half).astype(I32)
+        target = ((((local >> 1) * 2 + core) * 2 + (local & 1)) * (n_exp // 4)) + shard
+        places.append(jnp.where(kept, target * half + slot - core * half, -1))
+    row_id = iota((8, toks), 0)
+    rows = jnp.where(row_id == 0, places[0], jnp.where(row_id == 1, places[1], -1))
+    row_ref[...] = rows
+    col_ref[...] = jnp.transpose(rows.astype(F32)).astype(I32)
+    slots = sent_ref.shape[0]
+    spots = iota((slots, toks), 0)
+    picks = as_bf16((spots == places[0]) | (spots == places[1]))
+    sent_ref[...] = dot_nn(picks, cot_ref[...]).astype(BF16)
+
+
+def unpack_body(base, n_pieces, pos_ref, *refs):
+    pieces, rest = refs[:n_pieces], refs[n_pieces:]
+    earlier = rest[0] if len(rest) == 3 else None
+    out_ref, held = rest[-2], rest[-1]
+    size = pieces[0].shape[0]
+    for number, piece in enumerate(pieces):
+        held[number * size : (number + 1) * size, :] = piece[...]
+    total = size * n_pieces
+    rows = out_ref.shape[0]
+
+    def tile(start, count):
+        spots = pos_ref[pl.ds(start, count), :] - base
+        picks = as_bf16(spots == iota((count, total), 1))
+        value = dot_nn(picks, held[...])
+        if earlier is not None:
+            value = value + earlier[pl.ds(start, count), :].astype(F32)
+        out_ref[pl.ds(start, count), :] = value.astype(BF16)
+
+    whole = rows // 256
+
+    @pl.loop(0, whole)
+    def _(number):
+        tile(pl.multiple_of(number * 256, 256), 256)
+
+    if rows % 256:
+        tile(whole * 256, rows % 256)
+
+
+def normalize(values):
+    center = values - jnp.mean(values, axis=-1, keepdims=True)
+    spread = jnp.mean(center * center, axis=-1, keepdims=True)
+    scale = lax.rsqrt(spread + NORM_EPSILON)
+    return center * scale, scale
+
+
+def head_lanes(head, rows):
+    return (iota((rows, LANES), 1) // HEAD_DIM) == head
+
+
+def column_of(ref, start, count, lane):
+    block = ref[pl.ds(start, count), :]
+    return jnp.sum(jnp.where(iota(block.shape, 1) == lane, block, 0.0), axis=1, keepdims=True)
+
+
+def row_of(ref, line):
+    return ref[pl.ds(line, 1), :]
+
+
+def forward_body(
+    n_exp, own_ref, other_ref, keep_ref, w_ref, pos_ref,
+    qkv_ref, normed_ref, attended_ref, residual_ref, prob_ref, sent_ref, lse_col_ref, lse_row_ref,
+    mixed_ref,
+):
+    toks, width = own_ref.shape
+    router = 4 * width
+    gain_one = w_ref[router + n_exp : router + n_exp + 16, :].astype(F32)
+    gain_two = gain_one[1:2, :]
+    gain_one = gain_one[0:1, :]
+    for part, ref in enumerate((own_ref, other_ref)):
+        normed = normalize(ref[...].astype(F32))[0] * gain_one
+        low = normed.astype(BF16)
+        if part == 0:
+            normed_ref[...] = low
+        rows = pl.ds(part * toks, toks)
+        for third in range(3):
+            made = dot_nt(low, w_ref[third * width : (third + 1) * width, :]).astype(BF16)
+            if third == 0:
+                made = made * jnp.asarray(HEAD_DIM ** (-0.5), BF16)
+            qkv_ref[rows, third * width : (third + 1) * width] = made
+    keep = keep_ref[...] > 0.0
+    step = 128
+    lse_col_ref[...] = jnp.zeros_like(lse_col_ref)
+
+    @pl.loop(0, HEADS // 2)
+    def _(pair):
+        at = pl.multiple_of(pair * LANES, LANES)
+        keys = qkv_ref[:, pl.ds(pl.multiple_of(width + at, LANES), LANES)]
+        values = qkv_ref[:, pl.ds(pl.multiple_of(2 * width + at, LANES), LANES)]
+
+        @pl.loop(0, toks // step)
+        def _(number):
+            start = pl.multiple_of(number * step, step)
+            queries = qkv_ref[pl.ds(start, step), pl.ds(at, LANES)]
+            made = []
+            logs = lse_col_ref[pl.ds(start, step), :]
+            for head in range(2):
+                mine = head_lanes(head, step)
+                score = dot_nt(jnp.where(mine, queries, jnp.zeros_like(queries)), keys)
+                score = jnp.where(keep, score, MASKED)
+                top = jnp.max(score, axis=-1, keepdims=True)
+                grown = jnp.exp(score - top)
+                total = jnp.sum(grown, axis=-1, keepdims=True)
+                log_sum = top + jnp.log(total)
+                prob = (grown * (1.0 / total)).astype(BF16)
+                made.append(dot_nn(prob, values))
+                logs = jnp.where(iota(logs.shape, 1) == pair * 2 + head, log_sum, logs)
+            lse_col_ref[pl.ds(start, step), :] = logs
+            attended_ref[pl.ds(start, step), pl.ds(at, LANES)] = jnp.where(
+                head_lanes(0, step), made[0], made[1]
+            )
+
+    lse_row_ref[...] = jnp.transpose(lse_col_ref[...])[:8, :]
+    branch = dot_nn(attended_ref[...].astype(BF16), w_ref[3 * width : 4 * width, :])
+    residual = own_ref[...].astype(F32) + branch
+    residual_ref[...] = residual
+    mixed = (normalize(residual)[0] * gain_two).astype(BF16)
+    mixed_ref[...] = mixed
+    logits = dot_nt(mixed, w_ref[router : router + n_exp, :])
+    prob_ref[...] = jax.nn.softmax(logits, axis=-1)
+    slots = sent_ref.shape[0]
+    spots = iota((slots, toks), 0)
+    picks = as_bf16((spots == pos_ref[0:1, :]) | (spots == pos_ref[1:2, :]))
+    sent_ref[...] = dot_nn(picks, mixed).astype(BF16)
+
+
+def gelu_parts(value):
+    size = jnp.abs(value)
+    share = 1.0 / (1.0 + (0.3275911 * 0.7071067811865476) * size)
+    series = share * (
+        0.254829592
+        + share * (-0.284496736 + share * (1.421413741 + share * (-1.453152027 + share * 1.061405429)))
+    )
+    bell = jnp.exp(-0.5 * value * value)
+    tail = 0.5 * series * bell
+    below = jnp.where(value >= 0.0, 1.0 - tail, tail)
+    return value * below, below + value * bell * 0.3989422804014327
+
+
+def expert_body(
+    n_exp, expert_ref, got_ref, cot_ref, w_in_ref, w_out_ref, router_ref,
+    active_ref, hidden_ref, scaled_ref, result_ref, back_ref, router_grad_ref,
+    prob, total, total_back,
+):
+    step = pl.program_id(0)
+    expert = expert_ref[0]
+    rows = got_ref.shape[0]
+    labels = iota((rows, n_exp), 1)
+
+    @pl.when(step == 0)
+    def _():
+        logits = dot_nt(got_ref[...], router_ref[...])
+        share = jax.nn.softmax(logits, axis=-1)
+        prob[...] = share
+        gate = jnp.sum(jnp.where(labels == expert, share, 0.0), axis=-1, keepdims=True)
+        scaled_ref[...] = (cot_ref[...].astype(F32) * gate).astype(BF16)
+        total[...] = jnp.zeros_like(total)
+        total_back[...] = jnp.zeros_like(total_back)
+
+    tile = 256
+
+    @pl.loop(0, rows // tile)
+    def _(number):
+        at = pl.ds(pl.multiple_of(number * tile, tile), tile)
+        pre = dot_nt(got_ref[at, :], w_in_ref[...])
+        active, slope = gelu_parts(pre)
+        low = active.astype(BF16)
+        active_ref[at, :] = low
+        total[at, :] += dot_nn(low, w_out_ref[...])
+        grad = (dot_nt(scaled_ref[at, :], w_out_ref[...]) * slope).astype(BF16)
+        hidden_ref[at, :] = grad
+        total_back[at, :] += dot_nn(grad, w_in_ref[...])
+
+    @pl.when(step == pl.num_programs(0) - 1)
+    def _():
+        result = total[...].astype(BF16)
+        result_ref[...] = result
+        inner = jnp.sum(result.astype(F32) * cot_ref[...].astype(F32), axis=-1, keepdims=True)
+        share = prob[...]
+        mine = labels == expert
+        gate = jnp.sum(jnp.where(mine, share, 0.0), axis=-1, keepdims=True)
+        grad = share * (jnp.where(mine, inner, 0.0) - gate * inner)
+        low = grad.astype(BF16)
+        back_ref[...] = (total_back[...] + dot_nn(low, router_ref[...])).astype(BF16)
+        router_grad_ref[...] = dot_tn(low, got_ref[...])
+
+
+def norm_back(hat, scale, gain, grad):
+    inner = grad * gain
+    first = jnp.mean(inner, axis=-1, keepdims=True)
+    second = jnp.mean(inner * hat, axis=-1, keepdims=True)
+    return (inner - first - hat * second) * scale
+
+
+def middle_body(
+    n_exp, back_ref, pos_ref, residual_ref, cot_ref, keep_ref, attended_ref, w_ref,
+    grad_ref, out_grad_ref, delta_col_ref, delta_row_ref, gain_ref,
+):
+    toks, width = residual_ref.shape
+    router = 4 * width
+    slots = back_ref.shape[0]
+    gain_two = w_ref[router + n_exp : router + n_exp + 16, :].astype(F32)[1:2, :]
+    spots = iota((toks, slots), 1)
+    picks = as_bf16((spots == pos_ref[:, 0:1]) | (spots == pos_ref[:, 1:2]))
+    grad_mixed = dot_nn(picks, back_ref[...])
+    hat, scale = normalize(residual_ref[...])
+    gain_ref[...] = jnp.broadcast_to(
+        jnp.sum(grad_mixed * hat, axis=0, keepdims=True), gain_ref.shape
+    )
+    grad_rows = cot_ref[...].astype(F32) * keep_ref[...]
+    grad = grad_rows + norm_back(hat, scale, gain_two, grad_mixed)
+    grad_ref[...] = grad
+    low = grad.astype(BF16)
+    out_grad = dot_nt(low, w_ref[3 * width : 4 * width, :]).astype(BF16)
+    out_grad_ref[...] = out_grad
+    product = out_grad.astype(F32) * attended_ref[...]
+    delta = jnp.zeros((toks, LANES), F32)
+    lane = iota((toks, LANES), 1)
+    for head in range(HEADS):
+        at = (head // 2) * LANES
+        part = jnp.where(head_lanes(head % 2, toks), product[:, at : at + LANES], 0.0)
+        delta = jnp.where(lane == head, jnp.sum(part, axis=-1, keepdims=True), delta)
+    delta_col_ref[...] = delta
+    delta_row_ref[...] = jnp.transpose(delta)[:8, :]
+
+
+def key_grads(qkv_ref, base, toks, width, out_grad_ref, lse_ref, delta_ref, keep_ref, store):
+    step = 128
+
+    @pl.loop(0, HEADS // 2)
+    def _(pair):
+        at = pl.multiple_of(pair * LANES, LANES)
+        queries = qkv_ref[pl.ds(base, toks), pl.ds(at, LANES)]
+        out_grad = out_grad_ref[:, pl.ds(at, LANES)]
+
+        @pl.loop(0, toks // step)
+        def _(number):
+            start = pl.multiple_of(number * step, step)
+            rows = pl.ds(start, step)
+            keys = qkv_ref[rows, pl.ds(pl.multiple_of(width + at, LANES), LANES)]
+            values = qkv_ref[rows, pl.ds(pl.multiple_of(2 * width + at, LANES), LANES)]
+            live = keep_ref[rows, :] > 0.0
+            made = []
+            for head in range(2):
+                mine = head_lanes(head, step)
+                score = dot_nt(jnp.where(mine, keys, jnp.zeros_like(keys)), queries)
+                score = jnp.where(live, score, MASKED)
+                prob = jnp.exp(score - row_of(lse_ref, pair * 2 + head))
+                slope = dot_nt(jnp.where(mine, values, jnp.zeros_like(values)), out_grad)
+                grad = (prob * (slope - row_of(delta_ref, pair * 2 + head))).astype(BF16)
+                made.append((dot_nn(grad, queries), dot_nn(prob.astype(BF16), out_grad)))
+            first = head_lanes(0, step)
+            store(rows, at, jnp.where(first, made[0][0], made[1][0]), jnp.where(first, made[0][1], made[1][1]))
+
+
+def inner_body(
+    n_exp, spread, qkv_ref, out_grad_ref, lse_col_ref, lse_row_ref, delta_col_ref, delta_row_ref,
+    keep_row_ref, keep_col_ref, attended_ref, grad_ref, router_grad_ref, gain_ref, pos_ref,
+    query_ref, kv_ref, early_ref, late,
+):
+    toks, width = out_grad_ref.shape
+    step = 128
+    keep = keep_row_ref[...] > 0.0
+
+    @pl.loop(0, HEADS // 2)
+    def _(pair):
+        at = pl.multiple_of(pair * LANES, LANES)
+        keys = qkv_ref[:, pl.ds(pl.multiple_of(width + at, LANES), LANES)]
+        values = qkv_ref[:, pl.ds(pl.multiple_of(2 * width + at, LANES), LANES)]
+
+        @pl.loop(0, toks // step)
+        def _(number):
+            start = pl.multiple_of(number * step, step)
+            rows = pl.ds(start, step)
+            queries = qkv_ref[rows, pl.ds(at, LANES)]
+            out_grad = out_grad_ref[rows, pl.ds(at, LANES)]
+            made = []
+            for head in range(2):
+                mine = head_lanes(head, step)
+                score = dot_nt(jnp.where(mine, queries, jnp.zeros_like(queries)), keys)
+                score = jnp.where(keep, score, MASKED)
+                prob = jnp.exp(score - column_of(lse_col_ref, start, step, pair * 2 + head))
+                slope = dot_nt(jnp.where(mine, out_grad, jnp.zeros_like(out_grad)), values)
+                delta = column_of(delta_col_ref, start, step, pair * 2 + head)
+                grad = (prob * (slope - delta)).astype(BF16)
+                made.append(dot_nn(grad, keys))
+            joined = jnp.where(head_lanes(0, step), made[0], made[1]) * HEAD_DIM ** (-0.5)
+            query_ref[rows, pl.ds(at, LANES)] = joined.astype(BF16)
+
+    def store(rows, at, key_grad, value_grad):
+        kv_ref[0, rows, pl.ds(at, LANES)] = key_grad
+        kv_ref[1, rows, pl.ds(at, LANES)] = value_grad
+
+    key_grads(qkv_ref, 0, toks, width, out_grad_ref, lse_row_ref, delta_row_ref, keep_col_ref, store)
+    late[0:width, :] = dot_tn(attended_ref[...].astype(BF16), grad_ref[...].astype(BF16)).astype(BF16)
+    late[width : width + n_exp, :] = router_grad_ref[...].astype(BF16)
+    row_id = iota((16, width), 0)
+    late[width + n_exp : width + n_exp + 16, :] = jnp.where(
+        row_id == 1, gain_ref[0:1, :], 0.0
+    ).astype(BF16)
+    count = late.shape[0]
+    picks_at = pos_ref[:, 3 * width : 3 * width + count]
+    tile = 272
+
+    @pl.loop(0, early_ref.shape[0] // tile)
+    def _(number):
+        start = pl.multiple_of(number * tile, tile)
+        picks = as_bf16(iota((tile, count), 0) + start == picks_at)
+        early_ref[pl.ds(start, tile), :] = dot_nn(picks, late[...]).astype(BF16)
+
+
+def outer_body(
+    n_exp, qkv_ref, out_grad_ref, lse_ref, delta_ref, keep_col_ref, query_ref, kv_ref,
+    normed_ref, own_ref, w_ref, grad_ref, pos_ref, early_ref,
+    tokens_ref, pieces_ref, sent_ref, held,
+):
+    toks, width = query_ref.shape
+    held[:, 0:width] = query_ref[...]
+
+    def store(rows, at, key_grad, value_grad):
+        key_grad = kv_ref[0, rows, pl.ds(at, LANES)] + key_grad
+        value_grad = kv_ref[1, rows, pl.ds(at, LANES)] + value_grad
+        held[rows, pl.ds(pl.multiple_of(width + at, LANES), LANES)] = key_grad.astype(BF16)
+        held[rows, pl.ds(pl.multiple_of(2 * width + at, LANES), LANES)] = value_grad.astype(BF16)
+
+    key_grads(qkv_ref, toks, toks, width, out_grad_ref, lse_ref, delta_ref, keep_col_ref, store)
+    router = 4 * width
+    gain_one = w_ref[router + n_exp : router + n_exp + 16, :].astype(F32)[0:1, :]
+    grad_normed = dot_nn(held[...], w_ref[0 : 3 * width, :])
+    hat, scale = normalize(own_ref[...].astype(F32))
+    tokens_ref[...] = grad_ref[...] + norm_back(hat, scale, gain_one, grad_normed)
+    gain_grad = jnp.sum(grad_normed * hat, axis=0, keepdims=True)
+    for third in range(3):
+        pieces_ref[third * width : (third + 1) * width, :] = dot_tn(
+            held[:, third * width : (third + 1) * width], normed_ref[...]
+        ).astype(BF16)
+    row_id = iota((16, width), 0)
+    pieces_ref[3 * width : 3 * width + 16, :] = jnp.where(row_id == 0, gain_grad, 0.0).astype(BF16)
+    spread_rows(pos_ref, pieces_ref, early_ref, sent_ref, early_ref.shape[0] // 2, width, n_exp)
+
+
+def spread_rows(pos_ref, pieces_ref, early_ref, out_ref, base, width, n_exp):
+    count = pieces_ref.shape[0]
+    tile = 272
+    gain_at = 4 * width + n_exp
+    main_at = pos_ref[:, 0 : 3 * width]
+    one_at = pos_ref[:, gain_at : gain_at + 1]
+
+    @pl.loop(0, out_ref.shape[0] // tile)
+    def _(number):
+        start = pl.multiple_of(number * tile, tile)
+        spots = iota((tile, 3 * width), 0) + (start + base)
+        made = dot_nn(as_bf16(spots == main_at), pieces_ref[0 : 3 * width, :])
+        gain = pieces_ref[3 * width : 3 * width + 16, :].astype(F32)[0:1, :]
+        made = made + jnp.where(iota((tile, width), 0) + (start + base) == one_at, gain, 0.0)
+        early = early_ref[pl.ds(pl.multiple_of(start + base, 16), tile), :].astype(F32)
+        out_ref[pl.ds(start, tile), :] = (made + early).astype(BF16)
+
+
+def spread_body(width, n_exp, pos_ref, pieces_ref, early_ref, out_ref):
+    spread_rows(pos_ref, pieces_ref, early_ref, out_ref, 0, width, n_exp)
+
+
+def mixture_body(result_ref, pos_ref, ids_ref, prob_ref, residual_ref, out_ref):
+    toks = residual_ref.shape[0]
+    slots = result_ref.shape[0]
+    share = prob_ref[...]
+    total = residual_ref[...]
+    for number in range(2):
+        picks = as_bf16(iota((toks, slots), 1) == pos_ref[:, number : number + 1])
+        mine = iota(share.shape, 1) == ids_ref[:, number : number + 1]
+        gate = jnp.sum(jnp.where(mine, share, 0.0), axis=-1, keepdims=True)
+        total = total + gate * dot_nn(picks, result_ref[...])
+    out_ref[...] = total.astype(BF16)
+
+
+SWAP = [(0, 1), (1, 0)]
+SWAP_CORE = [(0, 1), (1, 0), (2, 3), (3, 2)]
+SWAP_Y = [(0, 2), (2, 0), (1, 3), (3, 1)]
+
+
+def swap_x(value):
+    return lax.ppermute(value, "ctx", SWAP)
+
+
+def swap_y(value):
+    return lax.ppermute(value, "dp", SWAP_Y)
+
+
+def swap_core(value):
+    return lax.ppermute(value, "dp", SWAP_CORE)
+
+
+def shift_z(value, by):
+    count = lax.axis_size("expert")
+    return lax.ppermute(value, "expert", [(i, (i + by) % count) for i in range(count)])
+
+
+def total_f32(first, second):
+    return first.astype(F32) + second.astype(F32)
+
+
+def on_chip_experts(
+    tokens, cotangent, pad_mask, expert_ids, slot_priority, shared_slots, shared_first, shared_second,
+    shared_owner, expert_slots, expert_first, expert_second, expert_owner,
+):
+    toks, width = tokens.shape[1], tokens.shape[2]
+    n_z = lax.axis_size("expert")
+    n_exp = EXP_DEV * n_z
+    capacity = (10 * toks + 4 * n_exp - 1) // (4 * n_exp)
+    slots = n_exp * capacity
+    everyone = ("dp", "ctx", "expert")
+    dp, mx, mz = lax.axis_index("dp"), lax.axis_index("ctx"), lax.axis_index("expert")
+    my, mc = dp // 2, dp % 2
+
+    own_count = shared_slots.shape[0]
+    stride = -(-own_count // 8) * 8
+    padded = jnp.pad(shared_slots, ((0, stride - own_count), (0, 0)))
+    line = [padded] + [shift_z(padded, by) for by in range(1, n_z)]
+    part_a = jnp.concatenate(line[: n_z // 2], axis=0)
+    part_b = jnp.concatenate(line[n_z // 2 :], axis=0)
+    a_y, b_x = swap_y(part_a), swap_x(part_b)
+    a_x, b_y = swap_x(part_a), swap_y(part_b)
+    a_yx, b_xy = swap_x(a_y), swap_y(b_x)
+    near = [part_a, a_y, a_x, a_yx, part_b, b_x, b_y, b_xy]
+    far = [swap_core(piece) for piece in near]
+
+    owner_dev, owner_row = shared_owner // own_count, shared_owner % own_count
+    o_z, o_x, o_dp = owner_dev % n_z, owner_dev // n_z % 2, owner_dev // (n_z * 2)
+    in_c, in_y, in_x = (o_dp % 2) ^ mc, (o_dp // 2) ^ my, o_x ^ mx
+    in_z = (mz - o_z + n_z) % n_z
+    late = in_z // (n_z // 2)
+    cross = jnp.where(late == 0, in_y + 2 * in_x, in_x + 2 * in_y)
+    place = (((in_c * 2 + late) * 4 + cross) * (n_z // 2) + in_z % (n_z // 2)) * stride + owner_row
+    total_slots = 8 * n_z * stride
+    row_count = -(-shared_owner.shape[0] // 16) * 16
+    wide_count = -(-shared_owner.shape[0] // LANES) * LANES
+    place_col = jnp.pad(place, (0, row_count - place.shape[0]), constant_values=-1)[:, None]
+    place_row = jnp.pad(place, (0, wide_count - place.shape[0]), constant_values=-1)[None, :]
+
+    own, other = tokens[0], swap_x(tokens[0])
+    ids = expert_ids[0]
+    live = pad_mask.astype(F32)
+    live_other = swap_x(pad_mask).astype(F32)
+    keep_row = jnp.concatenate([live, live_other], axis=1)
+    keep_col = live.reshape(toks, 1)
+    pos_row, pos_col, cot_sent = kernel_call(
+        functools.partial(route_body, n_exp, capacity),
+        (sds((8, toks), I32), sds((toks, 8), I32), sds((slots, width), BF16)),
+        cost=(2 * slots * toks * width, 4e6),
+    )(ids.T, slot_priority.astype(F32), live, cotangent[0])
+
+    def exchange(rows):
+        return lax.all_to_all(rows, everyone, split_axis=0, concat_axis=0, tiled=True)
+
+    cot_got = exchange(cot_sent)
+
+    half_slots = total_slots // 2
+    unpack_scratch = [pltpu.VMEM((half_slots, width), BF16)]
+    unpack_cost = (2 * row_count * half_slots * width, 8e6)
+    first_rows = kernel_call(
+        functools.partial(unpack_body, 0, len(near)), sds((row_count, width), BF16), unpack_scratch,
+        cost=unpack_cost,
+    )(place_col, *near)
+    weights = kernel_call(
+        functools.partial(unpack_body, half_slots, len(far)), sds((row_count, width), BF16),
+        unpack_scratch, cost=unpack_cost,
+    )(place_col, *far, first_rows)
+
+    all_expert = lax.all_gather(expert_slots[0], ("dp", "ctx"), axis=0, tiled=True)
+    local = my * 2 + mx
+    ff_rows = 2 * FF
+    my_rows = lax.dynamic_slice(expert_owner[0], (local * ff_rows,), (ff_rows,))
+    expert_rows = all_expert[my_rows]
+    w_in, w_out = expert_rows[:FF], expert_rows[FF:]
+
+    (qkv, normed, attended, residual, prob, sent, lse_col, lse_row) = kernel_call(
+        functools.partial(forward_body, n_exp),
+        (
+            sds((2 * toks, 3 * width), BF16), sds((toks, width), BF16), sds((toks, width), F32),
+            sds((toks, width), F32), sds((toks, n_exp), F32), sds((slots, width), BF16),
+            sds((toks, LANES), F32), sds((8, toks), F32),
+        ),
+        [pltpu.VMEM((toks, width), BF16)],
+        cost=(8e9, 1e7),
+    )(own, other, keep_row, weights, pos_row)
+    lse_other = swap_x(lse_row)
+    got = exchange(sent)
+
+    expert_id = (mz * EXP_DEV + local).astype(I32).reshape(1)
+    tile = 256
+    router_rows = weights[4 * width : 4 * width + n_exp]
+    whole = lambda shape: pl.BlockSpec(shape, lambda f: (0, 0))
+    active, hidden, scaled, result, back, router_grad = kernel_call(
+        functools.partial(expert_body, n_exp),
+        (
+            sds((slots, FF), BF16), sds((slots, FF), BF16), sds((slots, width), BF16),
+            sds((slots, width), BF16), sds((slots, width), BF16), sds((n_exp, width), F32),
+        ),
+        [pltpu.VMEM((slots, n_exp), F32), pltpu.VMEM((slots, width), F32), pltpu.VMEM((slots, width), F32)],
+        grid=(FF // tile,),
+        in_specs=[
+            pl.BlockSpec(memory_space=pltpu.SMEM), whole((slots, width)), whole((slots, width)),
+            pl.BlockSpec((tile, width), lambda f: (f, 0)), pl.BlockSpec((tile, width), lambda f: (f, 0)),
+            whole((n_exp, width)),
+        ],
+        out_specs=(
+            pl.BlockSpec((slots, tile), lambda f: (0, f)), pl.BlockSpec((slots, tile), lambda f: (0, f)),
+            whole((slots, width)), whole((slots, width)), whole((slots, width)), whole((n_exp, width)),
+        ),
+        cost=(8 * slots * FF * width, 3e7),
+    )(expert_id, got, cot_got, w_in, w_out, router_rows)
+    back_got = exchange(back)
+    result_got = exchange(result)
+
+    grad_in = dot_tn(hidden, got)
+    grad_out = dot_tn(active, scaled)
+    mine = jnp.where(mc == 0, grad_in, grad_out)
+    theirs = jnp.where(mc == 0, grad_out, grad_in).astype(BF16)
+    summed = (mine + swap_core(theirs).astype(F32)).astype(BF16)
+    all_grads = lax.all_gather(summed, ("dp", "ctx"), axis=0, tiled=True)
+
+    owned = expert_slots.shape[1]
+    base = (dp * 2 + mx) * owned
+    owner = expert_owner[0]
+    n_rows = owner.shape[0]
+    row_no = jnp.arange(n_rows, dtype=I32)
+    e_local, e_half, e_row = row_no // ff_rows, row_no // FF % 2, row_no % FF
+    lies = (((e_local // 2) * 2 + e_half) * 2 + e_local % 2) * FF + e_row
+    rel = owner - base
+    hit = (rel[:, None] >> 7) == jnp.arange(owned // LANES, dtype=I32)[None, :]
+    left = jnp.concatenate(
+        [jnp.where(hit, (lies >> 7)[:, None], 0), jnp.where(hit, (lies & 127)[:, None], 0)], axis=1
+    ).astype(BF16)
+    right = ((rel & 127)[:, None] == jnp.arange(LANES, dtype=I32)[None, :]).astype(BF16)
+    found = dot_tn(left, right)
+    n_hi = owned // LANES
+    source = (found[:n_hi] * 128.0 + found[n_hi:]).astype(I32).reshape(owned)
+    expert_grad = all_grads[source].astype(F32)
+
+    grad_residual, out_grad, delta_col, delta_row, gain_two = kernel_call(
+        functools.partial(middle_body, n_exp),
+        (
+            sds((toks, width), F32), sds((toks, width), BF16), sds((toks, LANES), F32),
+            sds((8, toks), F32), sds((8, width), F32),
+        ),
+        cost=(2e9, 1e7),
+    )(back_got, pos_col, residual, cotangent[0], keep_col, attended, weights)
+    out_grad_other, delta_other = swap_x(out_grad), swap_x(delta_row)
+    late_count = width + n_exp + 16
+    query_grad, kv_grad, early = kernel_call(
+        functools.partial(inner_body, n_exp, 0),
+        (sds((toks, width), BF16), sds((2, toks, width), F32), sds((total_slots, width), BF16)),
+        [pltpu.VMEM((late_count, width), BF16)],
+        cost=(8e9, 2e7),
+    )(
+        qkv, out_grad, lse_col, lse_row, delta_col, delta_row, keep_row, keep_col, attended,
+        grad_residual, router_grad, gain_two, place_row,
+    )
+    grad_tokens, pieces, far_rows = kernel_call(
+        functools.partial(outer_body, n_exp),
+        (sds((toks, width), F32), sds((3 * width + 16, width), BF16), sds((half_slots, width), BF16)),
+        [pltpu.VMEM((toks, 3 * width), BF16)],
+        cost=(8e9, 2e7),
+    )(
+        qkv, out_grad_other, lse_other, delta_other, keep_col, query_grad, kv_grad, normed, own,
+        weights, grad_residual, place_row, early,
+    )
+    far_got = swap_core(far_rows)
+    near_rows = kernel_call(
+        functools.partial(spread_body, width, n_exp), sds((half_slots, width), BF16),
+        cost=(2 * half_slots * 3 * width * width, 1e7),
+    )(place_row, pieces, early)
+    quarter = half_slots // 2
+    eighth, sixteenth = quarter // 2, quarter // 4
+    sum_a = total_f32(near_rows[:quarter], far_got[:quarter]).astype(BF16)
+    sum_b = total_f32(near_rows[quarter:], far_got[quarter:]).astype(BF16)
+    got_a, got_b = swap_x(sum_a[eighth:]), swap_y(sum_b[eighth:])
+    sum_a = total_f32(sum_a[:eighth], got_a).astype(BF16)
+    sum_b = total_f32(sum_b[:eighth], got_b).astype(BF16)
+    got_a, got_b = swap_y(sum_a[sixteenth:]), swap_x(sum_b[sixteenth:])
+    sum_a = total_f32(sum_a[:sixteenth], got_a).astype(BF16)
+    sum_b = total_f32(sum_b[:sixteenth], got_b).astype(BF16)
+    lines = [sum_a[i * stride : (i + 1) * stride] for i in range(n_z // 2)]
+    lines += [sum_b[i * stride : (i + 1) * stride] for i in range(n_z // 2)]
+    shared_grad = lines[0].astype(F32)
+    for by in range(1, n_z):
+        shared_grad = shared_grad + shift_z(lines[by], n_z - by).astype(F32)
+    shared_grad = shared_grad[:own_count]
+
+    output = kernel_call(
+        mixture_body, sds((toks, width), BF16), cost=(4 * slots * toks * width, 4e6)
+    )(result_got, pos_col, ids, prob, residual)
+
+    shared_new = adam_update(shared_grad, shared_first, shared_second, shared_slots.astype(F32))
+    expert_new = adam_update(expert_grad, expert_first[0], expert_second[0], expert_slots[0].astype(F32))
+    return (
+        output[None], grad_tokens[None], shared_grad, *shared_new,
+        expert_grad[None], *(value[None] for value in expert_new),
+    )
+
+
 def solution(mesh):
+    sizes = mesh.shape
+    chip_experts = (sizes["dp"], sizes["ctx"], sizes["expert"]) == (4, 2, 4)
     return jax.shard_map(
-        on_device,
+        on_chip_experts if chip_experts else on_device,
         mesh=mesh,
         in_specs=(
             P(("dp", "expert"), "ctx", None),

time: 978 us -> 444 us (0.45)
  local copies, waits for them, and re-layouts: 326 us -> 59.3 us
  blocking collectives: 201 us -> 0 us
  Pallas kernels: 0 us -> 175 us
  matrix products: 112 us -> 14.2 us
  waiting for transfers between devices: 200 us -> 104 us
  other arithmetic: 92.4 us -> 20.4 us
  starting transfers between devices: 20.9 us -> 48 us
    unnamed x1 -> x0, blocking collectives: 196 us -> none
    pallas_call x0 -> x10, Pallas kernels: none -> 175 us  [the longest x1 45.1 us: on_chip_experts(): kernel_call(functools.partial(expert_body, n_exp), (sds((slots, FF), BF16...]
    unnamed x184 -> x74, local copies, waits for them, and re-layouts: 106 us -> 7.15 us
    dot_general x29 -> x3, matrix products: 112 us -> 14.2 us  [dot_tn(): lax.dot_general(left, right, (((0,), (0,)), ((), ())), preferred_element_...]
    gather x17 -> x2, local copies, waits for them, and re-layouts: 133 us -> 40.9 us  [the longest x1 25.4 us: on_chip_experts(): expert_rows = all_expert[my_rows]]
    all_gather x4 -> x2, waiting for transfers between devices: 76.3 us -> 1.33 us  [the longest x1 1.33 us: on_chip_experts(): lax.all_gather(expert_slots[0], ('dp', 'ctx'), axis=0, tiled=True)]
    ppermute x0 -> x31, waiting for transfers between devices: none -> 72.8 us  [the longest x10 46.3 us: swap_x(): return lax.ppermute(value, 'ctx', SWAP)]
    reduce_scatter x2 -> x0, waiting for transfers between devices: 46.6 us -> none  [the longest x1 46.6 us: on_device(): lax.psum_scatter(expert_layout, ('dp', 'ctx'), scatter_dimension=1, tiled...]
  transfers between devices with their start and end apart: 12 -> 37, of which waited for: 7 -> 12; matrix products, arithmetic and copies ran while one was open for 51% -> 12% of each run, Pallas kernels for 0% -> 30%
where the time goes in v1:
time: 444 us; the launch traced here: 435 us
  Pallas kernels  175 us (39%)
  waiting for transfers between devices  104 us (23%)
  local copies, waits for them, and re-layouts  59.3 us (13%)
  starting transfers between devices  48 us (11%)
  other arithmetic  20.4 us (5%)
  between operations  15 us (3%)
  matrix products  14.2 us (3%)
    ppermute x10, waiting for transfers between devices, swap_x(): return lax.ppermute(value, 'ctx', SWAP)  46.3 us
    pallas_call x1, Pallas kernels, on_chip_experts(): kernel_call(functools.partial(expert_body, n_exp), (sds((slots, FF), BF16...  45.1 us
    pallas_call x1, Pallas kernels, on_chip_experts(): kernel_call(functools.partial(inner_body, n_exp, 0), (sds((toks, width),...  35.2 us
    all_to_all x4, waiting for transfers between devices, exchange(): lax.all_to_all(rows, everyone, split_axis=0, concat_axis=0, tiled=True)  29 us
    gather x1, local copies, waits for them, and re-layouts, on_chip_experts(): expert_rows = all_expert[my_rows]  25.4 us
    pallas_call x1, Pallas kernels, on_chip_experts(): kernel_call(functools.partial(outer_body, n_exp), (sds((toks, width), F32...  24.9 us
    pallas_call x1, Pallas kernels, on_chip_experts(): kernel_call(functools.partial(forward_body, n_exp), (sds((2 * toks, 3 * w...  24.1 us
    ppermute x5, waiting for transfers between devices, swap_y(): return lax.ppermute(value, 'dp', SWAP_Y)  20.7 us
  transfers between devices with their start and end apart: 37, of which 12 were waited for; matrix products, arithmetic and copies ran while one was open for 12% of the time, Pallas kernels for 30%

profile of v1, /device:TPU:0, one launch (start us, length us, event | category | flops | bytes accessed | tf_op | source)
XLA Modules:
  0.0 435.5 jit_solution(16296925300199272523)
XLA Ops:
  8.9 5.1 %collective-permute-start.11 = (bf16[136,512]{1,0:T(8,128)(2,1)S(1)}, bf16[136,512]{1,0:T(8,128)(2,1)S(1)}, u32[]{:S(2)}, u32[]{:S(2)}) collective-permute-start(bf16[136,512]{1,0:T(8,128)(2,1)S(1)} %pad.13), channel_id=1, source_target_pairs={{0,3},{1,0},{2,1},{3,2},{4,7},{5,4},{6,5},{7,6},{8,11},{9,8},{10,9... | collective-permute-start | bytes 417800 | tf_op jit(solution)/shard_map/ppermute | solution.py:825
  18.5 3.7 shard_map.206
  22.2 4.0 all-to-all-start.1
  30.6 28.6 %collective-permute-done.6.refs_2_ = bf16[272,512]{1,0:T(8,128)(2,1)S(1)} collective-permute-done((bf16[272,512]{1,0:T(8,128)(2,1)S(1)}, bf16[272,512]{1,0:T(8,128)(2,1)S(1)}, u32[]{:S(2)}, u32[]{:S(2)}) %collective-permute-start.6) | collective-permute-done | bytes 278560 | tf_op jit(solution)/shard_map/ppermute | solution.py:812
  59.7 9.4 %collective-permute-done.15.refs_6_ = bf16[272,512]{1,0:T(8,128)(2,1)S(1)} collective-permute-done((bf16[272,512]{1,0:T(8,128)(2,1)S(1)}, bf16[272,512]{1,0:T(8,128)(2,1)S(1)}, u32[]{:S(2)}, u32[]{:S(2)}) %collective-permute-start.15) | collective-permute-done | bytes 278560 | tf_op jit(solution)/shard_map/ppermute | solution.py:816
  75.3 3.7 collective-permute-done.8.refs_3_
  80.2 11.4 %shard_map.204.refs_8_ = bf16[2080,512]{1,0:T(8,128)(2,1)} custom-call(s32[2080,1]{1,0:T(8,128)} %broadcast_in_dim.49.pos_ref, bf16[272,512]{1,0:T(8,128)(2,1)} %copy-done.8, bf16[272,512]{1,0:T(8,128)(2,1)} %collective-permute-done.4.refs_1_, bf16[272,512]{1,0:T(8,128)(2,1)} %copy-done.20, bf16[272,512]{1,0:T(8,128)(2,1)} %copy-done.24, ...), custom_call_target="tpu_custom_call" | custom-call | flops 4634705920 | bytes 8000000 | tf_op jit(solution)/shard_map/pallas_call | solution.py:890
  93.2 11.2 %shard_map.205.w_ref = bf16[2080,512]{1,0:T(8,128)(2,1)} custom-call(s32[2080,1]{1,0:T(8,128)} %broadcast_in_dim.49.pos_ref, bf16[272,512]{1,0:T(8,128)(2,1)} %copy-done.19, bf16[272,512]{1,0:T(8,128)(2,1)} %copy-done.23, bf16[272,512]{1,0:T(8,128)(2,1)} %copy-done.25, bf16[272,512]{1,0:T(8,128)(2,1)} %copy-done.29, bf16[272,512]{1,0:T(8,128)(2,1)} %copy-done.22, ...), custom_call_target="tpu_custom_call" | custom-call | flops 4634705920 | bytes 8000000 | tf_op jit(solution)/shard_map/pallas_call | solution.py:894
  105.2 24.1 %shard_map.207 = (bf16[1024,1536]{1,0:T(8,128)(2,1)}, bf16[512,512]{1,0:T(8,128)(2,1)}, f32[512,512]{1,0:T(8,128)}, f32[512,512]{1,0:T(8,128)}, f32[512,16]{1,0:...) custom-call(bf16[512,512]{1,0:T(8,128)(2,1)} %bitcast.51, bf16[512,512]{1,0:T(8,128)(2,1)} %copy-done.17, ...), custom_call_target="tpu_custom_call" | custom-call | flops 8000000000 | bytes 10000000 | tf_op jit(solution)/shard_map/pallas_call | solution.py:906
  129.3 4.6 %all-to-all-start = ((bf16[32,40,512]{2,1,0:T(8,128)(2,1)}), bf16[32,40,512]{2,1,0:T(8,128)(2,1)S(1)}, u32[]{:S(2)}, u32[]{:S(2)}) async-start(bf16[32,40,512]{2,1,0:T(8,128)(2,1)} %bitcast.40), calls=%async_computation | async-start | bytes 2621440 | tf_op jit(solution)/shard_map/all_to_all | solution.py:883
  136.8 25.4 %gather_fusion = bf16[4096,512]{1,0:T(8,128)(2,1)} fusion(bf16[16384,512]{1,0:T(8,128)(2,1)} %bitcast.34, s32[4096]{0:T(1024)S(1)} %broadcast_clamp_fusion), kind=kCustom, calls=%fused_computation | custom fusion | bytes 8404992 | tf_op jit(solution)/shard_map/gather | solution.py:903
  162.2 4.6 %fusion.62 = (bf16[2048,512]{1,0:T(8,128)(2,1)}, bf16[2048,512]{1,0:T(8,128)(2,1)}) fusion(bf16[4096,512]{1,0:T(8,128)(2,1)} %gather_fusion), kind=kLoop, calls=%fused_computation.144 | loop fusion | bytes 8388608 | tf_op jit(solution)/shard_map/slice | solution.py:904
  167.8 45.1 %shard_map.208 = (bf16[1280,2048]{1,0:T(8,128)(2,1)}, bf16[1280,2048]{1,0:T(8,128)(2,1)}, bf16[1280,512]{1,0:T(8,128)(2,1)}, bf16[1280,512]{1,0:T(8,128)(2,1)}, ...) custom-call(s32[1]{0:T(128)} %bitcast.expert_ref, bf16[1280,512]{1,0:T(8,128)(2,1)} %bitcast.38, bf16[1280,512]{1,0:T(8,128)(2,1)} %bitcast.35, ...), custom_call_target="tpu_custom_call" | custom-call | flops 10737418240 | bytes 30000000 | tf_op jit(solution)/shard_map/pallas_call | solution.py:923
  212.9 5.4 %fusion.65 = f32[2048,512]{1,0:T(8,128)S(1)} fusion(bf16[1280,2048]{1,0:T(8,128)(2,1)} %get-tuple-element.63, bf16[1280,512]{1,0:T(8,128)(2,1)} %bitcast.39), kind=kOutput, calls=%fused_computation.147 | convolution fusion | flops 2684354560 | bytes 10747904 | tf_op jit(solution)/shard_map/dot_general | solution.py:379
  218.4 2.9 select_convert_fusion
  221.6 3.9 collective-permute-done.30
  225.5 2.6 add_convert_fusion
  228.1 4.9 %all-to-all-start.3 = ((bf16[32,40,512]{2,1,0:T(8,128)(2,1)}), bf16[32,40,512]{2,1,0:T(8,128)(2,1)S(1)}, u32[]{:S(2)}, u32[]{:S(2)}) async-start(bf16[32,40,512]{2,1,0:T(8,128)(2,1)} %bitcast.15), calls=%async_computation.3 | async-start | bytes 2621440 | tf_op jit(solution)/shard_map/all_to_all | solution.py:883
  236.3 28.9 %all-to-all-done.3 = bf16[32,40,512]{2,1,0:T(8,128)(2,1)S(1)} async-done(((bf16[32,40,512]{2,1,0:T(8,128)(2,1)}), bf16[32,40,512]{2,1,0:T(8,128)(2,1)S(1)}, u32[]{:S(2)}, u32[]{:S(2)}) %all-to-all-start.3) | async-done | bytes 1310752 | tf_op jit(solution)/shard_map/all_to_all | solution.py:883
  266.3 5.8 %shard_map.210 = (f32[512,512]{1,0:T(8,128)}, bf16[512,512]{1,0:T(8,128)(2,1)}, f32[512,128]{1,0:T(8,128)}, f32[8,512]{1,0:T(8,128)}, f32[8,512]{1,0:T(8,128)}) custom-call(bf16[1280,512]{1,0:T(8,128)(2,1)} %bitcast.41, s32[512,8]{1,0:T(8,128)} %get-tuple-element.42.pos_ref, f32[512,512]{1,0:T(8,128)} %get-tuple-element.44.residual_ref, ...), custom_call_target="tpu_custom_call" | custom-call | flops 2000000000 | bytes 10000000 | tf_op jit(solution)/shard_map/pallas_call | solution.py:970
  274.2 35.2 %shard_map.211 = (bf16[512,512]{1,0:T(8,128)(2,1)}, f32[2,512,512]{2,1,0:T(8,128)}, bf16[4352,512]{1,0:T(8,128)(2,1)}) custom-call(bf16[1024,1536]{1,0:T(8,128)(2,1)} %get-tuple-element.45.qkv_ref, bf16[512,512]{1,0:T(8,128)(2,1)} %get-tuple-element.48.out_grad_ref, f32[512,128]{1,0:T(8,128)} %get-tuple-element.51.lse_col_ref, ...), custom_call_target="tpu_custom_call" | custom-call | flops 8000000000 | bytes 20000000 | tf_op jit(solution)/shard_map/pallas_call | solution.py:980
  310.2 24.9 %shard_map.212 = (f32[512,512]{1,0:T(8,128)}, bf16[1552,512]{1,0:T(8,128)(2,1)}, bf16[2176,512]{1,0:T(8,128)(2,1)}) custom-call(bf16[1024,1536]{1,0:T(8,128)(2,1)} %get-tuple-element.45.qkv_ref, bf16[512,512]{1,0:T(8,128)(2,1)} %copy-done.18, f32[8,512]{1,0:T(8,128)} %copy-done.32, f32[8,512]{1,0:T(8,128)} %copy-done.33, ...), custom_call_target="tpu_custom_call" | custom-call | flops 8000000000 | bytes 20000000 | tf_op jit(solution)/shard_map/pallas_call | solution.py:989
  335.9 9.0 %shard_map.213 = bf16[2176,512]{1,0:T(8,128)(2,1)} custom-call(s32[1,2176]{1,0:T(1,128)} %broadcast_in_dim.44.pos_ref, bf16[1552,512]{1,0:T(8,128)(2,1)} %get-tuple-element.61.pieces_ref, bf16[4352,512]{1,0:T(8,128)(2,1)} %get-tuple-element.59.early_ref), custom_call_target="tpu_custom_call" | custom-call | flops 3422552064 | bytes 10000000 | tf_op jit(solution)/shard_map/pallas_call | solution.py:999
  350.6 2.7 all-to-all-start.2
  353.2 5.9 %fusion = f32[32,128]{1,0:T(8,128)S(1)} fusion(s32[16384]{0:T(1024)} %bitcast.45, bf16[16384,16]{0,1:T(8,128)(2,1)} %get-tuple-element.83, bf16[16384,16]{0,1:T(8,128)(2,1)} %get-tuple-element.82), kind=kOutput, calls=%fused_computation.3 | convolution fusion | flops 138412032 | bytes 1130496 | tf_op jit(solution)/shard_map/dot_general | solution.py:379
  360.9 11.3 %collective-permute-done.26 = bf16[544,512]{1,0:T(8,128)(2,1)} collective-permute-done((bf16[544,512]{1,0:T(8,128)(2,1)}, bf16[544,512]{1,0:T(8,128)(2,1)}, u32[]{:S(2)}, u32[]{:S(2)}) %collective-permute-start.26) | collective-permute-done | bytes 557088 | tf_op jit(solution)/shard_map/ppermute | solution.py:816
  374.1 5.1 %collective-permute-done.23 = bf16[544,512]{1,0:T(8,128)(2,1)S(1)} collective-permute-done((bf16[544,512]{1,0:T(8,128)(2,1)S(1)}, bf16[544,512]{1,0:T(8,128)(2,1)S(1)}, u32[]{:S(2)}, u32[]{:S(2)}) %collective-permute-start.23) | collective-permute-done | bytes 557088 | tf_op jit(solution)/shard_map/ppermute | solution.py:812
  381.0 7.0 %collective-permute-done.27 = bf16[272,512]{1,0:T(8,128)(2,1)S(1)} collective-permute-done((bf16[272,512]{1,0:T(8,128)(2,1)S(1)}, bf16[272,512]{1,0:T(8,128)(2,1)S(1)}, u32[]{:S(2)}, u32[]{:S(2)}) %collective-permute-start.27) | collective-permute-done | bytes 278560 | tf_op jit(solution)/shard_map/ppermute | solution.py:812
  390.5 2.6 collective-permute-start.29
  396.2 4.3 shard_map.209
  403.4 15.5 %gather_fusion.1 = bf16[2048,512]{1,0:T(8,128)(2,1)S(1)} fusion(bf16[16384,512]{1,0:T(8,128)(2,1)} %all-gather.4.cloned.1.call-done, s32[2048]{0:T(1024)S(1)} %broadcast_clamp_fusion.1), kind=kCustom, calls=%fused_computation.1 | custom fusion | bytes 4202496 | tf_op jit(solution)/shard_map/gather | solution.py:968
  418.9 9.3 %convert_subtract_fusion = (f32[1,2048,512]{2,1,0:T(8,128)}, f32[1,2048,512]{2,1,0:T(8,128)}, f32[1,2048,512]{2,1,0:T(8,128)}, f32[1,2048,512]{2,1,0:T(8,128)}) fusion(bf16[1,2048,512]{2,1,0:T(8,128)(2,1)} %param.22, f32[1,2048,512]{2,1,0:T(8,128)} %param.24, f32[1,2048,512]{2,1,0:T(8,128)} %param.23, bf16[2048,512]{1,0:T(8,128)(2,1)S(1)} %gather_fusion.1), kind=kLoop, calls=%fused_computation.6 | loop fusion | flops 14680064 | bytes 29360128 | tf_op jit(solution)/shard_map/sub | solution.py:137
  (171 shorter events, 52.5 us)
Async XLA Ops:
  7.2 129.6 %all-gather.6.cloned.1.call-start = ((), (), s32[]{:S(2)}) async-start(), calls=%async_computation.5 | async-start | bytes 18874368 | tf_op jit(solution)/shard_map/all_gather | solution.py:899
  8.9 20.8 %collective-permute-start.11 = (bf16[136,512]{1,0:T(8,128)(2,1)S(1)}, bf16[136,512]{1,0:T(8,128)(2,1)S(1)}, u32[]{:S(2)}, u32[]{:S(2)}) collective-permute-start(bf16[136,512]{1,0:T(8,128)(2,1)S(1)} %pad.13), channel_id=1, source_target_pairs={{0,3},{1,0},{2,1},{3,2},{4,7},{5,4},{6,5},{7,6},{8,11},{9,8},{10,9... | collective-permute-start | bytes 417800 | tf_op jit(solution)/shard_map/ppermute | solution.py:825
  14.0 15.7 %collective-permute-start.10 = (bf16[136,512]{1,0:T(8,128)(2,1)S(1)}, bf16[136,512]{1,0:T(8,128)(2,1)S(1)}, u32[]{:S(2)}, u32[]{:S(2)}) collective-permute-start(bf16[136,512]{1,0:T(8,128)(2,1)S(1)} %pad.13), channel_id=1, source_target_pairs={{0,2},{1,3},{2,0},{3,1},{4,6},{5,7},{6,4},{7,5},{8,10},{9,11},{10,... | collective-permute-start | bytes 417800 | tf_op jit(solution)/shard_map/ppermute | solution.py:825
  14.0 12.3 %collective-permute-start.2 = (bf16[136,512]{1,0:T(8,128)(2,1)S(1)}, bf16[136,512]{1,0:T(8,128)(2,1)S(1)}, u32[]{:S(2)}, u32[]{:S(2)}) collective-permute-start(bf16[136,512]{1,0:T(8,128)(2,1)S(1)} %pad.13), channel_id=1, source_target_pairs={{0,1},{1,2},{2,3},{3,0},{4,5},{5,6},{6,7},{7,4},{8,9},{9,10},{10,1... | collective-permute-start | bytes 417800 | tf_op jit(solution)/shard_map/ppermute | solution.py:825
  15.0 15.3 %collective-permute-start.1 = (s32[1,512]{1,0:T(1,128)S(1)}, s32[1,512]{1,0:T(1,128)S(1)}, u32[]{:S(2)}, u32[]{:S(2)}) collective-permute-start(s32[1,512]{1,0:T(1,128)S(1)} %copy-done.14), channel_id=1, source_target_pairs={{0,4},{4,0},{1,5},{5,1},{2,6},{6,2},{3,7},{7,3},{8,12},{12,8},{9,1... | collective-permute-start | bytes 6152 | tf_op jit(solution)/shard_map/ppermute | solution.py:812
  22.2 107.0 %all-to-all-start.1 = ((bf16[32,40,512]{2,1,0:T(8,128)(2,1)}), bf16[32,40,512]{2,1,0:T(8,128)(2,1)S(1)}, u32[]{:S(2)}, u32[]{:S(2)}) async-start(bf16[32,40,512]{2,1,0:T(8,128)(2,1)} %bitcast.36), calls=%async_computation.1 | async-start | bytes 2621440 | tf_op jit(solution)/shard_map/all_to_all | solution.py:883
  26.3 32.8 %collective-permute-start.6 = (bf16[272,512]{1,0:T(8,128)(2,1)S(1)}, bf16[272,512]{1,0:T(8,128)(2,1)S(1)}, u32[]{:S(2)}, u32[]{:S(2)}) collective-permute-start(bf16[272,512]{1,0:T(8,128)(2,1)S(1)} %pad_maximum_fusion.refs_0_), channel_id=1, source_target_pairs={{0,4},{4,0},{1,5},{5,1},{2,6},{6,2},{3,7},{7,3},{8,12},{12,8},{9,1... | collective-permute-start | bytes 835592 | tf_op jit(solution)/shard_map/ppermute | solution.py:812
  28.2 31.0 %collective-permute-start.4 = (bf16[272,512]{1,0:T(8,128)(2,1)S(1)}, bf16[272,512]{1,0:T(8,128)(2,1)}, u32[]{:S(2)}, u32[]{:S(2)}) collective-permute-start(bf16[272,512]{1,0:T(8,128)(2,1)S(1)} %pad_maximum_fusion.refs_0_), channel_id=1, source_target_pairs={{0,16},{16,0},{8,24},{24,8},{1,17},{17,1},{9,25},{25,9},{2,18},{18... | collective-permute-start | bytes 835592 | tf_op jit(solution)/shard_map/ppermute | solution.py:816
  29.6 29.8 %collective-permute-start.3 = (bf16[272,512]{1,0:T(8,128)(2,1)S(1)}, bf16[272,512]{1,0:T(8,128)(2,1)S(1)}, u32[]{:S(2)}, u32[]{:S(2)}) collective-permute-start(bf16[272,512]{1,0:T(8,128)(2,1)S(1)} %pad_maximum_fusion.refs_0_), channel_id=1, source_target_pairs={{0,8},{8,0},{16,24},{24,16},{1,9},{9,1},{17,25},{25,17},{2,10},{10... | collective-permute-start | bytes 835592 | tf_op jit(solution)/shard_map/ppermute | solution.py:820
  29.7 39.5 %collective-permute-start.15 = (bf16[272,512]{1,0:T(8,128)(2,1)S(1)}, bf16[272,512]{1,0:T(8,128)(2,1)S(1)}, u32[]{:S(2)}, u32[]{:S(2)}) collective-permute-start(bf16[272,512]{1,0:T(8,128)(2,1)S(1)} %constant_dynamic-update-slice_fusion.refs_4_), channel_id=1, source_target_pairs={{0,16},{16,0},{8,24},{24,8},{1,17},{17,1},{9,25},{25,9},{2,18},{18... | collective-permute-start | bytes 835592 | tf_op jit(solution)/shard_map/ppermute | solution.py:816
  30.3 40.9 %collective-permute-start.13 = (bf16[272,512]{1,0:T(8,128)(2,1)S(1)}, bf16[272,512]{1,0:T(8,128)(2,1)}, u32[]{:S(2)}, u32[]{:S(2)}) collective-permute-start(bf16[272,512]{1,0:T(8,128)(2,1)S(1)} %constant_dynamic-update-slice_fusion.refs_4_), channel_id=1, source_target_pairs={{0,4},{4,0},{1,5},{5,1},{2,6},{6,2},{3,7},{7,3},{8,12},{12,8},{9,1... | collective-permute-start | bytes 835592 | tf_op jit(solution)/shard_map/ppermute | solution.py:812
  59.1 15.5 %collective-permute-start.12 = (bf16[272,512]{1,0:T(8,128)(2,1)S(1)}, bf16[272,512]{1,0:T(8,128)(2,1)S(1)}, u32[]{:S(2)}, u32[]{:S(2)}) collective-permute-start(bf16[272,512]{1,0:T(8,128)(2,1)S(1)} %constant_dynamic-update-slice_fusion.refs_4_), channel_id=1, source_target_pairs={{0,8},{8,0},{16,24},{24,16},{1,9},{9,1},{17,25},{25,17},{2,10},{10... | collective-permute-start | bytes 835592 | tf_op jit(solution)/shard_map/ppermute | solution.py:820
  59.1 19.8 %collective-permute-start.8 = (bf16[272,512]{1,0:T(8,128)(2,1)}, bf16[272,512]{1,0:T(8,128)(2,1)S(1)}, u32[]{:S(2)}, u32[]{:S(2)}) collective-permute-start(bf16[272,512]{1,0:T(8,128)(2,1)} %collective-permute-done.4.refs_1_), channel_id=1, source_target_pairs={{0,4},{4,0},{1,5},{5,1},{2,6},{6,2},{3,7},{7,3},{8,12},{12,8},{9,1... | collective-permute-start | bytes 835592 | tf_op jit(solution)/shard_map/ppermute | solution.py:812
  59.4 19.6 %collective-permute-start.5 = (bf16[272,512]{1,0:T(8,128)(2,1)}, bf16[272,512]{1,0:T(8,128)(2,1)S(1)}, u32[]{:S(2)}, u32[]{:S(2)}) collective-permute-start(bf16[272,512]{1,0:T(8,128)(2,1)} %collective-permute-done.4.refs_1_), channel_id=1, source_target_pairs={{0,8},{8,0},{16,24},{24,16},{1,9},{9,1},{17,25},{25,17},{2,10},{10... | collective-permute-start | bytes 835592 | tf_op jit(solution)/shard_map/ppermute | solution.py:820
  74.6 29.7 %collective-permute-start = (bf16[512,512]{1,0:T(8,128)(2,1)S(1)}, bf16[512,512]{1,0:T(8,128)(2,1)S(1)}, u32[]{:S(2)}, u32[]{:S(2)}) collective-permute-start(bf16[512,512]{1,0:T(8,128)(2,1)S(1)} %bitcast.53), channel_id=1, source_target_pairs={{0,4},{4,0},{1,5},{5,1},{2,6},{6,2},{3,7},{7,3},{8,12},{12,8},{9,1... | collective-permute-start | bytes 1572872 | tf_op jit(solution)/shard_map/ppermute | solution.py:812
  75.3 16.4 %collective-permute-start.14 = (bf16[272,512]{1,0:T(8,128)(2,1)}, bf16[272,512]{1,0:T(8,128)(2,1)S(1)}, u32[]{:S(2)}, u32[]{:S(2)}) collective-permute-start(bf16[272,512]{1,0:T(8,128)(2,1)} %collective-permute-done.13.refs_5_), channel_id=1, source_target_pairs={{0,8},{8,0},{16,24},{24,16},{1,9},{9,1},{17,25},{25,17},{2,10},{10... | collective-permute-start | bytes 835592 | tf_op jit(solution)/shard_map/ppermute | solution.py:820
  79.0 12.6 %collective-permute-start.16 = (bf16[272,512]{1,0:T(8,128)(2,1)S(1)}, bf16[272,512]{1,0:T(8,128)(2,1)S(1)}, u32[]{:S(2)}, u32[]{:S(2)}) collective-permute-start(bf16[272,512]{1,0:T(8,128)(2,1)S(1)} %collective-permute-done.15.refs_6_), channel_id=1, source_target_pairs={{0,8},{8,0},{16,24},{24,16},{1,9},{9,1},{17,25},{25,17},{2,10},{10... | collective-permute-start | bytes 835592 | tf_op jit(solution)/shard_map/ppermute | solution.py:820
  79.0 12.7 %collective-permute-start.9 = (bf16[272,512]{1,0:T(8,128)(2,1)S(1)}, bf16[272,512]{1,0:T(8,128)(2,1)S(1)}, u32[]{:S(2)}, u32[]{:S(2)}) collective-permute-start(bf16[272,512]{1,0:T(8,128)(2,1)S(1)} %collective-permute-done.8.refs_3_), channel_id=1, source_target_pairs={{0,8},{8,0},{16,24},{24,16},{1,9},{9,1},{17,25},{25,17},{2,10},{10... | collective-permute-start | bytes 835592 | tf_op jit(solution)/shard_map/ppermute | solution.py:820
  79.5 12.2 %collective-permute-start.18 = (bf16[272,512]{1,0:T(8,128)(2,1)S(1)}, bf16[272,512]{1,0:T(8,128)(2,1)S(1)}, u32[]{:S(2)}, u32[]{:S(2)}) collective-permute-start(bf16[272,512]{1,0:T(8,128)(2,1)S(1)} %collective-permute-done.17.refs_7_), channel_id=1, source_target_pairs={{0,8},{8,0},{16,24},{24,16},{1,9},{9,1},{17,25},{25,17},{2,10},{10... | collective-permute-start | bytes 835592 | tf_op jit(solution)/shard_map/ppermute | solution.py:820
  129.3 37.5 %all-to-all-start = ((bf16[32,40,512]{2,1,0:T(8,128)(2,1)}), bf16[32,40,512]{2,1,0:T(8,128)(2,1)S(1)}, u32[]{:S(2)}, u32[]{:S(2)}) async-start(bf16[32,40,512]{2,1,0:T(8,128)(2,1)} %bitcast.40), calls=%async_computation | async-start | bytes 2621440 | tf_op jit(solution)/shard_map/all_to_all | solution.py:883
  133.8 269.5 %all-gather.4.cloned.1.call-start = ((), (), s32[]{:S(2)}) async-start(), calls=%async_computation.4 | async-start | bytes 18874368 | tf_op jit(solution)/shard_map/all_gather | solution.py:950
  228.1 37.2 %all-to-all-start.3 = ((bf16[32,40,512]{2,1,0:T(8,128)(2,1)}), bf16[32,40,512]{2,1,0:T(8,128)(2,1)S(1)}, u32[]{:S(2)}, u32[]{:S(2)}) async-start(bf16[32,40,512]{2,1,0:T(8,128)(2,1)} %bitcast.15), calls=%async_computation.3 | async-start | bytes 2621440 | tf_op jit(solution)/shard_map/all_to_all | solution.py:883
  234.5 74.9 %collective-permute-start.20 = (f32[8,512]{1,0:T(8,128)S(1)}, f32[8,512]{1,0:T(8,128)S(1)}, u32[]{:S(2)}, u32[]{:S(2)}) collective-permute-start(f32[8,512]{1,0:T(8,128)S(1)} %copy-done.31), channel_id=1, source_target_pairs={{0,4},{4,0},{1,5},{5,1},{2,6},{6,2},{3,7},{7,3},{8,12},{12,8},{9,1... | collective-permute-start | bytes 49160 | tf_op jit(solution)/shard_map/ppermute | solution.py:812
  272.2 37.3 %collective-permute-start.21 = (f32[8,512]{1,0:T(8,128)}, f32[8,512]{1,0:T(8,128)S(1)}, u32[]{:S(2)}, u32[]{:S(2)}) collective-permute-start(f32[8,512]{1,0:T(8,128)} %get-tuple-element.50.delta_row_ref), channel_id=1, source_target_pairs={{0,4},{4,0},{1,5},{5,1},{2,6},{6,2},{3,7},{7,3},{8,12},{12,8},{9,1... | collective-permute-start | bytes 49160 | tf_op jit(solution)/shard_map/ppermute | solution.py:812
  272.2 37.3 %collective-permute-start.19 = (bf16[512,512]{1,0:T(8,128)(2,1)}, bf16[512,512]{1,0:T(8,128)(2,1)S(1)}, u32[]{:S(2)}, u32[]{:S(2)}) collective-permute-start(bf16[512,512]{1,0:T(8,128)(2,1)} %get-tuple-element.48.out_grad_ref), channel_id=1, source_target_pairs={{0,4},{4,0},{1,5},{5,1},{2,6},{6,2},{3,7},{7,3},{8,12},{12,8},{9,1... | collective-permute-start | bytes 1572872 | tf_op jit(solution)/shard_map/ppermute | solution.py:812
  348.0 24.2 %collective-permute-start.26 = (bf16[544,512]{1,0:T(8,128)(2,1)}, bf16[544,512]{1,0:T(8,128)(2,1)}, u32[]{:S(2)}, u32[]{:S(2)}) collective-permute-start(bf16[544,512]{1,0:T(8,128)(2,1)} %slice.106), channel_id=1, source_target_pairs={{0,16},{16,0},{8,24},{24,8},{1,17},{17,1},{9,25},{25,9},{2,18},{18... | collective-permute-start | bytes 1671176 | tf_op jit(solution)/shard_map/ppermute | solution.py:816
  350.6 44.5 %all-to-all-start.2 = ((bf16[32,40,512]{2,1,0:T(8,128)(2,1)}), bf16[32,40,512]{2,1,0:T(8,128)(2,1)S(1)}, u32[]{:S(2)}, u32[]{:S(2)}) async-start(bf16[32,40,512]{2,1,0:T(8,128)(2,1)} %bitcast.12), calls=%async_computation.2 | async-start | bytes 2621440 | tf_op jit(solution)/shard_map/all_to_all | solution.py:883
  359.2 19.9 %collective-permute-start.23 = (bf16[544,512]{1,0:T(8,128)(2,1)S(1)}, bf16[544,512]{1,0:T(8,128)(2,1)S(1)}, u32[]{:S(2)}, u32[]{:S(2)}) collective-permute-start(bf16[544,512]{1,0:T(8,128)(2,1)S(1)} %slice.98), channel_id=1, source_target_pairs={{0,4},{4,0},{1,5},{5,1},{2,6},{6,2},{3,7},{7,3},{8,12},{12,8},{9,1... | collective-permute-start | bytes 1671176 | tf_op jit(solution)/shard_map/ppermute | solution.py:812
  373.4 14.5 %collective-permute-start.27 = (bf16[272,512]{1,0:T(8,128)(2,1)S(1)}, bf16[272,512]{1,0:T(8,128)(2,1)S(1)}, u32[]{:S(2)}, u32[]{:S(2)}) collective-permute-start(bf16[272,512]{1,0:T(8,128)(2,1)S(1)} %slice.108), channel_id=1, source_target_pairs={{0,4},{4,0},{1,5},{5,1},{2,6},{6,2},{3,7},{7,3},{8,12},{12,8},{9,1... | collective-permute-start | bytes 835592 | tf_op jit(solution)/shard_map/ppermute | solution.py:812
  379.4 13.8 %collective-permute-start.24 = (bf16[272,512]{1,0:T(8,128)(2,1)S(1)}, bf16[272,512]{1,0:T(8,128)(2,1)S(1)}, u32[]{:S(2)}, u32[]{:S(2)}) collective-permute-start(bf16[272,512]{1,0:T(8,128)(2,1)S(1)} %slice.100), channel_id=1, source_target_pairs={{0,16},{16,0},{8,24},{24,8},{1,17},{17,1},{9,25},{25,9},{2,18},{18... | collective-permute-start | bytes 835592 | tf_op jit(solution)/shard_map/ppermute | solution.py:816
  388.0 13.5 %collective-permute-start.28 = (bf16[136,512]{1,0:T(8,128)(2,1)S(1)}, bf16[136,512]{1,0:T(8,128)(2,1)S(1)}, u32[]{:S(2)}, u32[]{:S(2)}) collective-permute-start(bf16[136,512]{1,0:T(8,128)(2,1)S(1)} %get-tuple-element.80), channel_id=1, source_target_pairs={{0,2},{1,3},{2,0},{3,1},{4,6},{5,7},{6,4},{7,5},{8,10},{9,11},{10,... | collective-permute-start | bytes 417800 | tf_op jit(solution)/shard_map/ppermute | solution.py:825
  390.5 11.1 %collective-permute-start.29 = (bf16[136,512]{1,0:T(8,128)(2,1)S(1)}, bf16[136,512]{1,0:T(8,128)(2,1)S(1)}, u32[]{:S(2)}, u32[]{:S(2)}) collective-permute-start(bf16[136,512]{1,0:T(8,128)(2,1)S(1)} %get-tuple-element.81), channel_id=1, source_target_pairs={{0,1},{1,2},{2,3},{3,0},{4,5},{5,6},{6,7},{7,4},{8,9},{9,10},{10,1... | collective-permute-start | bytes 417800 | tf_op jit(solution)/shard_map/ppermute | solution.py:825
  (41 other events, 520.5 us)
Sparse Core Ops, SparseCore 0:
  9.9 126.8 all-gather.5
  228.2 105.8 all-gather.3

commit v2 on v0

--- a/solution.py
+++ b/solution.py
@@ -1,8 +1,11 @@
+import functools
 import math
 
 import jax
 import jax.numpy as jnp
 from jax import lax
+from jax.experimental import pallas as pl
+from jax.experimental.pallas import tpu as pltpu
 from jax.sharding import PartitionSpec as P
 
 HEADS = 8
@@ -356,9 +359,800 @@
     )
 
 
+F32 = jnp.float32
+BF16 = jnp.bfloat16
+I32 = jnp.int32
+LANES = 128
+MASKED = -1e30
+VMEM_LIMIT = 56 * 1024 * 1024
+MICRO = 1.15e9
+QUICK = (1e6, 1e3)
+THEIRS = 2
+
+
+def dot_nn(left, right):
+    return lax.dot_general(left, right, (((1,), (0,)), ((), ())), preferred_element_type=F32)
+
+
+def dot_nt(left, right):
+    return lax.dot_general(left, right, (((1,), (1,)), ((), ())), preferred_element_type=F32)
+
+
+def dot_tn(left, right):
+    return lax.dot_general(left, right, (((0,), (0,)), ((), ())), preferred_element_type=F32)
+
+
+def iota(shape, dim):
+    return lax.broadcasted_iota(I32, shape, dim)
+
+
+def as_bf16(mask):
+    return jnp.where(mask, 1.0, 0.0).astype(BF16)
+
+
+def kernel_call(body, out_shape, scratch=(), grid=None, in_specs=None, out_specs=None, cost=None):
+    given = dict(grid=grid, in_specs=in_specs, out_specs=out_specs)
+    extra = {name: value for name, value in given.items() if value is not None}
+    flops, moved = cost if cost else (1e8, 1e6)
+    name = getattr(body, "func", body).__name__
+    return pl.pallas_call(
+        body,
+        name=name,
+        out_shape=out_shape,
+        scratch_shapes=list(scratch),
+        compiler_params=pltpu.CompilerParams(vmem_limit_bytes=VMEM_LIMIT),
+        cost_estimate=pl.CostEstimate(flops=int(flops), bytes_accessed=int(moved), transcendentals=0),
+        **extra,
+    )
+
+
+def sds(shape, dtype):
+    return jax.ShapeDtypeStruct(shape, dtype)
+
+
+def route_body(n_exp, capacity, ids_ref, prio_ref, live_ref, cot_ref, row_ref, col_ref, sent_ref):
+    toks = ids_ref.shape[1]
+    half = capacity // 2
+    prio_row = prio_ref[...]
+    prio_col = jnp.transpose(jnp.broadcast_to(prio_row, (8, toks)))[:, :1]
+    earlier = (prio_col < prio_row) | (
+        (prio_col == prio_row) & (iota((toks, toks), 0) < iota((toks, toks), 1))
+    )
+    live = live_ref[...] > 0.0
+    labels = iota((n_exp, toks), 0)
+    first, second = ids_ref[0:1, :], ids_ref[1:2, :]
+    wanted = ((labels == first) | (labels == second)) & live
+    taken = dot_nn(as_bf16(wanted), as_bf16(earlier))
+    places = []
+    for chosen in (first, second):
+        slot = jnp.sum(jnp.where(labels == chosen, taken, 0.0), axis=0, keepdims=True).astype(I32)
+        kept = live & (slot < capacity)
+        shard = chosen >> 2
+        local = chosen & 3
+        core = (slot >= half).astype(I32)
+        target = ((((local >> 1) * 2 + core) * 2 + (local & 1)) * (n_exp // 4)) + shard
+        places.append(jnp.where(kept, target * half + slot - core * half, -1))
+    row_id = iota((8, toks), 0)
+    rows = jnp.where(row_id == 0, places[0], jnp.where(row_id == 1, places[1], -1))
+    row_ref[...] = rows
+    col_ref[...] = jnp.transpose(rows.astype(F32)).astype(I32)
+    slots = sent_ref.shape[0]
+    spots = iota((slots, toks), 0)
+    picks = as_bf16((spots == places[0]) | (spots == places[1]))
+    sent_ref[...] = dot_nn(picks, cot_ref[...]).astype(BF16)
+
+
+def unpack_body(spots_at, n_earlier, pos_ref, *refs):
+    n_pieces = len(spots_at)
+    pieces, rest = refs[:n_pieces], refs[n_pieces:]
+    out_ref, held = rest[-2], rest[-1]
+
+    @pl.when(pl.program_id(0) == 0)
+    def _():
+        gather_pieces(pieces, held)
+
+    wanted = pos_ref[...]
+    size = pieces[0].shape[0]
+    place = jnp.full(wanted.shape, -1, I32)
+    for number, at in enumerate(spots_at):
+        inside = (wanted >= at) & (wanted < at + size)
+        place = jnp.where(inside, wanted - at + number * size, place)
+    picks = as_bf16(place == iota((wanted.shape[0], held.shape[0]), 1))
+    value = dot_nn(picks, held[...])
+    for earlier in rest[:n_earlier]:
+        value = value + earlier[...].astype(F32)
+    out_ref[...] = value.astype(BF16)
+
+
+def gather_pieces(pieces, held):
+    at = 0
+    for piece in pieces:
+        held[at : at + piece.shape[0], :] = piece[...]
+        at += piece.shape[0]
+
+
+def normalize(values):
+    center = values - jnp.mean(values, axis=-1, keepdims=True)
+    spread = jnp.mean(center * center, axis=-1, keepdims=True)
+    scale = lax.rsqrt(spread + NORM_EPSILON)
+    return center * scale, scale
+
+
+def head_lanes(head, rows):
+    return (iota((rows, LANES), 1) // HEAD_DIM) == head
+
+
+def of_head(values, head):
+    return jnp.where(head_lanes(head, values.shape[0]), values, jnp.zeros_like(values))
+
+
+def by_head(first, second):
+    return jnp.where(head_lanes(0, first.shape[0]), first, second)
+
+
+def forward_body(
+    n_exp, own_ref, other_ref, keep_ref, w_ref, pos_ref,
+    qkv_ref, normed_ref, attended_ref, residual_ref, prob_ref, sent_ref, lse_col_ref, lse_row_ref,
+    mixed_ref,
+):
+    toks, width = own_ref.shape
+    router = 4 * width
+    gain_one = w_ref[router + n_exp : router + n_exp + 16, :].astype(F32)
+    gain_two = gain_one[1:2, :]
+    gain_one = gain_one[0:1, :]
+    for part, ref in enumerate((own_ref, other_ref)):
+        normed = normalize(ref[...].astype(F32))[0] * gain_one
+        low = normed.astype(BF16)
+        if part == 0:
+            normed_ref[...] = low
+        rows = pl.ds(part * toks, toks)
+        for third in range(3):
+            made = dot_nt(low, w_ref[third * width : (third + 1) * width, :]).astype(BF16)
+            if third == 0:
+                made = made * jnp.asarray(HEAD_DIM ** (-0.5), BF16)
+            qkv_ref[rows, third * width : (third + 1) * width] = made
+    bias = jnp.where(keep_ref[...] > 0.0, 0.0, MASKED)
+    lane = iota((toks, LANES), 1)
+    logs = jnp.zeros((toks, LANES), F32)
+    for at in range(0, width, LANES):
+        queries = qkv_ref[0:toks, at : at + LANES]
+        keys = qkv_ref[:, width + at : width + at + LANES]
+        values = qkv_ref[:, 2 * width + at : 2 * width + at + LANES]
+        made = []
+        for head in range(2):
+            score = dot_nt(of_head(queries, head), keys) + bias
+            top = jnp.max(score, axis=-1, keepdims=True)
+            grown = jnp.exp(score - top)
+            total = jnp.sum(grown, axis=-1, keepdims=True)
+            made.append(dot_nn(grown.astype(BF16), values) * (1.0 / total))
+            logs = jnp.where(lane == 2 * (at // LANES) + head, top + jnp.log(total), logs)
+        attended_ref[:, at : at + LANES] = by_head(*made)
+    lse_col_ref[...] = logs
+    lse_row_ref[...] = jnp.transpose(lse_col_ref[...])[:8, :]
+    branch = dot_nn(attended_ref[...].astype(BF16), w_ref[3 * width : 4 * width, :])
+    residual = own_ref[...].astype(F32) + branch
+    residual_ref[...] = residual
+    mixed = (normalize(residual)[0] * gain_two).astype(BF16)
+    mixed_ref[...] = mixed
+    logits = dot_nt(mixed, w_ref[router : router + n_exp, :])
+    prob_ref[...] = jax.nn.softmax(logits, axis=-1)
+    slots = sent_ref.shape[0]
+    spots = iota((slots, toks), 0)
+    picks = as_bf16((spots == pos_ref[0:1, :]) | (spots == pos_ref[1:2, :]))
+    sent_ref[...] = dot_nn(picks, mixed).astype(BF16)
+
+
+def gelu_parts(value):
+    below = 0.5 + 0.5 * lax.erf(value * 0.7071067811865476)
+    return value * below, below + value * jnp.exp(-0.5 * value * value) * 0.3989422804014327
+
+
+def expert_body(
+    n_exp, expert_ref, got_ref, cot_ref, near_ref, far_in_ref, far_out_ref, router_ref,
+    active_ref, hidden_ref, scaled_ref, result_ref, back_ref, router_grad_ref,
+):
+    @pl.when(pl.program_id(0) == 0)
+    def _():
+        router_grad_ref[...] = jnp.zeros_like(router_grad_ref)
+
+    expert = expert_ref[0]
+    got, cot = got_ref[...], cot_ref[...]
+    labels = iota((got.shape[0], n_exp), 1)
+    share = jax.nn.softmax(dot_nt(got, router_ref[...]), axis=-1)
+    gate = jnp.sum(jnp.where(labels == expert, share, 0.0), axis=-1, keepdims=True)
+    scaled = (cot.astype(F32) * gate).astype(BF16)
+    scaled_ref[...] = scaled
+    half = near_ref.shape[0] // 2
+    total = total_back = 0.0
+    halves = ((near_ref[:half, :], near_ref[half:, :]), (far_in_ref[...], far_out_ref[...]))
+    for number, (w_in, w_out) in enumerate(halves):
+        at = slice(number * half, (number + 1) * half)
+        active, slope = gelu_parts(dot_nt(got, w_in))
+        low = active.astype(BF16)
+        active_ref[:, at] = low
+        grad = (dot_nt(scaled, w_out) * slope).astype(BF16)
+        hidden_ref[:, at] = grad
+        total = total + dot_nn(low, w_out)
+        total_back = total_back + dot_nn(grad, w_in)
+    result = total.astype(BF16)
+    result_ref[...] = result
+    inner = jnp.sum(result.astype(F32) * cot.astype(F32), axis=-1, keepdims=True)
+    grad = share * (jnp.where(labels == expert, inner, 0.0) - gate * inner)
+    low = grad.astype(BF16)
+    back_ref[...] = (total_back + dot_nn(low, router_ref[...])).astype(BF16)
+    router_grad_ref[...] += dot_tn(low, got)
+
+
+def weight_grad_body(hidden_ref, active_ref, got_ref, scaled_ref, mine_ref, *theirs_refs):
+    half = hidden_ref.shape[1] // 2
+    parts = max(len(theirs_refs) // 2, 1)
+    for number, ref in enumerate(theirs_refs):
+        size = ref.shape[0]
+        at = slice(half + number % parts * size, half + (number % parts + 1) * size)
+        left, right = ((hidden_ref, got_ref), (active_ref, scaled_ref))[number // parts]
+        ref[...] = dot_tn(left[:, at], right[...]).astype(ref.dtype)
+    mine_ref[:half, :] = dot_tn(hidden_ref[:, :half], got_ref[...])
+    mine_ref[half:, :] = dot_tn(active_ref[:, :half], scaled_ref[...])
+
+
+def norm_back(hat, scale, gain, grad):
+    inner = grad * gain
+    first = jnp.mean(inner, axis=-1, keepdims=True)
+    second = jnp.mean(inner * hat, axis=-1, keepdims=True)
+    return (inner - first - hat * second) * scale
+
+
+def middle_body(
+    n_exp, back_ref, pos_ref, residual_ref, cot_ref, keep_ref, attended_ref, w_ref,
+    grad_ref, out_grad_ref, delta_col_ref, delta_row_ref, gain_ref,
+):
+    toks, width = residual_ref.shape
+    router = 4 * width
+    slots = back_ref.shape[0]
+    gain_two = w_ref[router + n_exp : router + n_exp + 16, :].astype(F32)[1:2, :]
+    spots = iota((toks, slots), 1)
+    picks = as_bf16((spots == pos_ref[:, 0:1]) | (spots == pos_ref[:, 1:2]))
+    grad_mixed = dot_nn(picks, back_ref[...])
+    hat, scale = normalize(residual_ref[...])
+    gain_ref[...] = jnp.broadcast_to(
+        jnp.sum(grad_mixed * hat, axis=0, keepdims=True), gain_ref.shape
+    )
+    grad_rows = cot_ref[...].astype(F32) * keep_ref[...]
+    grad = grad_rows + norm_back(hat, scale, gain_two, grad_mixed)
+    grad_ref[...] = grad
+    low = grad.astype(BF16)
+    out_grad = dot_nt(low, w_ref[3 * width : 4 * width, :]).astype(BF16)
+    out_grad_ref[...] = out_grad
+    product = out_grad.astype(F32) * attended_ref[...]
+    delta = jnp.zeros((toks, LANES), F32)
+    lane = iota((toks, LANES), 1)
+    for head in range(HEADS):
+        at = (head // 2) * LANES
+        part = jnp.where(head_lanes(head % 2, toks), product[:, at : at + LANES], 0.0)
+        delta = jnp.where(lane == head, jnp.sum(part, axis=-1, keepdims=True), delta)
+    delta_col_ref[...] = delta
+    delta_row_ref[...] = jnp.transpose(delta)[:8, :]
+
+
+def inner_body(
+    n_exp, qkv_ref, out_grad_ref, lse_ref, delta_ref, keep_ref, attended_ref, grad_ref, router_grad_ref, gain_ref,
+    query_ref, kv_ref, early_ref,
+):
+    toks, width = out_grad_ref.shape
+    bias = jnp.where(keep_ref[...] > 0.0, 0.0, MASKED)
+    for at in range(0, width, LANES):
+        queries = qkv_ref[0:toks, at : at + LANES]
+        keys = qkv_ref[:, width + at : width + at + LANES]
+        values = qkv_ref[:, 2 * width + at : 2 * width + at + LANES]
+        out_grad = out_grad_ref[:, at : at + LANES]
+        made = []
+        for head in range(2):
+            line = 2 * (at // LANES) + head
+            score = dot_nt(of_head(queries, head), keys) + bias
+            prob = jnp.exp(score - lse_ref[:, line : line + 1])
+            slope = dot_nt(of_head(out_grad, head), values)
+            grad = (prob * (slope - delta_ref[:, line : line + 1])).astype(BF16)
+            made.append(
+                (dot_nn(grad, keys), dot_tn(grad[:, :toks], queries), dot_tn(prob[:, :toks].astype(BF16), out_grad))
+            )
+        query_ref[:, at : at + LANES] = (by_head(made[0][0], made[1][0]) * HEAD_DIM ** (-0.5)).astype(BF16)
+        kv_ref[0, :, at : at + LANES] = by_head(made[0][1], made[1][1])
+        kv_ref[1, :, at : at + LANES] = by_head(made[0][2], made[1][2])
+    early_ref[0:width, :] = dot_tn(attended_ref[...].astype(BF16), grad_ref[...].astype(BF16)).astype(BF16)
+    early_ref[width : width + n_exp, :] = router_grad_ref[...].astype(BF16)
+    row_id = iota((16, width), 0)
+    early_ref[width + n_exp : width + n_exp + 16, :] = jnp.where(
+        row_id == 0, gain_ref[0:1, :], 0.0
+    ).astype(BF16)
+
+
+def outer_body(
+    n_exp, qkv_ref, out_grad_ref, sums_ref, keep_ref, query_ref, kv_ref, normed_ref, own_ref, w_ref,
+    pieces_ref, grad_normed_ref, held,
+):
+    toks, width = query_ref.shape
+    held[:, 0:width] = query_ref[...]
+    bias = jnp.where(keep_ref[...] > 0.0, 0.0, MASKED)
+    for at in range(0, width, LANES):
+        queries = qkv_ref[toks : 2 * toks, at : at + LANES]
+        out_grad = out_grad_ref[:, at : at + LANES]
+        keys = qkv_ref[0:toks, width + at : width + at + LANES]
+        values = qkv_ref[0:toks, 2 * width + at : 2 * width + at + LANES]
+        made = []
+        for head in range(2):
+            line = 2 * (at // LANES) + head
+            score = dot_nt(of_head(keys, head), queries) + bias
+            prob = jnp.exp(score - sums_ref[line : line + 1, :])
+            slope = dot_nt(of_head(values, head), out_grad)
+            grad = (prob * (slope - sums_ref[HEADS + line : HEADS + line + 1, :])).astype(BF16)
+            made.append((dot_nn(grad, queries), dot_nn(prob.astype(BF16), out_grad)))
+        for number in range(2):
+            total = kv_ref[number, :, at : at + LANES] + by_head(made[0][number], made[1][number])
+            held[:, (number + 1) * width + at : (number + 1) * width + at + LANES] = total.astype(BF16)
+    pieces_ref[0 : 3 * width, :] = dot_tn(held[...], normed_ref[...]).astype(BF16)
+    grad_normed = dot_nn(held[...], w_ref[0 : 3 * width, :])
+    grad_normed_ref[...] = grad_normed
+    gain_grad = jnp.sum(grad_normed * normalize(own_ref[...].astype(F32))[0], axis=0, keepdims=True)
+    pieces_ref[3 * width : 3 * width + 16, :] = jnp.where(
+        iota((16, width), 0) == 0, gain_grad, 0.0
+    ).astype(BF16)
+
+
+def tokens_body(n_exp, grad_normed_ref, own_ref, w_ref, grad_ref, out_ref):
+    at = 4 * own_ref.shape[1] + n_exp
+    gain_one = w_ref[at : at + 16, :].astype(F32)[0:1, :]
+    hat, scale = normalize(own_ref[...].astype(F32))
+    out_ref[...] = grad_ref[...] + norm_back(hat, scale, gain_one, grad_normed_ref[...])
+
+
+def spread_body(starts, pos_ref, late_ref, late_far_ref, early_ref, early_far_ref, out_ref, held):
+    cut = late_ref.shape[0]
+    held[0:cut, :] = total_f32(late_ref[...], late_far_ref[...]).astype(BF16)
+    held[cut:, :] = total_f32(early_ref[...], early_far_ref[...]).astype(BF16)
+    size = out_ref.shape[1]
+    for number, start in enumerate(starts):
+        picks = as_bf16(iota((size, held.shape[0]), 0) + start == pos_ref[...])
+        out_ref[number] = dot_nn(picks, held[...]).astype(BF16)
+
+
+def room_of(owned, n_dev):
+    return min(owned, -(-(owned // n_dev * 5 // 4) // 16) * 16)
+
+
+def sent_at(partner):
+    return ((partner >> 1) & 1) * 4 + ((partner >> 2) & 1) * 2 + (partner & 1)
+
+
+def got_at(partner):
+    return ((partner >> 2) & 1) * 4 + (partner & 1) * 2 + ((partner >> 1) & 1)
+
+
+def plan_body(n_dev, room, me_ref, owner_ref, row_ref, col_ref, most_ref):
+    me = me_ref[0]
+    owned = owner_ref.shape[1]
+    source = owner_ref[...] >> (owned.bit_length() - 1)
+    spot = owner_ref[...] & (owned - 1)
+    total = n_dev * n_dev
+    classes = iota((n_dev, owned), 0)
+    member = jnp.concatenate([classes == source[t : t + 1, :] for t in range(n_dev)], axis=0)
+    ones = as_bf16(member)
+    step = 256
+    before = as_bf16(iota((step, step), 0) < iota((step, step), 1))
+    count = jnp.zeros((total, 1), F32)
+    ranks = []
+    for at in range(0, owned, step):
+        part = ones[:, at : at + step]
+        ranks.append(dot_nn(part, before) + count)
+        count = count + jnp.sum(part.astype(F32), axis=1, keepdims=True)
+    most_ref[...] = jnp.broadcast_to(jnp.max(count, axis=0, keepdims=True).astype(I32), most_ref.shape)
+    line = iota((total, 1), 0)
+    to, of = line // n_dev, line % n_dev
+    rank = jnp.concatenate(ranks, axis=1)
+    turn = ((rank + 0.5) * (1.0 / room)).astype(I32)
+    inside = rank.astype(I32) + turn * ((n_dev - 1) * room)
+    arrives = jnp.sum(
+        jnp.where(member & (to == me), inside + got_at(of ^ to) * room, 0), axis=0, keepdims=True
+    )
+    leaves = inside + sent_at(of ^ to) * room
+    half = owned // LANES
+    found = jnp.zeros((2 * half, LANES), F32)
+    high, lanes = iota((half, owned), 0), iota((LANES, owned), 0)
+    for t in range(n_dev):
+        mine = slice(t * n_dev, (t + 1) * n_dev)
+        chosen = member[mine] & (of[mine] == me)
+        place = jnp.sum(jnp.where(chosen, leaves[mine], 0), axis=0, keepdims=True)
+        hit = (spot[t : t + 1, :] // LANES == high) & (source[t : t + 1, :] == me)
+        left = jnp.concatenate(
+            [jnp.where(hit, place // LANES, 0), jnp.where(hit, place % LANES, 0)], axis=0
+        ).astype(F32).astype(BF16)
+        found = found + dot_nt(left, as_bf16((spot[t : t + 1, :] % LANES) == lanes))
+    found = found[:half] * float(LANES) + found[half:]
+    leave_row = jnp.concatenate([found[a : a + 1, :] for a in range(half)], axis=1)
+    rows = jnp.concatenate([leave_row, arrives.astype(F32), jnp.zeros((6, owned), F32)], axis=0)
+    row_ref[...] = rows.astype(I32)
+    col_ref[...] = jnp.transpose(rows).astype(I32)
+
+
+LEAVES, ARRIVES = 0, 1
+
+
+def put_rows(line, base_ref, pos_ref, held, outs, tile):
+    wanted = pos_ref[line : line + 1, :] - base_ref[0]
+    base = 0
+    for out in outs:
+        for at in range(0, out.shape[0], tile):
+            picks = as_bf16(iota((tile, held.shape[0]), 0) + (base + at) == wanted)
+            out[at : at + tile, :] = dot_nn(picks, held[...]).astype(BF16)
+        base += out.shape[0]
+
+
+def put_body(line, tile, base_ref, pos_ref, rows_ref, *outs):
+    put_rows(line, base_ref, pos_ref, rows_ref, outs, tile)
+
+
+def sum_put_body(line, tile, n_in, base_ref, pos_ref, mine_ref, *refs):
+    others, outs, held = refs[:n_in], refs[n_in:-1], refs[-1]
+    gather_pieces(others, held)
+    held[...] = total_f32(mine_ref[...], held[...]).astype(BF16)
+    put_rows(line, base_ref, pos_ref, held, outs, tile)
+
+
+def take_body(line, tile, base_ref, pos_ref, *refs):
+    pieces, out, held = refs[:-2], refs[-2], refs[-1]
+    gather_pieces(pieces, held)
+    for at in range(0, out.shape[0], tile):
+        wanted = pos_ref[at : at + tile, line : line + 1] - base_ref[0]
+        picks = as_bf16(iota((tile, held.shape[0]), 1) == wanted)
+        out[at : at + tile, :] = dot_nn(picks, held[...]).astype(BF16)
+
+
+def take_more_body(line, tile, base_ref, pos_ref, *refs):
+    pieces, more, out, held = refs[:-3], refs[-3], refs[-2], refs[-1]
+    gather_pieces(pieces, held)
+    for at in range(0, out.shape[0], tile):
+        wanted = pos_ref[at : at + tile, line : line + 1] - base_ref[0]
+        picks = as_bf16(iota((tile, held.shape[0]), 1) == wanted)
+        out[at : at + tile, :] = (dot_nn(picks, held[...]) + more[at : at + tile, :].astype(F32)).astype(BF16)
+
+
+def adam_body(n_in, pos_ref, *refs):
+    pieces = refs[:n_in]
+    more_ref, first_ref, second_ref, weight_ref, grad_ref, first_new, second_new, weight_new, held = refs[n_in:]
+
+    @pl.when(pl.program_id(0) == 0)
+    def _():
+        gather_pieces(pieces, held)
+
+    picks = as_bf16(iota((grad_ref.shape[0], held.shape[0]), 1) == pos_ref[:, LEAVES : LEAVES + 1])
+    grad = dot_nn(picks, held[...]) + more_ref[...].astype(F32)
+    grad_ref[...] = grad
+    made = adam_update(grad, first_ref[...], second_ref[...], weight_ref[...].astype(F32))
+    first_new[...], second_new[...], weight_new[...] = made
+
+
+def mixture_body(result_ref, pos_ref, ids_ref, prob_ref, residual_ref, out_ref):
+    toks = residual_ref.shape[0]
+    slots = result_ref.shape[0]
+    share = prob_ref[...]
+    total = residual_ref[...]
+    for number in range(2):
+        picks = as_bf16(iota((toks, slots), 1) == pos_ref[:, number : number + 1])
+        mine = iota(share.shape, 1) == ids_ref[:, number : number + 1]
+        gate = jnp.sum(jnp.where(mine, share, 0.0), axis=-1, keepdims=True)
+        total = total + gate * dot_nn(picks, result_ref[...])
+    out_ref[...] = total.astype(BF16)
+
+
+SWAP = [(0, 1), (1, 0)]
+SWAP_CORE = [(0, 1), (1, 0), (2, 3), (3, 2)]
+SWAP_Y = [(0, 2), (2, 0), (1, 3), (3, 1)]
+
+
+def swap_x(value):
+    return lax.ppermute(value, "ctx", SWAP)
+
+
+def swap_y(value):
+    return lax.ppermute(value, "dp", SWAP_Y)
+
+
+def swap_x_y(value):
+    return lax.ppermute(value, ("dp", "ctx"), [(i, i ^ 5) for i in range(8)])
+
+
+def swap_core(value):
+    return lax.ppermute(value, "dp", SWAP_CORE)
+
+
+def shift_z(value, by):
+    count = lax.axis_size("expert")
+    return lax.ppermute(value, "expert", [(i, (i + by) % count) for i in range(count)])
+
+
+def after(values, *others):
+    values = list(values)
+    return lax.optimization_barrier((*values, *others))[: len(values)]
+
+
+def total_f32(first, second):
+    return first.astype(F32) + second.astype(F32)
+
+
+def on_chip_experts(
+    tokens, cotangent, pad_mask, expert_ids, slot_priority, shared_slots, shared_first, shared_second,
+    shared_owner, expert_slots, expert_first, expert_second, expert_owner,
+):
+    toks, width = tokens.shape[1], tokens.shape[2]
+    n_z = lax.axis_size("expert")
+    n_exp = EXP_DEV * n_z
+    capacity = (10 * toks + 4 * n_exp - 1) // (4 * n_exp)
+    slots = n_exp * capacity
+    everyone = ("dp", "ctx", "expert")
+    dp, mx, mz = lax.axis_index("dp"), lax.axis_index("ctx"), lax.axis_index("expert")
+    my, mc = dp // 2, dp % 2
+
+    own_count = shared_slots.shape[0]
+    stride = -(-own_count // 8) * 8
+    padded = jnp.pad(shared_slots, ((0, stride - own_count), (0, 0)))
+    line = [padded] + [shift_z(padded, by) for by in range(1, n_z)]
+    part_a = jnp.concatenate(line[: n_z // 2], axis=0)
+    part_b = jnp.concatenate(line[n_z // 2 :], axis=0)
+    a_y, b_x = swap_y(part_a), swap_x(part_b)
+    pair_a, pair_b = jnp.concatenate([part_a, a_y], axis=0), jnp.concatenate([part_b, b_x], axis=0)
+    first_near, last_near = [pair_a, pair_b], [swap_x(pair_a), swap_y(pair_b)]
+    first_far = [swap_core(piece) for piece in first_near]
+    last_far = [swap_core(piece) for piece in last_near]
+
+    owner_dev, owner_row = shared_owner // own_count, shared_owner % own_count
+    o_z, o_x, o_dp = owner_dev % n_z, owner_dev // n_z % 2, owner_dev // (n_z * 2)
+    in_c, in_y, in_x = (o_dp % 2) ^ mc, (o_dp // 2) ^ my, o_x ^ mx
+    in_z = (mz - o_z + n_z) % n_z
+    late = in_z // (n_z // 2)
+    cross = jnp.where(late == 0, in_y + 2 * in_x, in_x + 2 * in_y)
+    place = (((in_c * 2 + late) * 4 + cross) * (n_z // 2) + in_z % (n_z // 2)) * stride + owner_row
+    total_slots = 8 * n_z * stride
+    row_count = -(-shared_owner.shape[0] // 16) * 16
+    place_col = jnp.pad(place, (0, row_count - place.shape[0]), constant_values=-1)[:, None]
+    gain_at = 4 * width + n_exp
+    none = jnp.full((15,), -1, I32)
+    place_row = jnp.concatenate(
+        [place[: 3 * width], place[gain_at : gain_at + 1], none, place[3 * width : gain_at], place[gain_at + 1 :], none]
+    )[None, :]
+
+    own, other = tokens[0], swap_x(after([tokens[0]], *last_near)[0])
+    ids = expert_ids[0]
+    live = pad_mask.astype(F32)
+    live_other = swap_x(pad_mask).astype(F32)
+    keep_row = jnp.concatenate([live, live_other], axis=1)
+    keep_col = live.reshape(toks, 1)
+    pos_row, pos_col, cot_sent = kernel_call(
+        functools.partial(route_body, n_exp, capacity),
+        (sds((8, toks), I32), sds((toks, 8), I32), sds((slots, width), BF16)),
+        cost=(4 * MICRO, 1e6),
+    )(ids.T, slot_priority.astype(F32), live, cotangent[0])
+
+    def exchange(rows):
+        return lax.all_to_all(rows, everyone, split_axis=0, concat_axis=0, tiled=True)
+
+    cot_got = exchange(after([cot_sent], part_a, part_b)[0])
+
+    local = my * 2 + mx
+    group, n_dev = dp * 2 + mx, 8
+    owned = expert_slots.shape[1]
+    room = room_of(owned, n_dev)
+    owner = jnp.transpose(
+        expert_owner[0].reshape(2, 2, 2, 2, FF // 2), (0, 3, 1, 2, 4)
+    ).reshape(n_dev, owned)
+    held = [pltpu.VMEM((n_dev * room, width), BF16)]
+    sent_shapes, got_shapes = [sds((4 * room, width), BF16)] * 2, [sds((2 * room, width), BF16)] * 4
+    smem, vmem = pl.BlockSpec(memory_space=pltpu.SMEM), pl.BlockSpec(memory_space=pltpu.VMEM)
+    plan_row, plan_col, most = kernel_call(
+        functools.partial(plan_body, n_dev, room),
+        (sds((8, owned), I32), sds((owned, 8), I32), sds((8, LANES), I32)), cost=(5 * MICRO, 1e6),
+        in_specs=[smem, vmem],
+    )(group.astype(I32).reshape(1), *after([owner], pos_row))
+    rounds = (most[0, 0] + room - 1) // room
+    swaps = (swap_x, swap_y, swap_x_y)
+
+    def with_base(body, out_shape, scratch, arrays, number=0):
+        base = jnp.full((1,), number * n_dev * room, I32)
+        return kernel_call(
+            body, out_shape, scratch, in_specs=[smem] + [vmem] * len(arrays), cost=(8 * MICRO, 1e6)
+        )(base, *arrays)
+
+    def send_pieces(near, far):
+        got = [near[:room], far[:room]]
+        for by, swap in enumerate(swaps, 1):
+            rows = slice(by * room, (by + 1) * room)
+            got.append(swap(jnp.concatenate([near[rows], far[rows]], axis=0)))
+        return got
+
+    def return_near(pieces, *others):
+        x, y, x_y = after(pieces[1:], *others) if others else pieces[1:]
+        return [pieces[0], swap_x(x), swap_y(pieces[2]), swap_x_y(x_y)]
+
+    def return_far(got):
+        near = [piece[:room] for piece in got]
+        return [*near, swap_core(jnp.concatenate([piece[room:] for piece in got], axis=0))]
+
+    put_leaving = functools.partial(put_body, LEAVES, room)
+    take_tile = 256 if owned % 256 == 0 else owned
+    take_more = functools.partial(take_body, ARRIVES, take_tile)
+
+    def more_weights(number, total):
+        near, far = with_base(put_leaving, sent_shapes, (), [plan_row, expert_slots[0]], number)
+        moved = send_pieces(near, swap_core(far))
+        part = with_base(take_more, sds((owned, width), BF16), held, [plan_col, *moved], number)
+        return total + part
+
+    more_rows = lax.fori_loop(1, rounds, more_weights, jnp.zeros((owned, width), BF16))
+    near, far = with_base(put_leaving, sent_shapes, (), [*after([plan_row], part_a, part_b, more_rows), expert_slots[0]])
+    near_sent, far_sent = after([near, far], *last_near)
+    far_sent = swap_core(far_sent)
+    moved = send_pieces(*after([near_sent, far_sent], other))
+
+    half_slots = total_slots // 2
+    piece = half_slots // 4
+    row_tile = row_count // 5 if row_count % 80 == 0 else row_count
+
+    def unpack(spots, pieces, earlier):
+        rows_of = lambda columns: pl.BlockSpec((row_tile, columns), lambda i: (i, 0))
+        return kernel_call(
+            functools.partial(unpack_body, spots, len(earlier)), sds((row_count, width), BF16),
+            [pltpu.VMEM((len(pieces) * piece, width), BF16)],
+            grid=(row_count // row_tile,),
+            in_specs=[rows_of(1)] + [pl.BlockSpec((piece, width), lambda i: (0, 0))] * len(pieces)
+            + [rows_of(width)] * len(earlier),
+            out_specs=rows_of(width),
+            cost=(7 * MICRO, 1e6),
+        )(place_col, *pieces, *earlier)
+
+    first_rows = unpack(
+        [0, 2 * piece, half_slots, half_slots + 2 * piece], [*after(first_near, near), *first_far], []
+    )
+    near_rows = unpack([piece, 3 * piece], last_near, [first_rows])
+    weights = unpack([half_slots + piece, half_slots + 3 * piece], last_far, [near_rows])
+
+    (qkv, normed, attended, residual, prob, sent, lse_col, lse_row) = kernel_call(
+        functools.partial(forward_body, n_exp),
+        (
+            sds((2 * toks, 3 * width), BF16), sds((toks, width), BF16), sds((toks, width), F32),
+            sds((toks, width), F32), sds((toks, n_exp), F32), sds((slots, width), BF16),
+            sds((toks, LANES), F32), sds((8, toks), F32),
+        ),
+        [pltpu.VMEM((toks, width), BF16)],
+        cost=(13 * MICRO, 1e6),
+    )(own, other, keep_row, weights, pos_row)
+    got = exchange(sent)
+    near_weights = with_base(
+        functools.partial(take_more_body, ARRIVES, take_tile), sds((owned, width), BF16), held,
+        [*after([plan_col], sent), *moved, more_rows],
+    )
+
+    far_weights = [swap_core(near_weights[: FF // 2]), swap_core(near_weights[FF // 2 :])]
+
+    expert_id = (mz * EXP_DEV + local).astype(I32).reshape(1)
+    tile = 256 if slots % 256 == 0 else slots
+    router_rows = weights[4 * width : 4 * width + n_exp]
+    whole = lambda shape: pl.BlockSpec(shape, lambda i: (0, 0))
+    rows_of = lambda columns: pl.BlockSpec((tile, columns), lambda i: (i, 0))
+    active, hidden, scaled, result, back, router_grad = kernel_call(
+        functools.partial(expert_body, n_exp),
+        (
+            sds((slots, FF), BF16), sds((slots, FF), BF16), sds((slots, width), BF16),
+            sds((slots, width), BF16), sds((slots, width), BF16), sds((n_exp, width), F32),
+        ),
+        grid=(slots // tile,),
+        in_specs=[
+            pl.BlockSpec(memory_space=pltpu.SMEM), rows_of(width), rows_of(width),
+            whole((FF, width)), whole((FF // 2, width)), whole((FF // 2, width)), whole((n_exp, width)),
+        ],
+        out_specs=(
+            rows_of(FF), rows_of(FF), rows_of(width), rows_of(width), rows_of(width), whole((n_exp, width)),
+        ),
+        cost=(19 * MICRO, 1e6),
+    )(expert_id, got, cot_got, near_weights, *far_weights, router_rows)
+    back_got = exchange(back)
+
+    mine, *theirs = kernel_call(
+        weight_grad_body, [sds((FF, width), F32)] + [sds((FF // THEIRS, width), BF16)] * THEIRS, cost=(10 * MICRO, 1e7)
+    )(hidden, active, got, scaled)
+    theirs_got = [swap_core(part) for part in theirs]
+    put_returning = functools.partial(sum_put_body, ARRIVES, room, THEIRS)
+    held_owned = [pltpu.VMEM((owned, width), BF16)]
+    moved = with_base(put_returning, got_shapes, held_owned, [plan_row, mine, *theirs_got])
+    back_got, *moved = after([back_got, *moved])
+
+    def more_grads(number, total):
+        parts = with_base(put_returning, got_shapes, held_owned, [plan_row, mine, *theirs_got], number)
+        parts = return_far(return_near(parts))
+        take = functools.partial(take_body, LEAVES, take_tile)
+        return total + with_base(take, sds((owned, width), BF16), held, [plan_col, *parts], number)
+
+    more = lax.fori_loop(1, rounds, more_grads, after([jnp.zeros((owned, width), BF16)], back_got)[0])
+    grad_residual, out_grad, delta_col, delta_row, gain_two = kernel_call(
+        functools.partial(middle_body, n_exp),
+        (
+            sds((toks, width), F32), sds((toks, width), BF16), sds((toks, LANES), F32),
+            sds((8, toks), F32), sds((8, width), F32),
+        ),
+        cost=(6 * MICRO, 1e6),
+    )(back_got, pos_col, residual, cotangent[0], keep_col, attended, weights)
+    out_grad_other = swap_x(out_grad)
+    sums_other = swap_x(jnp.concatenate([lse_row, delta_row], axis=0))
+    moved = return_near(moved, out_grad_other)
+    result_got = exchange(after([result], out_grad_other, more)[0])
+    query_grad, kv_grad, early = kernel_call(
+        functools.partial(inner_body, n_exp),
+        (sds((toks, width), BF16), sds((2, toks, width), F32), sds((width + n_exp + 16, width), BF16)),
+        cost=(15 * MICRO, 1e6),
+    )(qkv, out_grad, lse_col, delta_col, keep_row, attended, grad_residual, router_grad, gain_two)
+    early_far = swap_core(early)
+    late, grad_normed = kernel_call(
+        functools.partial(outer_body, n_exp),
+        (sds((3 * width + 16, width), BF16), sds((toks, width), F32)),
+        [pltpu.VMEM((toks, 3 * width), BF16)],
+        cost=(12 * MICRO, 1e6),
+    )(
+        qkv, *after([out_grad_other], moved[2]), sums_other, keep_col, query_grad, kv_grad, normed, own, weights,
+    )
+    late_far = swap_core(late)
+    grad_tokens = kernel_call(
+        functools.partial(tokens_body, n_exp), sds((toks, width), F32), cost=(2 * MICRO, 4e6)
+    )(grad_normed, own, weights, grad_residual)
+    quarter = half_slots // 2
+    eighth, sixteenth = quarter // 2, quarter // 4
+    count = place_row.shape[1]
+
+    def spread(starts, *others):
+        return kernel_call(
+            functools.partial(spread_body, starts), sds((2, eighth, width), BF16),
+            [pltpu.VMEM((count, width), BF16)], cost=(6 * MICRO, 1e6),
+        )(*after([place_row], *others), late, late_far, early, early_far)
+
+    sends = spread((eighth, quarter + eighth))
+    got_a, got_b = swap_x(sends[0]), swap_y(sends[1])
+    keeps = spread((0, quarter), sends)
+    moved = return_far(after(moved, keeps))
+
+    tile = 256 if owned % 256 == 0 else owned
+    rows_of = lambda columns: pl.BlockSpec((tile, columns), lambda i: (i, 0))
+    expert_new = kernel_call(
+        functools.partial(adam_body, len(moved)), [sds((owned, width), F32)] * 4, held,
+        grid=(owned // tile,),
+        in_specs=[rows_of(8)] + [pl.BlockSpec(piece.shape, lambda i: (0, 0)) for piece in moved] + [rows_of(width)] * 4,
+        out_specs=[rows_of(width)] * 4,
+        cost=(14 * MICRO, 3e7),
+    )(plan_col, *moved, more, expert_first[0], expert_second[0], expert_slots[0])
+
+    sum_a = total_f32(keeps[0], got_a).astype(BF16)
+    sum_b = total_f32(keeps[1], got_b).astype(BF16)
+    got_a, got_b = swap_y(sum_a[sixteenth:]), swap_x(sum_b[sixteenth:])
+    sum_a = total_f32(sum_a[:sixteenth], got_a).astype(BF16)
+    sum_b = total_f32(sum_b[:sixteenth], got_b).astype(BF16)
+    lines = [sum_a[i * stride : (i + 1) * stride] for i in range(n_z // 2)]
+    lines += [sum_b[i * stride : (i + 1) * stride] for i in range(n_z // 2)]
+    shared_grad = lines[0].astype(F32)
+    for by in range(1, n_z):
+        shared_grad = shared_grad + shift_z(lines[by], n_z - by).astype(F32)
+    shared_grad = shared_grad[:own_count]
+
+    output = kernel_call(
+        mixture_body, sds((toks, width), BF16), cost=(4 * slots * toks * width, 4e6)
+    )(result_got, pos_col, ids, prob, residual)
+
+    shared_new = adam_update(shared_grad, shared_first, shared_second, shared_slots.astype(F32))
+    return (
+        output[None], grad_tokens[None], shared_grad, *shared_new,
+        *(value[None] for value in expert_new),
+    )
+
+
 def solution(mesh):
+    sizes = mesh.shape
+    chip_experts = (sizes["dp"], sizes["ctx"], sizes["expert"]) == (4, 2, 4)
     return jax.shard_map(
-        on_device,
+        on_chip_experts if chip_experts else on_device,
         mesh=mesh,
         in_specs=(
             P(("dp", "expert"), "ctx", None),

time: 978 us -> 359 us (0.37)
  local copies, waits for them, and re-layouts: 326 us -> 29.4 us
  blocking collectives: 201 us -> 0 us
  Pallas kernels: 0 us -> 170 us
  waiting for transfers between devices: 200 us -> 79.3 us
  matrix products: 112 us -> 0 us
  other arithmetic: 92.4 us -> 13.3 us
  starting transfers between devices: 20.9 us -> 56.4 us
  between operations: 16.2 us -> 2 us
    unnamed x1 -> x0, blocking collectives: 196 us -> none
    pallas_call x0 -> x19, Pallas kernels: none -> 170 us  [the longest x3 26.2 us: with_base(): kernel_call(body, out_shape, scratch, in_specs=[smem] + [vmem] * len(arra...]
    gather x17 -> x0, local copies, waits for them, and re-layouts: 133 us -> none  [the longest x1 75 us: on_device(): all_expert[0][expert_owner[0]].reshape(EXP_DEV, 2, FF, features)]
    dot_general x29 -> x0, matrix products: 112 us -> none  [the longest x1 14.8 us: on_device(): jnp.einsum('ecd,efd->ecf', grad_received, w_out, preferred_element_type=j...]
    unnamed x184 -> x74, local copies, waits for them, and re-layouts: 106 us -> 9.29 us
    all_gather x4 -> x0, waiting for transfers between devices: 76.3 us -> none  [the longest x1 65.7 us: on_device(): lax.all_gather(shared_slots, ('dp', 'ctx', 'expert'), axis=0, tiled=True)]
    ppermute x0 -> x36, waiting for transfers between devices: none -> 72.5 us  [the longest x10 34.4 us: swap_x(): return lax.ppermute(value, 'ctx', SWAP)]
    all_to_all x4, waiting for transfers between devices: 75.5 us -> 6.75 us  [exchange(): lax.all_to_all(rows, everyone, split_axis=0, concat_axis=0, tiled=True)]
  transfers between devices with their start and end apart: 12 -> 40, of which waited for: 7 -> 12; matrix products, arithmetic and copies ran while one was open for 51% -> 10% of each run, Pallas kernels for 0% -> 37%
where the time goes in v2:
time: 359 us; the launch traced here: 353 us
  Pallas kernels  170 us (47%)
  waiting for transfers between devices  79.3 us (22%)
  starting transfers between devices  56.4 us (16%)
  local copies, waits for them, and re-layouts  29.4 us (8%)
  other arithmetic  13.3 us (4%)
    ppermute x10, waiting for transfers between devices, swap_x(): return lax.ppermute(value, 'ctx', SWAP)  34.4 us
    pallas_call x3, Pallas kernels, with_base(): kernel_call(body, out_shape, scratch, in_specs=[smem] + [vmem] * len(arra...  26.2 us
    pallas_call x3, Pallas kernels, unpack(): kernel_call(functools.partial(unpack_body, spots, len(earlier)), sds((row...  23.9 us
    all_to_all x4, starting transfers between devices, exchange(): lax.all_to_all(rows, everyone, split_axis=0, concat_axis=0, tiled=True)  20.1 us
    ppermute x6, waiting for transfers between devices, swap_y(): return lax.ppermute(value, 'dp', SWAP_Y)  19 us
    pallas_call x1, Pallas kernels, on_chip_experts(): kernel_call(functools.partial(expert_body, n_exp), (sds((slots, FF), BF16...  18.8 us
    ppermute x2, waiting for transfers between devices, swap_x_y(): return lax.ppermute(value, ('dp', 'ctx'), [(i, i ^ 5) for i in range(8)])  16 us
    pallas_call x1, Pallas kernels, on_chip_experts(): kernel_call(functools.partial(adam_body, len(moved)), [sds((owned, width)...  15.7 us
  transfers between devices with their start and end apart: 40, of which 12 were waited for; matrix products, arithmetic and copies ran while one was open for 10% of the time, Pallas kernels for 37%

profile of v2, /device:TPU:0, one launch (start us, length us, event | category | flops | bytes accessed | tf_op | source)
XLA Modules:
  0.0 353.3 jit_solution(15663156385486776739)
XLA Ops:
  1.6 3.1 collective-permute-start.8
  4.7 2.6 collective-permute-start.11
  16.4 3.6 %route_body.1 = (s32[8,512]{1,0:T(8,128)}, s32[512,8]{1,0:T(8,128)}, bf16[1280,512]{1,0:T(8,128)(2,1)}) custom-call(s32[2,512]{1,0:T(2,128)} %copy.28.ids_ref, f32[1,512]{1,0:T(1,128)} %convert_element_type.70.prio_ref, f32[1,512]{1,0:T(1,128)} %get-tuple-element.414.live_ref, bf16[512,512]{1,0:T(8,128)(2,1)} %bitcast.71), custom_call_target="tpu_custom_call" | custom-call | flops 4600000000 | bytes 1000000 | tf_op jit(solution)/shard_map/route_body/pallas_call | solution.py:928
  20.0 4.4 %plan_body.1 = (s32[8,2048]{1,0:T(8,128)}, s32[2048,8]{1,0:T(8,128)}, s32[8,128]{1,0:T(8,128)}) custom-call(s32[1]{0:T(128)} %bitcast.5.me_ref, s32[8,2048]{1,0:T(8,128)} %bitcast.65), custom_call_target="tpu_custom_call" | custom-call | flops 5750000128 | bytes 1000000 | tf_op jit(solution)/shard_map/plan_body/pallas_call | solution.py:949
  33.1 5.7 %all-to-all-start.1 = ((bf16[32,40,512]{2,1,0:T(8,128)(2,1)}), bf16[32,40,512]{2,1,0:T(8,128)(2,1)S(1)}, u32[]{:S(2)}, u32[]{:S(2)}) async-start(bf16[32,40,512]{2,1,0:T(8,128)(2,1)} %bitcast.56), calls=%async_computation.1 | async-start | bytes 2621440 | tf_op jit(solution)/shard_map/all_to_all | solution.py:935
  43.6 8.2 %put_body.5 = (bf16[1280,512]{1,0:T(8,128)(2,1)}, bf16[1280,512]{1,0:T(8,128)(2,1)}) custom-call(s32[1]{0:T(128)} %constant.173.clone.1.base_ref, s32[8,2048]{1,0:T(8,128)S(1)} %copy-done.35, bf16[2048,512]{1,0:T(8,128)(2,1)} %bitcast.69), custom_call_target="tpu_custom_call" | custom-call | flops 9200000000 | bytes 1000000 | tf_op jit(solution)/shard_map/put_body/pallas_call | solution.py:959
  51.8 10.3 %collective-permute-done.10.refs_0_ = bf16[544,512]{1,0:T(8,128)(2,1)S(1)} collective-permute-done((bf16[544,512]{1,0:T(8,128)(2,1)S(1)}, bf16[544,512]{1,0:T(8,128)(2,1)S(1)}, u32[]{:S(2)}, u32[]{:S(2)}) %collective-permute-start.10) | collective-permute-done | bytes 557088 | tf_op jit(solution)/shard_map/ppermute | solution.py:852
  67.6 9.1 %unpack_body.3.refs_2_ = bf16[2080,512]{1,0:T(8,128)(2,1)} custom-call(s32[2080,1]{1,0:T(8,128)} %broadcast_in_dim.40.pos_ref, bf16[544,512]{1,0:T(8,128)(2,1)} %copy-done.11, bf16[544,512]{1,0:T(8,128)(2,1)} %constant_dynamic-update-slice_fusion.2.refs_1_, bf16[544,512]{1,0:T(8,128)(2,1)} %copy-done.28, bf16[544,512]{1,0:T(8,128)(2,1)} %copy-done.30), custom_call_target="tpu_custom_call" | custom-call | flops 8049999872 | bytes 1000000 | tf_op jit(solution)/shard_map/unpack_body/pallas_call | solution.py:1000
  76.7 7.3 %unpack_body.4.refs_2_ = bf16[2080,512]{1,0:T(8,128)(2,1)} custom-call(s32[2080,1]{1,0:T(8,128)} %broadcast_in_dim.40.pos_ref, bf16[544,512]{1,0:T(8,128)(2,1)} %copy-done.27, bf16[544,512]{1,0:T(8,128)(2,1)} %copy-done.29, bf16[2080,512]{1,0:T(8,128)(2,1)} %unpack_body.3.refs_2_), custom_call_target="tpu_custom_call" | custom-call | flops 8049999872 | bytes 1000000 | tf_op jit(solution)/shard_map/unpack_body/pallas_call | solution.py:1000
  84.8 7.5 %unpack_body.5.w_ref = bf16[2080,512]{1,0:T(8,128)(2,1)} custom-call(s32[2080,1]{1,0:T(8,128)} %broadcast_in_dim.40.pos_ref, bf16[544,512]{1,0:T(8,128)(2,1)} %collective-permute-done.17.refs_0_, bf16[544,512]{1,0:T(8,128)(2,1)} %copy-done.31, bf16[2080,512]{1,0:T(8,128)(2,1)} %unpack_body.4.refs_2_), custom_call_target="tpu_custom_call" | custom-call | flops 8049999872 | bytes 1000000 | tf_op jit(solution)/shard_map/unpack_body/pallas_call | solution.py:1000
  99.6 12.5 %forward_body.1 = (bf16[1024,1536]{1,0:T(8,128)(2,1)}, bf16[512,512]{1,0:T(8,128)(2,1)}, f32[512,512]{1,0:T(8,128)}, f32[512,512]{1,0:T(8,128)}, f32[512,16]{1,0...) custom-call(bf16[512,512]{1,0:T(8,128)(2,1)} %bitcast.4.own_ref, ...), custom_call_target="tpu_custom_call" | custom-call | flops 14949999616 | bytes 1000000 | tf_op jit(solution)/shard_map/forward_body/pallas_call | solution.py:1016
  113.1 6.0 %all-to-all-start = ((bf16[32,40,512]{2,1,0:T(8,128)(2,1)}), bf16[32,40,512]{2,1,0:T(8,128)(2,1)}, u32[]{:S(2)}, u32[]{:S(2)}) async-start(bf16[32,40,512]{2,1,0:T(8,128)(2,1)} %bitcast.59), calls=%async_computation | async-start | bytes 2621440 | tf_op jit(solution)/shard_map/all_to_all | solution.py:935
  119.2 16.8 %collective-permute-done.23.refs_3_ = bf16[640,512]{1,0:T(8,128)(2,1)} collective-permute-done((bf16[640,512]{1,0:T(8,128)(2,1)}, bf16[640,512]{1,0:T(8,128)(2,1)}, u32[]{:S(2)}, u32[]{:S(2)}) %collective-permute-start.23) | collective-permute-done | bytes 655392 | tf_op jit(solution)/shard_map/ppermute | solution.py:856
  136.0 8.9 %take_more_body.1.near_ref = bf16[2048,512]{1,0:T(8,128)(2,1)} custom-call(s32[1]{0:T(128)} %constant.173.clone.1.base_ref, s32[2048,8]{1,0:T(8,128)} %get-tuple-element.675, bf16[320,512]{1,0:T(8,128)(2,1)} %get-tuple-element.386.refs_0_, bf16[320,512]{1,0:T(8,128)(2,1)} %get-tuple-element.415.refs_1_, bf16[640,512]{1,0:T(8,128)(2,1)} %collective-permute-done.22.refs_2_, ...), custom_call_target="tpu_custom_call" | custom-call | flops 9200000000 | bytes 1000000 | tf_op jit(solution)/shard_map/take_more_body/pallas_call | solution.py:959
  151.5 18.8 %expert_body.1 = (bf16[1280,2048]{1,0:T(8,128)(2,1)}, bf16[1280,2048]{1,0:T(8,128)(2,1)}, bf16[1280,512]{1,0:T(8,128)(2,1)}, bf16[1280,512]{1,0:T(8,128)(2,1)}, ...) custom-call(s32[1]{0:T(128)} %bitcast.3.expert_ref, bf16[1280,512]{1,0:T(8,128)(2,1)} %bitcast.14.got_ref, ...), custom_call_target="tpu_custom_call" | custom-call | flops 21849999360 | bytes 1000000 | tf_op jit(solution)/shard_map/expert_body/pallas_call | solution.py:1039
  170.3 5.7 %all-to-all-start.2 = ((bf16[32,40,512]{2,1,0:T(8,128)(2,1)}), bf16[32,40,512]{2,1,0:T(8,128)(2,1)S(1)}, u32[]{:S(2)}, u32[]{:S(2)}) async-start(bf16[32,40,512]{2,1,0:T(8,128)(2,1)} %bitcast.61), calls=%async_computation.2 | async-start | bytes 2621440 | tf_op jit(solution)/shard_map/all_to_all | solution.py:935
  176.1 12.4 %weight_grad_body.1 = (f32[2048,512]{1,0:T(8,128)}, bf16[1024,512]{1,0:T(8,128)(2,1)}, bf16[1024,512]{1,0:T(8,128)(2,1)}) custom-call(bf16[1280,2048]{1,0:T(8,128)(2,1)} %get-tuple-element.284.hidden_ref, bf16[1280,2048]{1,0:T(8,128)(2,1)} %get-tuple-element.285.active_ref, bf16[1280,512]{1,0:T(8,128)(2,1)} %bitcast.14.got_ref, ...), custom_call_target="tpu_custom_call" | custom-call | flops 11500000256 | bytes 10000000 | tf_op jit(solution)/shard_map/weight_grad_body/pallas_call | solution.py:1057
  193.0 9.0 %sum_put_body.5 = (bf16[640,512]{1,0:T(8,128)(2,1)}, bf16[640,512]{1,0:T(8,128)(2,1)}, bf16[640,512]{1,0:T(8,128)(2,1)}, bf16[640,512]{1,0:T(8,128)(2,1)}) custom-call(s32[1]{0:T(128)} %constant.173.clone.1.base_ref, s32[8,2048]{1,0:T(8,128)S(1)} %copy-done.36, f32[2048,512]{1,0:T(8,128)} %get-tuple-element.579.mine_ref, ...), custom_call_target="tpu_custom_call" | custom-call | flops 9200000000 | bytes 1000000 | tf_op jit(solution)/shard_map/sum_put_body/pallas_call | solution.py:959
  202.0 6.2 %all-to-all-done.2 = bf16[32,40,512]{2,1,0:T(8,128)(2,1)S(1)} async-done(((bf16[32,40,512]{2,1,0:T(8,128)(2,1)}), bf16[32,40,512]{2,1,0:T(8,128)(2,1)S(1)}, u32[]{:S(2)}, u32[]{:S(2)}) %all-to-all-start.2) | async-done | bytes 1310752 | tf_op jit(solution)/shard_map/all_to_all | solution.py:935
  209.3 5.9 %middle_body.1 = (f32[512,512]{1,0:T(8,128)}, bf16[512,512]{1,0:T(8,128)(2,1)}, f32[512,128]{1,0:T(8,128)}, f32[8,512]{1,0:T(8,128)}, f32[8,512]{1,0:T(8,128)}) custom-call(bf16[1280,512]{1,0:T(8,128)(2,1)} %bitcast.60, s32[512,8]{1,0:T(8,128)} %get-tuple-element.295.pos_ref, f32[512,512]{1,0:T(8,128)} %get-tuple-element.296.residual_ref, ...), custom_call_target="tpu_custom_call" | custom-call | flops 6899999744 | bytes 1000000 | tf_op jit(solution)/shard_map/middle_body/pallas_call | solution.py:1073
  219.4 14.7 %inner_body.1 = (bf16[512,512]{1,0:T(8,128)(2,1)}, f32[2,512,512]{2,1,0:T(8,128)}, bf16[544,512]{1,0:T(8,128)(2,1)}) custom-call(bf16[1024,1536]{1,0:T(8,128)(2,1)} %get-tuple-element.303.qkv_ref, bf16[512,512]{1,0:T(8,128)(2,1)} %get-tuple-element.298.out_grad_ref, f32[512,128]{1,0:T(8,128)} %get-tuple-element.308.lse_ref, ...), custom_call_target="tpu_custom_call" | custom-call | flops 17250000896 | bytes 1000000 | tf_op jit(solution)/shard_map/inner_body/pallas_call | solution.py:1085
  235.0 11.9 %outer_body.1 = (bf16[1552,512]{1,0:T(8,128)(2,1)}, f32[512,512]{1,0:T(8,128)}) custom-call(bf16[1024,1536]{1,0:T(8,128)(2,1)} %get-tuple-element.303.qkv_ref, bf16[512,512]{1,0:T(8,128)(2,1)} %copy-done.32, f32[16,512]{1,0:T(8,128)} %copy-done.33, f32[512,1]{1,0:T(8,128)} %copy.32.keep_ref, bf16[512,512]{1,0:T(8,128)(2,1)} %get-tuple-element.313.query_ref, ...), custom_call_target="tpu_custom_call" | custom-call | flops 13799999488 | bytes 1000000 | tf_op jit(solution)/shard_map/outer_body/pallas_call | solution.py:1091
  249.9 2.7 all-to-all-start.3
  255.8 6.0 %spread_body.2 = bf16[2,544,512]{2,1,0:T(8,128)(2,1)} custom-call(s32[1,2096]{1,0:T(1,128)} %broadcast_in_dim.35.pos_ref, bf16[1552,512]{1,0:T(8,128)(2,1)} %get-tuple-element.317.late_ref, bf16[1552,512]{1,0:T(8,128)(2,1)} %collective-permute-done.32.late_far_ref, bf16[544,512]{1,0:T(8,128)(2,1)} %get-tuple-element.318.early_ref, ...), custom_call_target="tpu_custom_call" | custom-call | flops 6899999744 | bytes 1000000 | tf_op jit(solution)/shard_map/spread_body/pallas_call | solution.py:1108
  265.2 6.0 %spread_body.3 = bf16[2,544,512]{2,1,0:T(8,128)(2,1)} custom-call(s32[1,2096]{1,0:T(1,128)} %broadcast_in_dim.35.pos_ref, bf16[1552,512]{1,0:T(8,128)(2,1)} %get-tuple-element.317.late_ref, bf16[1552,512]{1,0:T(8,128)(2,1)} %collective-permute-done.32.late_far_ref, bf16[544,512]{1,0:T(8,128)(2,1)} %get-tuple-element.318.early_ref, ...), custom_call_target="tpu_custom_call" | custom-call | flops 6899999744 | bytes 1000000 | tf_op jit(solution)/shard_map/spread_body/pallas_call | solution.py:1108
  271.1 11.7 %collective-permute-done.41 = bf16[640,512]{1,0:T(8,128)(2,1)S(1)} collective-permute-done((bf16[640,512]{1,0:T(8,128)(2,1)}, bf16[640,512]{1,0:T(8,128)(2,1)S(1)}, u32[]{:S(2)}, u32[]{:S(2)}) %collective-permute-start.41) | collective-permute-done | bytes 655392 | tf_op jit(solution)/shard_map/ppermute | solution.py:852
  282.9 16.0 %collective-permute-done.42 = bf16[640,512]{1,0:T(8,128)(2,1)S(1)} collective-permute-done((bf16[640,512]{1,0:T(8,128)(2,1)}, bf16[640,512]{1,0:T(8,128)(2,1)S(1)}, u32[]{:S(2)}, u32[]{:S(2)}) %collective-permute-start.42) | collective-permute-done | bytes 655392 | tf_op jit(solution)/shard_map/ppermute | solution.py:860
  301.2 8.2 %collective-permute-done.34 = bf16[544,512]{1,0:T(8,128)(2,1)S(1)} collective-permute-done((bf16[544,512]{1,0:T(8,128)(2,1)S(1)}, bf16[544,512]{1,0:T(8,128)(2,1)S(1)}, u32[]{:S(2)}, u32[]{:S(2)}) %collective-permute-start.34) | collective-permute-done | bytes 557088 | tf_op jit(solution)/shard_map/ppermute | solution.py:852
  313.9 4.2 %collective-permute-done.38 = bf16[272,512]{1,0:T(8,128)(2,1)S(1)} collective-permute-done((bf16[272,512]{1,0:T(8,128)(2,1)S(1)}, bf16[272,512]{1,0:T(8,128)(2,1)S(1)}, u32[]{:S(2)}, u32[]{:S(2)}) %collective-permute-start.38) | collective-permute-done | bytes 278560 | tf_op jit(solution)/shard_map/ppermute | solution.py:852
  325.6 4.0 %tokens_body.1 = f32[512,512]{1,0:T(8,128)} custom-call(f32[512,512]{1,0:T(8,128)} %get-tuple-element.316.grad_normed_ref, bf16[512,512]{1,0:T(8,128)(2,1)} %bitcast.4.own_ref, bf16[2080,512]{1,0:T(8,128)(2,1)} %unpack_body.5.w_ref, f32[512,512]{1,0:T(8,128)} %get-tuple-element.310.grad_ref), custom_call_target="tpu_custom_call" | custom-call | flops 2300000000 | bytes 4000000 | tf_op jit(solution)/shard_map/tokens_body/pallas_call | solution.py:1100
  330.7 4.4 %mixture_body.1 = bf16[512,512]{1,0:T(8,128)(2,1)} custom-call(bf16[1280,512]{1,0:T(8,128)(2,1)} %bitcast.58, s32[512,8]{1,0:T(8,128)} %get-tuple-element.295.pos_ref, s32[512,2]{1,0:T(8,128)} %bitcast.63, f32[512,16]{1,0:T(8,128)} %get-tuple-element.302.prob_ref, f32[512,512]{1,0:T(8,128)} %get-tuple-element.296.residual_ref), custom_call_target="tpu_custom_call" | custom-call | flops 1342177280 | bytes 4000000 | tf_op jit(solution)/shard_map/mixture_body/pallas_call | solution.py:1140
  337.4 15.7 %adam_body.1 = (f32[2048,512]{1,0:T(8,128)}, f32[2048,512]{1,0:T(8,128)}, f32[2048,512]{1,0:T(8,128)}, f32[2048,512]{1,0:T(8,128)}) custom-call(s32[2048,8]{1,0:T(8,128)S(1)} %copy-done.34, bf16[320,512]{1,0:T(8,128)(2,1)} %get-tuple-element.396.refs_0_, bf16[320,512]{1,0:T(8,128)(2,1)} %get-tuple-element.398.refs_1_, ...), custom_call_target="tpu_custom_call" | custom-call | flops 16099999744 | bytes 30000000 | tf_op jit(solution)/shard_map/adam_body/pallas_call | solution.py:1120
  (191 shorter events, 81.8 us)
Async XLA Ops:
  1.6 26.8 %collective-permute-start.8 = (bf16[136,512]{1,0:T(8,128)(2,1)S(1)}, bf16[136,512]{1,0:T(8,128)(2,1)S(1)}, u32[]{:S(2)}, u32[]{:S(2)}) collective-permute-start(bf16[136,512]{1,0:T(8,128)(2,1)S(1)} %pad.8), channel_id=1, source_target_pairs={{0,1},{1,2},{2,3},{3,0},{4,5},{5,6},{6,7},{7,4},{8,9},{9,10},{10,1... | collective-permute-start | bytes 417800 | tf_op jit(solution)/shard_map/ppermute | solution.py:869
  4.7 26.0 %collective-permute-start.11 = (bf16[136,512]{1,0:T(8,128)(2,1)S(1)}, bf16[136,512]{1,0:T(8,128)(2,1)S(1)}, u32[]{:S(2)}, u32[]{:S(2)}) collective-permute-start(bf16[136,512]{1,0:T(8,128)(2,1)S(1)} %pad.8), channel_id=1, source_target_pairs={{0,2},{1,3},{2,0},{3,1},{4,6},{5,7},{6,4},{7,5},{8,10},{9,11},{10,... | collective-permute-start | bytes 417800 | tf_op jit(solution)/shard_map/ppermute | solution.py:869
  7.2 24.1 %collective-permute-start.12 = (bf16[136,512]{1,0:T(8,128)(2,1)S(1)}, bf16[136,512]{1,0:T(8,128)(2,1)S(1)}, u32[]{:S(2)}, u32[]{:S(2)}) collective-permute-start(bf16[136,512]{1,0:T(8,128)(2,1)S(1)} %pad.8), channel_id=1, source_target_pairs={{0,3},{1,0},{2,1},{3,2},{4,7},{5,4},{6,5},{7,6},{8,11},{9,8},{10,9... | collective-permute-start | bytes 417800 | tf_op jit(solution)/shard_map/ppermute | solution.py:869
  8.6 19.2 %collective-permute-start.16 = (s32[1,512]{1,0:T(1,128)}, s32[1,512]{1,0:T(1,128)S(1)}, u32[]{:S(2)}, u32[]{:S(2)}) collective-permute-start(s32[1,512]{1,0:T(1,128)} %param.19), channel_id=1, source_target_pairs={{0,4},{4,0},{1,5},{5,1},{2,6},{6,2},{3,7},{7,3},{8,12},{12,8},{9,1... | collective-permute-start | bytes 6152 | tf_op jit(solution)/shard_map/ppermute | solution.py:852
  33.1 79.0 %all-to-all-start.1 = ((bf16[32,40,512]{2,1,0:T(8,128)(2,1)}), bf16[32,40,512]{2,1,0:T(8,128)(2,1)S(1)}, u32[]{:S(2)}, u32[]{:S(2)}) async-start(bf16[32,40,512]{2,1,0:T(8,128)(2,1)} %bitcast.56), calls=%async_computation.1 | async-start | bytes 2621440 | tf_op jit(solution)/shard_map/all_to_all | solution.py:935
  39.9 22.3 %collective-permute-start.10 = (bf16[544,512]{1,0:T(8,128)(2,1)S(1)}, bf16[544,512]{1,0:T(8,128)(2,1)S(1)}, u32[]{:S(2)}, u32[]{:S(2)}) collective-permute-start(bf16[544,512]{1,0:T(8,128)(2,1)S(1)} %pad_maximum_fusion.8.refs_0_), channel_id=1, source_target_pairs={{0,4},{4,0},{1,5},{5,1},{2,6},{6,2},{3,7},{7,3},{8,12},{12,8},{9,1... | collective-permute-start | bytes 1671176 | tf_op jit(solution)/shard_map/ppermute | solution.py:852
  41.2 24.8 %collective-permute-start.19 = (bf16[544,512]{1,0:T(8,128)(2,1)S(1)}, bf16[544,512]{1,0:T(8,128)(2,1)S(1)}, u32[]{:S(2)}, u32[]{:S(2)}) collective-permute-start(bf16[544,512]{1,0:T(8,128)(2,1)S(1)} %pad_maximum_fusion.8.refs_0_), channel_id=1, source_target_pairs={{0,8},{8,0},{16,24},{24,16},{1,9},{9,1},{17,25},{25,17},{2,10},{10... | collective-permute-start | bytes 1671176 | tf_op jit(solution)/shard_map/ppermute | solution.py:864
  42.9 21.5 %collective-permute-start.14 = (bf16[544,512]{1,0:T(8,128)(2,1)}, bf16[544,512]{1,0:T(8,128)(2,1)S(1)}, u32[]{:S(2)}, u32[]{:S(2)}) collective-permute-start(bf16[544,512]{1,0:T(8,128)(2,1)} %constant_dynamic-update-slice_fusion.2.refs_1_), channel_id=1, source_target_pairs={{0,16},{16,0},{8,24},{24,8},{1,17},{17,1},{9,25},{25,9},{2,18},{18... | collective-permute-start | bytes 1671176 | tf_op jit(solution)/shard_map/ppermute | solution.py:856
  43.4 22.7 %collective-permute-start.20 = (bf16[544,512]{1,0:T(8,128)(2,1)}, bf16[544,512]{1,0:T(8,128)(2,1)S(1)}, u32[]{:S(2)}, u32[]{:S(2)}) collective-permute-start(bf16[544,512]{1,0:T(8,128)(2,1)} %constant_dynamic-update-slice_fusion.2.refs_1_), channel_id=1, source_target_pairs={{0,8},{8,0},{16,24},{24,16},{1,9},{9,1},{17,25},{25,17},{2,10},{10... | collective-permute-start | bytes 1671176 | tf_op jit(solution)/shard_map/ppermute | solution.py:864
  64.3 28.0 %collective-permute-start.15 = (bf16[512,512]{1,0:T(8,128)(2,1)}, bf16[512,512]{1,0:T(8,128)(2,1)}, u32[]{:S(2)}, u32[]{:S(2)}) collective-permute-start(bf16[512,512]{1,0:T(8,128)(2,1)} %bitcast.4.own_ref), channel_id=1, source_target_pairs={{0,4},{4,0},{1,5},{5,1},{2,6},{6,2},{3,7},{7,3},{8,12},{12,8},{9,1... | collective-permute-start | bytes 1572872 | tf_op jit(solution)/shard_map/ppermute | solution.py:852
  65.5 26.9 %collective-permute-start.21 = (bf16[1280,512]{1,0:T(8,128)(2,1)}, bf16[1280,512]{1,0:T(8,128)(2,1)S(1)}, u32[]{:S(2)}, u32[]{:S(2)}) collective-permute-start(bf16[1280,512]{1,0:T(8,128)(2,1)} %get-tuple-element.279), channel_id=1, source_target_pairs={{0,8},{8,0},{16,24},{24,16},{1,9},{9,1},{17,25},{25,17},{2,10},{10... | collective-permute-start | bytes 3932168 | tf_op jit(solution)/shard_map/ppermute | solution.py:864
  65.5 18.5 %collective-permute-start.17 = (bf16[544,512]{1,0:T(8,128)(2,1)S(1)}, bf16[544,512]{1,0:T(8,128)(2,1)}, u32[]{:S(2)}, u32[]{:S(2)}) collective-permute-start(bf16[544,512]{1,0:T(8,128)(2,1)S(1)} %collective-permute-done.10.refs_0_), channel_id=1, source_target_pairs={{0,8},{8,0},{16,24},{24,16},{1,9},{9,1},{17,25},{25,17},{2,10},{10... | collective-permute-start | bytes 1671176 | tf_op jit(solution)/shard_map/ppermute | solution.py:864
  66.0 18.0 %collective-permute-start.18 = (bf16[544,512]{1,0:T(8,128)(2,1)S(1)}, bf16[544,512]{1,0:T(8,128)(2,1)S(1)}, u32[]{:S(2)}, u32[]{:S(2)}) collective-permute-start(bf16[544,512]{1,0:T(8,128)(2,1)S(1)} %collective-permute-done.14.refs_1_), channel_id=1, source_target_pairs={{0,8},{8,0},{16,24},{24,16},{1,9},{9,1},{17,25},{25,17},{2,10},{10... | collective-permute-start | bytes 1671176 | tf_op jit(solution)/shard_map/ppermute | solution.py:864
  94.3 24.9 %collective-permute-start.22 = (bf16[640,512]{1,0:T(8,128)(2,1)}, bf16[640,512]{1,0:T(8,128)(2,1)}, u32[]{:S(2)}, u32[]{:S(2)}) collective-permute-start(bf16[640,512]{1,0:T(8,128)(2,1)} %pad_maximum_fusion.5), channel_id=1, source_target_pairs={{0,4},{4,0},{1,5},{5,1},{2,6},{6,2},{3,7},{7,3},{8,12},{12,8},{9,1... | collective-permute-start | bytes 1966088 | tf_op jit(solution)/shard_map/ppermute | solution.py:852
  96.1 39.9 %collective-permute-start.23 = (bf16[640,512]{1,0:T(8,128)(2,1)}, bf16[640,512]{1,0:T(8,128)(2,1)}, u32[]{:S(2)}, u32[]{:S(2)}) collective-permute-start(bf16[640,512]{1,0:T(8,128)(2,1)} %pad_maximum_fusion.6), channel_id=1, source_target_pairs={{0,16},{16,0},{8,24},{24,8},{1,17},{17,1},{9,25},{25,9},{2,18},{18... | collective-permute-start | bytes 1966088 | tf_op jit(solution)/shard_map/ppermute | solution.py:856
  98.0 38.0 %collective-permute-start.24 = (bf16[640,512]{1,0:T(8,128)(2,1)}, bf16[640,512]{1,0:T(8,128)(2,1)}, u32[]{:S(2)}, u32[]{:S(2)}) collective-permute-start(bf16[640,512]{1,0:T(8,128)(2,1)} %pad_maximum_fusion.7), channel_id=1, source_target_pairs={{0,20},{4,16},{8,28},{12,24},{16,4},{20,0},{24,12},{28,8},{1,21},{... | collective-permute-start | bytes 1966088 | tf_op jit(solution)/shard_map/ppermute | solution.py:860
  113.1 38.3 %all-to-all-start = ((bf16[32,40,512]{2,1,0:T(8,128)(2,1)}), bf16[32,40,512]{2,1,0:T(8,128)(2,1)}, u32[]{:S(2)}, u32[]{:S(2)}) async-start(bf16[32,40,512]{2,1,0:T(8,128)(2,1)} %bitcast.59), calls=%async_computation | async-start | bytes 2621440 | tf_op jit(solution)/shard_map/all_to_all | solution.py:935
  170.3 37.9 %all-to-all-start.2 = ((bf16[32,40,512]{2,1,0:T(8,128)(2,1)}), bf16[32,40,512]{2,1,0:T(8,128)(2,1)S(1)}, u32[]{:S(2)}, u32[]{:S(2)}) async-start(bf16[32,40,512]{2,1,0:T(8,128)(2,1)} %bitcast.61), calls=%async_computation.2 | async-start | bytes 2621440 | tf_op jit(solution)/shard_map/all_to_all | solution.py:935
  215.2 19.0 %collective-permute-start.29 = (bf16[512,512]{1,0:T(8,128)(2,1)}, bf16[512,512]{1,0:T(8,128)(2,1)S(1)}, u32[]{:S(2)}, u32[]{:S(2)}) collective-permute-start(bf16[512,512]{1,0:T(8,128)(2,1)} %get-tuple-element.298.out_grad_ref), channel_id=1, source_target_pairs={{0,4},{4,0},{1,5},{5,1},{2,6},{6,2},{3,7},{7,3},{8,12},{12,8},{9,1... | collective-permute-start | bytes 1572872 | tf_op jit(solution)/shard_map/ppermute | solution.py:852
  215.2 19.0 %collective-permute-start.30 = (bf16[640,512]{1,0:T(8,128)(2,1)S(1)}, bf16[640,512]{1,0:T(8,128)(2,1)S(1)}, u32[]{:S(2)}, u32[]{:S(2)}) collective-permute-start(bf16[640,512]{1,0:T(8,128)(2,1)S(1)} %copy-done.26), channel_id=1, source_target_pairs={{0,16},{16,0},{8,24},{24,8},{1,17},{17,1},{9,25},{25,9},{2,18},{18... | collective-permute-start | bytes 1966088 | tf_op jit(solution)/shard_map/ppermute | solution.py:856
  217.5 16.7 %collective-permute-start.31 = (f32[16,512]{1,0:T(8,128)S(1)}, f32[16,512]{1,0:T(8,128)S(1)}, u32[]{:S(2)}, u32[]{:S(2)}) collective-permute-start(f32[16,512]{1,0:T(8,128)S(1)} %pad_maximum_fusion.10), channel_id=1, source_target_pairs={{0,4},{4,0},{1,5},{5,1},{2,6},{6,2},{3,7},{7,3},{8,12},{12,8},{9,1... | collective-permute-start | bytes 98312 | tf_op jit(solution)/shard_map/ppermute | solution.py:852
  234.2 21.6 %collective-permute-start.33 = (bf16[544,512]{1,0:T(8,128)(2,1)}, bf16[544,512]{1,0:T(8,128)(2,1)}, u32[]{:S(2)}, u32[]{:S(2)}) collective-permute-start(bf16[544,512]{1,0:T(8,128)(2,1)} %get-tuple-element.318.early_ref), channel_id=1, source_target_pairs={{0,8},{8,0},{16,24},{24,16},{1,9},{9,1},{17,25},{25,17},{2,10},{10... | collective-permute-start | bytes 1671176 | tf_op jit(solution)/shard_map/ppermute | solution.py:864
  249.9 79.6 %all-to-all-start.3 = ((bf16[32,40,512]{2,1,0:T(8,128)(2,1)}), bf16[32,40,512]{2,1,0:T(8,128)(2,1)S(1)}, u32[]{:S(2)}, u32[]{:S(2)}) async-start(bf16[32,40,512]{2,1,0:T(8,128)(2,1)} %bitcast.55), calls=%async_computation.3 | async-start | bytes 2621440 | tf_op jit(solution)/shard_map/all_to_all | solution.py:935
  252.6 30.2 %collective-permute-start.41 = (bf16[640,512]{1,0:T(8,128)(2,1)}, bf16[640,512]{1,0:T(8,128)(2,1)S(1)}, u32[]{:S(2)}, u32[]{:S(2)}) collective-permute-start(bf16[640,512]{1,0:T(8,128)(2,1)} %get-tuple-element.323), channel_id=1, source_target_pairs={{0,4},{4,0},{1,5},{5,1},{2,6},{6,2},{3,7},{7,3},{8,12},{12,8},{9,1... | collective-permute-start | bytes 1966088 | tf_op jit(solution)/shard_map/ppermute | solution.py:852
  254.3 44.6 %collective-permute-start.42 = (bf16[640,512]{1,0:T(8,128)(2,1)}, bf16[640,512]{1,0:T(8,128)(2,1)S(1)}, u32[]{:S(2)}, u32[]{:S(2)}) collective-permute-start(bf16[640,512]{1,0:T(8,128)(2,1)} %get-tuple-element.324), channel_id=1, source_target_pairs={{0,20},{4,16},{8,28},{12,24},{16,4},{20,0},{24,12},{28,8},{1,21},{... | collective-permute-start | bytes 1966088 | tf_op jit(solution)/shard_map/ppermute | solution.py:860
  263.1 46.4 %collective-permute-start.34 = (bf16[544,512]{1,0:T(8,128)(2,1)S(1)}, bf16[544,512]{1,0:T(8,128)(2,1)S(1)}, u32[]{:S(2)}, u32[]{:S(2)}) collective-permute-start(bf16[544,512]{1,0:T(8,128)(2,1)S(1)} %get-tuple-element.393), channel_id=1, source_target_pairs={{0,4},{4,0},{1,5},{5,1},{2,6},{6,2},{3,7},{7,3},{8,12},{12,8},{9,1... | collective-permute-start | bytes 1671176 | tf_op jit(solution)/shard_map/ppermute | solution.py:852
  264.6 44.8 %collective-permute-start.37 = (bf16[544,512]{1,0:T(8,128)(2,1)S(1)}, bf16[544,512]{1,0:T(8,128)(2,1)S(1)}, u32[]{:S(2)}, u32[]{:S(2)}) collective-permute-start(bf16[544,512]{1,0:T(8,128)(2,1)S(1)} %get-tuple-element.394), channel_id=1, source_target_pairs={{0,16},{16,0},{8,24},{24,8},{1,17},{17,1},{9,25},{25,9},{2,18},{18... | collective-permute-start | bytes 1671176 | tf_op jit(solution)/shard_map/ppermute | solution.py:856
  312.2 25.2 %collective-permute-start.43 = (bf16[1280,512]{1,0:T(8,128)(2,1)}, bf16[1280,512]{1,0:T(8,128)(2,1)}, u32[]{:S(2)}, u32[]{:S(2)}) collective-permute-start(bf16[1280,512]{1,0:T(8,128)(2,1)} %pad_maximum_fusion.4), channel_id=1, source_target_pairs={{0,8},{8,0},{16,24},{24,16},{1,9},{9,1},{17,25},{25,17},{2,10},{10... | collective-permute-start | bytes 3932168 | tf_op jit(solution)/shard_map/ppermute | solution.py:864
  312.2 10.9 %collective-permute-start.35 = (bf16[272,512]{1,0:T(8,128)(2,1)S(1)}, bf16[272,512]{1,0:T(8,128)(2,1)S(1)}, u32[]{:S(2)}, u32[]{:S(2)}) collective-permute-start(bf16[272,512]{1,0:T(8,128)(2,1)S(1)} %slice.246), channel_id=1, source_target_pairs={{0,16},{16,0},{8,24},{24,8},{1,17},{17,1},{9,25},{25,9},{2,18},{18... | collective-permute-start | bytes 835592 | tf_op jit(solution)/shard_map/ppermute | solution.py:856
  318.9 16.2 %collective-permute-start.40 = (bf16[136,512]{1,0:T(8,128)(2,1)}, bf16[136,512]{1,0:T(8,128)(2,1)}, u32[]{:S(2)}, u32[]{:S(2)}) collective-permute-start(bf16[136,512]{1,0:T(8,128)(2,1)} %get-tuple-element.406), channel_id=1, source_target_pairs={{0,1},{1,2},{2,3},{3,0},{4,5},{5,6},{6,7},{7,4},{8,9},{9,10},{10,1... | collective-permute-start | bytes 417800 | tf_op jit(solution)/shard_map/ppermute | solution.py:869
  320.7 14.3 %collective-permute-start.39 = (bf16[136,512]{1,0:T(8,128)(2,1)}, bf16[136,512]{1,0:T(8,128)(2,1)}, u32[]{:S(2)}, u32[]{:S(2)}) collective-permute-start(bf16[136,512]{1,0:T(8,128)(2,1)} %get-tuple-element.405), channel_id=1, source_target_pairs={{0,2},{1,3},{2,0},{3,1},{4,6},{5,7},{6,4},{7,5},{8,10},{9,11},{10,... | collective-permute-start | bytes 417800 | tf_op jit(solution)/shard_map/ppermute | solution.py:869
  323.9 11.2 %collective-permute-start.36 = (bf16[136,512]{1,0:T(8,128)(2,1)}, bf16[136,512]{1,0:T(8,128)(2,1)}, u32[]{:S(2)}, u32[]{:S(2)}) collective-permute-start(bf16[136,512]{1,0:T(8,128)(2,1)} %get-tuple-element.404), channel_id=1, source_target_pairs={{0,3},{1,0},{2,1},{3,2},{4,7},{5,4},{6,5},{7,6},{8,11},{9,8},{10,9... | collective-permute-start | bytes 417800 | tf_op jit(solution)/shard_map/ppermute | solution.py:869
  (44 other events, 336.8 us)

commit v3 on v2

--- a/solution.py
+++ b/solution.py
@@ -390,7 +390,9 @@
     return jnp.where(mask, 1.0, 0.0).astype(BF16)
 
 
-def kernel_call(body, out_shape, scratch=(), grid=None, in_specs=None, out_specs=None, cost=None):
+def kernel_call(
+    body, out_shape, scratch=(), grid=None, in_specs=None, out_specs=None, cost=None, aliases=None
+):
     given = dict(grid=grid, in_specs=in_specs, out_specs=out_specs)
     extra = {name: value for name, value in given.items() if value is not None}
     flops, moved = cost if cost else (1e8, 1e6)
@@ -400,6 +402,7 @@
         name=name,
         out_shape=out_shape,
         scratch_shapes=list(scratch),
+        input_output_aliases=aliases or {},
         compiler_params=pltpu.CompilerParams(vmem_limit_bytes=VMEM_LIMIT),
         cost_estimate=pl.CostEstimate(flops=int(flops), bytes_accessed=int(moved), transcendentals=0),
         **extra,
@@ -467,6 +470,16 @@
 def gather_pieces(pieces, held):
     at = 0
     for piece in pieces:
+        held[at : at + piece.shape[0], :] = piece[...]
+        at += piece.shape[0]
+
+
+def gather_halves(pieces, held):
+    size = pieces[0].shape[0] // 2
+    for number, piece in enumerate(pieces[:4]):
+        held[number * size : (number + 1) * size, :] = piece[:size, :]
+    at = 4 * size
+    for piece in pieces[4:]:
         held[at : at + piece.shape[0], :] = piece[...]
         at += piece.shape[0]
 
@@ -583,16 +596,12 @@
     router_grad_ref[...] += dot_tn(low, got)
 
 
-def weight_grad_body(hidden_ref, active_ref, got_ref, scaled_ref, mine_ref, *theirs_refs):
-    half = hidden_ref.shape[1] // 2
-    parts = max(len(theirs_refs) // 2, 1)
-    for number, ref in enumerate(theirs_refs):
-        size = ref.shape[0]
-        at = slice(half + number % parts * size, half + (number % parts + 1) * size)
-        left, right = ((hidden_ref, got_ref), (active_ref, scaled_ref))[number // parts]
-        ref[...] = dot_tn(left[:, at], right[...]).astype(ref.dtype)
-    mine_ref[:half, :] = dot_tn(hidden_ref[:, :half], got_ref[...])
-    mine_ref[half:, :] = dot_tn(active_ref[:, :half], scaled_ref[...])
+def weight_grad_body(hidden_ref, active_ref, got_ref, scaled_ref, *outs):
+    size = outs[0].shape[0]
+    for number, out in enumerate(outs):
+        left, right = ((hidden_ref, got_ref), (active_ref, scaled_ref))[number % 2]
+        at = slice((1 - number // 2) * size, (2 - number // 2) * size)
+        out[...] = dot_tn(left[:, at], right[...]).astype(out.dtype)
 
 
 def norm_back(hat, scale, gain, grad):
@@ -667,7 +676,7 @@
 
 
 def outer_body(
-    n_exp, qkv_ref, out_grad_ref, sums_ref, keep_ref, query_ref, kv_ref, normed_ref, own_ref, w_ref,
+    n_exp, qkv_ref, out_grad_ref, sums_ref, keep_ref, query_ref, kv_ref, normed_ref, own_ref, w_ref, early_ref,
     pieces_ref, grad_normed_ref, held,
 ):
     toks, width = query_ref.shape
@@ -696,6 +705,7 @@
     pieces_ref[3 * width : 3 * width + 16, :] = jnp.where(
         iota((16, width), 0) == 0, gain_grad, 0.0
     ).astype(BF16)
+    pieces_ref[3 * width + 16 :, :] = early_ref[...]
 
 
 def tokens_body(n_exp, grad_normed_ref, own_ref, w_ref, grad_ref, out_ref):
@@ -705,14 +715,13 @@
     out_ref[...] = grad_ref[...] + norm_back(hat, scale, gain_one, grad_normed_ref[...])
 
 
-def spread_body(starts, pos_ref, late_ref, late_far_ref, early_ref, early_far_ref, out_ref, held):
-    cut = late_ref.shape[0]
-    held[0:cut, :] = total_f32(late_ref[...], late_far_ref[...]).astype(BF16)
-    held[cut:, :] = total_f32(early_ref[...], early_far_ref[...]).astype(BF16)
-    size = out_ref.shape[1]
+def spread_body(starts, pos_ref, mine_ref, far_ref, *outs):
+    held, outs = outs[-1], outs[:-1]
+    held[...] = total_f32(mine_ref[...], far_ref[...]).astype(BF16)
+    size = outs[0].shape[0]
     for number, start in enumerate(starts):
         picks = as_bf16(iota((size, held.shape[0]), 0) + start == pos_ref[...])
-        out_ref[number] = dot_nn(picks, held[...]).astype(BF16)
+        outs[number][...] = dot_nn(picks, held[...]).astype(BF16)
 
 
 def room_of(owned, n_dev):
@@ -720,11 +729,15 @@
 
 
 def sent_at(partner):
+    return ((partner >> 2) & 1) * 4 + (partner & 1) * 2 + ((partner >> 1) & 1)
+
+
+def got_at(partner):
     return ((partner >> 1) & 1) * 4 + ((partner >> 2) & 1) * 2 + (partner & 1)
 
 
-def got_at(partner):
-    return ((partner >> 2) & 1) * 4 + (partner & 1) * 2 + ((partner >> 1) & 1)
+def sent_cell(cell):
+    return (cell >> 2) * 4 + (cell & 1) * 2 + ((cell >> 1) & 1)
 
 
 def plan_body(n_dev, room, me_ref, owner_ref, row_ref, col_ref, most_ref):
@@ -750,9 +763,9 @@
     rank = jnp.concatenate(ranks, axis=1)
     turn = ((rank + 0.5) * (1.0 / room)).astype(I32)
     inside = rank.astype(I32) + turn * ((n_dev - 1) * room)
-    arrives = jnp.sum(
-        jnp.where(member & (to == me), inside + got_at(of ^ to) * room, 0), axis=0, keepdims=True
-    )
+    wanted = member & (to == me)
+    arrives = jnp.sum(jnp.where(wanted, inside + got_at(of ^ to) * room, 0), axis=0, keepdims=True)
+    returns = jnp.sum(jnp.where(wanted, inside + sent_at(of ^ to) * room, 0), axis=0, keepdims=True)
     leaves = inside + sent_at(of ^ to) * room
     half = owned // LANES
     found = jnp.zeros((2 * half, LANES), F32)
@@ -768,12 +781,17 @@
         found = found + dot_nt(left, as_bf16((spot[t : t + 1, :] % LANES) == lanes))
     found = found[:half] * float(LANES) + found[half:]
     leave_row = jnp.concatenate([found[a : a + 1, :] for a in range(half)], axis=1)
-    rows = jnp.concatenate([leave_row, arrives.astype(F32), jnp.zeros((6, owned), F32)], axis=0)
+    block = ((leave_row + 0.5) * (1.0 / room)).astype(I32)
+    round_no, cell = block // n_dev, block % n_dev
+    comes = leave_row.astype(I32) + (round_no * n_dev + got_at(sent_cell(cell)) - block) * room
+    rows = jnp.concatenate(
+        [leave_row, arrives.astype(F32), returns.astype(F32), comes.astype(F32), jnp.zeros((4, owned), F32)], axis=0
+    )
     row_ref[...] = rows.astype(I32)
     col_ref[...] = jnp.transpose(rows).astype(I32)
 
 
-LEAVES, ARRIVES = 0, 1
+LEAVES, ARRIVES, RETURNS, COMES = range(4)
 
 
 def put_rows(line, base_ref, pos_ref, held, outs, tile):
@@ -790,41 +808,37 @@
     put_rows(line, base_ref, pos_ref, rows_ref, outs, tile)
 
 
-def sum_put_body(line, tile, n_in, base_ref, pos_ref, mine_ref, *refs):
-    others, outs, held = refs[:n_in], refs[n_in:-1], refs[-1]
-    gather_pieces(others, held)
-    held[...] = total_f32(mine_ref[...], held[...]).astype(BF16)
-    put_rows(line, base_ref, pos_ref, held, outs, tile)
+def sum_put_body(line, tile, cells, n_in, base_ref, pos_ref, *refs):
+    mine, theirs, outs, held = refs[:n_in], refs[n_in : 2 * n_in], refs[2 * n_in : -1], refs[-1]
+    size = mine[0].shape[0]
+    for number in range(n_in):
+        held[number * size : (number + 1) * size, :] = total_f32(mine[number][...], theirs[number][...]).astype(BF16)
+    wanted = pos_ref[line : line + 1, :] - base_ref[0]
+    for cell, out in zip(cells, outs):
+        for at in range(0, out.shape[0], tile):
+            picks = as_bf16(iota((tile, held.shape[0]), 0) + (cell * out.shape[0] + at) == wanted)
+            out[at : at + tile, :] = dot_nn(picks, held[...]).astype(BF16)
 
 
 def take_body(line, tile, base_ref, pos_ref, *refs):
     pieces, out, held = refs[:-2], refs[-2], refs[-1]
-    gather_pieces(pieces, held)
+    gather_halves(pieces, held)
     for at in range(0, out.shape[0], tile):
         wanted = pos_ref[at : at + tile, line : line + 1] - base_ref[0]
         picks = as_bf16(iota((tile, held.shape[0]), 1) == wanted)
         out[at : at + tile, :] = dot_nn(picks, held[...]).astype(BF16)
 
 
-def take_more_body(line, tile, base_ref, pos_ref, *refs):
-    pieces, more, out, held = refs[:-3], refs[-3], refs[-2], refs[-1]
-    gather_pieces(pieces, held)
-    for at in range(0, out.shape[0], tile):
-        wanted = pos_ref[at : at + tile, line : line + 1] - base_ref[0]
-        picks = as_bf16(iota((tile, held.shape[0]), 1) == wanted)
-        out[at : at + tile, :] = (dot_nn(picks, held[...]) + more[at : at + tile, :].astype(F32)).astype(BF16)
-
-
-def adam_body(n_in, pos_ref, *refs):
-    pieces = refs[:n_in]
-    more_ref, first_ref, second_ref, weight_ref, grad_ref, first_new, second_new, weight_new, held = refs[n_in:]
+def adam_body(n_in, n_made, pos_ref, *refs):
+    pieces, (first_ref, second_ref, weight_ref) = refs[:n_in], refs[n_in : n_in + 3]
+    grad_ref, first_new, second_new, weight_new, held = refs[n_in + 3 + n_made :]
 
     @pl.when(pl.program_id(0) == 0)
     def _():
-        gather_pieces(pieces, held)
-
-    picks = as_bf16(iota((grad_ref.shape[0], held.shape[0]), 1) == pos_ref[:, LEAVES : LEAVES + 1])
-    grad = dot_nn(picks, held[...]) + more_ref[...].astype(F32)
+        gather_halves(pieces, held)
+
+    picks = as_bf16(iota((grad_ref.shape[0], held.shape[0]), 1) == pos_ref[:, COMES : COMES + 1])
+    grad = dot_nn(picks, held[...])
     grad_ref[...] = grad
     made = adam_update(grad, first_ref[...], second_ref[...], weight_ref[...].astype(F32))
     first_new[...], second_new[...], weight_new[...] = made
@@ -901,7 +915,6 @@
     pair_a, pair_b = jnp.concatenate([part_a, a_y], axis=0), jnp.concatenate([part_b, b_x], axis=0)
     first_near, last_near = [pair_a, pair_b], [swap_x(pair_a), swap_y(pair_b)]
     first_far = [swap_core(piece) for piece in first_near]
-    last_far = [swap_core(piece) for piece in last_near]
 
     owner_dev, owner_row = shared_owner // own_count, shared_owner % own_count
     o_z, o_x, o_dp = owner_dev % n_z, owner_dev // n_z % 2, owner_dev // (n_z * 2)
@@ -919,78 +932,6 @@
         [place[: 3 * width], place[gain_at : gain_at + 1], none, place[3 * width : gain_at], place[gain_at + 1 :], none]
     )[None, :]
 
-    own, other = tokens[0], swap_x(after([tokens[0]], *last_near)[0])
-    ids = expert_ids[0]
-    live = pad_mask.astype(F32)
-    live_other = swap_x(pad_mask).astype(F32)
-    keep_row = jnp.concatenate([live, live_other], axis=1)
-    keep_col = live.reshape(toks, 1)
-    pos_row, pos_col, cot_sent = kernel_call(
-        functools.partial(route_body, n_exp, capacity),
-        (sds((8, toks), I32), sds((toks, 8), I32), sds((slots, width), BF16)),
-        cost=(4 * MICRO, 1e6),
-    )(ids.T, slot_priority.astype(F32), live, cotangent[0])
-
-    def exchange(rows):
-        return lax.all_to_all(rows, everyone, split_axis=0, concat_axis=0, tiled=True)
-
-    cot_got = exchange(after([cot_sent], part_a, part_b)[0])
-
-    local = my * 2 + mx
-    group, n_dev = dp * 2 + mx, 8
-    owned = expert_slots.shape[1]
-    room = room_of(owned, n_dev)
-    owner = jnp.transpose(
-        expert_owner[0].reshape(2, 2, 2, 2, FF // 2), (0, 3, 1, 2, 4)
-    ).reshape(n_dev, owned)
-    held = [pltpu.VMEM((n_dev * room, width), BF16)]
-    sent_shapes, got_shapes = [sds((4 * room, width), BF16)] * 2, [sds((2 * room, width), BF16)] * 4
-    smem, vmem = pl.BlockSpec(memory_space=pltpu.SMEM), pl.BlockSpec(memory_space=pltpu.VMEM)
-    plan_row, plan_col, most = kernel_call(
-        functools.partial(plan_body, n_dev, room),
-        (sds((8, owned), I32), sds((owned, 8), I32), sds((8, LANES), I32)), cost=(5 * MICRO, 1e6),
-        in_specs=[smem, vmem],
-    )(group.astype(I32).reshape(1), *after([owner], pos_row))
-    rounds = (most[0, 0] + room - 1) // room
-    swaps = (swap_x, swap_y, swap_x_y)
-
-    def with_base(body, out_shape, scratch, arrays, number=0):
-        base = jnp.full((1,), number * n_dev * room, I32)
-        return kernel_call(
-            body, out_shape, scratch, in_specs=[smem] + [vmem] * len(arrays), cost=(8 * MICRO, 1e6)
-        )(base, *arrays)
-
-    def send_pieces(near, far):
-        got = [near[:room], far[:room]]
-        for by, swap in enumerate(swaps, 1):
-            rows = slice(by * room, (by + 1) * room)
-            got.append(swap(jnp.concatenate([near[rows], far[rows]], axis=0)))
-        return got
-
-    def return_near(pieces, *others):
-        x, y, x_y = after(pieces[1:], *others) if others else pieces[1:]
-        return [pieces[0], swap_x(x), swap_y(pieces[2]), swap_x_y(x_y)]
-
-    def return_far(got):
-        near = [piece[:room] for piece in got]
-        return [*near, swap_core(jnp.concatenate([piece[room:] for piece in got], axis=0))]
-
-    put_leaving = functools.partial(put_body, LEAVES, room)
-    take_tile = 256 if owned % 256 == 0 else owned
-    take_more = functools.partial(take_body, ARRIVES, take_tile)
-
-    def more_weights(number, total):
-        near, far = with_base(put_leaving, sent_shapes, (), [plan_row, expert_slots[0]], number)
-        moved = send_pieces(near, swap_core(far))
-        part = with_base(take_more, sds((owned, width), BF16), held, [plan_col, *moved], number)
-        return total + part
-
-    more_rows = lax.fori_loop(1, rounds, more_weights, jnp.zeros((owned, width), BF16))
-    near, far = with_base(put_leaving, sent_shapes, (), [*after([plan_row], part_a, part_b, more_rows), expert_slots[0]])
-    near_sent, far_sent = after([near, far], *last_near)
-    far_sent = swap_core(far_sent)
-    moved = send_pieces(*after([near_sent, far_sent], other))
-
     half_slots = total_slots // 2
     piece = half_slots // 4
     row_tile = row_count // 5 if row_count % 80 == 0 else row_count
@@ -1008,10 +949,68 @@
         )(place_col, *pieces, *earlier)
 
     first_rows = unpack(
-        [0, 2 * piece, half_slots, half_slots + 2 * piece], [*after(first_near, near), *first_far], []
-    )
-    near_rows = unpack([piece, 3 * piece], last_near, [first_rows])
-    weights = unpack([half_slots + piece, half_slots + 3 * piece], last_far, [near_rows])
+        [0, 2 * piece, half_slots, half_slots + 2 * piece], [*first_near, *first_far], []
+    )
+    last_near = after(last_near, first_rows)
+    last_far = [swap_core(piece) for piece in last_near]
+
+    own, other = tokens[0], swap_x(tokens[0])
+    ids = expert_ids[0]
+    live = pad_mask.astype(F32)
+    live_other = swap_x(pad_mask).astype(F32)
+    keep_row = jnp.concatenate([live, live_other], axis=1)
+    keep_col = live.reshape(toks, 1)
+    pos_row, pos_col, cot_sent = kernel_call(
+        functools.partial(route_body, n_exp, capacity),
+        (sds((8, toks), I32), sds((toks, 8), I32), sds((slots, width), BF16)),
+        cost=(4 * MICRO, 1e6),
+    )(*after([ids.T], other), slot_priority.astype(F32), live, cotangent[0])
+
+    def exchange(rows):
+        return lax.all_to_all(rows, everyone, split_axis=0, concat_axis=0, tiled=True)
+
+    cot_got = exchange(after([cot_sent], a_y, b_x)[0])
+
+    local = my * 2 + mx
+    group, n_dev = dp * 2 + mx, 8
+    owned = expert_slots.shape[1]
+    room = room_of(owned, n_dev)
+    owner = jnp.transpose(
+        expert_owner[0].reshape(2, 2, 2, 2, FF // 2), (0, 3, 1, 2, 4)
+    ).reshape(n_dev, owned)
+    held = [pltpu.VMEM((n_dev * room, width), BF16)]
+    sent_shapes = [sds((2 * room, width), BF16)] * 4
+    smem, vmem = pl.BlockSpec(memory_space=pltpu.SMEM), pl.BlockSpec(memory_space=pltpu.VMEM)
+    plan_row, plan_col, most = kernel_call(
+        functools.partial(plan_body, n_dev, room),
+        (sds((8, owned), I32), sds((owned, 8), I32), sds((8, LANES), I32)), cost=(5 * MICRO, 1e6),
+        in_specs=[smem, vmem],
+    )(group.astype(I32).reshape(1), *after([owner], part_a, part_b, pos_row, other))
+    rounds = (most[0, 0] + room - 1) // room
+    def with_base(body, out_shape, scratch, arrays, number=0, cost=QUICK):
+        base = jnp.full((1,), number * n_dev * room, I32)
+        return kernel_call(
+            body, out_shape, scratch, in_specs=[smem] + [vmem] * len(arrays), cost=cost
+        )(base, *arrays)
+
+    def over_links(pieces):
+        return [pieces[0], swap_x(pieces[1]), swap_y(pieces[2]), swap_x_y(pieces[3])]
+
+    def over_cores(got):
+        far = [jnp.concatenate([got[at][room:], got[at + 1][room:]], axis=0) for at in (0, 2)]
+        return [*got, swap_core(far[0]), swap_core(far[1])]
+
+    put_leaving = functools.partial(put_body, LEAVES, room)
+    take_tile = 256 if owned % 256 == 0 else owned
+    take_arrived = functools.partial(take_body, ARRIVES, take_tile)
+    leaving = with_base(
+        put_leaving, sent_shapes, (), [*after([plan_row], a_y, b_x), expert_slots[0]], 0, (8 * MICRO, 1e6)
+    )
+    moved = over_links(after(leaving, *last_near))
+
+    weights = unpack(
+        [piece, 3 * piece, half_slots + piece, half_slots + 3 * piece], [*last_near, *last_far], [first_rows]
+    )
 
     (qkv, normed, attended, residual, prob, sent, lse_col, lse_row) = kernel_call(
         functools.partial(forward_body, n_exp),
@@ -1022,14 +1021,21 @@
         ),
         [pltpu.VMEM((toks, width), BF16)],
         cost=(13 * MICRO, 1e6),
-    )(own, other, keep_row, weights, pos_row)
+    )(*after([own], cot_got), other, keep_row, weights, pos_row)
     got = exchange(sent)
-    near_weights = with_base(
-        functools.partial(take_more_body, ARRIVES, take_tile), sds((owned, width), BF16), held,
-        [*after([plan_col], sent), *moved, more_rows],
-    )
-
+    moved = over_cores(after(moved, sent))
+    near_weights = with_base(take_arrived, sds((owned, width), BF16), held, [plan_col, *moved])
     far_weights = [swap_core(near_weights[: FF // 2]), swap_core(near_weights[FF // 2 :])]
+
+    def more_weights(number, totals):
+        leaving = with_base(put_leaving, sent_shapes, (), [plan_row, expert_slots[0]], number)
+        moved = over_cores(over_links(leaving))
+        part = with_base(take_arrived, sds((owned, width), BF16), held, [plan_col, *moved], number)
+        there = swap_core(part)
+        return totals[0] + part, totals[1] + there[: FF // 2], totals[2] + there[FF // 2 :]
+
+    got, *expert_weights = after([got, near_weights, *far_weights])
+    near_weights, *far_weights = lax.fori_loop(1, rounds, more_weights, tuple(expert_weights))
 
     expert_id = (mz * EXP_DEV + local).astype(I32).reshape(1)
     tile = 256 if slots % 256 == 0 else slots
@@ -1054,22 +1060,22 @@
     )(expert_id, got, cot_got, near_weights, *far_weights, router_rows)
     back_got = exchange(back)
 
-    mine, *theirs = kernel_call(
-        weight_grad_body, [sds((FF, width), F32)] + [sds((FF // THEIRS, width), BF16)] * THEIRS, cost=(10 * MICRO, 1e7)
-    )(hidden, active, got, scaled)
-    theirs_got = [swap_core(part) for part in theirs]
-    put_returning = functools.partial(sum_put_body, ARRIVES, room, THEIRS)
+    halves = [sds((FF // 2, width), BF16)] * 2 + [sds((FF // 2, width), F32)] * 2
+    *theirs, mine_in, mine_out = kernel_call(weight_grad_body, halves, cost=(10 * MICRO, 1e6))(
+        hidden, active, got, scaled
+    )
+    theirs_got, mine = [swap_core(part) for part in theirs], (mine_in, mine_out)
     held_owned = [pltpu.VMEM((owned, width), BF16)]
-    moved = with_base(put_returning, got_shapes, held_owned, [plan_row, mine, *theirs_got])
-    back_got, *moved = after([back_got, *moved])
-
-    def more_grads(number, total):
-        parts = with_base(put_returning, got_shapes, held_owned, [plan_row, mine, *theirs_got], number)
-        parts = return_far(return_near(parts))
-        take = functools.partial(take_body, LEAVES, take_tile)
-        return total + with_base(take, sds((owned, width), BF16), held, [plan_col, *parts], number)
-
-    more = lax.fori_loop(1, rounds, more_grads, after([jnp.zeros((owned, width), BF16)], back_got)[0])
+
+    def returning(cells, number=0):
+        body = functools.partial(sum_put_body, RETURNS, room, cells, 2)
+        return with_base(body, [sent_shapes[0]] * len(cells), held_owned, [plan_row, *mine, *theirs_got], number, (4 * MICRO, 1e6))
+
+    moved_x, moved_xy = returning((1, 3))
+    moved_0, moved_y = returning((0, 2))
+    moved = [moved_0, moved_x, moved_y, moved_xy]
+    back_got = after([back_got], moved[0])[0]
+
     grad_residual, out_grad, delta_col, delta_row, gain_two = kernel_call(
         functools.partial(middle_body, n_exp),
         (
@@ -1080,67 +1086,86 @@
     )(back_got, pos_col, residual, cotangent[0], keep_col, attended, weights)
     out_grad_other = swap_x(out_grad)
     sums_other = swap_x(jnp.concatenate([lse_row, delta_row], axis=0))
-    moved = return_near(moved, out_grad_other)
-    result_got = exchange(after([result], out_grad_other, more)[0])
+    moved = over_links(moved)
     query_grad, kv_grad, early = kernel_call(
         functools.partial(inner_body, n_exp),
         (sds((toks, width), BF16), sds((2, toks, width), F32), sds((width + n_exp + 16, width), BF16)),
         cost=(15 * MICRO, 1e6),
     )(qkv, out_grad, lse_col, delta_col, keep_row, attended, grad_residual, router_grad, gain_two)
-    early_far = swap_core(early)
+    result_got = exchange(after([result], query_grad)[0])
     late, grad_normed = kernel_call(
         functools.partial(outer_body, n_exp),
-        (sds((3 * width + 16, width), BF16), sds((toks, width), F32)),
+        (sds((place_row.shape[1], width), BF16), sds((toks, width), F32)),
         [pltpu.VMEM((toks, 3 * width), BF16)],
-        cost=(12 * MICRO, 1e6),
+        cost=QUICK,
     )(
-        qkv, *after([out_grad_other], moved[2]), sums_other, keep_col, query_grad, kv_grad, normed, own, weights,
+        qkv, *after([out_grad_other], *moved), sums_other, keep_col, query_grad, kv_grad, normed, own, weights, early,
     )
     late_far = swap_core(late)
-    grad_tokens = kernel_call(
-        functools.partial(tokens_body, n_exp), sds((toks, width), F32), cost=(2 * MICRO, 4e6)
-    )(grad_normed, own, weights, grad_residual)
     quarter = half_slots // 2
     eighth, sixteenth = quarter // 2, quarter // 4
     count = place_row.shape[1]
 
     def spread(starts, *others):
         return kernel_call(
-            functools.partial(spread_body, starts), sds((2, eighth, width), BF16),
-            [pltpu.VMEM((count, width), BF16)], cost=(6 * MICRO, 1e6),
-        )(*after([place_row], *others), late, late_far, early, early_far)
+            functools.partial(spread_body, starts), [sds((eighth, width), BF16)] * 2,
+            [pltpu.VMEM((count, width), BF16)], cost=QUICK,
+        )(*after([place_row], *others), late, late_far)
 
     sends = spread((eighth, quarter + eighth))
     got_a, got_b = swap_x(sends[0]), swap_y(sends[1])
-    keeps = spread((0, quarter), sends)
-    moved = return_far(after(moved, keeps))
-
-    tile = 256 if owned % 256 == 0 else owned
-    rows_of = lambda columns: pl.BlockSpec((tile, columns), lambda i: (i, 0))
-    expert_new = kernel_call(
-        functools.partial(adam_body, len(moved)), [sds((owned, width), F32)] * 4, held,
-        grid=(owned // tile,),
-        in_specs=[rows_of(8)] + [pl.BlockSpec(piece.shape, lambda i: (0, 0)) for piece in moved] + [rows_of(width)] * 4,
-        out_specs=[rows_of(width)] * 4,
-        cost=(14 * MICRO, 3e7),
-    )(plan_col, *moved, more, expert_first[0], expert_second[0], expert_slots[0])
-
+    keeps = spread((0, quarter), *sends)
+    grad_tokens = kernel_call(
+        functools.partial(tokens_body, n_exp), sds((toks, width), F32), cost=QUICK
+    )(*after([grad_normed], *sends), own, weights, grad_residual)
+    moved = over_cores(after(moved, *keeps))
+
+    tile = 256 if owned % 512 == 0 else owned // 2
+    steps = owned // tile // 2
+
+    def adam_half(number, made, *others):
+        rows_of = lambda columns: pl.BlockSpec((tile, columns), lambda i: (i + number * steps, 0))
+        n_given = 1 + len(moved) + 3
+        return kernel_call(
+            functools.partial(adam_body, len(moved), len(made)), [sds((owned, width), F32)] * 4, held,
+            grid=(steps,),
+            in_specs=[rows_of(8)] + [pl.BlockSpec(piece.shape, lambda i: (0, 0)) for piece in moved]
+            + [rows_of(width)] * 3 + [pl.BlockSpec(memory_space=pl.ANY)] * len(made),
+            out_specs=[rows_of(width)] * 4,
+            cost=QUICK,
+            aliases={n_given + at: at for at in range(len(made))},
+        )(*after([plan_col], *others), *moved, expert_first[0], expert_second[0], expert_slots[0], *made)
+
+    got_a, got_b = after([got_a, got_b], grad_tokens)
     sum_a = total_f32(keeps[0], got_a).astype(BF16)
     sum_b = total_f32(keeps[1], got_b).astype(BF16)
     got_a, got_b = swap_y(sum_a[sixteenth:]), swap_x(sum_b[sixteenth:])
+    half_new = adam_half(0, [], sum_a, sum_b)
+    got_a, got_b = after([got_a, got_b], half_new[0])
     sum_a = total_f32(sum_a[:sixteenth], got_a).astype(BF16)
     sum_b = total_f32(sum_b[:sixteenth], got_b).astype(BF16)
     lines = [sum_a[i * stride : (i + 1) * stride] for i in range(n_z // 2)]
     lines += [sum_b[i * stride : (i + 1) * stride] for i in range(n_z // 2)]
+    output = kernel_call(
+        mixture_body, sds((toks, width), BF16), cost=QUICK
+    )(*after([result_got], *lines), pos_col, ids, prob, residual)
+    expert_new = adam_half(1, half_new, *lines)
     shared_grad = lines[0].astype(F32)
     for by in range(1, n_z):
         shared_grad = shared_grad + shift_z(lines[by], n_z - by).astype(F32)
     shared_grad = shared_grad[:own_count]
 
-    output = kernel_call(
-        mixture_body, sds((toks, width), BF16), cost=(4 * slots * toks * width, 4e6)
-    )(result_got, pos_col, ids, prob, residual)
-
+
+    def more_grads(number, made):
+        parts = returning(range(4), number)
+        parts = over_cores(over_links(parts))
+        take = functools.partial(take_body, COMES, take_tile)
+        part = with_base(take, sds((owned, width), BF16), held, [plan_col, *parts], number)
+        grad = made[0] + part.astype(F32)
+        return (grad, *adam_update(grad, expert_first[0], expert_second[0], expert_slots[0].astype(F32)))
+
+    shared_grad, *expert_new = after([shared_grad, *expert_new], output)
+    expert_new = lax.fori_loop(1, rounds, more_grads, tuple(expert_new))
     shared_new = adam_update(shared_grad, shared_first, shared_second, shared_slots.astype(F32))
     return (
         output[None], grad_tokens[None], shared_grad, *shared_new,

time: 359 us -> 312 us (0.87)
  waiting for transfers between devices: 79.3 us -> 37.6 us
  Pallas kernels: 170 us -> 166 us
    ppermute x10, waiting for transfers between devices: 34.4 us -> 10.1 us  [swap_x(): return lax.ppermute(value, 'ctx', SWAP)]
    ppermute x2, waiting for transfers between devices: 16 us -> 2.26 us  [swap_x_y(): return lax.ppermute(value, ('dp', 'ctx'), [(i, i ^ 5) for i in range(8)])]
    ppermute x6, waiting for transfers between devices: 19 us -> 7.24 us  [swap_y(): return lax.ppermute(value, 'dp', SWAP_Y)]
    pallas_call x3 -> x2, Pallas kernels: 23.9 us -> 18.6 us  [unpack(): kernel_call(functools.partial(unpack_body, spots, len(earlier)), sds((row...]
    pallas_call x6 -> x7, Pallas kernels: 56.4 us -> 58.3 us  [the longest x2 18.2 us: adam_half(): kernel_call(functools.partial(adam_body, len(moved), len(made)), [sds((ow...]
    unnamed x74 -> x57, local copies, waits for them, and re-layouts: 9.29 us -> 8.44 us
    pallas_call x3 -> x4, Pallas kernels: 26.2 us -> 26.3 us  [with_base(): kernel_call(body, out_shape, scratch, in_specs=[smem] + [vmem] * len(arra...]
  transfers between devices with their start and end apart: 40 -> 41, of which waited for: 12 -> 14; matrix products, arithmetic and copies ran while one was open for 10% -> 12% of each run, Pallas kernels for 37% -> 44%
where the time goes in v3:
time: 312 us; the launch traced here: 307 us
  Pallas kernels  166 us (53%)
  starting transfers between devices  58.2 us (19%)
  waiting for transfers between devices  37.6 us (12%)
  local copies, waits for them, and re-layouts  29.8 us (10%)
  other arithmetic  13.8 us (4%)
    pallas_call x4, Pallas kernels, with_base(): kernel_call(body, out_shape, scratch, in_specs=[smem] + [vmem] * len(arra...  26.3 us
    all_to_all x4, starting transfers between devices, exchange(): lax.all_to_all(rows, everyone, split_axis=0, concat_axis=0, tiled=True)  20.4 us
    pallas_call x1, Pallas kernels, on_chip_experts(): kernel_call(functools.partial(expert_body, n_exp), (sds((slots, FF), BF16...  18.8 us
    pallas_call x2, Pallas kernels, unpack(): kernel_call(functools.partial(unpack_body, spots, len(earlier)), sds((row...  18.6 us
    pallas_call x2, Pallas kernels, adam_half(): kernel_call(functools.partial(adam_body, len(moved), len(made)), [sds((ow...  18.2 us
    pallas_call x1, Pallas kernels, on_chip_experts(): kernel_call(functools.partial(inner_body, n_exp), (sds((toks, width), BF1...  14.5 us
    ppermute x6, starting transfers between devices, shift_z(): lax.ppermute(value, 'expert', [(i, (i + by) % count) for i in range(count)])  13.9 us
    pallas_call x1, Pallas kernels, on_chip_experts(): kernel_call(functools.partial(forward_body, n_exp), (sds((2 * toks, 3 * w...  12.5 us
  transfers between devices with their start and end apart: 41, of which 14 were waited for; matrix products, arithmetic and copies ran while one was open for 12% of the time, Pallas kernels for 44%

profile of v3, /device:TPU:0, one launch (start us, length us, event | category | flops | bytes accessed | tf_op | source)
XLA Modules:
  0.0 307.2 jit_solution(2817734143238009706)
XLA Ops:
  1.6 3.1 %collective-permute-start.12 = (bf16[136,512]{1,0:T(8,128)(2,1)S(1)}, bf16[136,512]{1,0:T(8,128)(2,1)S(1)}, u32[]{:S(2)}, u32[]{:S(2)}) collective-permute-start(bf16[136,512]{1,0:T(8,128)(2,1)S(1)} %pad.8), channel_id=1, source_target_pairs={{0,1},{1,2},{2,3},{3,0},{4,5},{5,6},{6,7},{7,4},{8,9},{9,10},{10,1... | collective-permute-start | bytes 417800 | tf_op jit(solution)/shard_map/ppermute | solution.py:883
  4.7 2.6 collective-permute-start.14
  13.2 3.3 %collective-permute-done.14 = bf16[136,512]{1,0:T(8,128)(2,1)S(1)} collective-permute-done((bf16[136,512]{1,0:T(8,128)(2,1)S(1)}, bf16[136,512]{1,0:T(8,128)(2,1)S(1)}, u32[]{:S(2)}, u32[]{:S(2)}) %collective-permute-start.14) | collective-permute-done | bytes 139296 | tf_op jit(solution)/shard_map/ppermute | solution.py:883
  30.7 3.6 %route_body.1 = (s32[8,512]{1,0:T(8,128)}, s32[512,8]{1,0:T(8,128)}, bf16[1280,512]{1,0:T(8,128)(2,1)}) custom-call(s32[2,512]{1,0:T(2,128)} %copy.31.ids_ref, f32[1,512]{1,0:T(1,128)} %convert_element_type.77.prio_ref, f32[1,512]{1,0:T(1,128)} %copy-done.29, bf16[512,512]{1,0:T(8,128)(2,1)} %bitcast.78), custom_call_target="tpu_custom_call" | custom-call | flops 4600000000 | bytes 1000000 | tf_op jit(solution)/shard_map/route_body/pallas_call | solution.py:963
  34.3 6.4 %all-to-all-start = ((bf16[32,40,512]{2,1,0:T(8,128)(2,1)}), bf16[32,40,512]{2,1,0:T(8,128)(2,1)}, u32[]{:S(2)}, u32[]{:S(2)}) async-start(bf16[32,40,512]{2,1,0:T(8,128)(2,1)} %bitcast.72), calls=%async_computation | async-start | bytes 2621440 | tf_op jit(solution)/shard_map/all_to_all | solution.py:970
  40.7 3.4 %plan_body.1 = (s32[8,2048]{1,0:T(8,128)S(1)}, s32[2048,8]{1,0:T(8,128)S(1)}, s32[8,128]{1,0:T(8,128)}) custom-call(s32[1]{0:T(128)} %bitcast.16.me_ref, s32[8,2048]{1,0:T(8,128)} %bitcast.77), custom_call_target="tpu_custom_call" | custom-call | flops 5750000128 | bytes 1000000 | tf_op jit(solution)/shard_map/plan_body/pallas_call | solution.py:984
  44.1 9.2 %unpack_body.2.refs_4_ = bf16[2080,512]{1,0:T(8,128)(2,1)} custom-call(s32[2080,1]{1,0:T(8,128)} %broadcast_in_dim.40.pos_ref, bf16[544,512]{1,0:T(8,128)(2,1)} %pad_maximum_fusion.8.refs_0_, bf16[544,512]{1,0:T(8,128)(2,1)} %constant_dynamic-update-slice_fusion.2.refs_1_, bf16[544,512]{1,0:T(8,128)(2,1)} %collective-permute-done.20.refs_2_, ...), custom_call_target="tpu_custom_call" | custom-call | flops 8049999872 | bytes 1000000 | tf_op jit(solution)/shard_map/unpack_body/pallas_call | solution.py:941
  53.9 6.6 %put_body.5 = (bf16[640,512]{1,0:T(8,128)(2,1)}, bf16[640,512]{1,0:T(8,128)(2,1)}, bf16[640,512]{1,0:T(8,128)(2,1)}, bf16[640,512]{1,0:T(8,128)(2,1)}) custom-call(s32[1]{0:T(128)} %constant.192.clone.1.base_ref, s32[8,2048]{1,0:T(8,128)S(1)} %get-tuple-element.400.pos_ref, bf16[2048,512]{1,0:T(8,128)(2,1)S(1)} %bitcast.52), custom_call_target="tpu_custom_call" | custom-call | flops 9200000000 | bytes 1000000 | tf_op jit(solution)/shard_map/put_body/pallas_call | solution.py:992
  65.7 9.4 %unpack_body.3.w_ref = bf16[2080,512]{1,0:T(8,128)(2,1)} custom-call(s32[2080,1]{1,0:T(8,128)} %broadcast_in_dim.40.pos_ref, bf16[544,512]{1,0:T(8,128)(2,1)} %collective-permute-done.18.refs_0_, bf16[544,512]{1,0:T(8,128)(2,1)} %collective-permute-done.19.refs_1_, bf16[544,512]{1,0:T(8,128)(2,1)} %copy-done.30, bf16[544,512]{1,0:T(8,128)(2,1)} %copy-done.31, ...), custom_call_target="tpu_custom_call" | custom-call | flops 8049999872 | bytes 1000000 | tf_op jit(solution)/shard_map/unpack_body/pallas_call | solution.py:941
  75.1 12.5 %forward_body.1 = (bf16[1024,1536]{1,0:T(8,128)(2,1)}, bf16[512,512]{1,0:T(8,128)(2,1)}, f32[512,512]{1,0:T(8,128)}, f32[512,512]{1,0:T(8,128)}, f32[512,16]{1,0...) custom-call(bf16[512,512]{1,0:T(8,128)(2,1)} %bitcast.67, ...), custom_call_target="tpu_custom_call" | custom-call | flops 14949999616 | bytes 1000000 | tf_op jit(solution)/shard_map/forward_body/pallas_call | solution.py:1015
  87.6 6.5 %all-to-all-start.1 = ((bf16[32,40,512]{2,1,0:T(8,128)(2,1)}), bf16[32,40,512]{2,1,0:T(8,128)(2,1)}, u32[]{:S(2)}, u32[]{:S(2)}) async-start(bf16[32,40,512]{2,1,0:T(8,128)(2,1)} %bitcast.71), calls=%async_computation.1 | async-start | bytes 2621440 | tf_op jit(solution)/shard_map/all_to_all | solution.py:970
  94.1 2.3 collective-permute-done.26.refs_3_
  103.7 7.7 %take_body.9 = bf16[2048,512]{1,0:T(8,128)(2,1)S(1)} custom-call(s32[1]{0:T(128)} %constant.192.clone.1.base_ref, s32[2048,8]{1,0:T(8,128)S(1)} %get-tuple-element.473.pos_ref, bf16[640,512]{1,0:T(8,128)(2,1)} %get-tuple-element.409.refs_0_, bf16[640,512]{1,0:T(8,128)(2,1)} %collective-permute-done.24.refs_1_, ...), custom_call_target="tpu_custom_call" | custom-call | flops 1000000 | bytes 1000 | tf_op jit(solution)/shard_map/take_body/pallas_call | solution.py:992
  117.9 8.5 %all-to-all-done.1 = bf16[32,40,512]{2,1,0:T(8,128)(2,1)} async-done(((bf16[32,40,512]{2,1,0:T(8,128)(2,1)}), bf16[32,40,512]{2,1,0:T(8,128)(2,1)}, u32[]{:S(2)}, u32[]{:S(2)}) %all-to-all-start.1) | async-done | bytes 1310752 | tf_op jit(solution)/shard_map/all_to_all | solution.py:970
  126.4 18.8 %expert_body.1 = (bf16[1280,2048]{1,0:T(8,128)(2,1)}, bf16[1280,2048]{1,0:T(8,128)(2,1)}, bf16[1280,512]{1,0:T(8,128)(2,1)}, bf16[1280,512]{1,0:T(8,128)(2,1)}, ...) custom-call(s32[1]{0:T(128)} %bitcast.7.expert_ref, bf16[1280,512]{1,0:T(8,128)(2,1)} %bitcast.15.got_ref, ...), custom_call_target="tpu_custom_call" | custom-call | flops 21849999360 | bytes 1000000 | tf_op jit(solution)/shard_map/expert_body/pallas_call | solution.py:1045
  145.2 3.6 %all-to-all-start.2 = ((bf16[32,40,512]{2,1,0:T(8,128)(2,1)}), bf16[32,40,512]{2,1,0:T(8,128)(2,1)}, u32[]{:S(2)}, u32[]{:S(2)}) async-start(bf16[32,40,512]{2,1,0:T(8,128)(2,1)} %bitcast.73), calls=%async_computation.2 | async-start | bytes 2621440 | tf_op jit(solution)/shard_map/all_to_all | solution.py:970
  148.8 11.7 %weight_grad_body.1 = (bf16[1024,512]{1,0:T(8,128)(2,1)}, bf16[1024,512]{1,0:T(8,128)(2,1)}, f32[1024,512]{1,0:T(8,128)}, f32[1024,512]{1,0:T(8,128)}) custom-call(bf16[1280,2048]{1,0:T(8,128)(2,1)} %get-tuple-element.424.hidden_ref, bf16[1280,2048]{1,0:T(8,128)(2,1)} %get-tuple-element.425.active_ref, bf16[1280,512]{1,0:T(8,128)(2,1)} %bitcast.15.got_ref, ...), custom_call_target="tpu_custom_call" | custom-call | flops 11500000256 | bytes 1000000 | tf_op jit(solution)/shard_map/weight_grad_body/pallas_call | solution.py:1064
  164.9 6.7 %sum_put_body.7 = (bf16[640,512]{1,0:T(8,128)(2,1)}, bf16[640,512]{1,0:T(8,128)(2,1)}) custom-call(s32[1]{0:T(128)} %constant.192.clone.1.base_ref, s32[8,2048]{1,0:T(8,128)S(1)} %get-tuple-element.822, f32[1024,512]{1,0:T(8,128)} %get-tuple-element.762.refs_0_, f32[1024,512]{1,0:T(8,128)} %get-tuple-element.763.refs_1_, ...), custom_call_target="tpu_custom_call" | custom-call | flops 4600000000 | bytes 1000000 | tf_op jit(solution)/shard_map/sum_put_body/pallas_call | solution.py:992
  173.2 5.3 %sum_put_body.6 = (bf16[640,512]{1,0:T(8,128)(2,1)}, bf16[640,512]{1,0:T(8,128)(2,1)}) custom-call(s32[1]{0:T(128)} %constant.192.clone.1.base_ref, s32[8,2048]{1,0:T(8,128)S(1)} %get-tuple-element.822, f32[1024,512]{1,0:T(8,128)S(1)} %copy-done.33, f32[1024,512]{1,0:T(8,128)S(1)} %copy-done.34, bf16[1024,512]{1,0:T(8,128)(2,1)} %collective-permute-done.31.refs_2_, ...), custom_call_target="tpu_custom_call" | custom-call | flops 4600000000 | bytes 1000000 | tf_op jit(solution)/shard_map/sum_put_body/pallas_call | solution.py:992
  180.9 5.8 %middle_body.1 = (f32[512,512]{1,0:T(8,128)}, bf16[512,512]{1,0:T(8,128)(2,1)}, f32[512,128]{1,0:T(8,128)}, f32[8,512]{1,0:T(8,128)}, f32[8,512]{1,0:T(8,128)}) custom-call(bf16[1280,512]{1,0:T(8,128)(2,1)} %bitcast.22.back_ref, s32[512,8]{1,0:T(8,128)} %get-tuple-element.433.pos_ref, f32[512,512]{1,0:T(8,128)} %get-tuple-element.434.residual_ref, ...), custom_call_target="tpu_custom_call" | custom-call | flops 6899999744 | bytes 1000000 | tf_op jit(solution)/shard_map/middle_body/pallas_call | solution.py:1079
  189.5 14.5 %inner_body.1 = (bf16[512,512]{1,0:T(8,128)(2,1)}, f32[2,512,512]{2,1,0:T(8,128)}, bf16[544,512]{1,0:T(8,128)(2,1)}) custom-call(bf16[1024,1536]{1,0:T(8,128)(2,1)} %get-tuple-element.422.qkv_ref, bf16[512,512]{1,0:T(8,128)(2,1)} %get-tuple-element.436.out_grad_ref, f32[512,128]{1,0:T(8,128)} %get-tuple-element.437.lse_ref, ...), custom_call_target="tpu_custom_call" | custom-call | flops 17250000896 | bytes 1000000 | tf_op jit(solution)/shard_map/inner_body/pallas_call | solution.py:1090
  204.0 5.3 %collective-permute-done.35.refs_2_ = bf16[640,512]{1,0:T(8,128)(2,1)} collective-permute-done((bf16[640,512]{1,0:T(8,128)(2,1)}, bf16[640,512]{1,0:T(8,128)(2,1)}, u32[]{:S(2)}, u32[]{:S(2)}) %collective-permute-start.35) | collective-permute-done | bytes 655392 | tf_op jit(solution)/shard_map/ppermute | solution.py:870
  209.3 8.0 %collective-permute-done.33.out_grad_ref = bf16[512,512]{1,0:T(8,128)(2,1)S(1)} collective-permute-done((bf16[512,512]{1,0:T(8,128)(2,1)}, bf16[512,512]{1,0:T(8,128)(2,1)S(1)}, u32[]{:S(2)}, u32[]{:S(2)}) %collective-permute-start.33) | collective-permute-done | bytes 524320 | tf_op jit(solution)/shard_map/ppermute | solution.py:866
  218.3 12.5 %outer_body.1 = (bf16[2096,512]{1,0:T(8,128)(2,1)}, f32[512,512]{1,0:T(8,128)}) custom-call(bf16[1024,1536]{1,0:T(8,128)(2,1)} %get-tuple-element.422.qkv_ref, bf16[512,512]{1,0:T(8,128)(2,1)} %copy-done.21, f32[16,512]{1,0:T(8,128)} %copy-done.27, f32[512,1]{1,0:T(8,128)} %copy.35.keep_ref, bf16[512,512]{1,0:T(8,128)(2,1)} %get-tuple-element.442.query_ref, ...), custom_call_target="tpu_custom_call" | custom-call | flops 1000000 | bytes 1000 | tf_op jit(solution)/shard_map/outer_body/pallas_call | solution.py:1096
  230.9 4.0 %all-to-all-start.3 = ((bf16[32,40,512]{2,1,0:T(8,128)(2,1)}), bf16[32,40,512]{2,1,0:T(8,128)(2,1)}, u32[]{:S(2)}, u32[]{:S(2)}) async-start(bf16[32,40,512]{2,1,0:T(8,128)(2,1)} %bitcast.70), calls=%async_computation.3 | async-start | bytes 2621440 | tf_op jit(solution)/shard_map/all_to_all | solution.py:970
  237.5 5.8 %spread_body.2 = (bf16[544,512]{1,0:T(8,128)(2,1)}, bf16[544,512]{1,0:T(8,128)(2,1)}) custom-call(s32[1,2096]{1,0:T(1,128)} %broadcast_in_dim.33.pos_ref, bf16[2096,512]{1,0:T(8,128)(2,1)} %get-tuple-element.453.mine_ref, bf16[2096,512]{1,0:T(8,128)(2,1)} %collective-permute-done.38.far_ref), custom_call_target="tpu_custom_call" | custom-call | flops 1000000 | bytes 1000 | tf_op jit(solution)/shard_map/spread_body/pallas_call | solution.py:1110
  246.5 5.9 %spread_body.3 = (bf16[544,512]{1,0:T(8,128)(2,1)}, bf16[544,512]{1,0:T(8,128)(2,1)}) custom-call(s32[1,2096]{1,0:T(1,128)} %broadcast_in_dim.33.pos_ref, bf16[2096,512]{1,0:T(8,128)(2,1)} %get-tuple-element.453.mine_ref, bf16[2096,512]{1,0:T(8,128)(2,1)} %collective-permute-done.38.far_ref), custom_call_target="tpu_custom_call" | custom-call | flops 1000000 | bytes 1000 | tf_op jit(solution)/shard_map/spread_body/pallas_call | solution.py:1110
  257.7 4.0 %tokens_body.1 = f32[512,512]{1,0:T(8,128)} custom-call(f32[512,512]{1,0:T(8,128)} %get-tuple-element.459.grad_normed_ref, bf16[512,512]{1,0:T(8,128)(2,1)} %bitcast.69, bf16[2080,512]{1,0:T(8,128)(2,1)} %unpack_body.3.w_ref, f32[512,512]{1,0:T(8,128)} %get-tuple-element.439.grad_ref), custom_call_target="tpu_custom_call" | custom-call | flops 1000000 | bytes 1000 | tf_op jit(solution)/shard_map/tokens_body/pallas_call | solution.py:1118
  272.0 8.7 %adam_body.2 = (f32[2048,512]{1,0:T(8,128)}, f32[2048,512]{1,0:T(8,128)}, f32[2048,512]{1,0:T(8,128)}, f32[2048,512]{1,0:T(8,128)}) custom-call(s32[2048,8]{1,0:T(8,128)S(1)} %get-tuple-element.808, bf16[640,512]{1,0:T(8,128)(2,1)} %get-tuple-element.464.refs_0_, bf16[640,512]{1,0:T(8,128)(2,1)} %collective-permute-done.34.refs_1_, ...), custom_call_target="tpu_custom_call" | custom-call | flops 1000000 | bytes 1000 | tf_op jit(solution)/shard_map/adam_body/pallas_call | solution.py:1129
  282.8 3.8 %collective-permute-start.47 = (bf16[136,512]{1,0:T(8,128)(2,1)}, bf16[136,512]{1,0:T(8,128)(2,1)}, u32[]{:S(2)}, u32[]{:S(2)}) collective-permute-start(bf16[136,512]{1,0:T(8,128)(2,1)} %get-tuple-element.547), channel_id=1, source_target_pairs={{0,1},{1,2},{2,3},{3,0},{4,5},{5,6},{6,7},{7,4},{8,9},{9,10},{10,1... | collective-permute-start | bytes 417800 | tf_op jit(solution)/shard_map/ppermute | solution.py:883
  290.4 4.2 %mixture_body.1 = bf16[512,512]{1,0:T(8,128)(2,1)} custom-call(bf16[1280,512]{1,0:T(8,128)(2,1)} %bitcast.25.result_ref, s32[512,8]{1,0:T(8,128)} %get-tuple-element.433.pos_ref, s32[512,2]{1,0:T(8,128)} %bitcast.65, f32[512,16]{1,0:T(8,128)} %get-tuple-element.472.prob_ref, f32[512,512]{1,0:T(8,128)} %get-tuple-element.434.residual_ref), custom_call_target="tpu_custom_call" | custom-call | flops 1000000 | bytes 1000 | tf_op jit(solution)/shard_map/mixture_body/pallas_call | solution.py:1149
  294.7 9.4 %adam_body.3 = (f32[2048,512]{1,0:T(8,128)}, f32[2048,512]{1,0:T(8,128)}, f32[2048,512]{1,0:T(8,128)}, f32[2048,512]{1,0:T(8,128)}) custom-call(s32[2048,8]{1,0:T(8,128)S(1)} %get-tuple-element.808, bf16[640,512]{1,0:T(8,128)(2,1)} %get-tuple-element.464.refs_0_, ...), custom_call_target="tpu_custom_call", output_to_operand_aliasing={{0}: (10, {}), {1}: (11, {}), {2}: (12, {}), {3}: (13, {})} | custom-call | flops 1000000 | bytes 1000 | tf_op jit(solution)/shard_map/adam_body/pallas_call | solution.py:1129
  (177 shorter events, 82.2 us)
Async XLA Ops:
  1.6 9.9 %collective-permute-start.12 = (bf16[136,512]{1,0:T(8,128)(2,1)S(1)}, bf16[136,512]{1,0:T(8,128)(2,1)S(1)}, u32[]{:S(2)}, u32[]{:S(2)}) collective-permute-start(bf16[136,512]{1,0:T(8,128)(2,1)S(1)} %pad.8), channel_id=1, source_target_pairs={{0,1},{1,2},{2,3},{3,0},{4,5},{5,6},{6,7},{7,4},{8,9},{9,10},{10,1... | collective-permute-start | bytes 417800 | tf_op jit(solution)/shard_map/ppermute | solution.py:883
  4.7 11.8 %collective-permute-start.14 = (bf16[136,512]{1,0:T(8,128)(2,1)S(1)}, bf16[136,512]{1,0:T(8,128)(2,1)S(1)}, u32[]{:S(2)}, u32[]{:S(2)}) collective-permute-start(bf16[136,512]{1,0:T(8,128)(2,1)S(1)} %pad.8), channel_id=1, source_target_pairs={{0,2},{1,3},{2,0},{3,1},{4,6},{5,7},{6,4},{7,5},{8,10},{9,11},{10,... | collective-permute-start | bytes 417800 | tf_op jit(solution)/shard_map/ppermute | solution.py:883
  8.6 21.4 %collective-permute-start.11 = (bf16[512,512]{1,0:T(8,128)(2,1)}, bf16[512,512]{1,0:T(8,128)(2,1)S(1)}, u32[]{:S(2)}, u32[]{:S(2)}) collective-permute-start(bf16[512,512]{1,0:T(8,128)(2,1)} %bitcast.66), channel_id=1, source_target_pairs={{0,4},{4,0},{1,5},{5,1},{2,6},{6,2},{3,7},{7,3},{8,12},{12,8},{9,1... | collective-permute-start | bytes 1572872 | tf_op jit(solution)/shard_map/ppermute | solution.py:866
  10.9 14.6 %collective-permute-start.17 = (s32[1,512]{1,0:T(1,128)}, s32[1,512]{1,0:T(1,128)S(1)}, u32[]{:S(2)}, u32[]{:S(2)}) collective-permute-start(s32[1,512]{1,0:T(1,128)} %param.19), channel_id=1, source_target_pairs={{0,4},{4,0},{1,5},{5,1},{2,6},{6,2},{3,7},{7,3},{8,12},{12,8},{9,1... | collective-permute-start | bytes 6152 | tf_op jit(solution)/shard_map/ppermute | solution.py:866
  11.5 14.6 %collective-permute-start.13 = (bf16[272,512]{1,0:T(8,128)(2,1)S(1)}, bf16[272,512]{1,0:T(8,128)(2,1)S(1)}, u32[]{:S(2)}, u32[]{:S(2)}) collective-permute-start(bf16[272,512]{1,0:T(8,128)(2,1)S(1)} %pad_maximum_fusion.9), channel_id=1, source_target_pairs={{0,16},{16,0},{8,24},{24,8},{1,17},{17,1},{9,25},{25,9},{2,18},{18... | collective-permute-start | bytes 835592 | tf_op jit(solution)/shard_map/ppermute | solution.py:870
  27.0 26.4 %collective-permute-start.18 = (bf16[544,512]{1,0:T(8,128)(2,1)}, bf16[544,512]{1,0:T(8,128)(2,1)}, u32[]{:S(2)}, u32[]{:S(2)}) collective-permute-start(bf16[544,512]{1,0:T(8,128)(2,1)} %pad_maximum_fusion.8.refs_0_), channel_id=1, source_target_pairs={{0,4},{4,0},{1,5},{5,1},{2,6},{6,2},{3,7},{7,3},{8,12},{12,8},{9,1... | collective-permute-start | bytes 1671176 | tf_op jit(solution)/shard_map/ppermute | solution.py:866
  27.5 16.6 %collective-permute-start.20 = (bf16[544,512]{1,0:T(8,128)(2,1)}, bf16[544,512]{1,0:T(8,128)(2,1)}, u32[]{:S(2)}, u32[]{:S(2)}) collective-permute-start(bf16[544,512]{1,0:T(8,128)(2,1)} %pad_maximum_fusion.8.refs_0_), channel_id=1, source_target_pairs={{0,8},{8,0},{16,24},{24,16},{1,9},{9,1},{17,25},{25,17},{2,10},{10... | collective-permute-start | bytes 1671176 | tf_op jit(solution)/shard_map/ppermute | solution.py:878
  28.4 24.9 %collective-permute-start.19 = (bf16[544,512]{1,0:T(8,128)(2,1)}, bf16[544,512]{1,0:T(8,128)(2,1)}, u32[]{:S(2)}, u32[]{:S(2)}) collective-permute-start(bf16[544,512]{1,0:T(8,128)(2,1)} %constant_dynamic-update-slice_fusion.2.refs_1_), channel_id=1, source_target_pairs={{0,16},{16,0},{8,24},{24,8},{1,17},{17,1},{9,25},{25,9},{2,18},{18... | collective-permute-start | bytes 1671176 | tf_op jit(solution)/shard_map/ppermute | solution.py:870
  29.9 14.2 %collective-permute-start.21 = (bf16[544,512]{1,0:T(8,128)(2,1)}, bf16[544,512]{1,0:T(8,128)(2,1)}, u32[]{:S(2)}, u32[]{:S(2)}) collective-permute-start(bf16[544,512]{1,0:T(8,128)(2,1)} %constant_dynamic-update-slice_fusion.2.refs_1_), channel_id=1, source_target_pairs={{0,8},{8,0},{16,24},{24,16},{1,9},{9,1},{17,25},{25,17},{2,10},{10... | collective-permute-start | bytes 1671176 | tf_op jit(solution)/shard_map/ppermute | solution.py:878
  34.3 40.7 %all-to-all-start = ((bf16[32,40,512]{2,1,0:T(8,128)(2,1)}), bf16[32,40,512]{2,1,0:T(8,128)(2,1)}, u32[]{:S(2)}, u32[]{:S(2)}) async-start(bf16[32,40,512]{2,1,0:T(8,128)(2,1)} %bitcast.72), calls=%async_computation | async-start | bytes 2621440 | tf_op jit(solution)/shard_map/all_to_all | solution.py:970
  53.3 10.7 %collective-permute-start.22 = (bf16[544,512]{1,0:T(8,128)(2,1)}, bf16[544,512]{1,0:T(8,128)(2,1)S(1)}, u32[]{:S(2)}, u32[]{:S(2)}) collective-permute-start(bf16[544,512]{1,0:T(8,128)(2,1)} %collective-permute-done.18.refs_0_), channel_id=1, source_target_pairs={{0,8},{8,0},{16,24},{24,16},{1,9},{9,1},{17,25},{25,17},{2,10},{10... | collective-permute-start | bytes 1671176 | tf_op jit(solution)/shard_map/ppermute | solution.py:878
  53.8 10.3 %collective-permute-start.23 = (bf16[544,512]{1,0:T(8,128)(2,1)}, bf16[544,512]{1,0:T(8,128)(2,1)S(1)}, u32[]{:S(2)}, u32[]{:S(2)}) collective-permute-start(bf16[544,512]{1,0:T(8,128)(2,1)} %collective-permute-done.19.refs_1_), channel_id=1, source_target_pairs={{0,8},{8,0},{16,24},{24,16},{1,9},{9,1},{17,25},{25,17},{2,10},{10... | collective-permute-start | bytes 1671176 | tf_op jit(solution)/shard_map/ppermute | solution.py:878
  60.5 33.5 %collective-permute-start.24 = (bf16[640,512]{1,0:T(8,128)(2,1)}, bf16[640,512]{1,0:T(8,128)(2,1)}, u32[]{:S(2)}, u32[]{:S(2)}) collective-permute-start(bf16[640,512]{1,0:T(8,128)(2,1)} %get-tuple-element.406), channel_id=1, source_target_pairs={{0,4},{4,0},{1,5},{5,1},{2,6},{6,2},{3,7},{7,3},{8,12},{12,8},{9,1... | collective-permute-start | bytes 1966088 | tf_op jit(solution)/shard_map/ppermute | solution.py:866
  62.4 31.6 %collective-permute-start.25 = (bf16[640,512]{1,0:T(8,128)(2,1)}, bf16[640,512]{1,0:T(8,128)(2,1)}, u32[]{:S(2)}, u32[]{:S(2)}) collective-permute-start(bf16[640,512]{1,0:T(8,128)(2,1)} %get-tuple-element.407), channel_id=1, source_target_pairs={{0,16},{16,0},{8,24},{24,8},{1,17},{17,1},{9,25},{25,9},{2,18},{18... | collective-permute-start | bytes 1966088 | tf_op jit(solution)/shard_map/ppermute | solution.py:870
  63.9 32.5 %collective-permute-start.26 = (bf16[640,512]{1,0:T(8,128)(2,1)}, bf16[640,512]{1,0:T(8,128)(2,1)}, u32[]{:S(2)}, u32[]{:S(2)}) collective-permute-start(bf16[640,512]{1,0:T(8,128)(2,1)} %get-tuple-element.408), channel_id=1, source_target_pairs={{0,20},{4,16},{8,28},{12,24},{16,4},{20,0},{24,12},{28,8},{1,21},{... | collective-permute-start | bytes 1966088 | tf_op jit(solution)/shard_map/ppermute | solution.py:874
  87.6 38.8 %all-to-all-start.1 = ((bf16[32,40,512]{2,1,0:T(8,128)(2,1)}), bf16[32,40,512]{2,1,0:T(8,128)(2,1)}, u32[]{:S(2)}, u32[]{:S(2)}) async-start(bf16[32,40,512]{2,1,0:T(8,128)(2,1)} %bitcast.71), calls=%async_computation.1 | async-start | bytes 2621440 | tf_op jit(solution)/shard_map/all_to_all | solution.py:970
  145.2 35.7 %all-to-all-start.2 = ((bf16[32,40,512]{2,1,0:T(8,128)(2,1)}), bf16[32,40,512]{2,1,0:T(8,128)(2,1)}, u32[]{:S(2)}, u32[]{:S(2)}) async-start(bf16[32,40,512]{2,1,0:T(8,128)(2,1)} %bitcast.73), calls=%async_computation.2 | async-start | bytes 2621440 | tf_op jit(solution)/shard_map/all_to_all | solution.py:970
  171.6 32.4 %collective-permute-start.34 = (bf16[640,512]{1,0:T(8,128)(2,1)}, bf16[640,512]{1,0:T(8,128)(2,1)}, u32[]{:S(2)}, u32[]{:S(2)}) collective-permute-start(bf16[640,512]{1,0:T(8,128)(2,1)} %get-tuple-element.444), channel_id=1, source_target_pairs={{0,4},{4,0},{1,5},{5,1},{2,6},{6,2},{3,7},{7,3},{8,12},{12,8},{9,1... | collective-permute-start | bytes 1966088 | tf_op jit(solution)/shard_map/ppermute | solution.py:866
  178.5 30.9 %collective-permute-start.35 = (bf16[640,512]{1,0:T(8,128)(2,1)}, bf16[640,512]{1,0:T(8,128)(2,1)}, u32[]{:S(2)}, u32[]{:S(2)}) collective-permute-start(bf16[640,512]{1,0:T(8,128)(2,1)} %get-tuple-element.445), channel_id=1, source_target_pairs={{0,16},{16,0},{8,24},{24,8},{1,17},{17,1},{9,25},{25,9},{2,18},{18... | collective-permute-start | bytes 1966088 | tf_op jit(solution)/shard_map/ppermute | solution.py:870
  180.0 29.4 %collective-permute-start.36 = (bf16[640,512]{1,0:T(8,128)(2,1)}, bf16[640,512]{1,0:T(8,128)(2,1)}, u32[]{:S(2)}, u32[]{:S(2)}) collective-permute-start(bf16[640,512]{1,0:T(8,128)(2,1)} %get-tuple-element.446), channel_id=1, source_target_pairs={{0,20},{4,16},{8,28},{12,24},{16,4},{20,0},{24,12},{28,8},{1,21},{... | collective-permute-start | bytes 1966088 | tf_op jit(solution)/shard_map/ppermute | solution.py:874
  186.7 30.6 %collective-permute-start.33 = (bf16[512,512]{1,0:T(8,128)(2,1)}, bf16[512,512]{1,0:T(8,128)(2,1)S(1)}, u32[]{:S(2)}, u32[]{:S(2)}) collective-permute-start(bf16[512,512]{1,0:T(8,128)(2,1)} %get-tuple-element.436.out_grad_ref), channel_id=1, source_target_pairs={{0,4},{4,0},{1,5},{5,1},{2,6},{6,2},{3,7},{7,3},{8,12},{12,8},{9,1... | collective-permute-start | bytes 1572872 | tf_op jit(solution)/shard_map/ppermute | solution.py:866
  188.5 29.2 %collective-permute-start.37 = (f32[16,512]{1,0:T(8,128)S(1)}, f32[16,512]{1,0:T(8,128)S(1)}, u32[]{:S(2)}, u32[]{:S(2)}) collective-permute-start(f32[16,512]{1,0:T(8,128)S(1)} %pad_maximum_fusion.10), channel_id=1, source_target_pairs={{0,4},{4,0},{1,5},{5,1},{2,6},{6,2},{3,7},{7,3},{8,12},{12,8},{9,1... | collective-permute-start | bytes 98312 | tf_op jit(solution)/shard_map/ppermute | solution.py:866
  230.9 59.5 %all-to-all-start.3 = ((bf16[32,40,512]{2,1,0:T(8,128)(2,1)}), bf16[32,40,512]{2,1,0:T(8,128)(2,1)}, u32[]{:S(2)}, u32[]{:S(2)}) async-start(bf16[32,40,512]{2,1,0:T(8,128)(2,1)} %bitcast.70), calls=%async_computation.3 | async-start | bytes 2621440 | tf_op jit(solution)/shard_map/all_to_all | solution.py:970
  243.3 20.0 %collective-permute-start.39 = (bf16[544,512]{1,0:T(8,128)(2,1)}, bf16[544,512]{1,0:T(8,128)(2,1)}, u32[]{:S(2)}, u32[]{:S(2)}) collective-permute-start(bf16[544,512]{1,0:T(8,128)(2,1)} %get-tuple-element.454), channel_id=1, source_target_pairs={{0,4},{4,0},{1,5},{5,1},{2,6},{6,2},{3,7},{7,3},{8,12},{12,8},{9,1... | collective-permute-start | bytes 1671176 | tf_op jit(solution)/shard_map/ppermute | solution.py:866
  245.0 20.2 %collective-permute-start.40 = (bf16[544,512]{1,0:T(8,128)(2,1)}, bf16[544,512]{1,0:T(8,128)(2,1)}, u32[]{:S(2)}, u32[]{:S(2)}) collective-permute-start(bf16[544,512]{1,0:T(8,128)(2,1)} %get-tuple-element.455), channel_id=1, source_target_pairs={{0,16},{16,0},{8,24},{24,8},{1,17},{17,1},{9,25},{25,9},{2,18},{18... | collective-permute-start | bytes 1671176 | tf_op jit(solution)/shard_map/ppermute | solution.py:870
  254.3 16.8 %collective-permute-start.43 = (bf16[640,512]{1,0:T(8,128)(2,1)}, bf16[640,512]{1,0:T(8,128)(2,1)S(1)}, u32[]{:S(2)}, u32[]{:S(2)}) collective-permute-start(bf16[640,512]{1,0:T(8,128)(2,1)} %pad_maximum_fusion.6), channel_id=1, source_target_pairs={{0,8},{8,0},{16,24},{24,16},{1,9},{9,1},{17,25},{25,17},{2,10},{10... | collective-permute-start | bytes 1966088 | tf_op jit(solution)/shard_map/ppermute | solution.py:878
  257.2 13.9 %collective-permute-start.44 = (bf16[640,512]{1,0:T(8,128)(2,1)}, bf16[640,512]{1,0:T(8,128)(2,1)}, u32[]{:S(2)}, u32[]{:S(2)}) collective-permute-start(bf16[640,512]{1,0:T(8,128)(2,1)} %pad_maximum_fusion.7), channel_id=1, source_target_pairs={{0,8},{8,0},{16,24},{24,16},{1,9},{9,1},{17,25},{25,17},{2,10},{10... | collective-permute-start | bytes 1966088 | tf_op jit(solution)/shard_map/ppermute | solution.py:878
  267.4 13.3 %collective-permute-start.41 = (bf16[272,512]{1,0:T(8,128)(2,1)}, bf16[272,512]{1,0:T(8,128)(2,1)}, u32[]{:S(2)}, u32[]{:S(2)}) collective-permute-start(bf16[272,512]{1,0:T(8,128)(2,1)} %slice.176), channel_id=1, source_target_pairs={{0,16},{16,0},{8,24},{24,8},{1,17},{17,1},{9,25},{25,9},{2,18},{18... | collective-permute-start | bytes 835592 | tf_op jit(solution)/shard_map/ppermute | solution.py:870
  270.4 10.3 %collective-permute-start.42 = (bf16[272,512]{1,0:T(8,128)(2,1)}, bf16[272,512]{1,0:T(8,128)(2,1)}, u32[]{:S(2)}, u32[]{:S(2)}) collective-permute-start(bf16[272,512]{1,0:T(8,128)(2,1)} %slice.177), channel_id=1, source_target_pairs={{0,4},{4,0},{1,5},{5,1},{2,6},{6,2},{3,7},{7,3},{8,12},{12,8},{9,1... | collective-permute-start | bytes 835592 | tf_op jit(solution)/shard_map/ppermute | solution.py:866
  282.8 21.3 %collective-permute-start.47 = (bf16[136,512]{1,0:T(8,128)(2,1)}, bf16[136,512]{1,0:T(8,128)(2,1)}, u32[]{:S(2)}, u32[]{:S(2)}) collective-permute-start(bf16[136,512]{1,0:T(8,128)(2,1)} %get-tuple-element.547), channel_id=1, source_target_pairs={{0,1},{1,2},{2,3},{3,0},{4,5},{5,6},{6,7},{7,4},{8,9},{9,10},{10,1... | collective-permute-start | bytes 417800 | tf_op jit(solution)/shard_map/ppermute | solution.py:883
  287.3 16.8 %collective-permute-start.46 = (bf16[136,512]{1,0:T(8,128)(2,1)}, bf16[136,512]{1,0:T(8,128)(2,1)}, u32[]{:S(2)}, u32[]{:S(2)}) collective-permute-start(bf16[136,512]{1,0:T(8,128)(2,1)} %get-tuple-element.548), channel_id=1, source_target_pairs={{0,2},{1,3},{2,0},{3,1},{4,6},{5,7},{6,4},{7,5},{8,10},{9,11},{10,... | collective-permute-start | bytes 417800 | tf_op jit(solution)/shard_map/ppermute | solution.py:883
  288.9 15.2 %collective-permute-start.45 = (bf16[136,512]{1,0:T(8,128)(2,1)}, bf16[136,512]{1,0:T(8,128)(2,1)}, u32[]{:S(2)}, u32[]{:S(2)}) collective-permute-start(bf16[136,512]{1,0:T(8,128)(2,1)} %get-tuple-element.549), channel_id=1, source_target_pairs={{0,3},{1,0},{2,1},{3,2},{4,7},{5,4},{6,5},{7,6},{8,11},{9,8},{10,9... | collective-permute-start | bytes 417800 | tf_op jit(solution)/shard_map/ppermute | solution.py:883
  (36 other events, 219.4 us)

commit v4 on v3

--- a/solution.py
+++ b/solution.py
@@ -391,7 +391,7 @@
 
 
 def kernel_call(
-    body, out_shape, scratch=(), grid=None, in_specs=None, out_specs=None, cost=None, aliases=None
+    body, out_shape, scratch=(), grid=None, in_specs=None, out_specs=None, cost=None
 ):
     given = dict(grid=grid, in_specs=in_specs, out_specs=out_specs)
     extra = {name: value for name, value in given.items() if value is not None}
@@ -402,7 +402,6 @@
         name=name,
         out_shape=out_shape,
         scratch_shapes=list(scratch),
-        input_output_aliases=aliases or {},
         compiler_params=pltpu.CompilerParams(vmem_limit_bytes=VMEM_LIMIT),
         cost_estimate=pl.CostEstimate(flops=int(flops), bytes_accessed=int(moved), transcendentals=0),
         **extra,
@@ -677,7 +676,7 @@
 
 def outer_body(
     n_exp, qkv_ref, out_grad_ref, sums_ref, keep_ref, query_ref, kv_ref, normed_ref, own_ref, w_ref, early_ref,
-    pieces_ref, grad_normed_ref, held,
+    query_rows_ref, key_rows_ref, value_rows_ref, rest_ref, grad_normed_ref, held,
 ):
     toks, width = query_ref.shape
     held[:, 0:width] = query_ref[...]
@@ -698,14 +697,22 @@
         for number in range(2):
             total = kv_ref[number, :, at : at + LANES] + by_head(made[0][number], made[1][number])
             held[:, (number + 1) * width + at : (number + 1) * width + at + LANES] = total.astype(BF16)
-    pieces_ref[0 : 3 * width, :] = dot_tn(held[...], normed_ref[...]).astype(BF16)
+    for third, ref in enumerate((query_rows_ref, key_rows_ref, value_rows_ref)):
+        ref[...] = dot_tn(held[:, third * width : (third + 1) * width], normed_ref[...]).astype(BF16)
     grad_normed = dot_nn(held[...], w_ref[0 : 3 * width, :])
     grad_normed_ref[...] = grad_normed
     gain_grad = jnp.sum(grad_normed * normalize(own_ref[...].astype(F32))[0], axis=0, keepdims=True)
-    pieces_ref[3 * width : 3 * width + 16, :] = jnp.where(
+    rest_ref[0:16, :] = jnp.where(
         iota((16, width), 0) == 0, gain_grad, 0.0
     ).astype(BF16)
-    pieces_ref[3 * width + 16 :, :] = early_ref[...]
+    rest_ref[16:, :] = early_ref[...]
+
+
+def step_body(keep_a, got_a, keep_b, got_b, go_a, go_b, stay_a, stay_b):
+    half = go_a.shape[0]
+    for keep, got, go, stay in ((keep_a, got_a, go_a, stay_a), (keep_b, got_b, go_b, stay_b)):
+        go[...] = total_f32(keep[half:, :], got[half:, :]).astype(BF16)
+        stay[...] = total_f32(keep[:half, :], got[:half, :]).astype(BF16)
 
 
 def tokens_body(n_exp, grad_normed_ref, own_ref, w_ref, grad_ref, out_ref):
@@ -715,9 +722,12 @@
     out_ref[...] = grad_ref[...] + norm_back(hat, scale, gain_one, grad_normed_ref[...])
 
 
-def spread_body(starts, pos_ref, mine_ref, far_ref, *outs):
-    held, outs = outs[-1], outs[:-1]
-    held[...] = total_f32(mine_ref[...], far_ref[...]).astype(BF16)
+def spread_body(starts, n_in, pos_ref, *refs):
+    mine, far, outs, held = refs[:n_in], refs[n_in : 2 * n_in], refs[2 * n_in : -1], refs[-1]
+    at = 0
+    for one, two in zip(mine, far):
+        held[at : at + one.shape[0], :] = total_f32(one[...], two[...]).astype(BF16)
+        at += one.shape[0]
     size = outs[0].shape[0]
     for number, start in enumerate(starts):
         picks = as_bf16(iota((size, held.shape[0]), 0) + start == pos_ref[...])
@@ -829,9 +839,9 @@
         out[at : at + tile, :] = dot_nn(picks, held[...]).astype(BF16)
 
 
-def adam_body(n_in, n_made, pos_ref, *refs):
+def adam_body(n_in, pos_ref, *refs):
     pieces, (first_ref, second_ref, weight_ref) = refs[:n_in], refs[n_in : n_in + 3]
-    grad_ref, first_new, second_new, weight_new, held = refs[n_in + 3 + n_made :]
+    grad_ref, first_new, second_new, weight_new, held = refs[n_in + 3 :]
 
     @pl.when(pl.program_id(0) == 0)
     def _():
@@ -934,7 +944,7 @@
 
     half_slots = total_slots // 2
     piece = half_slots // 4
-    row_tile = row_count // 5 if row_count % 80 == 0 else row_count
+    row_tile = row_count // 2 if row_count % 32 == 0 else row_count
 
     def unpack(spots, pieces, earlier):
         rows_of = lambda columns: pl.BlockSpec((row_tile, columns), lambda i: (i, 0))
@@ -993,8 +1003,9 @@
             body, out_shape, scratch, in_specs=[smem] + [vmem] * len(arrays), cost=cost
         )(base, *arrays)
 
-    def over_links(pieces):
-        return [pieces[0], swap_x(pieces[1]), swap_y(pieces[2]), swap_x_y(pieces[3])]
+    def over_links(pieces, *others):
+        last = after(pieces[3:], *others)[0] if others else pieces[3]
+        return [pieces[0], swap_x(pieces[1]), swap_y(pieces[2]), swap_x_y(last)]
 
     def over_cores(got):
         far = [jnp.concatenate([got[at][room:], got[at + 1][room:]], axis=0) for at in (0, 2)]
@@ -1074,7 +1085,7 @@
     moved_x, moved_xy = returning((1, 3))
     moved_0, moved_y = returning((0, 2))
     moved = [moved_0, moved_x, moved_y, moved_xy]
-    back_got = after([back_got], moved[0])[0]
+    back_got = after([back_got], *moved)[0]
 
     grad_residual, out_grad, delta_col, delta_row, gain_two = kernel_call(
         functools.partial(middle_body, n_exp),
@@ -1086,73 +1097,66 @@
     )(back_got, pos_col, residual, cotangent[0], keep_col, attended, weights)
     out_grad_other = swap_x(out_grad)
     sums_other = swap_x(jnp.concatenate([lse_row, delta_row], axis=0))
-    moved = over_links(moved)
     query_grad, kv_grad, early = kernel_call(
         functools.partial(inner_body, n_exp),
         (sds((toks, width), BF16), sds((2, toks, width), F32), sds((width + n_exp + 16, width), BF16)),
         cost=(15 * MICRO, 1e6),
     )(qkv, out_grad, lse_col, delta_col, keep_row, attended, grad_residual, router_grad, gain_two)
+    moved = over_links(moved, out_grad_other, query_grad, sums_other)
     result_got = exchange(after([result], query_grad)[0])
-    late, grad_normed = kernel_call(
+    *late, grad_normed = kernel_call(
         functools.partial(outer_body, n_exp),
-        (sds((place_row.shape[1], width), BF16), sds((toks, width), F32)),
+        [sds((rows, width), BF16) for rows in (width, width, width, place_row.shape[1] - 3 * width)]
+        + [sds((toks, width), F32)],
         [pltpu.VMEM((toks, 3 * width), BF16)],
         cost=QUICK,
     )(
-        qkv, *after([out_grad_other], *moved), sums_other, keep_col, query_grad, kv_grad, normed, own, weights, early,
-    )
-    late_far = swap_core(late)
+        qkv, *after([out_grad_other], *moved[1:3]), sums_other, keep_col, query_grad, kv_grad, normed, own, weights, early,
+    )
+    late_far = [swap_core(part) for part in late]
     quarter = half_slots // 2
     eighth, sixteenth = quarter // 2, quarter // 4
     count = place_row.shape[1]
 
     def spread(starts, *others):
         return kernel_call(
-            functools.partial(spread_body, starts), [sds((eighth, width), BF16)] * 2,
+            functools.partial(spread_body, starts, len(late)), [sds((eighth, width), BF16)] * 2,
             [pltpu.VMEM((count, width), BF16)], cost=QUICK,
-        )(*after([place_row], *others), late, late_far)
-
-    sends = spread((eighth, quarter + eighth))
+        )(*after([place_row], *others), *late, *late_far)
+
+    sends = spread((eighth, quarter + eighth), moved[3])
     got_a, got_b = swap_x(sends[0]), swap_y(sends[1])
     keeps = spread((0, quarter), *sends)
     grad_tokens = kernel_call(
         functools.partial(tokens_body, n_exp), sds((toks, width), F32), cost=QUICK
     )(*after([grad_normed], *sends), own, weights, grad_residual)
-    moved = over_cores(after(moved, *keeps))
-
-    tile = 256 if owned % 512 == 0 else owned // 2
-    steps = owned // tile // 2
-
-    def adam_half(number, made, *others):
-        rows_of = lambda columns: pl.BlockSpec((tile, columns), lambda i: (i + number * steps, 0))
-        n_given = 1 + len(moved) + 3
-        return kernel_call(
-            functools.partial(adam_body, len(moved), len(made)), [sds((owned, width), F32)] * 4, held,
-            grid=(steps,),
-            in_specs=[rows_of(8)] + [pl.BlockSpec(piece.shape, lambda i: (0, 0)) for piece in moved]
-            + [rows_of(width)] * 3 + [pl.BlockSpec(memory_space=pl.ANY)] * len(made),
-            out_specs=[rows_of(width)] * 4,
-            cost=QUICK,
-            aliases={n_given + at: at for at in range(len(made))},
-        )(*after([plan_col], *others), *moved, expert_first[0], expert_second[0], expert_slots[0], *made)
 
     got_a, got_b = after([got_a, got_b], grad_tokens)
-    sum_a = total_f32(keeps[0], got_a).astype(BF16)
-    sum_b = total_f32(keeps[1], got_b).astype(BF16)
-    got_a, got_b = swap_y(sum_a[sixteenth:]), swap_x(sum_b[sixteenth:])
-    half_new = adam_half(0, [], sum_a, sum_b)
-    got_a, got_b = after([got_a, got_b], half_new[0])
-    sum_a = total_f32(sum_a[:sixteenth], got_a).astype(BF16)
-    sum_b = total_f32(sum_b[:sixteenth], got_b).astype(BF16)
+    go_a, go_b, sum_a, sum_b = kernel_call(
+        step_body, [sds((sixteenth, width), BF16)] * 4, cost=QUICK
+    )(keeps[0], got_a, keeps[1], got_b)
+    got_a, got_b = swap_y(go_a), swap_x(go_b)
+    moved = over_cores(after(moved, go_a))
+    sum_a = total_f32(sum_a, got_a).astype(BF16)
+    sum_b = total_f32(sum_b, got_b).astype(BF16)
     lines = [sum_a[i * stride : (i + 1) * stride] for i in range(n_z // 2)]
     lines += [sum_b[i * stride : (i + 1) * stride] for i in range(n_z // 2)]
     output = kernel_call(
         mixture_body, sds((toks, width), BF16), cost=QUICK
     )(*after([result_got], *lines), pos_col, ids, prob, residual)
-    expert_new = adam_half(1, half_new, *lines)
+    tile = 256 if owned % 256 == 0 else owned
+    rows_of = lambda columns: pl.BlockSpec((tile, columns), lambda i: (i, 0))
+    expert_new = kernel_call(
+        functools.partial(adam_body, len(moved)), [sds((owned, width), F32)] * 4, held,
+        grid=(owned // tile,),
+        in_specs=[rows_of(8)] + [pl.BlockSpec(piece.shape, lambda i: (0, 0)) for piece in moved] + [rows_of(width)] * 3,
+        out_specs=[rows_of(width)] * 4,
+        cost=QUICK,
+    )(*after([plan_col], output), *moved, expert_first[0], expert_second[0], expert_slots[0])
     shared_grad = lines[0].astype(F32)
     for by in range(1, n_z):
-        shared_grad = shared_grad + shift_z(lines[by], n_z - by).astype(F32)
+        came = after([shift_z(lines[by], n_z - by)], expert_new[0])[0]
+        shared_grad = shared_grad + came.astype(F32)
     shared_grad = shared_grad[:own_count]
 
 

time: 312 us -> 300 us (0.962)
  waiting for transfers between devices: 37.6 us -> 31.4 us
    ppermute x10, waiting for transfers between devices: 10.1 us -> 2.09 us  [swap_x(): return lax.ppermute(value, 'ctx', SWAP)]
    ppermute x6, waiting for transfers between devices: 7.24 us -> 0.02 us  [swap_y(): return lax.ppermute(value, 'dp', SWAP_Y)]
    ppermute x2, waiting for transfers between devices: 2.26 us -> 8.24 us  [swap_x_y(): return lax.ppermute(value, ('dp', 'ctx'), [(i, i ^ 5) for i in range(8)])]
    convert_element_type x3 -> x2, other arithmetic: 4.08 us -> 0.14 us  [the longest x1 0.07 us: on_chip_experts(): sum_b = total_f32(sum_b, got_b).astype(BF16)]
    ppermute x13 -> x16, waiting for transfers between devices: 5.68 us -> 6.36 us  [swap_core(): return lax.ppermute(value, 'dp', SWAP_CORE)]
    unnamed x57 -> x61, local copies, waits for them, and re-layouts: 8.44 us -> 7.88 us
  transfers between devices with their start and end apart: 41 -> 44, of which waited for: 14 -> 12; matrix products, arithmetic and copies ran while one was open for 12% -> 10% of each run, Pallas kernels for 44% -> 49%
where the time goes in v4:
time: 300 us; the launch traced here: 295 us
  Pallas kernels  165 us (55%)
  starting transfers between devices  59 us (20%)
  waiting for transfers between devices  31.4 us (10%)
  local copies, waits for them, and re-layouts  27.7 us (9%)
  other arithmetic  10.7 us (4%)
    pallas_call x4, Pallas kernels, with_base(): kernel_call(body, out_shape, scratch, in_specs=[smem] + [vmem] * len(arra...  26.3 us
    all_to_all x4, starting transfers between devices, exchange(): lax.all_to_all(rows, everyone, split_axis=0, concat_axis=0, tiled=True)  20.5 us
    pallas_call x1, Pallas kernels, on_chip_experts(): kernel_call(functools.partial(expert_body, n_exp), (sds((slots, FF), BF16...  18.8 us
    pallas_call x2, Pallas kernels, unpack(): kernel_call(functools.partial(unpack_body, spots, len(earlier)), sds((row...  18.2 us
    pallas_call x1, Pallas kernels, on_chip_experts(): kernel_call(functools.partial(adam_body, len(moved)), [sds((owned, width)...  15.7 us
    pallas_call x1, Pallas kernels, on_chip_experts(): kernel_call(functools.partial(inner_body, n_exp), (sds((toks, width), BF1...  14.5 us
    pallas_call x1, Pallas kernels, on_chip_experts(): kernel_call(functools.partial(forward_body, n_exp), (sds((2 * toks, 3 * w...  12.5 us
    ppermute x6, starting transfers between devices, shift_z(): lax.ppermute(value, 'expert', [(i, (i + by) % count) for i in range(count)])  12.2 us
  transfers between devices with their start and end apart: 44, of which 12 were waited for; matrix products, arithmetic and copies ran while one was open for 10% of the time, Pallas kernels for 49%

profile of v4, /device:TPU:0, one launch (start us, length us, event | category | flops | bytes accessed | tf_op | source)
XLA Modules:
  0.0 295.4 jit_solution(2402885806549671597)
XLA Ops:
  1.6 5.1 %collective-permute-start.15 = (bf16[136,512]{1,0:T(8,128)(2,1)S(1)}, bf16[136,512]{1,0:T(8,128)(2,1)S(1)}, u32[]{:S(2)}, u32[]{:S(2)}) collective-permute-start(bf16[136,512]{1,0:T(8,128)(2,1)S(1)} %pad.8), channel_id=1, source_target_pairs={{0,3},{1,0},{2,1},{3,2},{4,7},{5,4},{6,5},{7,6},{8,11},{9,8},{10,9... | collective-permute-start | bytes 417800 | tf_op jit(solution)/shard_map/ppermute | solution.py:893
  10.6 6.0 %collective-permute-done.12 = bf16[136,512]{1,0:T(8,128)(2,1)S(1)} collective-permute-done((bf16[136,512]{1,0:T(8,128)(2,1)S(1)}, bf16[136,512]{1,0:T(8,128)(2,1)S(1)}, u32[]{:S(2)}, u32[]{:S(2)}) %collective-permute-start.12) | collective-permute-done | bytes 139296 | tf_op jit(solution)/shard_map/ppermute | solution.py:893
  32.9 3.6 %route_body.1 = (s32[8,512]{1,0:T(8,128)}, s32[512,8]{1,0:T(8,128)}, bf16[1280,512]{1,0:T(8,128)(2,1)}) custom-call(s32[2,512]{1,0:T(2,128)} %copy.27.ids_ref, f32[1,512]{1,0:T(1,128)} %convert_element_type.59.prio_ref, f32[1,512]{1,0:T(1,128)} %copy-done.30, bf16[512,512]{1,0:T(8,128)(2,1)} %bitcast.75), custom_call_target="tpu_custom_call" | custom-call | flops 4600000000 | bytes 1000000 | tf_op jit(solution)/shard_map/route_body/pallas_call | solution.py:973
  36.5 6.2 %all-to-all-start = ((bf16[32,40,512]{2,1,0:T(8,128)(2,1)}), bf16[32,40,512]{2,1,0:T(8,128)(2,1)}, u32[]{:S(2)}, u32[]{:S(2)}) async-start(bf16[32,40,512]{2,1,0:T(8,128)(2,1)} %bitcast.66), calls=%async_computation | async-start | bytes 2621440 | tf_op jit(solution)/shard_map/all_to_all | solution.py:980
  42.7 3.4 %plan_body.1 = (s32[8,2048]{1,0:T(8,128)S(1)}, s32[2048,8]{1,0:T(8,128)S(1)}, s32[8,128]{1,0:T(8,128)}) custom-call(s32[1]{0:T(128)} %bitcast.16.me_ref, s32[8,2048]{1,0:T(8,128)} %bitcast.71), custom_call_target="tpu_custom_call" | custom-call | flops 5750000128 | bytes 1000000 | tf_op jit(solution)/shard_map/plan_body/pallas_call | solution.py:994
  46.1 8.9 %unpack_body.2.refs_4_ = bf16[2080,512]{1,0:T(8,128)(2,1)} custom-call(s32[2080,1]{1,0:T(8,128)} %broadcast_in_dim.40.pos_ref, bf16[544,512]{1,0:T(8,128)(2,1)} %pad_maximum_fusion.8.refs_0_, bf16[544,512]{1,0:T(8,128)(2,1)} %constant_dynamic-update-slice_fusion.2.refs_1_, bf16[544,512]{1,0:T(8,128)(2,1)} %collective-permute-done.20.refs_2_, ...), custom_call_target="tpu_custom_call" | custom-call | flops 8049999872 | bytes 1000000 | tf_op jit(solution)/shard_map/unpack_body/pallas_call | solution.py:951
  55.6 6.6 %put_body.5 = (bf16[640,512]{1,0:T(8,128)(2,1)}, bf16[640,512]{1,0:T(8,128)(2,1)}, bf16[640,512]{1,0:T(8,128)(2,1)}, bf16[640,512]{1,0:T(8,128)(2,1)}) custom-call(s32[1]{0:T(128)} %constant.192.clone.1.base_ref, s32[8,2048]{1,0:T(8,128)S(1)} %get-tuple-element.405.pos_ref, bf16[2048,512]{1,0:T(8,128)(2,1)S(1)} %bitcast.52), custom_call_target="tpu_custom_call" | custom-call | flops 9200000000 | bytes 1000000 | tf_op jit(solution)/shard_map/put_body/pallas_call | solution.py:1002
  67.3 9.3 %unpack_body.3.w_ref = bf16[2080,512]{1,0:T(8,128)(2,1)} custom-call(s32[2080,1]{1,0:T(8,128)} %broadcast_in_dim.40.pos_ref, bf16[544,512]{1,0:T(8,128)(2,1)} %collective-permute-done.18.refs_0_, bf16[544,512]{1,0:T(8,128)(2,1)} %collective-permute-done.19.refs_1_, bf16[544,512]{1,0:T(8,128)(2,1)} %copy-done.32, bf16[544,512]{1,0:T(8,128)(2,1)} %copy-done.33, ...), custom_call_target="tpu_custom_call" | custom-call | flops 8049999872 | bytes 1000000 | tf_op jit(solution)/shard_map/unpack_body/pallas_call | solution.py:951
  76.6 12.5 %forward_body.1 = (bf16[1024,1536]{1,0:T(8,128)(2,1)}, bf16[512,512]{1,0:T(8,128)(2,1)}, f32[512,512]{1,0:T(8,128)}, f32[512,512]{1,0:T(8,128)}, f32[512,16]{1,0...) custom-call(bf16[512,512]{1,0:T(8,128)(2,1)} %bitcast.61, ...), custom_call_target="tpu_custom_call" | custom-call | flops 14949999616 | bytes 1000000 | tf_op jit(solution)/shard_map/forward_body/pallas_call | solution.py:1026
  89.1 6.4 %all-to-all-start.1 = ((bf16[32,40,512]{2,1,0:T(8,128)(2,1)}), bf16[32,40,512]{2,1,0:T(8,128)(2,1)}, u32[]{:S(2)}, u32[]{:S(2)}) async-start(bf16[32,40,512]{2,1,0:T(8,128)(2,1)} %bitcast.65), calls=%async_computation.1 | async-start | bytes 2621440 | tf_op jit(solution)/shard_map/all_to_all | solution.py:980
  95.6 2.5 collective-permute-done.26.refs_3_
  106.0 7.7 %take_body.9 = bf16[2048,512]{1,0:T(8,128)(2,1)S(1)} custom-call(s32[1]{0:T(128)} %constant.192.clone.1.base_ref, s32[2048,8]{1,0:T(8,128)S(1)} %get-tuple-element.479.pos_ref, bf16[640,512]{1,0:T(8,128)(2,1)} %get-tuple-element.414.refs_0_, bf16[640,512]{1,0:T(8,128)(2,1)} %collective-permute-done.24.refs_1_, ...), custom_call_target="tpu_custom_call" | custom-call | flops 1000000 | bytes 1000 | tf_op jit(solution)/shard_map/take_body/pallas_call | solution.py:1002
  120.2 7.6 %all-to-all-done.1 = bf16[32,40,512]{2,1,0:T(8,128)(2,1)} async-done(((bf16[32,40,512]{2,1,0:T(8,128)(2,1)}), bf16[32,40,512]{2,1,0:T(8,128)(2,1)}, u32[]{:S(2)}, u32[]{:S(2)}) %all-to-all-start.1) | async-done | bytes 1310752 | tf_op jit(solution)/shard_map/all_to_all | solution.py:980
  127.8 18.8 %expert_body.1 = (bf16[1280,2048]{1,0:T(8,128)(2,1)}, bf16[1280,2048]{1,0:T(8,128)(2,1)}, bf16[1280,512]{1,0:T(8,128)(2,1)}, bf16[1280,512]{1,0:T(8,128)(2,1)}, ...) custom-call(s32[1]{0:T(128)} %bitcast.7.expert_ref, bf16[1280,512]{1,0:T(8,128)(2,1)} %bitcast.15.got_ref, ...), custom_call_target="tpu_custom_call" | custom-call | flops 21849999360 | bytes 1000000 | tf_op jit(solution)/shard_map/expert_body/pallas_call | solution.py:1056
  146.6 3.6 %all-to-all-start.2 = ((bf16[32,40,512]{2,1,0:T(8,128)(2,1)}), bf16[32,40,512]{2,1,0:T(8,128)(2,1)}, u32[]{:S(2)}, u32[]{:S(2)}) async-start(bf16[32,40,512]{2,1,0:T(8,128)(2,1)} %bitcast.67), calls=%async_computation.2 | async-start | bytes 2621440 | tf_op jit(solution)/shard_map/all_to_all | solution.py:980
  150.2 11.7 %weight_grad_body.1 = (bf16[1024,512]{1,0:T(8,128)(2,1)}, bf16[1024,512]{1,0:T(8,128)(2,1)}, f32[1024,512]{1,0:T(8,128)}, f32[1024,512]{1,0:T(8,128)}) custom-call(bf16[1280,2048]{1,0:T(8,128)(2,1)} %get-tuple-element.429.hidden_ref, bf16[1280,2048]{1,0:T(8,128)(2,1)} %get-tuple-element.430.active_ref, bf16[1280,512]{1,0:T(8,128)(2,1)} %bitcast.15.got_ref, ...), custom_call_target="tpu_custom_call" | custom-call | flops 11500000256 | bytes 1000000 | tf_op jit(solution)/shard_map/weight_grad_body/pallas_call | solution.py:1075
  166.4 6.7 %sum_put_body.7 = (bf16[640,512]{1,0:T(8,128)(2,1)}, bf16[640,512]{1,0:T(8,128)(2,1)}) custom-call(s32[1]{0:T(128)} %constant.192.clone.1.base_ref, s32[8,2048]{1,0:T(8,128)S(1)} %get-tuple-element.832, f32[1024,512]{1,0:T(8,128)} %get-tuple-element.770.refs_0_, f32[1024,512]{1,0:T(8,128)} %get-tuple-element.771.refs_1_, ...), custom_call_target="tpu_custom_call" | custom-call | flops 4600000000 | bytes 1000000 | tf_op jit(solution)/shard_map/sum_put_body/pallas_call | solution.py:1002
  174.7 5.4 %sum_put_body.6 = (bf16[640,512]{1,0:T(8,128)(2,1)}, bf16[640,512]{1,0:T(8,128)(2,1)}) custom-call(s32[1]{0:T(128)} %constant.192.clone.1.base_ref, s32[8,2048]{1,0:T(8,128)S(1)} %get-tuple-element.832, f32[1024,512]{1,0:T(8,128)S(1)} %copy-done.35, f32[1024,512]{1,0:T(8,128)S(1)} %copy-done.36, bf16[1024,512]{1,0:T(8,128)(2,1)} %collective-permute-done.31.refs_2_, ...), custom_call_target="tpu_custom_call" | custom-call | flops 4600000000 | bytes 1000000 | tf_op jit(solution)/shard_map/sum_put_body/pallas_call | solution.py:1002
  182.4 5.8 %middle_body.1 = (f32[512,512]{1,0:T(8,128)}, bf16[512,512]{1,0:T(8,128)(2,1)}, f32[512,128]{1,0:T(8,128)}, f32[8,512]{1,0:T(8,128)}, f32[8,512]{1,0:T(8,128)}) custom-call(bf16[1280,512]{1,0:T(8,128)(2,1)} %bitcast.22.back_ref, s32[512,8]{1,0:T(8,128)} %get-tuple-element.441.pos_ref, f32[512,512]{1,0:T(8,128)} %get-tuple-element.442.residual_ref, ...), custom_call_target="tpu_custom_call" | custom-call | flops 6899999744 | bytes 1000000 | tf_op jit(solution)/shard_map/middle_body/pallas_call | solution.py:1090
  188.9 2.0 collective-permute-start.33
  191.0 14.5 %inner_body.1 = (bf16[512,512]{1,0:T(8,128)(2,1)}, f32[2,512,512]{2,1,0:T(8,128)}, bf16[544,512]{1,0:T(8,128)(2,1)}) custom-call(bf16[1024,1536]{1,0:T(8,128)(2,1)} %get-tuple-element.427.qkv_ref, bf16[512,512]{1,0:T(8,128)(2,1)} %get-tuple-element.444.out_grad_ref, f32[512,128]{1,0:T(8,128)} %get-tuple-element.445.lse_ref, ...), custom_call_target="tpu_custom_call" | custom-call | flops 17250000896 | bytes 1000000 | tf_op jit(solution)/shard_map/inner_body/pallas_call | solution.py:1100
  207.2 4.3 %all-to-all-start.3 = ((bf16[32,40,512]{2,1,0:T(8,128)(2,1)}), bf16[32,40,512]{2,1,0:T(8,128)(2,1)}, u32[]{:S(2)}, u32[]{:S(2)}) async-start(bf16[32,40,512]{2,1,0:T(8,128)(2,1)} %bitcast.64), calls=%async_computation.3 | async-start | bytes 2621440 | tf_op jit(solution)/shard_map/all_to_all | solution.py:980
  211.6 11.5 %outer_body.1 = (bf16[512,512]{1,0:T(8,128)(2,1)}, bf16[512,512]{1,0:T(8,128)(2,1)}, bf16[512,512]{1,0:T(8,128)(2,1)}, bf16[560,512]{1,0:T(8,128)(2,1)}, f32[512,512]{1,0:T(8,128)}) custom-call(bf16[1024,1536]{1,0:T(8,128)(2,1)} %get-tuple-element.427.qkv_ref, bf16[512,512]{1,0:T(8,128)(2,1)} %collective-permute-done.33.out_grad_ref, f32[16,512]{1,0:T(8,128)} %copy-done.28, ...), custom_call_target="tpu_custom_call" | custom-call | flops 1000000 | bytes 1000 | tf_op jit(solution)/shard_map/outer_body/pallas_call | solution.py:1107
  226.7 5.8 %collective-permute-done.35.refs_3_ = bf16[640,512]{1,0:T(8,128)(2,1)} collective-permute-done((bf16[640,512]{1,0:T(8,128)(2,1)}, bf16[640,512]{1,0:T(8,128)(2,1)}, u32[]{:S(2)}, u32[]{:S(2)}) %collective-permute-start.35) | collective-permute-done | bytes 655392 | tf_op jit(solution)/shard_map/ppermute | solution.py:884
  232.5 5.8 %spread_body.2 = (bf16[544,512]{1,0:T(8,128)(2,1)}, bf16[544,512]{1,0:T(8,128)(2,1)}) custom-call(s32[1,2096]{1,0:T(1,128)} %broadcast_in_dim.33.pos_ref, bf16[512,512]{1,0:T(8,128)(2,1)} %get-tuple-element.460.refs_0_, bf16[512,512]{1,0:T(8,128)(2,1)} %get-tuple-element.461.refs_1_, bf16[512,512]{1,0:T(8,128)(2,1)} %get-tuple-element.462.refs_2_, ...), custom_call_target="tpu_custom_call" | custom-call | flops 1000000 | bytes 1000 | tf_op jit(solution)/shard_map/spread_body/pallas_call | solution.py:1122
  240.8 4.0 %tokens_body.1 = f32[512,512]{1,0:T(8,128)} custom-call(f32[512,512]{1,0:T(8,128)} %get-tuple-element.469.grad_normed_ref, bf16[512,512]{1,0:T(8,128)(2,1)} %bitcast.63, bf16[2080,512]{1,0:T(8,128)(2,1)} %unpack_body.3.w_ref, f32[512,512]{1,0:T(8,128)} %get-tuple-element.447.grad_ref), custom_call_target="tpu_custom_call" | custom-call | flops 1000000 | bytes 1000 | tf_op jit(solution)/shard_map/tokens_body/pallas_call | solution.py:1130
  244.8 5.8 %spread_body.3 = (bf16[544,512]{1,0:T(8,128)(2,1)}, bf16[544,512]{1,0:T(8,128)(2,1)}) custom-call(s32[1,2096]{1,0:T(1,128)} %broadcast_in_dim.33.pos_ref, bf16[512,512]{1,0:T(8,128)(2,1)} %get-tuple-element.460.refs_0_, bf16[512,512]{1,0:T(8,128)(2,1)} %get-tuple-element.461.refs_1_, bf16[512,512]{1,0:T(8,128)(2,1)} %get-tuple-element.462.refs_2_, ...), custom_call_target="tpu_custom_call" | custom-call | flops 1000000 | bytes 1000 | tf_op jit(solution)/shard_map/spread_body/pallas_call | solution.py:1122
  250.6 2.1 collective-permute-done.42.got_a
  253.6 2.8 step_body.1
  264.8 3.0 %collective-permute-start.50 = (bf16[136,512]{1,0:T(8,128)(2,1)}, bf16[136,512]{1,0:T(8,128)(2,1)S(1)}, u32[]{:S(2)}, u32[]{:S(2)}) collective-permute-start(bf16[136,512]{1,0:T(8,128)(2,1)} %get-tuple-element.557), channel_id=1, source_target_pairs={{0,1},{1,2},{2,3},{3,0},{4,5},{5,6},{6,7},{7,4},{8,9},{9,10},{10,1... | collective-permute-start | bytes 417800 | tf_op jit(solution)/shard_map/ppermute | solution.py:893
  271.7 4.2 %mixture_body.1 = bf16[512,512]{1,0:T(8,128)(2,1)} custom-call(bf16[1280,512]{1,0:T(8,128)(2,1)} %bitcast.25.result_ref, s32[512,8]{1,0:T(8,128)} %get-tuple-element.441.pos_ref, s32[512,2]{1,0:T(8,128)} %bitcast.59, f32[512,16]{1,0:T(8,128)} %get-tuple-element.478.prob_ref, f32[512,512]{1,0:T(8,128)} %get-tuple-element.442.residual_ref), custom_call_target="tpu_custom_call" | custom-call | flops 1000000 | bytes 1000 | tf_op jit(solution)/shard_map/mixture_body/pallas_call | solution.py:1144
  276.0 15.7 %adam_body.1 = (f32[2048,512]{1,0:T(8,128)}, f32[2048,512]{1,0:T(8,128)}, f32[2048,512]{1,0:T(8,128)}, f32[2048,512]{1,0:T(8,128)}) custom-call(s32[2048,8]{1,0:T(8,128)S(1)} %get-tuple-element.816, bf16[640,512]{1,0:T(8,128)(2,1)} %get-tuple-element.480.refs_0_, bf16[640,512]{1,0:T(8,128)(2,1)} %collective-permute-done.36.refs_1_, ...), custom_call_target="tpu_custom_call" | custom-call | flops 1000000 | bytes 1000 | tf_op jit(solution)/shard_map/adam_body/pallas_call | solution.py:1149
  (184 shorter events, 74.2 us)
Async XLA Ops:
  1.6 17.6 %collective-permute-start.15 = (bf16[136,512]{1,0:T(8,128)(2,1)S(1)}, bf16[136,512]{1,0:T(8,128)(2,1)S(1)}, u32[]{:S(2)}, u32[]{:S(2)}) collective-permute-start(bf16[136,512]{1,0:T(8,128)(2,1)S(1)} %pad.8), channel_id=1, source_target_pairs={{0,3},{1,0},{2,1},{3,2},{4,7},{5,4},{6,5},{7,6},{8,11},{9,8},{10,9... | collective-permute-start | bytes 417800 | tf_op jit(solution)/shard_map/ppermute | solution.py:893
  6.7 11.8 %collective-permute-start.14 = (bf16[136,512]{1,0:T(8,128)(2,1)S(1)}, bf16[136,512]{1,0:T(8,128)(2,1)S(1)}, u32[]{:S(2)}, u32[]{:S(2)}) collective-permute-start(bf16[136,512]{1,0:T(8,128)(2,1)S(1)} %pad.8), channel_id=1, source_target_pairs={{0,2},{1,3},{2,0},{3,1},{4,6},{5,7},{6,4},{7,5},{8,10},{9,11},{10,... | collective-permute-start | bytes 417800 | tf_op jit(solution)/shard_map/ppermute | solution.py:893
  6.7 9.9 %collective-permute-start.12 = (bf16[136,512]{1,0:T(8,128)(2,1)S(1)}, bf16[136,512]{1,0:T(8,128)(2,1)S(1)}, u32[]{:S(2)}, u32[]{:S(2)}) collective-permute-start(bf16[136,512]{1,0:T(8,128)(2,1)S(1)} %pad.8), channel_id=1, source_target_pairs={{0,1},{1,2},{2,3},{3,0},{4,5},{5,6},{6,7},{7,4},{8,9},{9,10},{10,1... | collective-permute-start | bytes 417800 | tf_op jit(solution)/shard_map/ppermute | solution.py:893
  7.7 20.0 %collective-permute-start.17 = (s32[1,512]{1,0:T(1,128)}, s32[1,512]{1,0:T(1,128)S(1)}, u32[]{:S(2)}, u32[]{:S(2)}) collective-permute-start(s32[1,512]{1,0:T(1,128)} %param.19), channel_id=1, source_target_pairs={{0,4},{4,0},{1,5},{5,1},{2,6},{6,2},{3,7},{7,3},{8,12},{12,8},{9,1... | collective-permute-start | bytes 6152 | tf_op jit(solution)/shard_map/ppermute | solution.py:876
  10.0 22.2 %collective-permute-start.11 = (bf16[512,512]{1,0:T(8,128)(2,1)}, bf16[512,512]{1,0:T(8,128)(2,1)S(1)}, u32[]{:S(2)}, u32[]{:S(2)}) collective-permute-start(bf16[512,512]{1,0:T(8,128)(2,1)} %bitcast.60), channel_id=1, source_target_pairs={{0,4},{4,0},{1,5},{5,1},{2,6},{6,2},{3,7},{7,3},{8,12},{12,8},{9,1... | collective-permute-start | bytes 1572872 | tf_op jit(solution)/shard_map/ppermute | solution.py:876
  16.6 11.7 %collective-permute-start.13 = (bf16[272,512]{1,0:T(8,128)(2,1)S(1)}, bf16[272,512]{1,0:T(8,128)(2,1)S(1)}, u32[]{:S(2)}, u32[]{:S(2)}) collective-permute-start(bf16[272,512]{1,0:T(8,128)(2,1)S(1)} %pad_maximum_fusion.9), channel_id=1, source_target_pairs={{0,16},{16,0},{8,24},{24,8},{1,17},{17,1},{9,25},{25,9},{2,18},{18... | collective-permute-start | bytes 835592 | tf_op jit(solution)/shard_map/ppermute | solution.py:880
  29.1 16.9 %collective-permute-start.20 = (bf16[544,512]{1,0:T(8,128)(2,1)}, bf16[544,512]{1,0:T(8,128)(2,1)}, u32[]{:S(2)}, u32[]{:S(2)}) collective-permute-start(bf16[544,512]{1,0:T(8,128)(2,1)} %pad_maximum_fusion.8.refs_0_), channel_id=1, source_target_pairs={{0,8},{8,0},{16,24},{24,16},{1,9},{9,1},{17,25},{25,17},{2,10},{10... | collective-permute-start | bytes 1671176 | tf_op jit(solution)/shard_map/ppermute | solution.py:888
  29.1 25.9 %collective-permute-start.18 = (bf16[544,512]{1,0:T(8,128)(2,1)}, bf16[544,512]{1,0:T(8,128)(2,1)}, u32[]{:S(2)}, u32[]{:S(2)}) collective-permute-start(bf16[544,512]{1,0:T(8,128)(2,1)} %pad_maximum_fusion.8.refs_0_), channel_id=1, source_target_pairs={{0,4},{4,0},{1,5},{5,1},{2,6},{6,2},{3,7},{7,3},{8,12},{12,8},{9,1... | collective-permute-start | bytes 1671176 | tf_op jit(solution)/shard_map/ppermute | solution.py:876
  30.4 15.7 %collective-permute-start.21 = (bf16[544,512]{1,0:T(8,128)(2,1)}, bf16[544,512]{1,0:T(8,128)(2,1)}, u32[]{:S(2)}, u32[]{:S(2)}) collective-permute-start(bf16[544,512]{1,0:T(8,128)(2,1)} %constant_dynamic-update-slice_fusion.2.refs_1_), channel_id=1, source_target_pairs={{0,8},{8,0},{16,24},{24,16},{1,9},{9,1},{17,25},{25,17},{2,10},{10... | collective-permute-start | bytes 1671176 | tf_op jit(solution)/shard_map/ppermute | solution.py:888
  30.6 24.4 %collective-permute-start.19 = (bf16[544,512]{1,0:T(8,128)(2,1)}, bf16[544,512]{1,0:T(8,128)(2,1)}, u32[]{:S(2)}, u32[]{:S(2)}) collective-permute-start(bf16[544,512]{1,0:T(8,128)(2,1)} %constant_dynamic-update-slice_fusion.2.refs_1_), channel_id=1, source_target_pairs={{0,16},{16,0},{8,24},{24,8},{1,17},{17,1},{9,25},{25,9},{2,18},{18... | collective-permute-start | bytes 1671176 | tf_op jit(solution)/shard_map/ppermute | solution.py:880
  36.5 40.0 %all-to-all-start = ((bf16[32,40,512]{2,1,0:T(8,128)(2,1)}), bf16[32,40,512]{2,1,0:T(8,128)(2,1)}, u32[]{:S(2)}, u32[]{:S(2)}) async-start(bf16[32,40,512]{2,1,0:T(8,128)(2,1)} %bitcast.66), calls=%async_computation | async-start | bytes 2621440 | tf_op jit(solution)/shard_map/all_to_all | solution.py:980
  55.0 10.7 %collective-permute-start.22 = (bf16[544,512]{1,0:T(8,128)(2,1)}, bf16[544,512]{1,0:T(8,128)(2,1)S(1)}, u32[]{:S(2)}, u32[]{:S(2)}) collective-permute-start(bf16[544,512]{1,0:T(8,128)(2,1)} %collective-permute-done.18.refs_0_), channel_id=1, source_target_pairs={{0,8},{8,0},{16,24},{24,16},{1,9},{9,1},{17,25},{25,17},{2,10},{10... | collective-permute-start | bytes 1671176 | tf_op jit(solution)/shard_map/ppermute | solution.py:888
  55.4 10.2 %collective-permute-start.23 = (bf16[544,512]{1,0:T(8,128)(2,1)}, bf16[544,512]{1,0:T(8,128)(2,1)S(1)}, u32[]{:S(2)}, u32[]{:S(2)}) collective-permute-start(bf16[544,512]{1,0:T(8,128)(2,1)} %collective-permute-done.19.refs_1_), channel_id=1, source_target_pairs={{0,8},{8,0},{16,24},{24,16},{1,9},{9,1},{17,25},{25,17},{2,10},{10... | collective-permute-start | bytes 1671176 | tf_op jit(solution)/shard_map/ppermute | solution.py:888
  62.2 33.4 %collective-permute-start.24 = (bf16[640,512]{1,0:T(8,128)(2,1)}, bf16[640,512]{1,0:T(8,128)(2,1)}, u32[]{:S(2)}, u32[]{:S(2)}) collective-permute-start(bf16[640,512]{1,0:T(8,128)(2,1)} %get-tuple-element.411), channel_id=1, source_target_pairs={{0,4},{4,0},{1,5},{5,1},{2,6},{6,2},{3,7},{7,3},{8,12},{12,8},{9,1... | collective-permute-start | bytes 1966088 | tf_op jit(solution)/shard_map/ppermute | solution.py:876
  64.1 31.5 %collective-permute-start.25 = (bf16[640,512]{1,0:T(8,128)(2,1)}, bf16[640,512]{1,0:T(8,128)(2,1)}, u32[]{:S(2)}, u32[]{:S(2)}) collective-permute-start(bf16[640,512]{1,0:T(8,128)(2,1)} %get-tuple-element.412), channel_id=1, source_target_pairs={{0,16},{16,0},{8,24},{24,8},{1,17},{17,1},{9,25},{25,9},{2,18},{18... | collective-permute-start | bytes 1966088 | tf_op jit(solution)/shard_map/ppermute | solution.py:880
  65.5 32.5 %collective-permute-start.26 = (bf16[640,512]{1,0:T(8,128)(2,1)}, bf16[640,512]{1,0:T(8,128)(2,1)}, u32[]{:S(2)}, u32[]{:S(2)}) collective-permute-start(bf16[640,512]{1,0:T(8,128)(2,1)} %get-tuple-element.413), channel_id=1, source_target_pairs={{0,20},{4,16},{8,28},{12,24},{16,4},{20,0},{24,12},{28,8},{1,21},{... | collective-permute-start | bytes 1966088 | tf_op jit(solution)/shard_map/ppermute | solution.py:884
  89.1 38.8 %all-to-all-start.1 = ((bf16[32,40,512]{2,1,0:T(8,128)(2,1)}), bf16[32,40,512]{2,1,0:T(8,128)(2,1)}, u32[]{:S(2)}, u32[]{:S(2)}) async-start(bf16[32,40,512]{2,1,0:T(8,128)(2,1)} %bitcast.65), calls=%async_computation.1 | async-start | bytes 2621440 | tf_op jit(solution)/shard_map/all_to_all | solution.py:980
  146.6 35.7 %all-to-all-start.2 = ((bf16[32,40,512]{2,1,0:T(8,128)(2,1)}), bf16[32,40,512]{2,1,0:T(8,128)(2,1)}, u32[]{:S(2)}, u32[]{:S(2)}) async-start(bf16[32,40,512]{2,1,0:T(8,128)(2,1)} %bitcast.67), calls=%async_computation.2 | async-start | bytes 2621440 | tf_op jit(solution)/shard_map/all_to_all | solution.py:980
  173.1 38.4 %collective-permute-start.36 = (bf16[640,512]{1,0:T(8,128)(2,1)}, bf16[640,512]{1,0:T(8,128)(2,1)}, u32[]{:S(2)}, u32[]{:S(2)}) collective-permute-start(bf16[640,512]{1,0:T(8,128)(2,1)} %get-tuple-element.437), channel_id=1, source_target_pairs={{0,4},{4,0},{1,5},{5,1},{2,6},{6,2},{3,7},{7,3},{8,12},{12,8},{9,1... | collective-permute-start | bytes 1966088 | tf_op jit(solution)/shard_map/ppermute | solution.py:876
  180.1 31.5 %collective-permute-start.37 = (bf16[640,512]{1,0:T(8,128)(2,1)}, bf16[640,512]{1,0:T(8,128)(2,1)}, u32[]{:S(2)}, u32[]{:S(2)}) collective-permute-start(bf16[640,512]{1,0:T(8,128)(2,1)} %get-tuple-element.438), channel_id=1, source_target_pairs={{0,16},{16,0},{8,24},{24,8},{1,17},{17,1},{9,25},{25,9},{2,18},{18... | collective-permute-start | bytes 1966088 | tf_op jit(solution)/shard_map/ppermute | solution.py:880
  188.9 16.6 %collective-permute-start.34 = (f32[16,512]{1,0:T(8,128)S(1)}, f32[16,512]{1,0:T(8,128)S(1)}, u32[]{:S(2)}, u32[]{:S(2)}) collective-permute-start(f32[16,512]{1,0:T(8,128)S(1)} %pad_maximum_fusion.10), channel_id=1, source_target_pairs={{0,4},{4,0},{1,5},{5,1},{2,6},{6,2},{3,7},{7,3},{8,12},{12,8},{9,1... | collective-permute-start | bytes 98312 | tf_op jit(solution)/shard_map/ppermute | solution.py:876
  188.9 16.6 %collective-permute-start.33 = (bf16[512,512]{1,0:T(8,128)(2,1)}, bf16[512,512]{1,0:T(8,128)(2,1)}, u32[]{:S(2)}, u32[]{:S(2)}) collective-permute-start(bf16[512,512]{1,0:T(8,128)(2,1)} %get-tuple-element.444.out_grad_ref), channel_id=1, source_target_pairs={{0,4},{4,0},{1,5},{5,1},{2,6},{6,2},{3,7},{7,3},{8,12},{12,8},{9,1... | collective-permute-start | bytes 1572872 | tf_op jit(solution)/shard_map/ppermute | solution.py:876
  205.5 27.0 %collective-permute-start.35 = (bf16[640,512]{1,0:T(8,128)(2,1)}, bf16[640,512]{1,0:T(8,128)(2,1)}, u32[]{:S(2)}, u32[]{:S(2)}) collective-permute-start(bf16[640,512]{1,0:T(8,128)(2,1)} %get-tuple-element.454), channel_id=1, source_target_pairs={{0,20},{4,16},{8,28},{12,24},{16,4},{20,0},{24,12},{28,8},{1,21},{... | collective-permute-start | bytes 1966088 | tf_op jit(solution)/shard_map/ppermute | solution.py:884
  207.2 64.5 %all-to-all-start.3 = ((bf16[32,40,512]{2,1,0:T(8,128)(2,1)}), bf16[32,40,512]{2,1,0:T(8,128)(2,1)}, u32[]{:S(2)}, u32[]{:S(2)}) async-start(bf16[32,40,512]{2,1,0:T(8,128)(2,1)} %bitcast.64), calls=%async_computation.3 | async-start | bytes 2621440 | tf_op jit(solution)/shard_map/all_to_all | solution.py:980
  238.3 14.3 %collective-permute-start.42 = (bf16[544,512]{1,0:T(8,128)(2,1)}, bf16[544,512]{1,0:T(8,128)(2,1)S(1)}, u32[]{:S(2)}, u32[]{:S(2)}) collective-permute-start(bf16[544,512]{1,0:T(8,128)(2,1)} %get-tuple-element.464), channel_id=1, source_target_pairs={{0,4},{4,0},{1,5},{5,1},{2,6},{6,2},{3,7},{7,3},{8,12},{12,8},{9,1... | collective-permute-start | bytes 1671176 | tf_op jit(solution)/shard_map/ppermute | solution.py:876
  239.0 13.7 %collective-permute-start.43 = (bf16[544,512]{1,0:T(8,128)(2,1)}, bf16[544,512]{1,0:T(8,128)(2,1)S(1)}, u32[]{:S(2)}, u32[]{:S(2)}) collective-permute-start(bf16[544,512]{1,0:T(8,128)(2,1)} %get-tuple-element.465), channel_id=1, source_target_pairs={{0,16},{16,0},{8,24},{24,8},{1,17},{17,1},{9,25},{25,9},{2,18},{18... | collective-permute-start | bytes 1671176 | tf_op jit(solution)/shard_map/ppermute | solution.py:880
  257.6 11.8 %collective-permute-start.44 = (bf16[272,512]{1,0:T(8,128)(2,1)}, bf16[272,512]{1,0:T(8,128)(2,1)S(1)}, u32[]{:S(2)}, u32[]{:S(2)}) collective-permute-start(bf16[272,512]{1,0:T(8,128)(2,1)} %get-tuple-element.474), channel_id=1, source_target_pairs={{0,16},{16,0},{8,24},{24,8},{1,17},{17,1},{9,25},{25,9},{2,18},{18... | collective-permute-start | bytes 835592 | tf_op jit(solution)/shard_map/ppermute | solution.py:880
  262.6 13.3 %collective-permute-start.48 = (bf16[640,512]{1,0:T(8,128)(2,1)}, bf16[640,512]{1,0:T(8,128)(2,1)}, u32[]{:S(2)}, u32[]{:S(2)}) collective-permute-start(bf16[640,512]{1,0:T(8,128)(2,1)} %pad_maximum_fusion.7), channel_id=1, source_target_pairs={{0,8},{8,0},{16,24},{24,16},{1,9},{9,1},{17,25},{25,17},{2,10},{10... | collective-permute-start | bytes 1966088 | tf_op jit(solution)/shard_map/ppermute | solution.py:888
  263.5 12.5 %collective-permute-start.47 = (bf16[640,512]{1,0:T(8,128)(2,1)}, bf16[640,512]{1,0:T(8,128)(2,1)}, u32[]{:S(2)}, u32[]{:S(2)}) collective-permute-start(bf16[640,512]{1,0:T(8,128)(2,1)} %pad_maximum_fusion.6), channel_id=1, source_target_pairs={{0,8},{8,0},{16,24},{24,16},{1,9},{9,1},{17,25},{25,17},{2,10},{10... | collective-permute-start | bytes 1966088 | tf_op jit(solution)/shard_map/ppermute | solution.py:888
  264.8 26.9 %collective-permute-start.50 = (bf16[136,512]{1,0:T(8,128)(2,1)}, bf16[136,512]{1,0:T(8,128)(2,1)S(1)}, u32[]{:S(2)}, u32[]{:S(2)}) collective-permute-start(bf16[136,512]{1,0:T(8,128)(2,1)} %get-tuple-element.557), channel_id=1, source_target_pairs={{0,1},{1,2},{2,3},{3,0},{4,5},{5,6},{6,7},{7,4},{8,9},{9,10},{10,1... | collective-permute-start | bytes 417800 | tf_op jit(solution)/shard_map/ppermute | solution.py:893
  267.8 23.8 %collective-permute-start.49 = (bf16[136,512]{1,0:T(8,128)(2,1)}, bf16[136,512]{1,0:T(8,128)(2,1)S(1)}, u32[]{:S(2)}, u32[]{:S(2)}) collective-permute-start(bf16[136,512]{1,0:T(8,128)(2,1)} %get-tuple-element.558), channel_id=1, source_target_pairs={{0,2},{1,3},{2,0},{3,1},{4,6},{5,7},{6,4},{7,5},{8,10},{9,11},{10,... | collective-permute-start | bytes 417800 | tf_op jit(solution)/shard_map/ppermute | solution.py:893
  270.2 22.8 %collective-permute-start.46 = (bf16[136,512]{1,0:T(8,128)(2,1)}, bf16[136,512]{1,0:T(8,128)(2,1)}, u32[]{:S(2)}, u32[]{:S(2)}) collective-permute-start(bf16[136,512]{1,0:T(8,128)(2,1)} %get-tuple-element.559), channel_id=1, source_target_pairs={{0,3},{1,0},{2,1},{3,2},{4,7},{5,4},{6,5},{7,6},{8,11},{9,8},{10,9... | collective-permute-start | bytes 417800 | tf_op jit(solution)/shard_map/ppermute | solution.py:893
  (41 other events, 305.7 us)

commit v5 on v4

--- a/solution.py
+++ b/solution.py
@@ -364,7 +364,7 @@
 I32 = jnp.int32
 LANES = 128
 MASKED = -1e30
-VMEM_LIMIT = 56 * 1024 * 1024
+VMEM_LIMIT = 60 * 1024 * 1024
 MICRO = 1.15e9
 QUICK = (1e6, 1e3)
 THEIRS = 2
@@ -1144,7 +1144,7 @@
     output = kernel_call(
         mixture_body, sds((toks, width), BF16), cost=QUICK
     )(*after([result_got], *lines), pos_col, ids, prob, residual)
-    tile = 256 if owned % 256 == 0 else owned
+    tile = 512 if owned % 512 == 0 else owned
     rows_of = lambda columns: pl.BlockSpec((tile, columns), lambda i: (i, 0))
     expert_new = kernel_call(
         functools.partial(adam_body, len(moved)), [sds((owned, width), F32)] * 4, held,

time: 300 us -> 296 us (0.987)
    unnamed x61 -> x39, local copies, waits for them, and re-layouts: 7.88 us -> 4.23 us
    all_to_all x4, waiting for transfers between devices: 8.4 us -> 5.13 us  [exchange(): lax.all_to_all(rows, everyone, split_axis=0, concat_axis=0, tiled=True)]
  transfers between devices with their start and end apart: 44 -> 44, of which waited for: 12 -> 11; matrix products, arithmetic and copies ran while one was open for 10% -> 11% of each run, Pallas kernels for 49% -> 50%
where the time goes in v5:
time: 296 us; the launch traced here: 292 us
  Pallas kernels  166 us (56%)
  starting transfers between devices  58.8 us (20%)
  waiting for transfers between devices  28.6 us (10%)
  local copies, waits for them, and re-layouts  25.5 us (9%)
  other arithmetic  11.6 us (4%)
    pallas_call x4, Pallas kernels, with_base(): kernel_call(body, out_shape, scratch, in_specs=[smem] + [vmem] * len(arra...  28.7 us
    all_to_all x4, starting transfers between devices, exchange(): lax.all_to_all(rows, everyone, split_axis=0, concat_axis=0, tiled=True)  21.5 us
    pallas_call x1, Pallas kernels, on_chip_experts(): kernel_call(functools.partial(expert_body, n_exp), (sds((slots, FF), BF16...  18.8 us
    pallas_call x2, Pallas kernels, unpack(): kernel_call(functools.partial(unpack_body, spots, len(earlier)), sds((row...  18.2 us
    pallas_call x1, Pallas kernels, on_chip_experts(): kernel_call(functools.partial(inner_body, n_exp), (sds((toks, width), BF1...  14.5 us
    pallas_call x1, Pallas kernels, on_chip_experts(): kernel_call(functools.partial(adam_body, len(moved)), [sds((owned, width)...  14.5 us
    pallas_call x1, Pallas kernels, on_chip_experts(): kernel_call(functools.partial(forward_body, n_exp), (sds((2 * toks, 3 * w...  12.5 us
    pallas_call x1, Pallas kernels, on_chip_experts(): kernel_call(weight_grad_body, halves, cost=(10 * MICRO, 1000000.0))  11.7 us
  transfers between devices with their start and end apart: 44, of which 11 were waited for; matrix products, arithmetic and copies ran while one was open for 11% of the time, Pallas kernels for 50%

profile of v5, /device:TPU:0, one launch (start us, length us, event | category | flops | bytes accessed | tf_op | source)
XLA Modules:
  0.0 292.2 jit_solution(10796079725434455977)
XLA Ops:
  1.6 5.1 %collective-permute-start.15 = (bf16[136,512]{1,0:T(8,128)(2,1)S(1)}, bf16[136,512]{1,0:T(8,128)(2,1)S(1)}, u32[]{:S(2)}, u32[]{:S(2)}) collective-permute-start(bf16[136,512]{1,0:T(8,128)(2,1)S(1)} %pad.8), channel_id=1, source_target_pairs={{0,3},{1,0},{2,1},{3,2},{4,7},{5,4},{6,5},{7,6},{8,11},{9,8},{10,9... | collective-permute-start | bytes 417800 | tf_op jit(solution)/shard_map/ppermute | solution.py:893
  10.6 6.0 %collective-permute-done.12 = bf16[136,512]{1,0:T(8,128)(2,1)S(1)} collective-permute-done((bf16[136,512]{1,0:T(8,128)(2,1)S(1)}, bf16[136,512]{1,0:T(8,128)(2,1)S(1)}, u32[]{:S(2)}, u32[]{:S(2)}) %collective-permute-start.12) | collective-permute-done | bytes 139296 | tf_op jit(solution)/shard_map/ppermute | solution.py:893
  32.9 3.6 %route_body.1 = (s32[8,512]{1,0:T(8,128)}, s32[512,8]{1,0:T(8,128)}, bf16[1280,512]{1,0:T(8,128)(2,1)}) custom-call(s32[2,512]{1,0:T(2,128)} %copy.27.ids_ref, f32[1,512]{1,0:T(1,128)} %convert_element_type.59.prio_ref, f32[1,512]{1,0:T(1,128)} %copy-done.21, bf16[512,512]{1,0:T(8,128)(2,1)} %bitcast.75), custom_call_target="tpu_custom_call" | custom-call | flops 4600000000 | bytes 1000000 | tf_op jit(solution)/shard_map/route_body/pallas_call | solution.py:973
  36.5 6.2 %all-to-all-start = ((bf16[32,40,512]{2,1,0:T(8,128)(2,1)}), bf16[32,40,512]{2,1,0:T(8,128)(2,1)}, u32[]{:S(2)}, u32[]{:S(2)}) async-start(bf16[32,40,512]{2,1,0:T(8,128)(2,1)} %bitcast.66), calls=%async_computation | async-start | bytes 2621440 | tf_op jit(solution)/shard_map/all_to_all | solution.py:980
  42.7 3.4 %plan_body.1 = (s32[8,2048]{1,0:T(8,128)S(1)}, s32[2048,8]{1,0:T(8,128)S(1)}, s32[8,128]{1,0:T(8,128)}) custom-call(s32[1]{0:T(128)} %bitcast.16.me_ref, s32[8,2048]{1,0:T(8,128)} %bitcast.71), custom_call_target="tpu_custom_call" | custom-call | flops 5750000128 | bytes 1000000 | tf_op jit(solution)/shard_map/plan_body/pallas_call | solution.py:994
  46.1 8.9 %unpack_body.2.refs_4_ = bf16[2080,512]{1,0:T(8,128)(2,1)} custom-call(s32[2080,1]{1,0:T(8,128)} %broadcast_in_dim.40.pos_ref, bf16[544,512]{1,0:T(8,128)(2,1)} %pad_maximum_fusion.8.refs_0_, bf16[544,512]{1,0:T(8,128)(2,1)} %constant_dynamic-update-slice_fusion.2.refs_1_, bf16[544,512]{1,0:T(8,128)(2,1)} %collective-permute-done.20.refs_2_, ...), custom_call_target="tpu_custom_call" | custom-call | flops 8049999872 | bytes 1000000 | tf_op jit(solution)/shard_map/unpack_body/pallas_call | solution.py:951
  55.6 6.6 %put_body.5 = (bf16[640,512]{1,0:T(8,128)(2,1)}, bf16[640,512]{1,0:T(8,128)(2,1)}, bf16[640,512]{1,0:T(8,128)(2,1)}, bf16[640,512]{1,0:T(8,128)(2,1)}) custom-call(s32[1]{0:T(128)} %constant.192.clone.1.base_ref, s32[8,2048]{1,0:T(8,128)S(1)} %get-tuple-element.405.pos_ref, bf16[2048,512]{1,0:T(8,128)(2,1)S(1)} %bitcast.52), custom_call_target="tpu_custom_call" | custom-call | flops 9200000000 | bytes 1000000 | tf_op jit(solution)/shard_map/put_body/pallas_call | solution.py:1002
  66.5 9.3 %unpack_body.3.w_ref = bf16[2080,512]{1,0:T(8,128)(2,1)} custom-call(s32[2080,1]{1,0:T(8,128)} %broadcast_in_dim.40.pos_ref, bf16[544,512]{1,0:T(8,128)(2,1)} %collective-permute-done.18.refs_0_, bf16[544,512]{1,0:T(8,128)(2,1)} %collective-permute-done.19.refs_1_, bf16[544,512]{1,0:T(8,128)(2,1)} %copy-done.23, ...), custom_call_target="tpu_custom_call" | custom-call | flops 8049999872 | bytes 1000000 | tf_op jit(solution)/shard_map/unpack_body/pallas_call | solution.py:951
  75.8 12.5 %forward_body.1 = (bf16[1024,1536]{1,0:T(8,128)(2,1)}, bf16[512,512]{1,0:T(8,128)(2,1)}, f32[512,512]{1,0:T(8,128)}, f32[512,512]{1,0:T(8,128)}, f32[512,16]{1,0...) custom-call(bf16[512,512]{1,0:T(8,128)(2,1)} %bitcast.61, ...), custom_call_target="tpu_custom_call" | custom-call | flops 14949999616 | bytes 1000000 | tf_op jit(solution)/shard_map/forward_body/pallas_call | solution.py:1026
  88.3 6.5 %all-to-all-start.1 = ((bf16[32,40,512]{2,1,0:T(8,128)(2,1)}), bf16[32,40,512]{2,1,0:T(8,128)(2,1)}, u32[]{:S(2)}, u32[]{:S(2)}) async-start(bf16[32,40,512]{2,1,0:T(8,128)(2,1)} %bitcast.65), calls=%async_computation.1 | async-start | bytes 2621440 | tf_op jit(solution)/shard_map/all_to_all | solution.py:980
  94.7 3.3 %collective-permute-done.26.refs_3_ = bf16[640,512]{1,0:T(8,128)(2,1)} collective-permute-done((bf16[640,512]{1,0:T(8,128)(2,1)}, bf16[640,512]{1,0:T(8,128)(2,1)}, u32[]{:S(2)}, u32[]{:S(2)}) %collective-permute-start.26) | collective-permute-done | bytes 655392 | tf_op jit(solution)/shard_map/ppermute | solution.py:884
  105.3 9.0 %take_body.9 = bf16[2048,512]{1,0:T(8,128)(2,1)} custom-call(s32[1]{0:T(128)} %constant.192.clone.1.base_ref, s32[2048,8]{1,0:T(8,128)S(1)} %get-tuple-element.479.pos_ref, bf16[640,512]{1,0:T(8,128)(2,1)} %get-tuple-element.414.refs_0_, bf16[640,512]{1,0:T(8,128)(2,1)} %collective-permute-done.24.refs_1_, bf16[640,512]{1,0:T(8,128)(2,1)} %collective-permute-done.25.refs_2_, ...), custom_call_target="tpu_custom_call" | custom-call | flops 1000000 | bytes 1000 | tf_op jit(solution)/shard_map/take_body/pallas_call | solution.py:1002
  114.4 3.0 %fusion.32 = (bf16[1024,512]{1,0:T(8,128)(2,1)}, bf16[1024,512]{1,0:T(8,128)(2,1)}) fusion(bf16[2048,512]{1,0:T(8,128)(2,1)} %take_body.9), kind=kLoop, calls=%fused_computation.92 | loop fusion | bytes 4194304 | tf_op jit(solution)/shard_map/slice | solution.py:1039
  121.9 5.1 %all-to-all-done.1 = bf16[32,40,512]{2,1,0:T(8,128)(2,1)} async-done(((bf16[32,40,512]{2,1,0:T(8,128)(2,1)}), bf16[32,40,512]{2,1,0:T(8,128)(2,1)}, u32[]{:S(2)}, u32[]{:S(2)}) %all-to-all-start.1) | async-done | bytes 1310752 | tf_op jit(solution)/shard_map/all_to_all | solution.py:980
  127.0 18.8 %expert_body.1 = (bf16[1280,2048]{1,0:T(8,128)(2,1)}, bf16[1280,2048]{1,0:T(8,128)(2,1)}, bf16[1280,512]{1,0:T(8,128)(2,1)}, bf16[1280,512]{1,0:T(8,128)(2,1)}, ...) custom-call(s32[1]{0:T(128)} %bitcast.7.expert_ref, bf16[1280,512]{1,0:T(8,128)(2,1)} %bitcast.15.got_ref, ...), custom_call_target="tpu_custom_call" | custom-call | flops 21849999360 | bytes 1000000 | tf_op jit(solution)/shard_map/expert_body/pallas_call | solution.py:1056
  145.9 3.6 %all-to-all-start.2 = ((bf16[32,40,512]{2,1,0:T(8,128)(2,1)}), bf16[32,40,512]{2,1,0:T(8,128)(2,1)}, u32[]{:S(2)}, u32[]{:S(2)}) async-start(bf16[32,40,512]{2,1,0:T(8,128)(2,1)} %bitcast.67), calls=%async_computation.2 | async-start | bytes 2621440 | tf_op jit(solution)/shard_map/all_to_all | solution.py:980
  149.4 11.7 %weight_grad_body.1 = (bf16[1024,512]{1,0:T(8,128)(2,1)}, bf16[1024,512]{1,0:T(8,128)(2,1)}, f32[1024,512]{1,0:T(8,128)}, f32[1024,512]{1,0:T(8,128)}) custom-call(bf16[1280,2048]{1,0:T(8,128)(2,1)} %get-tuple-element.429.hidden_ref, bf16[1280,2048]{1,0:T(8,128)(2,1)} %get-tuple-element.430.active_ref, bf16[1280,512]{1,0:T(8,128)(2,1)} %bitcast.15.got_ref, ...), custom_call_target="tpu_custom_call" | custom-call | flops 11500000256 | bytes 1000000 | tf_op jit(solution)/shard_map/weight_grad_body/pallas_call | solution.py:1075
  165.6 6.5 %sum_put_body.7 = (bf16[640,512]{1,0:T(8,128)(2,1)}, bf16[640,512]{1,0:T(8,128)(2,1)}) custom-call(s32[1]{0:T(128)} %constant.192.clone.1.base_ref, s32[8,2048]{1,0:T(8,128)S(1)} %get-tuple-element.832, f32[1024,512]{1,0:T(8,128)} %get-tuple-element.770.refs_0_, f32[1024,512]{1,0:T(8,128)} %get-tuple-element.771.refs_1_, ...), custom_call_target="tpu_custom_call" | custom-call | flops 4600000000 | bytes 1000000 | tf_op jit(solution)/shard_map/sum_put_body/pallas_call | solution.py:1002
  173.7 6.5 %sum_put_body.6 = (bf16[640,512]{1,0:T(8,128)(2,1)}, bf16[640,512]{1,0:T(8,128)(2,1)}) custom-call(s32[1]{0:T(128)} %constant.192.clone.1.base_ref, s32[8,2048]{1,0:T(8,128)S(1)} %get-tuple-element.832, f32[1024,512]{1,0:T(8,128)} %get-tuple-element.770.refs_0_, f32[1024,512]{1,0:T(8,128)} %get-tuple-element.771.refs_1_, ...), custom_call_target="tpu_custom_call" | custom-call | flops 4600000000 | bytes 1000000 | tf_op jit(solution)/shard_map/sum_put_body/pallas_call | solution.py:1002
  181.8 5.8 %middle_body.1 = (f32[512,512]{1,0:T(8,128)}, bf16[512,512]{1,0:T(8,128)(2,1)}, f32[512,128]{1,0:T(8,128)}, f32[8,512]{1,0:T(8,128)}, f32[8,512]{1,0:T(8,128)}) custom-call(bf16[1280,512]{1,0:T(8,128)(2,1)} %bitcast.22.back_ref, s32[512,8]{1,0:T(8,128)} %get-tuple-element.441.pos_ref, f32[512,512]{1,0:T(8,128)} %get-tuple-element.442.residual_ref, ...), custom_call_target="tpu_custom_call" | custom-call | flops 6899999744 | bytes 1000000 | tf_op jit(solution)/shard_map/middle_body/pallas_call | solution.py:1090
  190.3 14.5 %inner_body.1 = (bf16[512,512]{1,0:T(8,128)(2,1)}, f32[2,512,512]{2,1,0:T(8,128)}, bf16[544,512]{1,0:T(8,128)(2,1)}) custom-call(bf16[1024,1536]{1,0:T(8,128)(2,1)} %get-tuple-element.427.qkv_ref, bf16[512,512]{1,0:T(8,128)(2,1)} %get-tuple-element.444.out_grad_ref, f32[512,128]{1,0:T(8,128)} %get-tuple-element.445.lse_ref, ...), custom_call_target="tpu_custom_call" | custom-call | flops 17250000896 | bytes 1000000 | tf_op jit(solution)/shard_map/inner_body/pallas_call | solution.py:1100
  206.4 5.3 %all-to-all-start.3 = ((bf16[32,40,512]{2,1,0:T(8,128)(2,1)}), bf16[32,40,512]{2,1,0:T(8,128)(2,1)}, u32[]{:S(2)}, u32[]{:S(2)}) async-start(bf16[32,40,512]{2,1,0:T(8,128)(2,1)} %bitcast.64), calls=%async_computation.3 | async-start | bytes 2621440 | tf_op jit(solution)/shard_map/all_to_all | solution.py:980
  211.8 11.5 %outer_body.1 = (bf16[512,512]{1,0:T(8,128)(2,1)}, bf16[512,512]{1,0:T(8,128)(2,1)}, bf16[512,512]{1,0:T(8,128)(2,1)}, bf16[560,512]{1,0:T(8,128)(2,1)}, f32[512,512]{1,0:T(8,128)}) custom-call(bf16[1024,1536]{1,0:T(8,128)(2,1)} %get-tuple-element.427.qkv_ref, bf16[512,512]{1,0:T(8,128)(2,1)} %collective-permute-done.33.out_grad_ref, f32[16,512]{1,0:T(8,128)} %copy-done.19, ...), custom_call_target="tpu_custom_call" | custom-call | flops 1000000 | bytes 1000 | tf_op jit(solution)/shard_map/outer_body/pallas_call | solution.py:1107
  226.9 4.7 %collective-permute-done.35.refs_3_ = bf16[640,512]{1,0:T(8,128)(2,1)} collective-permute-done((bf16[640,512]{1,0:T(8,128)(2,1)}, bf16[640,512]{1,0:T(8,128)(2,1)}, u32[]{:S(2)}, u32[]{:S(2)}) %collective-permute-start.35) | collective-permute-done | bytes 655392 | tf_op jit(solution)/shard_map/ppermute | solution.py:884
  231.7 5.8 %spread_body.2 = (bf16[544,512]{1,0:T(8,128)(2,1)}, bf16[544,512]{1,0:T(8,128)(2,1)}) custom-call(s32[1,2096]{1,0:T(1,128)} %broadcast_in_dim.33.pos_ref, bf16[512,512]{1,0:T(8,128)(2,1)} %get-tuple-element.460.refs_0_, bf16[512,512]{1,0:T(8,128)(2,1)} %get-tuple-element.461.refs_1_, bf16[512,512]{1,0:T(8,128)(2,1)} %get-tuple-element.462.refs_2_, ...), custom_call_target="tpu_custom_call" | custom-call | flops 1000000 | bytes 1000 | tf_op jit(solution)/shard_map/spread_body/pallas_call | solution.py:1122
  239.9 4.0 %tokens_body.1 = f32[512,512]{1,0:T(8,128)} custom-call(f32[512,512]{1,0:T(8,128)} %get-tuple-element.469.grad_normed_ref, bf16[512,512]{1,0:T(8,128)(2,1)} %bitcast.63, bf16[2080,512]{1,0:T(8,128)(2,1)} %unpack_body.3.w_ref, f32[512,512]{1,0:T(8,128)} %get-tuple-element.447.grad_ref), custom_call_target="tpu_custom_call" | custom-call | flops 1000000 | bytes 1000 | tf_op jit(solution)/shard_map/tokens_body/pallas_call | solution.py:1130
  243.9 5.8 %spread_body.3 = (bf16[544,512]{1,0:T(8,128)(2,1)}, bf16[544,512]{1,0:T(8,128)(2,1)}) custom-call(s32[1,2096]{1,0:T(1,128)} %broadcast_in_dim.33.pos_ref, bf16[512,512]{1,0:T(8,128)(2,1)} %get-tuple-element.460.refs_0_, bf16[512,512]{1,0:T(8,128)(2,1)} %get-tuple-element.461.refs_1_, bf16[512,512]{1,0:T(8,128)(2,1)} %get-tuple-element.462.refs_2_, ...), custom_call_target="tpu_custom_call" | custom-call | flops 1000000 | bytes 1000 | tf_op jit(solution)/shard_map/spread_body/pallas_call | solution.py:1122
  249.7 2.6 collective-permute-done.42.got_a
  252.3 2.8 step_body.1
  264.9 3.7 %collective-permute-start.49 = (bf16[136,512]{1,0:T(8,128)(2,1)}, bf16[136,512]{1,0:T(8,128)(2,1)}, u32[]{:S(2)}, u32[]{:S(2)}) collective-permute-start(bf16[136,512]{1,0:T(8,128)(2,1)} %get-tuple-element.558), channel_id=1, source_target_pairs={{0,2},{1,3},{2,0},{3,1},{4,6},{5,7},{6,4},{7,5},{8,10},{9,11},{10,... | collective-permute-start | bytes 417800 | tf_op jit(solution)/shard_map/ppermute | solution.py:893
  269.4 4.2 %mixture_body.1 = bf16[512,512]{1,0:T(8,128)(2,1)} custom-call(bf16[1280,512]{1,0:T(8,128)(2,1)} %bitcast.25.result_ref, s32[512,8]{1,0:T(8,128)} %get-tuple-element.441.pos_ref, s32[512,2]{1,0:T(8,128)} %bitcast.59, f32[512,16]{1,0:T(8,128)} %get-tuple-element.478.prob_ref, f32[512,512]{1,0:T(8,128)} %get-tuple-element.442.residual_ref), custom_call_target="tpu_custom_call" | custom-call | flops 1000000 | bytes 1000 | tf_op jit(solution)/shard_map/mixture_body/pallas_call | solution.py:1144
  273.7 14.5 %adam_body.1 = (f32[2048,512]{1,0:T(8,128)}, f32[2048,512]{1,0:T(8,128)}, f32[2048,512]{1,0:T(8,128)}, f32[2048,512]{1,0:T(8,128)}) custom-call(s32[2048,8]{1,0:T(8,128)S(1)} %get-tuple-element.816, bf16[640,512]{1,0:T(8,128)(2,1)} %get-tuple-element.480.refs_0_, bf16[640,512]{1,0:T(8,128)(2,1)} %collective-permute-done.36.refs_1_, ...), custom_call_target="tpu_custom_call" | custom-call | flops 1000000 | bytes 1000 | tf_op jit(solution)/shard_map/adam_body/pallas_call | solution.py:1149
  (162 shorter events, 69.4 us)
Async XLA Ops:
  1.6 17.6 %collective-permute-start.15 = (bf16[136,512]{1,0:T(8,128)(2,1)S(1)}, bf16[136,512]{1,0:T(8,128)(2,1)S(1)}, u32[]{:S(2)}, u32[]{:S(2)}) collective-permute-start(bf16[136,512]{1,0:T(8,128)(2,1)S(1)} %pad.8), channel_id=1, source_target_pairs={{0,3},{1,0},{2,1},{3,2},{4,7},{5,4},{6,5},{7,6},{8,11},{9,8},{10,9... | collective-permute-start | bytes 417800 | tf_op jit(solution)/shard_map/ppermute | solution.py:893
  6.7 11.8 %collective-permute-start.14 = (bf16[136,512]{1,0:T(8,128)(2,1)S(1)}, bf16[136,512]{1,0:T(8,128)(2,1)S(1)}, u32[]{:S(2)}, u32[]{:S(2)}) collective-permute-start(bf16[136,512]{1,0:T(8,128)(2,1)S(1)} %pad.8), channel_id=1, source_target_pairs={{0,2},{1,3},{2,0},{3,1},{4,6},{5,7},{6,4},{7,5},{8,10},{9,11},{10,... | collective-permute-start | bytes 417800 | tf_op jit(solution)/shard_map/ppermute | solution.py:893
  6.7 9.9 %collective-permute-start.12 = (bf16[136,512]{1,0:T(8,128)(2,1)S(1)}, bf16[136,512]{1,0:T(8,128)(2,1)S(1)}, u32[]{:S(2)}, u32[]{:S(2)}) collective-permute-start(bf16[136,512]{1,0:T(8,128)(2,1)S(1)} %pad.8), channel_id=1, source_target_pairs={{0,1},{1,2},{2,3},{3,0},{4,5},{5,6},{6,7},{7,4},{8,9},{9,10},{10,1... | collective-permute-start | bytes 417800 | tf_op jit(solution)/shard_map/ppermute | solution.py:893
  7.7 20.0 %collective-permute-start.17 = (s32[1,512]{1,0:T(1,128)}, s32[1,512]{1,0:T(1,128)S(1)}, u32[]{:S(2)}, u32[]{:S(2)}) collective-permute-start(s32[1,512]{1,0:T(1,128)} %param.19), channel_id=1, source_target_pairs={{0,4},{4,0},{1,5},{5,1},{2,6},{6,2},{3,7},{7,3},{8,12},{12,8},{9,1... | collective-permute-start | bytes 6152 | tf_op jit(solution)/shard_map/ppermute | solution.py:876
  10.0 22.2 %collective-permute-start.11 = (bf16[512,512]{1,0:T(8,128)(2,1)}, bf16[512,512]{1,0:T(8,128)(2,1)S(1)}, u32[]{:S(2)}, u32[]{:S(2)}) collective-permute-start(bf16[512,512]{1,0:T(8,128)(2,1)} %bitcast.60), channel_id=1, source_target_pairs={{0,4},{4,0},{1,5},{5,1},{2,6},{6,2},{3,7},{7,3},{8,12},{12,8},{9,1... | collective-permute-start | bytes 1572872 | tf_op jit(solution)/shard_map/ppermute | solution.py:876
  16.6 11.7 %collective-permute-start.13 = (bf16[272,512]{1,0:T(8,128)(2,1)S(1)}, bf16[272,512]{1,0:T(8,128)(2,1)S(1)}, u32[]{:S(2)}, u32[]{:S(2)}) collective-permute-start(bf16[272,512]{1,0:T(8,128)(2,1)S(1)} %pad_maximum_fusion.9), channel_id=1, source_target_pairs={{0,16},{16,0},{8,24},{24,8},{1,17},{17,1},{9,25},{25,9},{2,18},{18... | collective-permute-start | bytes 835592 | tf_op jit(solution)/shard_map/ppermute | solution.py:880
  29.1 16.9 %collective-permute-start.20 = (bf16[544,512]{1,0:T(8,128)(2,1)}, bf16[544,512]{1,0:T(8,128)(2,1)}, u32[]{:S(2)}, u32[]{:S(2)}) collective-permute-start(bf16[544,512]{1,0:T(8,128)(2,1)} %pad_maximum_fusion.8.refs_0_), channel_id=1, source_target_pairs={{0,8},{8,0},{16,24},{24,16},{1,9},{9,1},{17,25},{25,17},{2,10},{10... | collective-permute-start | bytes 1671176 | tf_op jit(solution)/shard_map/ppermute | solution.py:888
  29.2 25.9 %collective-permute-start.18 = (bf16[544,512]{1,0:T(8,128)(2,1)}, bf16[544,512]{1,0:T(8,128)(2,1)}, u32[]{:S(2)}, u32[]{:S(2)}) collective-permute-start(bf16[544,512]{1,0:T(8,128)(2,1)} %pad_maximum_fusion.8.refs_0_), channel_id=1, source_target_pairs={{0,4},{4,0},{1,5},{5,1},{2,6},{6,2},{3,7},{7,3},{8,12},{12,8},{9,1... | collective-permute-start | bytes 1671176 | tf_op jit(solution)/shard_map/ppermute | solution.py:876
  30.4 15.7 %collective-permute-start.21 = (bf16[544,512]{1,0:T(8,128)(2,1)}, bf16[544,512]{1,0:T(8,128)(2,1)}, u32[]{:S(2)}, u32[]{:S(2)}) collective-permute-start(bf16[544,512]{1,0:T(8,128)(2,1)} %constant_dynamic-update-slice_fusion.2.refs_1_), channel_id=1, source_target_pairs={{0,8},{8,0},{16,24},{24,16},{1,9},{9,1},{17,25},{25,17},{2,10},{10... | collective-permute-start | bytes 1671176 | tf_op jit(solution)/shard_map/ppermute | solution.py:888
  30.6 24.4 %collective-permute-start.19 = (bf16[544,512]{1,0:T(8,128)(2,1)}, bf16[544,512]{1,0:T(8,128)(2,1)}, u32[]{:S(2)}, u32[]{:S(2)}) collective-permute-start(bf16[544,512]{1,0:T(8,128)(2,1)} %constant_dynamic-update-slice_fusion.2.refs_1_), channel_id=1, source_target_pairs={{0,16},{16,0},{8,24},{24,8},{1,17},{17,1},{9,25},{25,9},{2,18},{18... | collective-permute-start | bytes 1671176 | tf_op jit(solution)/shard_map/ppermute | solution.py:880
  36.5 39.2 %all-to-all-start = ((bf16[32,40,512]{2,1,0:T(8,128)(2,1)}), bf16[32,40,512]{2,1,0:T(8,128)(2,1)}, u32[]{:S(2)}, u32[]{:S(2)}) async-start(bf16[32,40,512]{2,1,0:T(8,128)(2,1)} %bitcast.66), calls=%async_computation | async-start | bytes 2621440 | tf_op jit(solution)/shard_map/all_to_all | solution.py:980
  55.0 10.7 %collective-permute-start.22 = (bf16[544,512]{1,0:T(8,128)(2,1)}, bf16[544,512]{1,0:T(8,128)(2,1)S(1)}, u32[]{:S(2)}, u32[]{:S(2)}) collective-permute-start(bf16[544,512]{1,0:T(8,128)(2,1)} %collective-permute-done.18.refs_0_), channel_id=1, source_target_pairs={{0,8},{8,0},{16,24},{24,16},{1,9},{9,1},{17,25},{25,17},{2,10},{10... | collective-permute-start | bytes 1671176 | tf_op jit(solution)/shard_map/ppermute | solution.py:888
  55.4 10.2 %collective-permute-start.23 = (bf16[544,512]{1,0:T(8,128)(2,1)}, bf16[544,512]{1,0:T(8,128)(2,1)}, u32[]{:S(2)}, u32[]{:S(2)}) collective-permute-start(bf16[544,512]{1,0:T(8,128)(2,1)} %collective-permute-done.19.refs_1_), channel_id=1, source_target_pairs={{0,8},{8,0},{16,24},{24,16},{1,9},{9,1},{17,25},{25,17},{2,10},{10... | collective-permute-start | bytes 1671176 | tf_op jit(solution)/shard_map/ppermute | solution.py:888
  62.2 32.6 %collective-permute-start.24 = (bf16[640,512]{1,0:T(8,128)(2,1)}, bf16[640,512]{1,0:T(8,128)(2,1)}, u32[]{:S(2)}, u32[]{:S(2)}) collective-permute-start(bf16[640,512]{1,0:T(8,128)(2,1)} %get-tuple-element.411), channel_id=1, source_target_pairs={{0,4},{4,0},{1,5},{5,1},{2,6},{6,2},{3,7},{7,3},{8,12},{12,8},{9,1... | collective-permute-start | bytes 1966088 | tf_op jit(solution)/shard_map/ppermute | solution.py:876
  64.0 30.7 %collective-permute-start.25 = (bf16[640,512]{1,0:T(8,128)(2,1)}, bf16[640,512]{1,0:T(8,128)(2,1)}, u32[]{:S(2)}, u32[]{:S(2)}) collective-permute-start(bf16[640,512]{1,0:T(8,128)(2,1)} %get-tuple-element.412), channel_id=1, source_target_pairs={{0,16},{16,0},{8,24},{24,8},{1,17},{17,1},{9,25},{25,9},{2,18},{18... | collective-permute-start | bytes 1966088 | tf_op jit(solution)/shard_map/ppermute | solution.py:880
  65.5 32.5 %collective-permute-start.26 = (bf16[640,512]{1,0:T(8,128)(2,1)}, bf16[640,512]{1,0:T(8,128)(2,1)}, u32[]{:S(2)}, u32[]{:S(2)}) collective-permute-start(bf16[640,512]{1,0:T(8,128)(2,1)} %get-tuple-element.413), channel_id=1, source_target_pairs={{0,20},{4,16},{8,28},{12,24},{16,4},{20,0},{24,12},{28,8},{1,21},{... | collective-permute-start | bytes 1966088 | tf_op jit(solution)/shard_map/ppermute | solution.py:884
  88.3 38.8 %all-to-all-start.1 = ((bf16[32,40,512]{2,1,0:T(8,128)(2,1)}), bf16[32,40,512]{2,1,0:T(8,128)(2,1)}, u32[]{:S(2)}, u32[]{:S(2)}) async-start(bf16[32,40,512]{2,1,0:T(8,128)(2,1)} %bitcast.65), calls=%async_computation.1 | async-start | bytes 2621440 | tf_op jit(solution)/shard_map/all_to_all | solution.py:980
  145.9 35.9 %all-to-all-start.2 = ((bf16[32,40,512]{2,1,0:T(8,128)(2,1)}), bf16[32,40,512]{2,1,0:T(8,128)(2,1)}, u32[]{:S(2)}, u32[]{:S(2)}) async-start(bf16[32,40,512]{2,1,0:T(8,128)(2,1)} %bitcast.67), calls=%async_computation.2 | async-start | bytes 2621440 | tf_op jit(solution)/shard_map/all_to_all | solution.py:980
  172.2 39.6 %collective-permute-start.36 = (bf16[640,512]{1,0:T(8,128)(2,1)}, bf16[640,512]{1,0:T(8,128)(2,1)}, u32[]{:S(2)}, u32[]{:S(2)}) collective-permute-start(bf16[640,512]{1,0:T(8,128)(2,1)} %get-tuple-element.437), channel_id=1, source_target_pairs={{0,4},{4,0},{1,5},{5,1},{2,6},{6,2},{3,7},{7,3},{8,12},{12,8},{9,1... | collective-permute-start | bytes 1966088 | tf_op jit(solution)/shard_map/ppermute | solution.py:876
  180.3 31.5 %collective-permute-start.37 = (bf16[640,512]{1,0:T(8,128)(2,1)}, bf16[640,512]{1,0:T(8,128)(2,1)}, u32[]{:S(2)}, u32[]{:S(2)}) collective-permute-start(bf16[640,512]{1,0:T(8,128)(2,1)} %get-tuple-element.438), channel_id=1, source_target_pairs={{0,16},{16,0},{8,24},{24,8},{1,17},{17,1},{9,25},{25,9},{2,18},{18... | collective-permute-start | bytes 1966088 | tf_op jit(solution)/shard_map/ppermute | solution.py:880
  188.3 16.6 %collective-permute-start.34 = (f32[16,512]{1,0:T(8,128)S(1)}, f32[16,512]{1,0:T(8,128)S(1)}, u32[]{:S(2)}, u32[]{:S(2)}) collective-permute-start(f32[16,512]{1,0:T(8,128)S(1)} %pad_maximum_fusion.10), channel_id=1, source_target_pairs={{0,4},{4,0},{1,5},{5,1},{2,6},{6,2},{3,7},{7,3},{8,12},{12,8},{9,1... | collective-permute-start | bytes 98312 | tf_op jit(solution)/shard_map/ppermute | solution.py:876
  188.9 16.0 %collective-permute-start.33 = (bf16[512,512]{1,0:T(8,128)(2,1)}, bf16[512,512]{1,0:T(8,128)(2,1)}, u32[]{:S(2)}, u32[]{:S(2)}) collective-permute-start(bf16[512,512]{1,0:T(8,128)(2,1)} %get-tuple-element.444.out_grad_ref), channel_id=1, source_target_pairs={{0,4},{4,0},{1,5},{5,1},{2,6},{6,2},{3,7},{7,3},{8,12},{12,8},{9,1... | collective-permute-start | bytes 1572872 | tf_op jit(solution)/shard_map/ppermute | solution.py:876
  204.9 26.7 %collective-permute-start.35 = (bf16[640,512]{1,0:T(8,128)(2,1)}, bf16[640,512]{1,0:T(8,128)(2,1)}, u32[]{:S(2)}, u32[]{:S(2)}) collective-permute-start(bf16[640,512]{1,0:T(8,128)(2,1)} %get-tuple-element.454), channel_id=1, source_target_pairs={{0,20},{4,16},{8,28},{12,24},{16,4},{20,0},{24,12},{28,8},{1,21},{... | collective-permute-start | bytes 1966088 | tf_op jit(solution)/shard_map/ppermute | solution.py:884
  206.4 63.1 %all-to-all-start.3 = ((bf16[32,40,512]{2,1,0:T(8,128)(2,1)}), bf16[32,40,512]{2,1,0:T(8,128)(2,1)}, u32[]{:S(2)}, u32[]{:S(2)}) async-start(bf16[32,40,512]{2,1,0:T(8,128)(2,1)} %bitcast.64), calls=%async_computation.3 | async-start | bytes 2621440 | tf_op jit(solution)/shard_map/all_to_all | solution.py:980
  237.4 14.9 %collective-permute-start.42 = (bf16[544,512]{1,0:T(8,128)(2,1)}, bf16[544,512]{1,0:T(8,128)(2,1)}, u32[]{:S(2)}, u32[]{:S(2)}) collective-permute-start(bf16[544,512]{1,0:T(8,128)(2,1)} %get-tuple-element.464), channel_id=1, source_target_pairs={{0,4},{4,0},{1,5},{5,1},{2,6},{6,2},{3,7},{7,3},{8,12},{12,8},{9,1... | collective-permute-start | bytes 1671176 | tf_op jit(solution)/shard_map/ppermute | solution.py:876
  238.2 14.1 %collective-permute-start.43 = (bf16[544,512]{1,0:T(8,128)(2,1)}, bf16[544,512]{1,0:T(8,128)(2,1)}, u32[]{:S(2)}, u32[]{:S(2)}) collective-permute-start(bf16[544,512]{1,0:T(8,128)(2,1)} %get-tuple-element.465), channel_id=1, source_target_pairs={{0,16},{16,0},{8,24},{24,8},{1,17},{17,1},{9,25},{25,9},{2,18},{18... | collective-permute-start | bytes 1671176 | tf_op jit(solution)/shard_map/ppermute | solution.py:880
  256.3 12.4 %collective-permute-start.44 = (bf16[272,512]{1,0:T(8,128)(2,1)}, bf16[272,512]{1,0:T(8,128)(2,1)S(1)}, u32[]{:S(2)}, u32[]{:S(2)}) collective-permute-start(bf16[272,512]{1,0:T(8,128)(2,1)} %get-tuple-element.474), channel_id=1, source_target_pairs={{0,16},{16,0},{8,24},{24,8},{1,17},{17,1},{9,25},{25,9},{2,18},{18... | collective-permute-start | bytes 835592 | tf_op jit(solution)/shard_map/ppermute | solution.py:880
  261.5 12.2 %collective-permute-start.48 = (bf16[640,512]{1,0:T(8,128)(2,1)}, bf16[640,512]{1,0:T(8,128)(2,1)}, u32[]{:S(2)}, u32[]{:S(2)}) collective-permute-start(bf16[640,512]{1,0:T(8,128)(2,1)} %pad_maximum_fusion.7), channel_id=1, source_target_pairs={{0,8},{8,0},{16,24},{24,16},{1,9},{9,1},{17,25},{25,17},{2,10},{10... | collective-permute-start | bytes 1966088 | tf_op jit(solution)/shard_map/ppermute | solution.py:888
  262.4 11.3 %collective-permute-start.47 = (bf16[640,512]{1,0:T(8,128)(2,1)}, bf16[640,512]{1,0:T(8,128)(2,1)}, u32[]{:S(2)}, u32[]{:S(2)}) collective-permute-start(bf16[640,512]{1,0:T(8,128)(2,1)} %pad_maximum_fusion.6), channel_id=1, source_target_pairs={{0,8},{8,0},{16,24},{24,16},{1,9},{9,1},{17,25},{25,17},{2,10},{10... | collective-permute-start | bytes 1966088 | tf_op jit(solution)/shard_map/ppermute | solution.py:888
  263.7 24.5 %collective-permute-start.50 = (bf16[136,512]{1,0:T(8,128)(2,1)}, bf16[136,512]{1,0:T(8,128)(2,1)}, u32[]{:S(2)}, u32[]{:S(2)}) collective-permute-start(bf16[136,512]{1,0:T(8,128)(2,1)} %get-tuple-element.557), channel_id=1, source_target_pairs={{0,1},{1,2},{2,3},{3,0},{4,5},{5,6},{6,7},{7,4},{8,9},{9,10},{10,1... | collective-permute-start | bytes 417800 | tf_op jit(solution)/shard_map/ppermute | solution.py:893
  264.9 23.2 %collective-permute-start.49 = (bf16[136,512]{1,0:T(8,128)(2,1)}, bf16[136,512]{1,0:T(8,128)(2,1)}, u32[]{:S(2)}, u32[]{:S(2)}) collective-permute-start(bf16[136,512]{1,0:T(8,128)(2,1)} %get-tuple-element.558), channel_id=1, source_target_pairs={{0,2},{1,3},{2,0},{3,1},{4,6},{5,7},{6,4},{7,5},{8,10},{9,11},{10,... | collective-permute-start | bytes 417800 | tf_op jit(solution)/shard_map/ppermute | solution.py:893
  269.4 18.7 %collective-permute-start.46 = (bf16[136,512]{1,0:T(8,128)(2,1)}, bf16[136,512]{1,0:T(8,128)(2,1)}, u32[]{:S(2)}, u32[]{:S(2)}) collective-permute-start(bf16[136,512]{1,0:T(8,128)(2,1)} %get-tuple-element.559), channel_id=1, source_target_pairs={{0,3},{1,0},{2,1},{3,2},{4,7},{5,4},{6,5},{7,6},{8,11},{9,8},{10,9... | collective-permute-start | bytes 417800 | tf_op jit(solution)/shard_map/ppermute | solution.py:893
  (30 other events, 240.3 us)

commit v6 on v5

--- a/solution.py
+++ b/solution.py
@@ -611,13 +611,12 @@
 
 
 def middle_body(
-    n_exp, back_ref, pos_ref, residual_ref, cot_ref, keep_ref, attended_ref, w_ref,
+    back_ref, pos_ref, residual_ref, cot_ref, keep_ref, attended_ref, w_ref, gains_ref,
     grad_ref, out_grad_ref, delta_col_ref, delta_row_ref, gain_ref,
 ):
     toks, width = residual_ref.shape
-    router = 4 * width
     slots = back_ref.shape[0]
-    gain_two = w_ref[router + n_exp : router + n_exp + 16, :].astype(F32)[1:2, :]
+    gain_two = gains_ref[...].astype(F32)[1:2, :]
     spots = iota((toks, slots), 1)
     picks = as_bf16((spots == pos_ref[:, 0:1]) | (spots == pos_ref[:, 1:2]))
     grad_mixed = dot_nn(picks, back_ref[...])
@@ -629,7 +628,7 @@
     grad = grad_rows + norm_back(hat, scale, gain_two, grad_mixed)
     grad_ref[...] = grad
     low = grad.astype(BF16)
-    out_grad = dot_nt(low, w_ref[3 * width : 4 * width, :]).astype(BF16)
+    out_grad = dot_nt(low, w_ref[...]).astype(BF16)
     out_grad_ref[...] = out_grad
     product = out_grad.astype(F32) * attended_ref[...]
     delta = jnp.zeros((toks, LANES), F32)
@@ -859,11 +858,12 @@
     slots = result_ref.shape[0]
     share = prob_ref[...]
     total = residual_ref[...]
+    picks = [as_bf16(iota((toks, slots), 1) == pos_ref[:, number : number + 1]) for number in range(2)]
+    picked = dot_nn(jnp.concatenate(picks, axis=0), result_ref[...])
     for number in range(2):
-        picks = as_bf16(iota((toks, slots), 1) == pos_ref[:, number : number + 1])
         mine = iota(share.shape, 1) == ids_ref[:, number : number + 1]
         gate = jnp.sum(jnp.where(mine, share, 0.0), axis=-1, keepdims=True)
-        total = total + gate * dot_nn(picks, result_ref[...])
+        total = total + gate * picked[number * toks : (number + 1) * toks, :]
     out_ref[...] = total.astype(BF16)
 
 
@@ -1088,13 +1088,17 @@
     back_got = after([back_got], *moved)[0]
 
     grad_residual, out_grad, delta_col, delta_row, gain_two = kernel_call(
-        functools.partial(middle_body, n_exp),
+        middle_body,
         (
             sds((toks, width), F32), sds((toks, width), BF16), sds((toks, LANES), F32),
             sds((8, toks), F32), sds((8, width), F32),
         ),
         cost=(6 * MICRO, 1e6),
-    )(back_got, pos_col, residual, cotangent[0], keep_col, attended, weights)
+        grid=(1,),
+        in_specs=[vmem] * 6
+        + [pl.BlockSpec((width, width), lambda i: (3, 0)), pl.BlockSpec((16, width), lambda i: (gain_at // 16, 0))],
+        out_specs=[vmem] * 5,
+    )(back_got, pos_col, residual, cotangent[0], keep_col, attended, weights, weights)
     out_grad_other = swap_x(out_grad)
     sums_other = swap_x(jnp.concatenate([lse_row, delta_row], axis=0))
     query_grad, kv_grad, early = kernel_call(

time: 296 us -> 297 us (level)
  no operation moved by 1% of the time
where the time goes in v6:
time: 297 us; the launch traced here: 292 us
  Pallas kernels  165 us (56%)
  starting transfers between devices  60.1 us (20%)
  waiting for transfers between devices  28.1 us (9%)
  local copies, waits for them, and re-layouts  25.5 us (9%)
  other arithmetic  11.6 us (4%)
    pallas_call x4, Pallas kernels, with_base(): kernel_call(body, out_shape, scratch, in_specs=[smem] + [vmem] * len(arra...  28.7 us
    all_to_all x4, starting transfers between devices, exchange(): lax.all_to_all(rows, everyone, split_axis=0, concat_axis=0, tiled=True)  21 us
    pallas_call x1, Pallas kernels, on_chip_experts(): kernel_call(functools.partial(expert_body, n_exp), (sds((slots, FF), BF16...  18.8 us
    pallas_call x2, Pallas kernels, unpack(): kernel_call(functools.partial(unpack_body, spots, len(earlier)), sds((row...  18.2 us
    pallas_call x1, Pallas kernels, on_chip_experts(): kernel_call(functools.partial(inner_body, n_exp), (sds((toks, width), BF1...  14.5 us
    pallas_call x1, Pallas kernels, on_chip_experts(): kernel_call(functools.partial(adam_body, len(moved)), [sds((owned, width)...  14.5 us
    pallas_call x1, Pallas kernels, on_chip_experts(): kernel_call(functools.partial(forward_body, n_exp), (sds((2 * toks, 3 * w...  12.5 us
    ppermute x10, starting transfers between devices, swap_x(): return lax.ppermute(value, 'ctx', SWAP)  12.1 us
  transfers between devices with their start and end apart: 44, of which 11 were waited for; matrix products, arithmetic and copies ran while one was open for 11% of the time, Pallas kernels for 50%

profile of v6, /device:TPU:0, one launch (start us, length us, event | category | flops | bytes accessed | tf_op | source)
XLA Modules:
  0.0 292.4 jit_solution(5617226739660707558)
XLA Ops:
  1.6 5.1 %collective-permute-start.15 = (bf16[136,512]{1,0:T(8,128)(2,1)S(1)}, bf16[136,512]{1,0:T(8,128)(2,1)S(1)}, u32[]{:S(2)}, u32[]{:S(2)}) collective-permute-start(bf16[136,512]{1,0:T(8,128)(2,1)S(1)} %pad.8), channel_id=1, source_target_pairs={{0,3},{1,0},{2,1},{3,2},{4,7},{5,4},{6,5},{7,6},{8,11},{9,8},{10,9... | collective-permute-start | bytes 417800 | tf_op jit(solution)/shard_map/ppermute | solution.py:893
  10.6 6.0 %collective-permute-done.12 = bf16[136,512]{1,0:T(8,128)(2,1)S(1)} collective-permute-done((bf16[136,512]{1,0:T(8,128)(2,1)S(1)}, bf16[136,512]{1,0:T(8,128)(2,1)S(1)}, u32[]{:S(2)}, u32[]{:S(2)}) %collective-permute-start.12) | collective-permute-done | bytes 139296 | tf_op jit(solution)/shard_map/ppermute | solution.py:893
  32.9 3.6 %route_body.1 = (s32[8,512]{1,0:T(8,128)}, s32[512,8]{1,0:T(8,128)}, bf16[1280,512]{1,0:T(8,128)(2,1)}) custom-call(s32[2,512]{1,0:T(2,128)} %copy.27.ids_ref, f32[1,512]{1,0:T(1,128)} %convert_element_type.59.prio_ref, f32[1,512]{1,0:T(1,128)} %copy-done.21, bf16[512,512]{1,0:T(8,128)(2,1)} %bitcast.75), custom_call_target="tpu_custom_call" | custom-call | flops 4600000000 | bytes 1000000 | tf_op jit(solution)/shard_map/route_body/pallas_call | solution.py:973
  36.5 6.2 %all-to-all-start = ((bf16[32,40,512]{2,1,0:T(8,128)(2,1)}), bf16[32,40,512]{2,1,0:T(8,128)(2,1)}, u32[]{:S(2)}, u32[]{:S(2)}) async-start(bf16[32,40,512]{2,1,0:T(8,128)(2,1)} %bitcast.66), calls=%async_computation | async-start | bytes 2621440 | tf_op jit(solution)/shard_map/all_to_all | solution.py:980
  42.7 3.4 %plan_body.1 = (s32[8,2048]{1,0:T(8,128)S(1)}, s32[2048,8]{1,0:T(8,128)S(1)}, s32[8,128]{1,0:T(8,128)}) custom-call(s32[1]{0:T(128)} %bitcast.16.me_ref, s32[8,2048]{1,0:T(8,128)} %bitcast.71), custom_call_target="tpu_custom_call" | custom-call | flops 5750000128 | bytes 1000000 | tf_op jit(solution)/shard_map/plan_body/pallas_call | solution.py:994
  46.1 8.9 %unpack_body.2.refs_4_ = bf16[2080,512]{1,0:T(8,128)(2,1)} custom-call(s32[2080,1]{1,0:T(8,128)} %broadcast_in_dim.40.pos_ref, bf16[544,512]{1,0:T(8,128)(2,1)} %pad_maximum_fusion.8.refs_0_, bf16[544,512]{1,0:T(8,128)(2,1)} %constant_dynamic-update-slice_fusion.2.refs_1_, bf16[544,512]{1,0:T(8,128)(2,1)} %collective-permute-done.20.refs_2_, ...), custom_call_target="tpu_custom_call" | custom-call | flops 8049999872 | bytes 1000000 | tf_op jit(solution)/shard_map/unpack_body/pallas_call | solution.py:951
  55.6 6.6 %put_body.5 = (bf16[640,512]{1,0:T(8,128)(2,1)}, bf16[640,512]{1,0:T(8,128)(2,1)}, bf16[640,512]{1,0:T(8,128)(2,1)}, bf16[640,512]{1,0:T(8,128)(2,1)}) custom-call(s32[1]{0:T(128)} %constant.192.clone.1.base_ref, s32[8,2048]{1,0:T(8,128)S(1)} %get-tuple-element.405.pos_ref, bf16[2048,512]{1,0:T(8,128)(2,1)S(1)} %bitcast.52), custom_call_target="tpu_custom_call" | custom-call | flops 9200000000 | bytes 1000000 | tf_op jit(solution)/shard_map/put_body/pallas_call | solution.py:1002
  66.5 9.3 %unpack_body.3.w_ref.gains_ref = bf16[2080,512]{1,0:T(8,128)(2,1)} custom-call(s32[2080,1]{1,0:T(8,128)} %broadcast_in_dim.40.pos_ref, bf16[544,512]{1,0:T(8,128)(2,1)} %collective-permute-done.18.refs_0_, bf16[544,512]{1,0:T(8,128)(2,1)} %collective-permute-done.19.refs_1_, bf16[544,512]{1,0:T(8,128)(2,1)} %copy-done.23, ...), custom_call_target="tpu_custom_call" | custom-call | flops 8049999872 | bytes 1000000 | tf_op jit(solution)/shard_map/unpack_body/pallas_call | solution.py:951
  75.8 12.5 %forward_body.1 = (bf16[1024,1536]{1,0:T(8,128)(2,1)}, bf16[512,512]{1,0:T(8,128)(2,1)}, f32[512,512]{1,0:T(8,128)}, f32[512,512]{1,0:T(8,128)}, f32[512,16]{1,0...) custom-call(bf16[512,512]{1,0:T(8,128)(2,1)} %bitcast.61, ...), custom_call_target="tpu_custom_call" | custom-call | flops 14949999616 | bytes 1000000 | tf_op jit(solution)/shard_map/forward_body/pallas_call | solution.py:1026
  88.3 6.5 %all-to-all-start.1 = ((bf16[32,40,512]{2,1,0:T(8,128)(2,1)}), bf16[32,40,512]{2,1,0:T(8,128)(2,1)}, u32[]{:S(2)}, u32[]{:S(2)}) async-start(bf16[32,40,512]{2,1,0:T(8,128)(2,1)} %bitcast.65), calls=%async_computation.1 | async-start | bytes 2621440 | tf_op jit(solution)/shard_map/all_to_all | solution.py:980
  94.7 3.3 %collective-permute-done.26.refs_3_ = bf16[640,512]{1,0:T(8,128)(2,1)} collective-permute-done((bf16[640,512]{1,0:T(8,128)(2,1)}, bf16[640,512]{1,0:T(8,128)(2,1)}, u32[]{:S(2)}, u32[]{:S(2)}) %collective-permute-start.26) | collective-permute-done | bytes 655392 | tf_op jit(solution)/shard_map/ppermute | solution.py:884
  105.3 9.0 %take_body.9 = bf16[2048,512]{1,0:T(8,128)(2,1)} custom-call(s32[1]{0:T(128)} %constant.192.clone.1.base_ref, s32[2048,8]{1,0:T(8,128)S(1)} %get-tuple-element.479.pos_ref, bf16[640,512]{1,0:T(8,128)(2,1)} %get-tuple-element.414.refs_0_, bf16[640,512]{1,0:T(8,128)(2,1)} %collective-permute-done.24.refs_1_, bf16[640,512]{1,0:T(8,128)(2,1)} %collective-permute-done.25.refs_2_, ...), custom_call_target="tpu_custom_call" | custom-call | flops 1000000 | bytes 1000 | tf_op jit(solution)/shard_map/take_body/pallas_call | solution.py:1002
  114.4 3.0 %fusion.32 = (bf16[1024,512]{1,0:T(8,128)(2,1)}, bf16[1024,512]{1,0:T(8,128)(2,1)}) fusion(bf16[2048,512]{1,0:T(8,128)(2,1)} %take_body.9), kind=kLoop, calls=%fused_computation.92 | loop fusion | bytes 4194304 | tf_op jit(solution)/shard_map/slice | solution.py:1039
  121.9 5.1 %all-to-all-done.1 = bf16[32,40,512]{2,1,0:T(8,128)(2,1)} async-done(((bf16[32,40,512]{2,1,0:T(8,128)(2,1)}), bf16[32,40,512]{2,1,0:T(8,128)(2,1)}, u32[]{:S(2)}, u32[]{:S(2)}) %all-to-all-start.1) | async-done | bytes 1310752 | tf_op jit(solution)/shard_map/all_to_all | solution.py:980
  127.0 18.8 %expert_body.1 = (bf16[1280,2048]{1,0:T(8,128)(2,1)}, bf16[1280,2048]{1,0:T(8,128)(2,1)}, bf16[1280,512]{1,0:T(8,128)(2,1)}, bf16[1280,512]{1,0:T(8,128)(2,1)}, ...) custom-call(s32[1]{0:T(128)} %bitcast.7.expert_ref, bf16[1280,512]{1,0:T(8,128)(2,1)} %bitcast.15.got_ref, ...), custom_call_target="tpu_custom_call" | custom-call | flops 21849999360 | bytes 1000000 | tf_op jit(solution)/shard_map/expert_body/pallas_call | solution.py:1056
  145.9 3.6 %all-to-all-start.2 = ((bf16[32,40,512]{2,1,0:T(8,128)(2,1)}), bf16[32,40,512]{2,1,0:T(8,128)(2,1)}, u32[]{:S(2)}, u32[]{:S(2)}) async-start(bf16[32,40,512]{2,1,0:T(8,128)(2,1)} %bitcast.67), calls=%async_computation.2 | async-start | bytes 2621440 | tf_op jit(solution)/shard_map/all_to_all | solution.py:980
  149.4 11.7 %weight_grad_body.1 = (bf16[1024,512]{1,0:T(8,128)(2,1)}, bf16[1024,512]{1,0:T(8,128)(2,1)}, f32[1024,512]{1,0:T(8,128)}, f32[1024,512]{1,0:T(8,128)}) custom-call(bf16[1280,2048]{1,0:T(8,128)(2,1)} %get-tuple-element.429.hidden_ref, bf16[1280,2048]{1,0:T(8,128)(2,1)} %get-tuple-element.430.active_ref, bf16[1280,512]{1,0:T(8,128)(2,1)} %bitcast.15.got_ref, ...), custom_call_target="tpu_custom_call" | custom-call | flops 11500000256 | bytes 1000000 | tf_op jit(solution)/shard_map/weight_grad_body/pallas_call | solution.py:1075
  165.6 6.5 %sum_put_body.7 = (bf16[640,512]{1,0:T(8,128)(2,1)}, bf16[640,512]{1,0:T(8,128)(2,1)}) custom-call(s32[1]{0:T(128)} %constant.192.clone.1.base_ref, s32[8,2048]{1,0:T(8,128)S(1)} %get-tuple-element.832, f32[1024,512]{1,0:T(8,128)} %get-tuple-element.770.refs_0_, f32[1024,512]{1,0:T(8,128)} %get-tuple-element.771.refs_1_, ...), custom_call_target="tpu_custom_call" | custom-call | flops 4600000000 | bytes 1000000 | tf_op jit(solution)/shard_map/sum_put_body/pallas_call | solution.py:1002
  173.7 6.5 %sum_put_body.6 = (bf16[640,512]{1,0:T(8,128)(2,1)}, bf16[640,512]{1,0:T(8,128)(2,1)}) custom-call(s32[1]{0:T(128)} %constant.192.clone.1.base_ref, s32[8,2048]{1,0:T(8,128)S(1)} %get-tuple-element.832, f32[1024,512]{1,0:T(8,128)} %get-tuple-element.770.refs_0_, f32[1024,512]{1,0:T(8,128)} %get-tuple-element.771.refs_1_, ...), custom_call_target="tpu_custom_call" | custom-call | flops 4600000000 | bytes 1000000 | tf_op jit(solution)/shard_map/sum_put_body/pallas_call | solution.py:1002
  181.8 5.2 %middle_body.1 = (f32[512,512]{1,0:T(8,128)}, bf16[512,512]{1,0:T(8,128)(2,1)}, f32[512,128]{1,0:T(8,128)}, f32[8,512]{1,0:T(8,128)}, f32[8,512]{1,0:T(8,128)}) custom-call(bf16[1280,512]{1,0:T(8,128)(2,1)} %bitcast.22.back_ref, s32[512,8]{1,0:T(8,128)} %get-tuple-element.441.pos_ref, f32[512,512]{1,0:T(8,128)} %get-tuple-element.442.residual_ref, ...), custom_call_target="tpu_custom_call" | custom-call | flops 6899999744 | bytes 1000000 | tf_op jit(solution)/shard_map/middle_body/pallas_call | solution.py:1090
  189.8 14.5 %inner_body.1 = (bf16[512,512]{1,0:T(8,128)(2,1)}, f32[2,512,512]{2,1,0:T(8,128)}, bf16[544,512]{1,0:T(8,128)(2,1)}) custom-call(bf16[1024,1536]{1,0:T(8,128)(2,1)} %get-tuple-element.427.qkv_ref, bf16[512,512]{1,0:T(8,128)(2,1)} %get-tuple-element.444.out_grad_ref, f32[512,128]{1,0:T(8,128)} %get-tuple-element.445.lse_ref, ...), custom_call_target="tpu_custom_call" | custom-call | flops 17250000896 | bytes 1000000 | tf_op jit(solution)/shard_map/inner_body/pallas_call | solution.py:1104
  204.3 2.1 collective-permute-start.35
  206.4 4.8 %all-to-all-start.3 = ((bf16[32,40,512]{2,1,0:T(8,128)(2,1)}), bf16[32,40,512]{2,1,0:T(8,128)(2,1)}, u32[]{:S(2)}, u32[]{:S(2)}) async-start(bf16[32,40,512]{2,1,0:T(8,128)(2,1)} %bitcast.64), calls=%async_computation.3 | async-start | bytes 2621440 | tf_op jit(solution)/shard_map/all_to_all | solution.py:980
  211.2 11.5 %outer_body.1 = (bf16[512,512]{1,0:T(8,128)(2,1)}, bf16[512,512]{1,0:T(8,128)(2,1)}, bf16[512,512]{1,0:T(8,128)(2,1)}, bf16[560,512]{1,0:T(8,128)(2,1)}, f32[512,512]{1,0:T(8,128)}) custom-call(bf16[1024,1536]{1,0:T(8,128)(2,1)} %get-tuple-element.427.qkv_ref, bf16[512,512]{1,0:T(8,128)(2,1)} %collective-permute-done.33.out_grad_ref, f32[16,512]{1,0:T(8,128)} %copy-done.19, ...), custom_call_target="tpu_custom_call" | custom-call | flops 1000000 | bytes 1000 | tf_op jit(solution)/shard_map/outer_body/pallas_call | solution.py:1111
  226.4 4.9 %collective-permute-done.35.refs_3_ = bf16[640,512]{1,0:T(8,128)(2,1)} collective-permute-done((bf16[640,512]{1,0:T(8,128)(2,1)}, bf16[640,512]{1,0:T(8,128)(2,1)}, u32[]{:S(2)}, u32[]{:S(2)}) %collective-permute-start.35) | collective-permute-done | bytes 655392 | tf_op jit(solution)/shard_map/ppermute | solution.py:884
  231.3 5.8 %spread_body.2 = (bf16[544,512]{1,0:T(8,128)(2,1)}, bf16[544,512]{1,0:T(8,128)(2,1)}) custom-call(s32[1,2096]{1,0:T(1,128)} %broadcast_in_dim.33.pos_ref, bf16[512,512]{1,0:T(8,128)(2,1)} %get-tuple-element.460.refs_0_, bf16[512,512]{1,0:T(8,128)(2,1)} %get-tuple-element.461.refs_1_, bf16[512,512]{1,0:T(8,128)(2,1)} %get-tuple-element.462.refs_2_, ...), custom_call_target="tpu_custom_call" | custom-call | flops 1000000 | bytes 1000 | tf_op jit(solution)/shard_map/spread_body/pallas_call | solution.py:1126
  240.0 4.0 %tokens_body.1 = f32[512,512]{1,0:T(8,128)} custom-call(f32[512,512]{1,0:T(8,128)} %get-tuple-element.469.grad_normed_ref, bf16[512,512]{1,0:T(8,128)(2,1)} %bitcast.63, bf16[2080,512]{1,0:T(8,128)(2,1)} %unpack_body.3.w_ref.gains_ref, f32[512,512]{1,0:T(8,128)} %get-tuple-element.447.grad_ref), custom_call_target="tpu_custom_call" | custom-call | flops 1000000 | bytes 1000 | tf_op jit(solution)/shard_map/tokens_body/pallas_call | solution.py:1134
  244.0 5.8 %spread_body.3 = (bf16[544,512]{1,0:T(8,128)(2,1)}, bf16[544,512]{1,0:T(8,128)(2,1)}) custom-call(s32[1,2096]{1,0:T(1,128)} %broadcast_in_dim.33.pos_ref, bf16[512,512]{1,0:T(8,128)(2,1)} %get-tuple-element.460.refs_0_, bf16[512,512]{1,0:T(8,128)(2,1)} %get-tuple-element.461.refs_1_, bf16[512,512]{1,0:T(8,128)(2,1)} %get-tuple-element.462.refs_2_, ...), custom_call_target="tpu_custom_call" | custom-call | flops 1000000 | bytes 1000 | tf_op jit(solution)/shard_map/spread_body/pallas_call | solution.py:1126
  251.7 2.8 step_body.1
  264.4 3.7 %collective-permute-start.49 = (bf16[136,512]{1,0:T(8,128)(2,1)}, bf16[136,512]{1,0:T(8,128)(2,1)}, u32[]{:S(2)}, u32[]{:S(2)}) collective-permute-start(bf16[136,512]{1,0:T(8,128)(2,1)} %get-tuple-element.558), channel_id=1, source_target_pairs={{0,2},{1,3},{2,0},{3,1},{4,6},{5,7},{6,4},{7,5},{8,10},{9,11},{10,... | collective-permute-start | bytes 417800 | tf_op jit(solution)/shard_map/ppermute | solution.py:893
  269.6 4.2 %mixture_body.1 = bf16[512,512]{1,0:T(8,128)(2,1)} custom-call(bf16[1280,512]{1,0:T(8,128)(2,1)} %bitcast.25.result_ref, s32[512,8]{1,0:T(8,128)} %get-tuple-element.441.pos_ref, s32[512,2]{1,0:T(8,128)} %bitcast.59, f32[512,16]{1,0:T(8,128)} %get-tuple-element.478.prob_ref, f32[512,512]{1,0:T(8,128)} %get-tuple-element.442.residual_ref), custom_call_target="tpu_custom_call" | custom-call | flops 1000000 | bytes 1000 | tf_op jit(solution)/shard_map/mixture_body/pallas_call | solution.py:1148
  273.9 14.5 %adam_body.1 = (f32[2048,512]{1,0:T(8,128)}, f32[2048,512]{1,0:T(8,128)}, f32[2048,512]{1,0:T(8,128)}, f32[2048,512]{1,0:T(8,128)}) custom-call(s32[2048,8]{1,0:T(8,128)S(1)} %get-tuple-element.816, bf16[640,512]{1,0:T(8,128)(2,1)} %get-tuple-element.480.refs_0_, bf16[640,512]{1,0:T(8,128)(2,1)} %collective-permute-done.36.refs_1_, ...), custom_call_target="tpu_custom_call" | custom-call | flops 1000000 | bytes 1000 | tf_op jit(solution)/shard_map/adam_body/pallas_call | solution.py:1153
  (162 shorter events, 71.1 us)
Async XLA Ops:
  1.6 17.6 %collective-permute-start.15 = (bf16[136,512]{1,0:T(8,128)(2,1)S(1)}, bf16[136,512]{1,0:T(8,128)(2,1)S(1)}, u32[]{:S(2)}, u32[]{:S(2)}) collective-permute-start(bf16[136,512]{1,0:T(8,128)(2,1)S(1)} %pad.8), channel_id=1, source_target_pairs={{0,3},{1,0},{2,1},{3,2},{4,7},{5,4},{6,5},{7,6},{8,11},{9,8},{10,9... | collective-permute-start | bytes 417800 | tf_op jit(solution)/shard_map/ppermute | solution.py:893
  6.7 11.8 %collective-permute-start.14 = (bf16[136,512]{1,0:T(8,128)(2,1)S(1)}, bf16[136,512]{1,0:T(8,128)(2,1)S(1)}, u32[]{:S(2)}, u32[]{:S(2)}) collective-permute-start(bf16[136,512]{1,0:T(8,128)(2,1)S(1)} %pad.8), channel_id=1, source_target_pairs={{0,2},{1,3},{2,0},{3,1},{4,6},{5,7},{6,4},{7,5},{8,10},{9,11},{10,... | collective-permute-start | bytes 417800 | tf_op jit(solution)/shard_map/ppermute | solution.py:893
  6.7 9.9 %collective-permute-start.12 = (bf16[136,512]{1,0:T(8,128)(2,1)S(1)}, bf16[136,512]{1,0:T(8,128)(2,1)S(1)}, u32[]{:S(2)}, u32[]{:S(2)}) collective-permute-start(bf16[136,512]{1,0:T(8,128)(2,1)S(1)} %pad.8), channel_id=1, source_target_pairs={{0,1},{1,2},{2,3},{3,0},{4,5},{5,6},{6,7},{7,4},{8,9},{9,10},{10,1... | collective-permute-start | bytes 417800 | tf_op jit(solution)/shard_map/ppermute | solution.py:893
  7.7 20.0 %collective-permute-start.17 = (s32[1,512]{1,0:T(1,128)}, s32[1,512]{1,0:T(1,128)S(1)}, u32[]{:S(2)}, u32[]{:S(2)}) collective-permute-start(s32[1,512]{1,0:T(1,128)} %param.19), channel_id=1, source_target_pairs={{0,4},{4,0},{1,5},{5,1},{2,6},{6,2},{3,7},{7,3},{8,12},{12,8},{9,1... | collective-permute-start | bytes 6152 | tf_op jit(solution)/shard_map/ppermute | solution.py:876
  10.0 22.2 %collective-permute-start.11 = (bf16[512,512]{1,0:T(8,128)(2,1)}, bf16[512,512]{1,0:T(8,128)(2,1)S(1)}, u32[]{:S(2)}, u32[]{:S(2)}) collective-permute-start(bf16[512,512]{1,0:T(8,128)(2,1)} %bitcast.60), channel_id=1, source_target_pairs={{0,4},{4,0},{1,5},{5,1},{2,6},{6,2},{3,7},{7,3},{8,12},{12,8},{9,1... | collective-permute-start | bytes 1572872 | tf_op jit(solution)/shard_map/ppermute | solution.py:876
  16.6 11.7 %collective-permute-start.13 = (bf16[272,512]{1,0:T(8,128)(2,1)S(1)}, bf16[272,512]{1,0:T(8,128)(2,1)S(1)}, u32[]{:S(2)}, u32[]{:S(2)}) collective-permute-start(bf16[272,512]{1,0:T(8,128)(2,1)S(1)} %pad_maximum_fusion.9), channel_id=1, source_target_pairs={{0,16},{16,0},{8,24},{24,8},{1,17},{17,1},{9,25},{25,9},{2,18},{18... | collective-permute-start | bytes 835592 | tf_op jit(solution)/shard_map/ppermute | solution.py:880
  29.1 16.9 %collective-permute-start.20 = (bf16[544,512]{1,0:T(8,128)(2,1)}, bf16[544,512]{1,0:T(8,128)(2,1)}, u32[]{:S(2)}, u32[]{:S(2)}) collective-permute-start(bf16[544,512]{1,0:T(8,128)(2,1)} %pad_maximum_fusion.8.refs_0_), channel_id=1, source_target_pairs={{0,8},{8,0},{16,24},{24,16},{1,9},{9,1},{17,25},{25,17},{2,10},{10... | collective-permute-start | bytes 1671176 | tf_op jit(solution)/shard_map/ppermute | solution.py:888
  29.2 25.9 %collective-permute-start.18 = (bf16[544,512]{1,0:T(8,128)(2,1)}, bf16[544,512]{1,0:T(8,128)(2,1)}, u32[]{:S(2)}, u32[]{:S(2)}) collective-permute-start(bf16[544,512]{1,0:T(8,128)(2,1)} %pad_maximum_fusion.8.refs_0_), channel_id=1, source_target_pairs={{0,4},{4,0},{1,5},{5,1},{2,6},{6,2},{3,7},{7,3},{8,12},{12,8},{9,1... | collective-permute-start | bytes 1671176 | tf_op jit(solution)/shard_map/ppermute | solution.py:876
  30.4 15.7 %collective-permute-start.21 = (bf16[544,512]{1,0:T(8,128)(2,1)}, bf16[544,512]{1,0:T(8,128)(2,1)}, u32[]{:S(2)}, u32[]{:S(2)}) collective-permute-start(bf16[544,512]{1,0:T(8,128)(2,1)} %constant_dynamic-update-slice_fusion.2.refs_1_), channel_id=1, source_target_pairs={{0,8},{8,0},{16,24},{24,16},{1,9},{9,1},{17,25},{25,17},{2,10},{10... | collective-permute-start | bytes 1671176 | tf_op jit(solution)/shard_map/ppermute | solution.py:888
  30.6 24.4 %collective-permute-start.19 = (bf16[544,512]{1,0:T(8,128)(2,1)}, bf16[544,512]{1,0:T(8,128)(2,1)}, u32[]{:S(2)}, u32[]{:S(2)}) collective-permute-start(bf16[544,512]{1,0:T(8,128)(2,1)} %constant_dynamic-update-slice_fusion.2.refs_1_), channel_id=1, source_target_pairs={{0,16},{16,0},{8,24},{24,8},{1,17},{17,1},{9,25},{25,9},{2,18},{18... | collective-permute-start | bytes 1671176 | tf_op jit(solution)/shard_map/ppermute | solution.py:880
  36.5 39.2 %all-to-all-start = ((bf16[32,40,512]{2,1,0:T(8,128)(2,1)}), bf16[32,40,512]{2,1,0:T(8,128)(2,1)}, u32[]{:S(2)}, u32[]{:S(2)}) async-start(bf16[32,40,512]{2,1,0:T(8,128)(2,1)} %bitcast.66), calls=%async_computation | async-start | bytes 2621440 | tf_op jit(solution)/shard_map/all_to_all | solution.py:980
  55.0 10.7 %collective-permute-start.22 = (bf16[544,512]{1,0:T(8,128)(2,1)}, bf16[544,512]{1,0:T(8,128)(2,1)S(1)}, u32[]{:S(2)}, u32[]{:S(2)}) collective-permute-start(bf16[544,512]{1,0:T(8,128)(2,1)} %collective-permute-done.18.refs_0_), channel_id=1, source_target_pairs={{0,8},{8,0},{16,24},{24,16},{1,9},{9,1},{17,25},{25,17},{2,10},{10... | collective-permute-start | bytes 1671176 | tf_op jit(solution)/shard_map/ppermute | solution.py:888
  55.4 10.2 %collective-permute-start.23 = (bf16[544,512]{1,0:T(8,128)(2,1)}, bf16[544,512]{1,0:T(8,128)(2,1)}, u32[]{:S(2)}, u32[]{:S(2)}) collective-permute-start(bf16[544,512]{1,0:T(8,128)(2,1)} %collective-permute-done.19.refs_1_), channel_id=1, source_target_pairs={{0,8},{8,0},{16,24},{24,16},{1,9},{9,1},{17,25},{25,17},{2,10},{10... | collective-permute-start | bytes 1671176 | tf_op jit(solution)/shard_map/ppermute | solution.py:888
  62.2 32.6 %collective-permute-start.24 = (bf16[640,512]{1,0:T(8,128)(2,1)}, bf16[640,512]{1,0:T(8,128)(2,1)}, u32[]{:S(2)}, u32[]{:S(2)}) collective-permute-start(bf16[640,512]{1,0:T(8,128)(2,1)} %get-tuple-element.411), channel_id=1, source_target_pairs={{0,4},{4,0},{1,5},{5,1},{2,6},{6,2},{3,7},{7,3},{8,12},{12,8},{9,1... | collective-permute-start | bytes 1966088 | tf_op jit(solution)/shard_map/ppermute | solution.py:876
  64.0 30.7 %collective-permute-start.25 = (bf16[640,512]{1,0:T(8,128)(2,1)}, bf16[640,512]{1,0:T(8,128)(2,1)}, u32[]{:S(2)}, u32[]{:S(2)}) collective-permute-start(bf16[640,512]{1,0:T(8,128)(2,1)} %get-tuple-element.412), channel_id=1, source_target_pairs={{0,16},{16,0},{8,24},{24,8},{1,17},{17,1},{9,25},{25,9},{2,18},{18... | collective-permute-start | bytes 1966088 | tf_op jit(solution)/shard_map/ppermute | solution.py:880
  65.5 32.5 %collective-permute-start.26 = (bf16[640,512]{1,0:T(8,128)(2,1)}, bf16[640,512]{1,0:T(8,128)(2,1)}, u32[]{:S(2)}, u32[]{:S(2)}) collective-permute-start(bf16[640,512]{1,0:T(8,128)(2,1)} %get-tuple-element.413), channel_id=1, source_target_pairs={{0,20},{4,16},{8,28},{12,24},{16,4},{20,0},{24,12},{28,8},{1,21},{... | collective-permute-start | bytes 1966088 | tf_op jit(solution)/shard_map/ppermute | solution.py:884
  88.3 38.8 %all-to-all-start.1 = ((bf16[32,40,512]{2,1,0:T(8,128)(2,1)}), bf16[32,40,512]{2,1,0:T(8,128)(2,1)}, u32[]{:S(2)}, u32[]{:S(2)}) async-start(bf16[32,40,512]{2,1,0:T(8,128)(2,1)} %bitcast.65), calls=%async_computation.1 | async-start | bytes 2621440 | tf_op jit(solution)/shard_map/all_to_all | solution.py:980
  145.9 35.9 %all-to-all-start.2 = ((bf16[32,40,512]{2,1,0:T(8,128)(2,1)}), bf16[32,40,512]{2,1,0:T(8,128)(2,1)}, u32[]{:S(2)}, u32[]{:S(2)}) async-start(bf16[32,40,512]{2,1,0:T(8,128)(2,1)} %bitcast.67), calls=%async_computation.2 | async-start | bytes 2621440 | tf_op jit(solution)/shard_map/all_to_all | solution.py:980
  172.2 39.0 %collective-permute-start.36 = (bf16[640,512]{1,0:T(8,128)(2,1)}, bf16[640,512]{1,0:T(8,128)(2,1)}, u32[]{:S(2)}, u32[]{:S(2)}) collective-permute-start(bf16[640,512]{1,0:T(8,128)(2,1)} %get-tuple-element.437), channel_id=1, source_target_pairs={{0,4},{4,0},{1,5},{5,1},{2,6},{6,2},{3,7},{7,3},{8,12},{12,8},{9,1... | collective-permute-start | bytes 1966088 | tf_op jit(solution)/shard_map/ppermute | solution.py:876
  180.3 30.9 %collective-permute-start.37 = (bf16[640,512]{1,0:T(8,128)(2,1)}, bf16[640,512]{1,0:T(8,128)(2,1)}, u32[]{:S(2)}, u32[]{:S(2)}) collective-permute-start(bf16[640,512]{1,0:T(8,128)(2,1)} %get-tuple-element.438), channel_id=1, source_target_pairs={{0,16},{16,0},{8,24},{24,8},{1,17},{17,1},{9,25},{25,9},{2,18},{18... | collective-permute-start | bytes 1966088 | tf_op jit(solution)/shard_map/ppermute | solution.py:880
  187.7 16.6 %collective-permute-start.34 = (f32[16,512]{1,0:T(8,128)S(1)}, f32[16,512]{1,0:T(8,128)S(1)}, u32[]{:S(2)}, u32[]{:S(2)}) collective-permute-start(f32[16,512]{1,0:T(8,128)S(1)} %pad_maximum_fusion.10), channel_id=1, source_target_pairs={{0,4},{4,0},{1,5},{5,1},{2,6},{6,2},{3,7},{7,3},{8,12},{12,8},{9,1... | collective-permute-start | bytes 98312 | tf_op jit(solution)/shard_map/ppermute | solution.py:876
  188.3 16.0 %collective-permute-start.33 = (bf16[512,512]{1,0:T(8,128)(2,1)}, bf16[512,512]{1,0:T(8,128)(2,1)}, u32[]{:S(2)}, u32[]{:S(2)}) collective-permute-start(bf16[512,512]{1,0:T(8,128)(2,1)} %get-tuple-element.444.out_grad_ref), channel_id=1, source_target_pairs={{0,4},{4,0},{1,5},{5,1},{2,6},{6,2},{3,7},{7,3},{8,12},{12,8},{9,1... | collective-permute-start | bytes 1572872 | tf_op jit(solution)/shard_map/ppermute | solution.py:876
  204.3 26.9 %collective-permute-start.35 = (bf16[640,512]{1,0:T(8,128)(2,1)}, bf16[640,512]{1,0:T(8,128)(2,1)}, u32[]{:S(2)}, u32[]{:S(2)}) collective-permute-start(bf16[640,512]{1,0:T(8,128)(2,1)} %get-tuple-element.454), channel_id=1, source_target_pairs={{0,20},{4,16},{8,28},{12,24},{16,4},{20,0},{24,12},{28,8},{1,21},{... | collective-permute-start | bytes 1966088 | tf_op jit(solution)/shard_map/ppermute | solution.py:884
  206.4 63.2 %all-to-all-start.3 = ((bf16[32,40,512]{2,1,0:T(8,128)(2,1)}), bf16[32,40,512]{2,1,0:T(8,128)(2,1)}, u32[]{:S(2)}, u32[]{:S(2)}) async-start(bf16[32,40,512]{2,1,0:T(8,128)(2,1)} %bitcast.64), calls=%async_computation.3 | async-start | bytes 2621440 | tf_op jit(solution)/shard_map/all_to_all | solution.py:980
  237.1 14.7 %collective-permute-start.42 = (bf16[544,512]{1,0:T(8,128)(2,1)}, bf16[544,512]{1,0:T(8,128)(2,1)}, u32[]{:S(2)}, u32[]{:S(2)}) collective-permute-start(bf16[544,512]{1,0:T(8,128)(2,1)} %get-tuple-element.464), channel_id=1, source_target_pairs={{0,4},{4,0},{1,5},{5,1},{2,6},{6,2},{3,7},{7,3},{8,12},{12,8},{9,1... | collective-permute-start | bytes 1671176 | tf_op jit(solution)/shard_map/ppermute | solution.py:876
  238.4 13.4 %collective-permute-start.43 = (bf16[544,512]{1,0:T(8,128)(2,1)}, bf16[544,512]{1,0:T(8,128)(2,1)}, u32[]{:S(2)}, u32[]{:S(2)}) collective-permute-start(bf16[544,512]{1,0:T(8,128)(2,1)} %get-tuple-element.465), channel_id=1, source_target_pairs={{0,16},{16,0},{8,24},{24,8},{1,17},{17,1},{9,25},{25,9},{2,18},{18... | collective-permute-start | bytes 1671176 | tf_op jit(solution)/shard_map/ppermute | solution.py:880
  255.7 12.4 %collective-permute-start.44 = (bf16[272,512]{1,0:T(8,128)(2,1)}, bf16[272,512]{1,0:T(8,128)(2,1)S(1)}, u32[]{:S(2)}, u32[]{:S(2)}) collective-permute-start(bf16[272,512]{1,0:T(8,128)(2,1)} %get-tuple-element.474), channel_id=1, source_target_pairs={{0,16},{16,0},{8,24},{24,8},{1,17},{17,1},{9,25},{25,9},{2,18},{18... | collective-permute-start | bytes 835592 | tf_op jit(solution)/shard_map/ppermute | solution.py:880
  261.2 12.7 %collective-permute-start.48 = (bf16[640,512]{1,0:T(8,128)(2,1)}, bf16[640,512]{1,0:T(8,128)(2,1)}, u32[]{:S(2)}, u32[]{:S(2)}) collective-permute-start(bf16[640,512]{1,0:T(8,128)(2,1)} %pad_maximum_fusion.7), channel_id=1, source_target_pairs={{0,8},{8,0},{16,24},{24,16},{1,9},{9,1},{17,25},{25,17},{2,10},{10... | collective-permute-start | bytes 1966088 | tf_op jit(solution)/shard_map/ppermute | solution.py:888
  262.1 11.8 %collective-permute-start.47 = (bf16[640,512]{1,0:T(8,128)(2,1)}, bf16[640,512]{1,0:T(8,128)(2,1)}, u32[]{:S(2)}, u32[]{:S(2)}) collective-permute-start(bf16[640,512]{1,0:T(8,128)(2,1)} %pad_maximum_fusion.6), channel_id=1, source_target_pairs={{0,8},{8,0},{16,24},{24,16},{1,9},{9,1},{17,25},{25,17},{2,10},{10... | collective-permute-start | bytes 1966088 | tf_op jit(solution)/shard_map/ppermute | solution.py:888
  263.4 25.0 %collective-permute-start.50 = (bf16[136,512]{1,0:T(8,128)(2,1)}, bf16[136,512]{1,0:T(8,128)(2,1)}, u32[]{:S(2)}, u32[]{:S(2)}) collective-permute-start(bf16[136,512]{1,0:T(8,128)(2,1)} %get-tuple-element.557), channel_id=1, source_target_pairs={{0,1},{1,2},{2,3},{3,0},{4,5},{5,6},{6,7},{7,4},{8,9},{9,10},{10,1... | collective-permute-start | bytes 417800 | tf_op jit(solution)/shard_map/ppermute | solution.py:893
  264.4 24.0 %collective-permute-start.49 = (bf16[136,512]{1,0:T(8,128)(2,1)}, bf16[136,512]{1,0:T(8,128)(2,1)}, u32[]{:S(2)}, u32[]{:S(2)}) collective-permute-start(bf16[136,512]{1,0:T(8,128)(2,1)} %get-tuple-element.558), channel_id=1, source_target_pairs={{0,2},{1,3},{2,0},{3,1},{4,6},{5,7},{6,4},{7,5},{8,10},{9,11},{10,... | collective-permute-start | bytes 417800 | tf_op jit(solution)/shard_map/ppermute | solution.py:893
  268.8 19.5 %collective-permute-start.46 = (bf16[136,512]{1,0:T(8,128)(2,1)}, bf16[136,512]{1,0:T(8,128)(2,1)}, u32[]{:S(2)}, u32[]{:S(2)}) collective-permute-start(bf16[136,512]{1,0:T(8,128)(2,1)} %get-tuple-element.559), channel_id=1, source_target_pairs={{0,3},{1,0},{2,1},{3,2},{4,7},{5,4},{6,5},{7,6},{8,11},{9,8},{10,9... | collective-permute-start | bytes 417800 | tf_op jit(solution)/shard_map/ppermute | solution.py:893
  (30 other events, 240.1 us)
